TPU v7x, 32 devices: a whole 2x2x4 slice. The times are simulated.
32 devices in a mesh: fsdp: 8 (over y, x, core), tp: 4 (over z).
Axes of the slice: x: 2, y: 2, z: 4, core: 2. Of those that a mesh axis runs over, the one named last changes fastest.
Arguments:
- states: bfloat16 [16384, 2048], P(('fsdp', 'tp')), may hold values from -6 to 6
- lengths: int32 [8, 4], P('fsdp'), may hold values from 1 to 2045, as said below
- padding: int32 [8, 2048], P('fsdp'), may hold values from 0 to 1, as said below
- teacher: bfloat16 [16384, 2048], P(('fsdp', 'tp')), may hold values from -6 to 6
- norm_attn: float32 [2048], replicated, may hold values from 0.25 to 1.75
- w_query: bfloat16 [2048, 2048], P('fsdp', 'tp'), may hold values from -0.125 to 0.125
- w_key: bfloat16 [2048, 1024], P('fsdp', 'tp'), may hold values from -0.125 to 0.125
- w_value: bfloat16 [2048, 1024], P('fsdp', 'tp'), may hold values from -0.125 to 0.125
- norm_query: float32 [128], replicated, may hold values from 0.25 to 1.75
- norm_key: float32 [128], replicated, may hold values from 0.25 to 1.75
- w_out: bfloat16 [2048, 2048], P('tp', 'fsdp'), may hold values from -0.75 to 0.75
- norm_mlp: float32 [2048], replicated, may hold values from 0.25 to 1.75
- w_gate: bfloat16 [2048, 6144], P('fsdp', 'tp'), may hold values from -0.125 to 0.125
- w_up: bfloat16 [2048, 6144], P('fsdp', 'tp'), may hold values from -0.125 to 0.125
- w_down: bfloat16 [6144, 2048], P('tp', 'fsdp'), may hold values from -0.078125 to 0.078125
Outputs:
- outputs: float32 [16384, 2048], P(('fsdp', 'tp'))
- loss: float32 [], replicated
- grad_x: float32 [16384, 2048], P(('fsdp', 'tp'))
- grad_norm_attn: float32 [2048], replicated
- grad_w_query: float32 [2048, 2048], P('fsdp', 'tp')
- grad_w_key: float32 [2048, 1024], P('fsdp', 'tp')
- grad_w_value: float32 [2048, 1024], P('fsdp', 'tp')
- grad_norm_query: float32 [128], replicated
- grad_norm_key: float32 [128], replicated
- grad_w_out: float32 [2048, 2048], P('tp', 'fsdp')
- grad_norm_mlp: float32 [2048], replicated
- grad_w_gate: float32 [2048, 6144], P('fsdp', 'tp')
- grad_w_up: float32 [2048, 6144], P('fsdp', 'tp')
- grad_w_down: float32 [6144, 2048], P('tp', 'fsdp')
Inputs may be any that keep to these rules, and one draw needn't show every extreme that they name: `lengths`: each row sums to 2048; each entry is at least 1, so none exceeds 2048 - 3. `padding`: each row is 1 on a leading run of 768 or more positions and 0 after it.
All inputs are finite; a program needn't handle non-finite values.
Results may differ from a plain program's by a relative error of at most 0.0085.
The roundings to bfloat16 on the way count: a program that leaves them out, or rounds other values in their place, can miss the bound.
Values may be sent and summed in bfloat16 or wider, within the bound.
A program may use at most 320 MiB of HBM per device.

v0:
```python
import jax
import jax.numpy as jnp
from jax import lax
from jax.sharding import PartitionSpec as P

D = 2048
HD = 128
WINDOW = 1024


EPS = 1e-06
THETA = 1000000.0
NEG = -1e30


def normalize_rows(values):
    factor = lax.rsqrt(jnp.mean(values * values, axis=-1, keepdims=True) + EPS)
    return (values * factor, factor)


def norm_back(grad, normed, factor, gain):
    scaled = grad * gain
    return factor * (scaled - normed * jnp.mean(scaled * normed, axis=-1, keepdims=True))


def rotate(values, cosine, sine):
    half = values.shape[-1] // 2
    first, second = (values[..., :half], values[..., half:])
    return jnp.concatenate(
        [first * cosine - second * sine, second * cosine + first * sine], axis=-1
    )


def rotate_back(grad, cosine, sine):
    half = grad.shape[-1] // 2
    first, second = (grad[..., :half], grad[..., half:])
    return jnp.concatenate(
        [first * cosine + second * sine, second * cosine - first * sine], axis=-1
    )


def doc_tables(length_row, number):
    places = jnp.arange(number, dtype=jnp.int32)
    ends = jnp.cumsum(length_row)
    passed = places[:, None] >= ends[None, :]
    doc_ids = jnp.sum(passed.astype(jnp.int32), axis=1)
    starts = jnp.sum(jnp.where(passed, length_row[None, :], 0), axis=1)
    return (doc_ids, places - starts)


def rope_tables(positions):
    freqs = THETA ** (-(jnp.arange(HD // 2).astype(jnp.float32) * 2.0 / HD))
    angles = positions.astype(jnp.float32)[:, None] * freqs[None, :]
    return (jnp.cos(angles)[:, None, :], jnp.sin(angles)[:, None, :])


def allowed(first, rows, doc_ids, key_live):
    query_idx = first + jnp.arange(rows, dtype=jnp.int32)
    key_idx = jnp.arange(doc_ids.shape[0], dtype=jnp.int32)
    query_doc = lax.dynamic_slice_in_dim(doc_ids, first, rows, 0)
    causal = (key_idx[None, :] <= query_idx[:, None]) & (
        query_idx[:, None] - key_idx[None, :] < WINDOW
    )
    same_doc = query_doc[:, None] == doc_ids[None, :]
    live_keys = (key_live[None, :] == 1) | (key_idx[None, :] == query_idx[:, None])
    return causal & same_doc & live_keys


def gather_rows(values):
    return lax.all_gather(values, "tp", axis=0, tiled=True)


def sum_rows(partial_sum):
    return lax.psum_scatter(partial_sum, "tp", scatter_dimension=0, tiled=True)


def contract_last(left, right):
    return lax.dot_general(
        left, right, (((1,), (1,)), ((), ())), preferred_element_type=jnp.float32
    )


def contract_first(left, right):
    return lax.dot_general(
        left, right, (((0,), (0,)), ((), ())), preferred_element_type=jnp.float32
    )


def project_in(whole_in, joined):
    result = jnp.dot(
        whole_in,
        lax.all_gather(joined, "fsdp", axis=0, tiled=True),
        preferred_element_type=jnp.float32,
    )
    return (result, joined)


def project_out(hidden, weight):
    result = jnp.dot(
        hidden,
        lax.all_gather(weight, "fsdp", axis=1, tiled=True),
        preferred_element_type=jnp.float32,
    )
    return (result, weight)


def back_out(grad_whole, weight):
    return contract_last(grad_whole, lax.all_gather(weight, "fsdp", axis=1, tiled=True))


def back_in(grad_joined, joined):
    return contract_last(grad_joined, lax.all_gather(joined, "fsdp", axis=0, tiled=True))


def weight_rows_grad(whole_in, grad_joined, shard_rows):

    def term(start, span_rows):
        return contract_first(whole_in, grad_joined)

    return lax.psum_scatter(
        term(jnp.int32(0), shard_rows * lax.axis_size("fsdp")),
        "fsdp",
        scatter_dimension=0,
        tiled=True,
    )


def weight_cols_grad(grad_whole, hidden, shard_cols):

    def term(start, span_rows):
        return contract_first(grad_whole, hidden)

    return lax.psum_scatter(
        term(jnp.int32(0), shard_cols * lax.axis_size("fsdp")),
        "fsdp",
        scatter_dimension=0,
        tiled=True,
    ).T


def shards(
    states,
    lengths,
    padding,
    teacher,
    norm_attn,
    w_query,
    w_key,
    w_value,
    norm_query,
    norm_key,
    w_out,
    norm_mlp,
    w_gate,
    w_up,
    w_down,
):
    local_rows = states.shape[0]
    seq_len = local_rows * lax.axis_size("tp")
    offset = lax.axis_index("tp") * local_rows
    doc_ids, positions = doc_tables(lengths[0], seq_len)
    cosine, sine = rope_tables(positions)
    key_live = padding[0]
    mine_live = lax.dynamic_slice_in_dim(key_live, offset, local_rows, 0).astype(jnp.float32)
    block = min(512, seq_len)
    blocks = seq_len // block
    scale = HD ** (-0.5)
    heads_dev = w_query.shape[1] // HD
    groups_dev = w_key.shape[1] // HD
    group_size = heads_dev // groups_dev
    width_query = w_query.shape[1]
    width_key = w_key.shape[1]
    hidden_units = w_gate.shape[1]
    inputs = states.astype(jnp.float32)
    normed_one, factor_one = normalize_rows(inputs)
    whole_one = gather_rows((normed_one * norm_attn).astype(jnp.bfloat16))
    joined_attn = jnp.concatenate((w_query, w_key, w_value), axis=1)
    projected, gathered_attn = project_in(whole_one, joined_attn)
    query_raw = projected[:, :width_query].reshape(seq_len, heads_dev, HD)
    key_raw = projected[:, width_query : width_query + width_key].reshape(seq_len, groups_dev, HD)
    value_rows = (
        projected[:, width_query + width_key :]
        .astype(jnp.bfloat16)
        .reshape(seq_len, groups_dev, HD)
    )
    query_normed, query_factor = normalize_rows(query_raw)
    key_normed, key_factor = normalize_rows(key_raw)
    query_rot = (
        rotate(query_normed * norm_query, cosine, sine)
        .astype(jnp.bfloat16)
        .reshape(seq_len, groups_dev, group_size, HD)
    )
    key_rot = rotate(key_normed * norm_key, cosine, sine).astype(jnp.bfloat16)

    def block_scores(index):
        first = index * block
        query_rows = lax.dynamic_slice_in_dim(query_rot, first, block, 0)
        scores = (
            jnp.einsum("qkgd,tkd->kgqt", query_rows, key_rot, preferred_element_type=jnp.float32)
            * scale
        )
        keep_mask = allowed(first, block, doc_ids, key_live)
        return (query_rows, jnp.where(keep_mask[None, None], scores, NEG))

    def attend(index):
        query_rows, scores = block_scores(index)
        row_max = jnp.max(scores, axis=-1, keepdims=True)
        exp_scores = jnp.exp(scores - row_max)
        row_total = jnp.sum(exp_scores, axis=-1, keepdims=True)
        probabilities = (exp_scores / row_total).astype(jnp.bfloat16)
        mixed = jnp.einsum(
            "kgqt,tkd->qkgd", probabilities, value_rows, preferred_element_type=jnp.float32
        )
        return (
            mixed.astype(jnp.bfloat16).reshape(block, heads_dev * HD),
            (row_max + jnp.log(row_total))[..., 0],
        )

    attended, log_sums = lax.map(attend, jnp.arange(blocks, dtype=jnp.int32))
    attended = attended.reshape(seq_len, heads_dev * HD)
    attn_part, gathered_out = project_out(attended, w_out)
    hidden_one = inputs + sum_rows(attn_part)
    normed_two, factor_two = normalize_rows(hidden_one)
    whole_two = gather_rows((normed_two * norm_mlp).astype(jnp.bfloat16))
    joined_mlp = jnp.concatenate((w_gate, w_up), axis=1)
    gate_up, gathered_mlp = project_in(whole_two, joined_mlp)
    gate_rows = gate_up[:, :hidden_units]
    up_rows = gate_up[:, hidden_units:]
    sigmoid_gate = jax.nn.sigmoid(gate_rows)
    silu_gate = gate_rows * sigmoid_gate
    product = (silu_gate * up_rows).astype(jnp.bfloat16)
    down_part, gathered_down = project_out(product, w_down)
    outputs = hidden_one + sum_rows(down_part)
    errors = (outputs - teacher.astype(jnp.float32)) * mine_live[:, None]
    count_all, squares_all = lax.psum(
        (jnp.sum(mine_live), jnp.sum(errors * errors)), ("fsdp", "tp")
    )
    loss = squares_all / (count_all * D)
    grad_out = errors * (2.0 / (count_all * D))
    grad_down_whole = gather_rows(grad_out.astype(jnp.bfloat16))
    grad_product = back_out(grad_down_whole, w_down)
    grad_w_down = weight_cols_grad(grad_down_whole, product, w_down.shape[1])
    grad_gate = (
        grad_product * up_rows * sigmoid_gate * (1.0 + gate_rows * (1.0 - sigmoid_gate))
    ).astype(jnp.bfloat16)
    grad_up = (grad_product * silu_gate).astype(jnp.bfloat16)
    grad_gate_up = jnp.concatenate((grad_gate, grad_up), axis=1)
    grad_mid = sum_rows(back_in(grad_gate_up, joined_mlp))
    grad_joined_mlp = weight_rows_grad(whole_two, grad_gate_up, w_gate.shape[0])
    grad_w_gate = grad_joined_mlp[:, :hidden_units]
    grad_w_up = grad_joined_mlp[:, hidden_units:]
    grad_norm_mlp = jnp.sum(grad_mid * normed_two, axis=0)
    grad_hidden = grad_out + norm_back(grad_mid, normed_two, factor_two, norm_mlp)
    grad_attn_whole = gather_rows(grad_hidden.astype(jnp.bfloat16))
    grad_attended = back_out(grad_attn_whole, w_out).astype(jnp.bfloat16)
    grad_w_out = weight_cols_grad(grad_attn_whole, attended, w_out.shape[1])
    grad_heads = grad_attended.reshape(seq_len, groups_dev, group_size, HD)

    def attend_back(carry, index):
        grad_key_sum, grad_value_sum = carry
        query_rows, scores = block_scores(index)
        probabilities = jnp.exp(scores - log_sums[index][..., None])
        grad_rows = lax.dynamic_slice_in_dim(grad_heads, index * block, block, 0)
        grad_probs = jnp.einsum(
            "qkgd,tkd->kgqt", grad_rows, value_rows, preferred_element_type=jnp.float32
        )
        centre = jnp.sum(probabilities * grad_probs, axis=-1, keepdims=True)
        grad_scores = (probabilities * (grad_probs - centre)).astype(jnp.bfloat16)
        grad_query = (
            jnp.einsum("kgqt,tkd->qkgd", grad_scores, key_rot, preferred_element_type=jnp.float32)
            * scale
        )
        grad_key_sum = (
            grad_key_sum
            + jnp.einsum(
                "kgqt,qkgd->tkd", grad_scores, query_rows, preferred_element_type=jnp.float32
            )
            * scale
        )
        grad_value_sum = grad_value_sum + jnp.einsum(
            "kgqt,qkgd->tkd",
            probabilities.astype(jnp.bfloat16),
            grad_rows,
            preferred_element_type=jnp.float32,
        )
        return ((grad_key_sum, grad_value_sum), grad_query)

    empty_keys = jnp.zeros((seq_len, groups_dev, HD), jnp.float32)
    (grad_key_rot, grad_value), grad_query_rot = lax.scan(
        attend_back, (empty_keys, empty_keys), jnp.arange(blocks, dtype=jnp.int32)
    )
    grad_query_rot = grad_query_rot.reshape(seq_len, heads_dev, HD)
    grad_query_normed = rotate_back(grad_query_rot, cosine, sine)
    grad_key_normed = rotate_back(grad_key_rot, cosine, sine)
    grad_norm_query = jnp.sum(grad_query_normed * query_normed, axis=(0, 1))
    grad_norm_key = jnp.sum(grad_key_normed * key_normed, axis=(0, 1))
    grad_query_raw = norm_back(grad_query_normed, query_normed, query_factor, norm_query)
    grad_key_raw = norm_back(grad_key_normed, key_normed, key_factor, norm_key)
    grad_joined_attn = jnp.concatenate(
        (
            grad_query_raw.reshape(seq_len, width_query),
            grad_key_raw.reshape(seq_len, width_key),
            grad_value.reshape(seq_len, width_key),
        ),
        axis=1,
    ).astype(jnp.bfloat16)
    grad_low = sum_rows(back_in(grad_joined_attn, joined_attn))
    grad_joined_weights = weight_rows_grad(whole_one, grad_joined_attn, w_query.shape[0])
    grad_w_query = grad_joined_weights[:, :width_query]
    grad_w_key = grad_joined_weights[:, width_query : width_query + width_key]
    grad_w_value = grad_joined_weights[:, width_query + width_key :]
    grad_norm_attn = jnp.sum(grad_low * normed_one, axis=0)
    grad_input = grad_hidden + norm_back(grad_low, normed_one, factor_one, norm_attn)
    grad_norm_attn, grad_norm_query, grad_norm_key, grad_norm_mlp = lax.psum(
        (grad_norm_attn, grad_norm_query, grad_norm_key, grad_norm_mlp), ("fsdp", "tp")
    )
    return (
        outputs,
        loss,
        grad_input,
        grad_norm_attn,
        grad_w_query,
        grad_w_key,
        grad_w_value,
        grad_norm_query,
        grad_norm_key,
        grad_w_out,
        grad_norm_mlp,
        grad_w_gate,
        grad_w_up,
        grad_w_down,
    )


def solution(mesh):
    in_specs = (
        P(("fsdp", "tp"), None),
        P("fsdp", None),
        P("fsdp", None),
        P(("fsdp", "tp"), None),
        P(),
        P("fsdp", "tp"),
        P("fsdp", "tp"),
        P("fsdp", "tp"),
        P(),
        P(),
        P("tp", "fsdp"),
        P(),
        P("fsdp", "tp"),
        P("fsdp", "tp"),
        P("tp", "fsdp"),
    )
    out_specs = (
        P(("fsdp", "tp"), None),
        P(),
        P(("fsdp", "tp"), None),
        P(),
        P("fsdp", "tp"),
        P("fsdp", "tp"),
        P("fsdp", "tp"),
        P(),
        P(),
        P("tp", "fsdp"),
        P(),
        P("fsdp", "tp"),
        P("fsdp", "tp"),
        P("tp", "fsdp"),
    )
    return jax.shard_map(shards, mesh=mesh, in_specs=in_specs, out_specs=out_specs, check_vma=False)
```

profile of v0, /device:TPU:0, one launch (start us, length us, event | category | flops | bytes accessed | tf_op | source)
XLA Modules:
  0.0 2604.2 jit_solution(1656139187036314120)
XLA Ops:
  19.4 30.5 %all-gather.11.cloned.1.call-done = bf16[2048,1024]{1,0:T(8,128)(2,1)} async-done(((bf16[256,1024]{1,0:T(8,128)(2,1)}), bf16[2048,1024]{1,0:T(8,128)(2,1)}) %all-gather.11.cloned.1.call-update) | async-done | bytes 4194320 | tf_op jit(solution)/shard_map/all_gather | solution.py:92
  49.9 151.8 %all-gather.9.cloned.1.call-done = bf16[2048,2048]{1,0:T(8,128)(2,1)} async-done(((bf16[512,2048]{1,0:T(8,128)(2,1)}), bf16[2048,2048]{1,0:T(8,128)(2,1)}) %all-gather.9.cloned.1.call-update) | async-done | bytes 8388624 | tf_op jit(solution)/shard_map/all_gather | solution.py:70
  238.9 79.2 %while.27 = (s32[]{:T(128)}, bf16[4,512,512]{2,1,0:T(8,128)(2,1)}, f32[4,2,2,512]{3,2,1,0:T(2,128)}, s32[4]{0:T(128)S(1)}, s32[2048]{0:T(1024)S(1)}, /*index=5*/...) while((s32[]{:T(128)}, bf16[4,512,512]{2,1,0:T(8,128)(2,1)}, ...), condition=%wide.region_9.10_spmd, body=%wide.region_6.9_spmd.sunk | while | flops 2207515136 | bytes 59866304 | solution.py:219
  335.0 274.7 %reduce-scatter.9.cloned.1.call-done = f32[512,2048]{1,0:T(8,128)} async-done(((f32[2048,2048]{1,0:T(8,128)}), f32[512,2048]{1,0:T(8,128)}) %reduce-scatter.9.cloned.1.call-update) | async-done | bytes 4194320 | tf_op jit(solution)/shard_map/reduce_scatter | solution.py:74
  617.1 68.0 %all-gather.17.cloned.1.call-done = bf16[2048,3072]{1,0:T(8,128)(2,1)} async-done(((bf16[256,3072]{1,0:T(8,128)(2,1)}), bf16[2048,3072]{1,0:T(8,128)(2,1)}) %all-gather.17.cloned.1.call-update) | async-done | bytes 12582928 | tf_op jit(solution)/shard_map/all_gather | solution.py:92
  685.1 151.7 %all-gather.15.cloned.1.call-done = bf16[2048,2048]{1,0:T(8,128)(2,1)} async-done(((bf16[512,2048]{1,0:T(8,128)(2,1)}), bf16[2048,2048]{1,0:T(8,128)(2,1)}) %all-gather.15.cloned.1.call-update) | async-done | bytes 8388624 | tf_op jit(solution)/shard_map/all_gather | solution.py:70
  836.8 30.7 %fusion.85 = f32[2048,3072]{1,0:T(8,128)S(1)} fusion(bf16[2048,2048]{1,0:T(8,128)(2,1)} %all-gather.15.cloned.1.call-done, bf16[2048,3072]{1,0:T(8,128)(2,1)} %all-gather.17.cloned.1.call-done), kind=kOutput, calls=%fused_computation.171 | convolution fusion | flops 25769803776 | bytes 46137344 | tf_op jit(solution)/shard_map/dot_general | solution.py:90
  883.8 19.4 fusion.86
  903.9 41.8 %psum.43 = f32[]{:T(128)} all-reduce(f32[]{:T(128)} %get-tuple-element.369), channel_id=1, replica_groups=mesh['fsdp'=8,'tp'=4] {'fsdp','tp'}, use_global_device_ids=true, to_apply=%region_16.17 | all-reduce | flops 1 | bytes 8 | tf_op jit(solution)/shard_map/psum | solution.py:235
  946.4 238.3 %reduce-scatter.11.cloned.1.call-done = f32[512,2048]{1,0:T(8,128)} async-done(((f32[2048,2048]{1,0:T(8,128)}), f32[512,2048]{1,0:T(8,128)}) %reduce-scatter.11.cloned.1.call-update) | async-done | bytes 4194320 | tf_op jit(solution)/shard_map/reduce_scatter | solution.py:74
  1192.7 150.3 %all-gather.21.cloned.1.call-done = bf16[2048,2048]{1,0:T(8,128)(2,1)} async-done(((bf16[512,2048]{1,0:T(8,128)(2,1)}), bf16[2048,2048]{1,0:T(8,128)(2,1)}) %all-gather.21.cloned.1.call-update) | async-done | bytes 8388624 | tf_op jit(solution)/shard_map/all_gather | solution.py:70
  1343.1 28.7 %multiply_convert_fusion.1 = (bf16[2048,1536]{1,0:T(8,128)(2,1)}, bf16[2048,1536]{1,0:T(8,128)(2,1)}) fusion(f32[2048,3072]{1,0:T(8,128)} %copy-done.10, bf16[2048,2048]{1,0:T(8,128)(2,1)} %all-gather.21.cloned.1.call-done, bf16[1536,2048]{1,0:T(8,128)(2,1)} %all-gather.19.cloned.1.call-done), kind=kOutput, calls=%fused_computation.72 | convolution fusion | flops 12925796352 | bytes 52428800 | tf_op jit(solution)/shard_map/dot_general | solution.py:78
  1371.8 34.3 %fusion.55 = f32[2048,2048]{1,0:T(8,128)} fusion(bf16[2048,3072]{1,0:T(8,128)(2,1)} %all-gather.17.cloned.1.call-done, bf16[2048,1536]{1,0:T(8,128)(2,1)} %get-tuple-element.378, bf16[2048,1536]{1,0:T(8,128)(2,1)} %get-tuple-element.377), kind=kOutput, calls=%fused_computation.77 | convolution fusion | flops 25794969600 | bytes 41943040 | tf_op jit(solution)/shard_map/dot_general | solution.py:78
  1406.6 278.2 %reduce-scatter.13.cloned.1.call-done = f32[512,2048]{1,0:T(8,128)} async-done(((f32[2048,2048]{1,0:T(8,128)}), f32[512,2048]{1,0:T(8,128)}) %reduce-scatter.13.cloned.1.call-update) | async-done | bytes 4194320 | tf_op jit(solution)/shard_map/reduce_scatter | solution.py:74
  1697.6 19.0 fusion.88
  1716.6 34.0 %fusion.54 = f32[2048,3072]{1,0:T(8,128)} fusion(bf16[2048,2048]{1,0:T(8,128)(2,1)} %all-gather.15.cloned.1.call-done, bf16[2048,1536]{1,0:T(8,128)(2,1)} %get-tuple-element.378, bf16[2048,1536]{1,0:T(8,128)(2,1)} %get-tuple-element.377), kind=kOutput, calls=%fused_computation.76 | convolution fusion | flops 25794969600 | bytes 46137344 | tf_op jit(solution)/shard_map/dot_general | solution.py:84
  1753.7 94.3 %all-gather.23.cloned.1.call-done = bf16[2048,2048]{1,0:T(8,128)(2,1)} async-done(((bf16[512,2048]{1,0:T(8,128)(2,1)}), bf16[2048,2048]{1,0:T(8,128)(2,1)}) %all-gather.23.cloned.1.call-update) | async-done | bytes 8388624 | tf_op jit(solution)/shard_map/all_gather | solution.py:70
  1871.1 280.2 %while.28 = (s32[]{:T(128)}, f32[2048,2,128]{0,2,1:T(8,128)S(1)}, f32[2048,2,128]{0,2,1:T(8,128)}, f32[4,512,2,2,128]{4,1,0,3,2:T(8,128)}, s32[4]{0:T(128)S(1)},...) while((s32[]{:T(128)}, f32[2048,2,128]{0,2,1:T(8,128)S(1)}, ...), condition=%wide.region_21.22_spmd.clone, body=%wide.region_19.21_spmd.clone.sunk | while | flops 5443944960 | bytes 182541136 | solution.py:289
  1954.3 19.5 fusion.144
  1973.8 14.6 fusion.145
  2192.9 15.0 fusion.74
  2217.2 44.2 %reduce-scatter.17.cloned.1.call-done = f32[256,1024]{1,0:T(8,128)} async-done(((f32[2048,1024]{1,0:T(8,128)}), f32[256,1024]{1,0:T(8,128)}) %reduce-scatter.17.cloned.1.call-update) | async-done | bytes 1048592 | tf_op jit(solution)/shard_map/reduce_scatter | solution.py:120
  2265.1 278.9 %reduce-scatter.15.cloned.1.call-done = f32[512,2048]{1,0:T(8,128)} async-done(((f32[2048,2048]{1,0:T(8,128)}), f32[512,2048]{1,0:T(8,128)}) %reduce-scatter.15.cloned.1.call-update) | async-done | bytes 4194320 | tf_op jit(solution)/shard_map/reduce_scatter | solution.py:74
  2547.4 41.5 %all-reduce = (f32[]{:T(128)}, f32[2048]{0:T(1024)}, f32[128]{0:T(128)}, f32[128]{0:T(128)}, f32[2048]{0:T(1024)}) all-reduce(f32[]{:T(128)} %get-tuple-element.383, f32[2048]{0:T(1024)S(1)} %get-tuple-element.312, f32[128]{0:T(128)S(1)} %bitcast_reduce_fusion.1, ...), channel_id=1, replica_groups=mesh['fsdp'=8,'tp'=4] {'fsdp','tp'}, use_global_device_ids=true, to_apply=%region_14.15 | all-reduce | flops 4353 | bytes 34824 | tf_op jit(solution)/shard_map/psum | solution.py:235
  (319 shorter events, 513.1 us)
Async XLA Ops:
  7.2 42.7 %all-gather.11.cloned.1.call-start = ((), (), s32[]{:S(2)}) async-start(), calls=%async_computation.9 | async-start | bytes 4718592 | tf_op jit(solution)/shard_map/all_gather | solution.py:92
  9.4 192.4 %all-gather.9.cloned.1.call-start = ((), (), s32[]{:S(2)}) async-start(), calls=%async_computation.8 | async-start | bytes 10485760 | tf_op jit(solution)/shard_map/all_gather | solution.py:70
  14.7 303.4 %all-gather.13.cloned.1.call-start = ((), (), s32[]{:S(2)}) async-start(), calls=%async_computation.10 | async-start | bytes 2359296 | tf_op jit(solution)/shard_map/all_gather | solution.py:101
  15.4 594.3 %reduce-scatter.9.cloned.1.call-start = ((), (), s32[]{:S(2)}) async-start(), calls=%async_computation.11 | async-start | bytes 20971520 | tf_op jit(solution)/shard_map/reduce_scatter | solution.py:74
  331.0 278.8 %copy-start.5 = (bf16[512,2048]{1,0:T(8,128)(2,1)S(1)}, bf16[512,2048]{1,0:T(8,128)(2,1)}, u32[]{:S(2)}) copy-start(bf16[512,2048]{1,0:T(8,128)(2,1)} %param.19) | copy-start | bytes 6291460
  331.0 354.1 %all-gather.17.cloned.1.call-start = ((), (), s32[]{:S(2)}) async-start(), calls=%async_computation.13 | async-start | bytes 14155776 | tf_op jit(solution)/shard_map/all_gather | solution.py:92
  334.6 280.0 %copy-start.34 = (f32[2048]{0:T(1024)S(1)}, f32[2048]{0:T(1024)}, u32[]{:S(2)}) copy-start(f32[2048]{0:T(1024)} %param.30) | copy-start | bytes 24580
  334.6 502.2 %all-gather.15.cloned.1.call-start = ((), (), s32[]{:S(2)}) async-start(), calls=%async_computation.12 | async-start | bytes 10485760 | tf_op jit(solution)/shard_map/all_gather | solution.py:70
  616.3 267.5 %all-gather.19.cloned.1.call-start = ((), (), s32[]{:S(2)}) async-start(), calls=%async_computation.14 | async-start | bytes 7077888 | tf_op jit(solution)/shard_map/all_gather | solution.py:101
  617.1 567.6 %reduce-scatter.11.cloned.1.call-start = ((), (), s32[]{:S(2)}) async-start(), calls=%async_computation.15 | async-start | bytes 20971520 | tf_op jit(solution)/shard_map/reduce_scatter | solution.py:74
  903.2 281.5 %copy-start.18 = (bf16[512,2048]{1,0:T(8,128)(2,1)S(1)}, bf16[512,2048]{1,0:T(8,128)(2,1)}, u32[]{:S(2)}) copy-start(bf16[512,2048]{1,0:T(8,128)(2,1)} %param.22) | copy-start | bytes 6291460
  903.2 439.8 %all-gather.21.cloned.1.call-start = ((), (), s32[]{:S(2)}) async-start(), calls=%async_computation.16 | async-start | bytes 10485760 | tf_op jit(solution)/shard_map/all_gather | solution.py:70
  1192.5 492.3 %reduce-scatter.13.cloned.1.call-start = ((), (), s32[]{:S(2)}) async-start(), calls=%async_computation.17 | async-start | bytes 20971520 | tf_op jit(solution)/shard_map/reduce_scatter | solution.py:74
  1406.1 278.7 %copy-start.38 = (f32[512]{0:T(512)S(1)}, f32[512]{0:T(512)}, u32[]{:S(2)}) copy-start(f32[512]{0:T(512)} %copy-done.37) | copy-start | bytes 6148
  1406.1 441.9 %all-gather.23.cloned.1.call-start = ((), (), s32[]{:S(2)}) async-start(), calls=%async_computation.18 | async-start | bytes 10485760 | tf_op jit(solution)/shard_map/all_gather | solution.py:70
  1697.5 510.5 %reduce-scatter.23.cloned.1.call-start = ((), (), s32[]{:S(2)}) async-start(), calls=%async_computation.23 | async-start | bytes 14155776 | tf_op jit(solution)/shard_map/reduce_scatter | solution.py:133
  1716.6 494.5 %reduce-scatter.21.cloned.1.call-start = ((), (), s32[]{:S(2)}) async-start(), calls=%async_computation.22 | async-start | bytes 28311552 | tf_op jit(solution)/shard_map/reduce_scatter | solution.py:120
  1750.6 464.4 %reduce-scatter.19.cloned.1.call-start = ((), (), s32[]{:S(2)}) async-start(), calls=%async_computation.21 | async-start | bytes 4718592 | tf_op jit(solution)/shard_map/reduce_scatter | solution.py:133
  1858.6 402.8 %reduce-scatter.17.cloned.1.call-start = ((), (), s32[]{:S(2)}) async-start(), calls=%async_computation.20 | async-start | bytes 9437184 | tf_op jit(solution)/shard_map/reduce_scatter | solution.py:120
  2191.4 352.7 %reduce-scatter.15.cloned.1.call-start = ((), (), s32[]{:S(2)}) async-start(), calls=%async_computation.19 | async-start | bytes 20971520 | tf_op jit(solution)/shard_map/reduce_scatter | solution.py:74
  2211.0 333.0 %copy-start.6 = (bf16[512,2048]{1,0:T(8,128)(2,1)S(1)}, bf16[512,2048]{1,0:T(8,128)(2,1)}, u32[]{:S(2)}) copy-start(bf16[512,2048]{1,0:T(8,128)(2,1)} %param.19) | copy-start | bytes 6291460
  2211.0 333.0 %copy-start.33 = (f32[2048]{0:T(1024)S(1)}, f32[2048]{0:T(1024)}, u32[]{:S(2)}) copy-start(f32[2048]{0:T(1024)} %param.23) | copy-start | bytes 24580
  2211.0 333.0 %copy-start.40 = (f32[512]{0:T(512)S(1)}, f32[512]{0:T(512)}, u32[]{:S(2)}) copy-start(f32[512]{0:T(512)} %copy-done.39) | copy-start | bytes 6148
  2217.2 330.2 %copy-start.36 = (f32[2048]{0:T(1024)S(1)}, f32[2048]{0:T(1024)}, u32[]{:S(2)}) copy-start(f32[2048]{0:T(1024)} %get-tuple-element.310) | copy-start | bytes 24580
  (52 other events, 1184.8 us)
Sparse Core Ops, SparseCore 0:
  10.5 39.4 all-gather.10
  52.1 149.6 all-gather.8
  203.6 26.4 all-gather.12
  331.1 278.5 reduce-scatter.8
  612.2 72.8 all-gather.16
  687.1 149.6 all-gather.14
  838.8 44.8 all-gather.18
  903.4 281.2 reduce-scatter.10
  1192.6 150.3 all-gather.20
  1406.2 278.5 reduce-scatter.12
  1697.6 150.3 all-gather.22
  1851.8 90.6 reduce-scatter.22
  1946.5 156.8 reduce-scatter.20
  2107.0 51.3 reduce-scatter.18
  2191.5 69.8 reduce-scatter.16
  2263.7 280.2 reduce-scatter.14
where the time goes:
time: 2610 us; the launch traced here: 2600 us
  waiting for transfers between devices  1760 us (67%)
  matrix products  470 us (18%)
  other arithmetic  175 us (7%)
  blocking collectives  83.3 us (3%)
  local copies, waits for them, and re-layouts  77.9 us (3%)
    reduce_scatter x4, waiting for transfers between devices, sum_rows(): return lax.psum_scatter(partial_sum, 'tp', scatter_dimension=0, tiled=True)  1070 us
    all_gather x4, waiting for transfers between devices, gather_rows(): return lax.all_gather(values, 'tp', axis=0, tiled=True)  548 us
    all_gather x2, waiting for transfers between devices, project_in(): lax.all_gather(joined, 'fsdp', axis=0, tiled=True)  98.5 us
    dot_general x4, matrix products, contract_last(): lax.dot_general(left, right, (((1,), (1,)), ((), ())), preferred_element_...  90.5 us
    psum x2, blocking collectives, shards(): lax.psum((jnp.sum(mine_live), jnp.sum(errors * errors)), ('fsdp', 'tp'))  83.3 us
    dot_general x4, matrix products, contract_first(): lax.dot_general(left, right, (((0,), (0,)), ((), ())), preferred_element_...  76.5 us
    dot_general x4, matrix products, attend_back(): jnp.einsum('qkgd,tkd->kgqt', grad_rows, value_rows, preferred_element_typ...  59.5 us
    dot_general x8, matrix products, block_scores(): jnp.einsum('qkgd,tkd->kgqt', query_rows, key_rot, preferred_element_type=...  57.1 us
  transfers between devices with their start and end apart: 16, of which 12 were waited for; matrix products, arithmetic and copies ran while one was open for 22% of the time, Pallas kernels for 0%

commit v1 on v0

v1 whole, which is shorter than its diff:
```python
import functools

import jax
import jax.numpy as jnp
from jax import lax
from jax.experimental import pallas as pl
from jax.experimental.pallas import tpu as pltpu
from jax.sharding import PartitionSpec as P

D = 2048
HD = 128
WINDOW = 1024

EPS = 1e-06
THETA = 1000000.0
NEG = -1e30
VMEM = 56 * 1024 * 1024


def normalize_rows(values):
    factor = lax.rsqrt(jnp.mean(values * values, axis=-1, keepdims=True) + EPS)
    return (values * factor, factor)


def norm_back(grad, normed, factor, gain):
    scaled = grad * gain
    return factor * (scaled - normed * jnp.mean(scaled * normed, axis=-1, keepdims=True))


def contract_last(left, right):
    return lax.dot_general(
        left, right, (((1,), (1,)), ((), ())), preferred_element_type=jnp.float32
    )


def contract_first(left, right):
    return lax.dot_general(
        left, right, (((0,), (0,)), ((), ())), preferred_element_type=jnp.float32
    )


def dot(left, right):
    return jnp.dot(left, right, preferred_element_type=jnp.float32)


MESH = pl.DeviceIdType.MESH
PARTS = 2


def flip(index, mask):
    bit = 1
    while bit <= mask:
        if mask & bit:
            index = index + bit - 2 * bit * lax.rem(lax.div(index, bit), 2)
        bit *= 2
    return index


def chip_bits(size):
    bits = []
    bit = 2
    while bit < size:
        bits.append(bit)
        bit *= 2
    return bits


def orders(size):
    bits = chip_bits(size)
    return (bits, bits[::-1])


def mask_of(pattern, order):
    return sum(bit for i, bit in enumerate(order) if pattern >> i & 1)


def top(pattern):
    return pattern.bit_length() - 1


def greet(me, size):
    barrier = pltpu.get_barrier_semaphore()
    bits = [1] + chip_bits(size)
    for bit in bits:
        pl.semaphore_signal(
            barrier, inc=1, device_id={"fsdp": flip(me, bit)}, device_id_type=MESH
        )
    pl.semaphore_wait(barrier, len(bits))


def pick(part, pair):
    return pair[0] + part * (pair[1] - pair[0])


class Gather:
    def __init__(self, size, me, whole, sems, parts=PARTS, lane=lambda part: part):
        self.size, self.me, self.whole, self.parts, self.lane = (size, me, whole, parts, lane)
        self.chip_send, self.chip_recv, self.core_send, self.core_recv = sems
        self.steps = len(chip_bits(size))
        self.patterns = sorted(range(1 << self.steps), key=lambda m: (top(m), m))

    def order(self, part):
        return orders(self.size)[part % 2]

    def slot(self, part, pattern, sibling):
        return flip(self.me, mask_of(pattern, self.order(part)) + sibling)

    def chip_copy(self, part, step, pattern):
        block = self.whole.at[self.slot(part, pattern, 0), self.lane(part)]
        number = (1 << step) - 1 + pattern
        return pltpu.make_async_remote_copy(
            src_ref=block,
            dst_ref=block,
            send_sem=self.chip_send.at[part, number],
            recv_sem=self.chip_recv.at[part, number],
            device_id={"fsdp": flip(self.me, self.order(part)[step])},
            device_id_type=MESH,
        )

    def core_copy(self, part, pattern):
        block = self.whole.at[self.slot(part, pattern, 0), self.lane(part)]
        return pltpu.make_async_remote_copy(
            src_ref=block,
            dst_ref=block,
            send_sem=self.core_send.at[part, pattern],
            recv_sem=self.core_recv.at[part, pattern],
            device_id={"fsdp": flip(self.me, 1)},
            device_id_type=MESH,
        )

    def arrive(self, part, pattern):
        if pattern:
            step = top(pattern)
            self.chip_copy(part, step, pattern - (1 << step)).wait_recv()

    def forward(self, part, pattern):
        for step in range(top(pattern) + 1, self.steps):
            self.chip_copy(part, step, pattern).start()
        self.core_copy(part, pattern).start()

    def pairs(self, work):
        for pattern in self.patterns:
            for part in range(self.parts):
                self.arrive(part, pattern)
            for part in range(self.parts):
                self.forward(part, pattern)
            work([self.slot(part, pattern, 0) for part in range(self.parts)])
            for part in range(self.parts):
                self.core_copy(part, pattern).wait_recv()
            work([self.slot(part, pattern, 1) for part in range(self.parts)])

    def finish(self):
        for pattern in self.patterns:
            for part in range(self.parts):
                for step in range(top(pattern) + 1, self.steps):
                    self.chip_copy(part, step, pattern).wait_send()
                self.core_copy(part, pattern).wait_send()


def gather_semaphores(size, parts=PARTS):
    moves = max(1, size // 2 - 1)
    return [
        pltpu.SemaphoreType.DMA((parts, moves)),
        pltpu.SemaphoreType.DMA((parts, moves)),
        pltpu.SemaphoreType.DMA((parts, size // 2)),
        pltpu.SemaphoreType.DMA((parts, size // 2)),
    ]


def scatter_rows_in(size, me, made, held, sent, came, sems, partial, final):
    chip_send, chip_recv, core_send, core_recv = sems
    steps = len(chip_bits(size))
    order = [bits[::-1] for bits in orders(size)]
    first = lambda m: (m & -m).bit_length() - 1 if m else steps
    patterns = sorted(range(1 << steps), key=lambda m: (first(m), -bin(m).count("1"), m))
    place = {m: q for q, m in enumerate(patterns)}
    width = final.shape[-1]
    chunk = min(512, width)

    def slots(pattern, sibling):
        return [flip(me, mask_of(pattern, order[part]) + sibling) for part in range(PARTS)]

    def core_copy(part, q):
        return pltpu.make_async_remote_copy(
            src_ref=made.at[part, q],
            dst_ref=held.at[part, q],
            send_sem=core_send.at[part, q],
            recv_sem=core_recv.at[part, q],
            device_id={"fsdp": flip(me, 1)},
            device_id_type=MESH,
        )

    def chip_copy(part, q):
        return pltpu.make_async_remote_copy(
            src_ref=sent.at[part, q],
            dst_ref=came.at[part, q],
            send_sem=chip_send.at[part, q],
            recv_sem=chip_recv.at[part, q],
            device_id={"fsdp": flip(me, order[part][first(patterns[q])])},
            device_id_type=MESH,
        )

    def for_sibling(q):
        pair = slots(patterns[q], 1)

        @pl.loop(0, PARTS)
        def _(part):
            @pl.loop(0, width // chunk)
            def _(index):
                columns = pl.ds(pl.multiple_of(index * chunk, chunk), chunk)
                made[part, q, :, columns] = partial(part, pick(part, pair), columns).astype(
                    jnp.bfloat16
                )

        for part in range(PARTS):
            core_copy(part, q).start()

    def for_chips(q):
        pattern = patterns[q]
        pair = slots(pattern, 0)
        arrivals = [place[pattern | 1 << step] for step in range(first(pattern))]
        for part in range(PARTS):
            core_copy(part, q).wait_recv()
            for arrival in arrivals:
                chip_copy(part, arrival).wait_recv()

        @pl.loop(0, PARTS)
        def _(part):
            @pl.loop(0, width // chunk)
            def _(index):
                columns = pl.ds(pl.multiple_of(index * chunk, chunk), chunk)
                total = partial(part, pick(part, pair), columns)
                total = total + held[part, q, :, columns].astype(jnp.float32)
                for arrival in arrivals:
                    total = total + came[part, arrival, :, columns].astype(jnp.float32)
                if pattern:
                    sent[part, q, :, columns] = total.astype(jnp.bfloat16)
                else:
                    final[part, :, columns] = total

        if pattern:
            for part in range(PARTS):
                chip_copy(part, q).start()

    for_sibling(0)
    for q in range(len(patterns)):
        if q + 1 < len(patterns):
            for_sibling(q + 1)
        for_chips(q)
    for q in range(len(patterns)):
        for part in range(PARTS):
            core_copy(part, q).wait_send()
            if patterns[q]:
                chip_copy(part, q).wait_send()


def scatter_scratch(size, rows, width):
    held = size // 2
    moved = max(1, held - 1)
    return [
        pltpu.VMEM((PARTS, held, rows, width), jnp.bfloat16),
        pltpu.VMEM((PARTS, held, rows, width), jnp.bfloat16),
        pltpu.VMEM((PARTS, moved, rows, width), jnp.bfloat16),
        pltpu.VMEM((PARTS, moved, rows, width), jnp.bfloat16),
        pltpu.SemaphoreType.DMA((PARTS, moved)),
        pltpu.SemaphoreType.DMA((PARTS, moved)),
        pltpu.SemaphoreType.DMA((PARTS, held)),
        pltpu.SemaphoreType.DMA((PARTS, held)),
    ]


def gate_up_kernel(
    size, x_ref, wg_ref, wu_ref, x_out, gate_out, up_out, prod_out, whole, gate, up, prod, load, keep, store, *sems
):
    me = lax.axis_index("fsdp")
    hidden = wg_ref.shape[0]
    chunk = 256 if hidden % 256 == 0 else 128
    own = pltpu.make_async_copy(x_ref, whole.at[me], load)
    own.start()
    own.wait()
    greet(me, size)
    state = {"count": 0, "last": None}

    def stores(part, at):
        return [
            pltpu.make_async_copy(buffer.at[part], out.at[at, part], store.at[part, i])
            for i, (buffer, out) in enumerate(((gate, gate_out), (up, up_out), (prod, prod_out)))
        ]

    def work(pair):
        count, last = (state["count"], state["last"])
        for part in range(PARTS):
            pltpu.make_async_copy(
                whole.at[pair[part], part], x_out.at[pair[part], part], keep.at[part, count]
            ).start()

        @pl.loop(0, PARTS)
        def _(part):
            at = pick(part, pair)
            if last is not None:
                for copy in stores(part, pick(part, last)):
                    copy.wait()

            @pl.loop(0, hidden // chunk)
            def _(index):
                units = pl.ds(pl.multiple_of(index * chunk, chunk), chunk)
                rows = whole[at, part]
                gates = contract_last(rows, wg_ref[units, :])
                ups = contract_last(rows, wu_ref[units, :])
                gate[part, :, units] = gates
                up[part, :, units] = ups
                prod[part, :, units] = (gates * jax.nn.sigmoid(gates) * ups).astype(jnp.bfloat16)

            for copy in stores(part, at):
                copy.start()

        state["count"], state["last"] = (count + 1, pair)
        state.setdefault("all", []).append(pair)

    gather = Gather(size, me, whole, sems)
    gather.pairs(work)
    gather.finish()
    for part in range(PARTS):
        for copy in stores(part, state["last"][part]):
            copy.wait()
        for count, pair in enumerate(state["all"]):
            pltpu.make_async_copy(
                whole.at[pair[part], part], x_out.at[pair[part], part], keep.at[part, count]
            ).wait()


def gate_up(size, values, rows_gate, rows_up):
    own, width = values.shape
    rows, hidden = (own // PARTS, rows_gate.shape[0])
    any_space = pl.BlockSpec(memory_space=pl.ANY)
    vmem = pl.BlockSpec(memory_space=pltpu.VMEM)
    shape = lambda columns, kind: jax.ShapeDtypeStruct((size, PARTS, rows, columns), kind)
    outs = pl.pallas_call(
        functools.partial(gate_up_kernel, size),
        out_shape=(
            shape(width, jnp.bfloat16),
            shape(hidden, jnp.float32),
            shape(hidden, jnp.float32),
            shape(hidden, jnp.bfloat16),
        ),
        in_specs=[any_space, vmem, vmem],
        out_specs=(any_space,) * 4,
        scratch_shapes=[
            pltpu.VMEM((size, PARTS, rows, width), jnp.bfloat16),
            pltpu.VMEM((PARTS, rows, hidden), jnp.float32),
            pltpu.VMEM((PARTS, rows, hidden), jnp.float32),
            pltpu.VMEM((PARTS, rows, hidden), jnp.bfloat16),
            pltpu.SemaphoreType.DMA,
            pltpu.SemaphoreType.DMA((PARTS, size)),
            pltpu.SemaphoreType.DMA((PARTS, 3)),
            *gather_semaphores(size),
        ],
        compiler_params=pltpu.CompilerParams(
            collective_id=1, has_side_effects=True, vmem_limit_bytes=VMEM
        ),
        cost_estimate=pl.CostEstimate(
            flops=4 * size * own * width * hidden, bytes_accessed=200 * 1024 * 1024, transcendentals=0
        ),
        name="gate_up",
    )(values.reshape(PARTS, rows, width), rows_gate, rows_up)
    return tuple(out.reshape(size * own, -1) for out in outs)


def grad_hidden_kernel(
    size, x_ref, wd_ref, gate_in, up_in, x_out, dgate_out, dup_out, whole, gate, up, dprod, dgate, dup, load, keep, fetch, store, *sems
):
    me = lax.axis_index("fsdp")
    hidden = wd_ref.shape[0]
    chunk = 256 if hidden % 256 == 0 else 128
    own = pltpu.make_async_copy(x_ref, whole.at[me], load)
    own.start()
    own.wait()
    greet(me, size)
    state = {"count": 0, "last": None, "all": []}

    def stores(part, at):
        return [
            pltpu.make_async_copy(buffer.at[part], out.at[at, part], store.at[part, i])
            for i, (buffer, out) in enumerate(((dgate, dgate_out), (dup, dup_out)))
        ]

    def fetches(part, at):
        return [
            pltpu.make_async_copy(source.at[at, part], buffer, fetch.at[i])
            for i, (source, buffer) in enumerate(((gate_in, gate), (up_in, up)))
        ]

    def work(pair):
        count, last = (state["count"], state["last"])
        for part in range(PARTS):
            pltpu.make_async_copy(
                whole.at[pair[part], part], x_out.at[pair[part], part], keep.at[part, count]
            ).start()

        @pl.loop(0, PARTS)
        def _(part):
            at = pick(part, pair)
            for copy in fetches(part, at):
                copy.start()
            if last is not None:
                for copy in stores(part, pick(part, last)):
                    copy.wait()

            @pl.loop(0, hidden // chunk)
            def _(index):
                units = pl.ds(pl.multiple_of(index * chunk, chunk), chunk)
                dprod[:, units] = contract_last(whole[at, part], wd_ref[units, :])

            for copy in fetches(part, at):
                copy.wait()

            @pl.loop(0, hidden // chunk)
            def _(index):
                units = pl.ds(pl.multiple_of(index * chunk, chunk), chunk)
                gates, grads = (gate[:, units], dprod[:, units])
                sigmoid = jax.nn.sigmoid(gates)
                dgate[part, :, units] = (
                    grads * up[:, units] * sigmoid * (1.0 + gates * (1.0 - sigmoid))
                ).astype(jnp.bfloat16)
                dup[part, :, units] = (grads * (gates * sigmoid)).astype(jnp.bfloat16)

            for copy in stores(part, at):
                copy.start()

        state["count"], state["last"] = (count + 1, pair)
        state["all"].append(pair)

    gather = Gather(size, me, whole, sems)
    gather.pairs(work)
    gather.finish()
    for part in range(PARTS):
        for copy in stores(part, state["last"][part]):
            copy.wait()
        for count, pair in enumerate(state["all"]):
            pltpu.make_async_copy(
                whole.at[pair[part], part], x_out.at[pair[part], part], keep.at[part, count]
            ).wait()


def grad_hidden_units(size, values, rows_down, gate, up):
    own, width = values.shape
    rows, hidden = (own // PARTS, rows_down.shape[0])
    any_space = pl.BlockSpec(memory_space=pl.ANY)
    vmem = pl.BlockSpec(memory_space=pltpu.VMEM)
    shape = lambda columns, kind: jax.ShapeDtypeStruct((size, PARTS, rows, columns), kind)
    blocks = lambda array: array.reshape(size, PARTS, rows, hidden)
    outs = pl.pallas_call(
        functools.partial(grad_hidden_kernel, size),
        out_shape=(
            shape(width, jnp.bfloat16),
            shape(hidden, jnp.bfloat16),
            shape(hidden, jnp.bfloat16),
        ),
        in_specs=[any_space, vmem, any_space, any_space],
        out_specs=(any_space,) * 3,
        scratch_shapes=[
            pltpu.VMEM((size, PARTS, rows, width), jnp.bfloat16),
            pltpu.VMEM((rows, hidden), jnp.float32),
            pltpu.VMEM((rows, hidden), jnp.float32),
            pltpu.VMEM((rows, hidden), jnp.float32),
            pltpu.VMEM((PARTS, rows, hidden), jnp.bfloat16),
            pltpu.VMEM((PARTS, rows, hidden), jnp.bfloat16),
            pltpu.SemaphoreType.DMA,
            pltpu.SemaphoreType.DMA((PARTS, size)),
            pltpu.SemaphoreType.DMA((2,)),
            pltpu.SemaphoreType.DMA((PARTS, 2)),
            *gather_semaphores(size),
        ],
        compiler_params=pltpu.CompilerParams(
            collective_id=3, has_side_effects=True, vmem_limit_bytes=VMEM
        ),
        cost_estimate=pl.CostEstimate(
            flops=2 * size * own * width * hidden, bytes_accessed=200 * 1024 * 1024, transcendentals=0
        ),
        name="grad_hidden_units",
    )(values.reshape(PARTS, rows, width), rows_down, blocks(gate), blocks(up))
    return tuple(out.reshape(size * own, -1) for out in outs)


def sum_products_kernel(size, terms, *refs):
    lefts, rights, out = (refs[:terms], refs[terms : 2 * terms], refs[2 * terms])
    made, held, sent, came, *sems = refs[2 * terms + 1 :]
    me = lax.axis_index("fsdp")
    greet(me, size)

    def partial(part, slot, columns):
        return sum(
            dot(left[slot, part], right[:, columns]) for left, right in zip(lefts, rights)
        )

    scatter_rows_in(size, me, made, held, sent, came, sems, partial, out)


def sum_products(size, number, lefts, rights):
    total, hidden = lefts[0].shape
    width = rights[0].shape[1]
    rows = total // size // PARTS
    vmem = pl.BlockSpec(memory_space=pltpu.VMEM)
    terms = len(lefts)
    out = pl.pallas_call(
        functools.partial(sum_products_kernel, size, terms),
        out_shape=jax.ShapeDtypeStruct((PARTS, rows, width), jnp.float32),
        in_specs=[vmem] * (2 * terms),
        out_specs=vmem,
        scratch_shapes=scatter_scratch(size, rows, width),
        compiler_params=pltpu.CompilerParams(
            collective_id=number, has_side_effects=True, vmem_limit_bytes=VMEM
        ),
        cost_estimate=pl.CostEstimate(
            flops=2 * total * hidden * width * terms, bytes_accessed=200 * 1024 * 1024, transcendentals=0
        ),
        name="sum_products",
    )(*[left.reshape(size, PARTS, rows, hidden) for left in lefts], *rights)
    return out.reshape(PARTS * rows, width)


def enter_kernel(size, lanes, back, x_ref, w_ref, before, whole, load, z_send, z_recv, x_send, x_recv, *sems):
    me, z = (lax.axis_index("fsdp"), lax.axis_index("tp"))
    own = pltpu.make_async_copy(w_ref, whole.at[me, z], load)
    own.start()
    barrier = pltpu.get_barrier_semaphore()
    peers = [{"fsdp": flip(me, bit)} for bit in [1] + chip_bits(size)]
    peers += [{"tp": lax.rem(z + hop, lanes)} for hop in range(1, lanes)]
    for peer in peers:
        pl.semaphore_signal(barrier, inc=1, device_id=peer, device_id_type=MESH)
    pl.semaphore_wait(barrier, len(peers))
    own.wait()

    def lane(part):
        return lax.rem(z + lanes - part, lanes)

    def lane_copy(hop):
        return pltpu.make_async_remote_copy(
            src_ref=w_ref,
            dst_ref=whole.at[me, z],
            send_sem=z_send.at[hop - 1],
            recv_sem=z_recv.at[hop - 1],
            device_id={"tp": lax.rem(z + hop, lanes)},
            device_id_type=MESH,
        )

    def token_copy(hop):
        return pltpu.make_async_remote_copy(
            src_ref=x_ref,
            dst_ref=before.at[hop - 1],
            send_sem=x_send.at[hop - 1],
            recv_sem=x_recv.at[hop - 1],
            device_id={"tp": lax.rem(z + hop, lanes)},
            device_id_type=MESH,
        )

    gather = Gather(size, me, whole, sems, lanes, lane)
    for hop in range(1, lanes):
        lane_copy(hop).start()
    gather.forward(0, 0)
    for hop in range(1, back + 1):

        @pl.when(z + hop < lanes)
        def _():
            token_copy(hop).start()

    events = [(part, pattern) for part in range(lanes) for pattern in gather.patterns]
    events.sort(key=lambda event: (2 * event[0] + top(event[1]) + 1, event))
    for part, pattern in events[1:]:
        if pattern:
            gather.arrive(part, pattern)
        else:
            lane_copy(part).wait_recv()
        gather.forward(part, pattern)
    for part, pattern in events:
        gather.core_copy(part, pattern).wait_recv()
    gather.finish()
    for hop in range(1, lanes):
        lane_copy(hop).wait_send()
    for hop in range(1, back + 1):

        @pl.when(z + hop < lanes)
        def _():
            token_copy(hop).wait_send()

        @pl.when(z >= hop)
        def _():
            token_copy(hop).wait_recv()


def enter(size, lanes, back, values, weights):
    any_space = pl.BlockSpec(memory_space=pl.ANY)
    return pl.pallas_call(
        functools.partial(enter_kernel, size, lanes, back),
        out_shape=(
            jax.ShapeDtypeStruct((back, *values.shape), values.dtype),
            jax.ShapeDtypeStruct((size, lanes, *weights.shape), weights.dtype),
        ),
        in_specs=[any_space, any_space],
        out_specs=(any_space, any_space),
        scratch_shapes=[
            pltpu.SemaphoreType.DMA,
            pltpu.SemaphoreType.DMA((lanes - 1,)),
            pltpu.SemaphoreType.DMA((lanes - 1,)),
            pltpu.SemaphoreType.DMA((back,)),
            pltpu.SemaphoreType.DMA((back,)),
            *gather_semaphores(size, lanes),
        ],
        compiler_params=pltpu.CompilerParams(collective_id=5, has_side_effects=True),
        cost_estimate=pl.CostEstimate(flops=0, bytes_accessed=400 * 1024 * 1024, transcendentals=0),
        name="enter",
    )(values, weights)


def project_kernel(
    wq, wk, before_ref, x_ref, gain_ref, w_ref, n_ref, q_ref, k_ref, v_ref, normed
):
    back, own, _ = before_ref.shape
    lead = back * own
    tile = min(256, own)
    z = lax.axis_index("tp")

    @pl.when(pl.program_id(0) == 0)
    def _():
        for hop in range(back + 1):

            @pl.loop(0, own // tile)
            def _(index):
                span = pl.ds(pl.multiple_of(index * tile, tile), tile)
                values = x_ref[span, :] if hop == 0 else before_ref[hop - 1, span, :]
                values = normalize_rows(values.astype(jnp.float32))[0] * gain_ref[...]
                values = values.astype(jnp.bfloat16)
                if hop:
                    values = jnp.where(z >= hop, values, jnp.zeros_like(values))
                else:
                    n_ref[span, :] = values
                at = lead - hop * own + index * tile
                normed[pl.ds(pl.multiple_of(at, tile), tile), :] = values

    weights = lambda start, size: w_ref[:, 0, :, start : start + size].reshape(D, size)

    @pl.loop(0, (lead + own) // tile)
    def _(index):
        span = pl.ds(pl.multiple_of(index * tile, tile), tile)
        pair = dot(normed[span, :], weights(wq, 2 * wk))
        k_ref[span, :] = pair[:, :wk]
        v_ref[span, :] = pair[:, wk:].astype(jnp.bfloat16)

    @pl.loop(0, own // tile)
    def _(index):
        span = pl.ds(pl.multiple_of(index * tile, tile), tile)
        from_lead = pl.ds(pl.multiple_of(lead + index * tile, tile), tile)
        q_ref[span, :] = dot(normed[from_lead, :], weights(0, wq))


def project(before, values, gain, weights, wq, wk):
    size, parts, rows_in, columns = weights.shape
    back, own, _ = before.shape
    rows = (back + 1) * own
    whole = lambda *_: (0, 0)
    return pl.pallas_call(
        functools.partial(project_kernel, wq, wk),
        grid=(parts,),
        out_shape=(
            jax.ShapeDtypeStruct((own, D), jnp.bfloat16),
            jax.ShapeDtypeStruct((own, parts * wq), jnp.float32),
            jax.ShapeDtypeStruct((rows, parts * wk), jnp.float32),
            jax.ShapeDtypeStruct((rows, parts * wk), jnp.bfloat16),
        ),
        in_specs=[
            pl.BlockSpec((back, own, D), lambda z: (0, 0, 0)),
            pl.BlockSpec((own, D), whole),
            pl.BlockSpec((1, D), whole),
            pl.BlockSpec((size, 1, rows_in, wq + 2 * wk), lambda z: (0, z, 0, 0)),
        ],
        out_specs=(
            pl.BlockSpec((own, D), whole),
            pl.BlockSpec((own, wq), lambda z: (0, z)),
            pl.BlockSpec((rows, wk), lambda z: (0, z)),
            pl.BlockSpec((rows, wk), lambda z: (0, z)),
        ),
        scratch_shapes=[pltpu.VMEM((rows, D), jnp.bfloat16)],
        compiler_params=pltpu.CompilerParams(vmem_limit_bytes=VMEM),
        cost_estimate=pl.CostEstimate(
            flops=2 * D * parts * (own * wq + rows * 2 * wk),
            bytes_accessed=2 * D * parts * (wq + 2 * wk) + 2 * rows * D,
            transcendentals=0,
        ),
        name="project_in",
    )(before, values, gain.reshape(1, D), weights)


def out_kernel(a_ref, w_ref, x_ref, o_ref):
    parts, _, width = w_ref.shape[1:]
    total = x_ref[...].astype(jnp.float32)
    for z in range(parts):
        total += contract_last(a_ref[:, z * width : (z + 1) * width], w_ref[0, z])
    o_ref[...] = total


def project_out(attended, weights, states, wo):
    size, parts, rows, columns = weights.shape
    own = states.shape[0]
    last = columns // wo - 1
    return pl.pallas_call(
        out_kernel,
        grid=(size,),
        out_shape=jax.ShapeDtypeStruct(states.shape, jnp.float32),
        in_specs=[
            pl.BlockSpec(attended.shape, lambda f: (0, 0)),
            pl.BlockSpec((1, parts, rows, wo), lambda f: (f, 0, 0, last)),
            pl.BlockSpec((own, rows), lambda f: (0, f)),
        ],
        out_specs=pl.BlockSpec((own, rows), lambda f: (0, f)),
        compiler_params=pltpu.CompilerParams(vmem_limit_bytes=VMEM),
        cost_estimate=pl.CostEstimate(
            flops=2 * own * D * parts * wo, bytes_accessed=24 * 1024 * 1024, transcendentals=0
        ),
        name="project_out",
    )(attended, weights, states)


def back_out_kernel(g_ref, w_ref, o_ref):
    size, _, rows, width = w_ref.shape
    o_ref[...] = dot(g_ref[...], w_ref[:, 0].reshape(size * rows, width)).astype(jnp.bfloat16)


def back_out(grad, weights, wo):
    size, parts, rows, columns = weights.shape
    own = grad.shape[0]
    last = columns // wo - 1
    return pl.pallas_call(
        back_out_kernel,
        grid=(parts,),
        out_shape=jax.ShapeDtypeStruct((own, parts * wo), jnp.bfloat16),
        in_specs=[
            pl.BlockSpec(grad.shape, lambda z: (0, 0)),
            pl.BlockSpec((size, 1, rows, wo), lambda z: (0, z, 0, last)),
        ],
        out_specs=pl.BlockSpec((own, wo), lambda z: (0, z)),
        compiler_params=pltpu.CompilerParams(vmem_limit_bytes=VMEM),
        cost_estimate=pl.CostEstimate(
            flops=2 * own * D * parts * wo, bytes_accessed=16 * 1024 * 1024, transcendentals=0
        ),
        name="back_out",
    )(grad, weights)


def back_in_kernel(q_ref, k_ref, v_ref, w_ref, o_ref):
    parts = w_ref.shape[1]
    total = jnp.zeros(o_ref.shape, jnp.float32)
    for z in range(parts):
        start = 0
        for ref in (q_ref, k_ref, v_ref):
            width = ref.shape[1] // parts
            total += contract_last(
                ref[:, z * width : (z + 1) * width], w_ref[0, z, :, start : start + width]
            )
            start += width
    o_ref[...] = total


def back_in(grad_query, grad_key, grad_value, weights):
    size, parts, rows, _ = weights.shape
    own = grad_query.shape[0]
    columns = (grad_query.shape[1] + 2 * grad_key.shape[1]) // parts
    whole = lambda f: (0, 0)
    return pl.pallas_call(
        back_in_kernel,
        grid=(size,),
        out_shape=jax.ShapeDtypeStruct((own, D), jnp.float32),
        in_specs=[
            pl.BlockSpec(grad_query.shape, whole),
            pl.BlockSpec(grad_key.shape, whole),
            pl.BlockSpec(grad_value.shape, whole),
            pl.BlockSpec((1, parts, rows, columns), lambda f: (f, 0, 0, 0)),
        ],
        out_specs=pl.BlockSpec((own, rows), lambda f: (0, f)),
        compiler_params=pltpu.CompilerParams(vmem_limit_bytes=VMEM),
        cost_estimate=pl.CostEstimate(
            flops=2 * own * D * parts * columns, bytes_accessed=24 * 1024 * 1024, transcendentals=0
        ),
        name="back_in",
    )(grad_query, grad_key, grad_value, weights)


def turn(values, cosine, sine):
    return values * cosine + pltpu.roll(values, HD // 2, 1) * sine


def turn_back(grad, cosine, sine):
    return grad * cosine - pltpu.roll(grad, HD // 2, 1) * sine


def split_heads(block, group):
    return jnp.concatenate([block[:, i * HD : (i + 1) * HD] for i in range(group)], axis=0)


def join_heads(stacked, group):
    rows = stacked.shape[0] // group
    return jnp.concatenate([stacked[i * rows : (i + 1) * rows] for i in range(group)], axis=1)


def head_probs(query, keys, bias, group, scale):
    scores = contract_last(query, keys) * scale
    rows, span = scores.shape
    scores = (scores.reshape(group, rows // group, span) + bias[None]).reshape(rows, span)
    weights = jnp.exp(scores - jnp.max(scores, axis=-1, keepdims=True))
    return weights * (1.0 / jnp.sum(weights, axis=-1, keepdims=True))


def attend_kernel(
    group, step, lead, q_ref, k_ref, v_ref, bias_ref, cos_ref, sin_ref, nq_ref, nk_ref, o_ref, keys
):
    tile, span = bias_ref.shape
    scale = HD ** (-0.5)
    index = pl.program_id(1)

    @pl.when(index == 0)
    def _():
        normed = normalize_rows(k_ref[...])[0] * nk_ref[...]
        keys[...] = turn(normed, cos_ref[...], sin_ref[...]).astype(jnp.bfloat16)

    here = pl.ds(pl.multiple_of(lead + index * tile, tile), tile)
    cosine, sine = (cos_ref[here, :], sin_ref[here, :])
    normed = normalize_rows(split_heads(q_ref[...], group))[0] * nq_ref[...]
    cosine, sine = (jnp.concatenate([cosine] * group, 0), jnp.concatenate([sine] * group, 0))
    query = turn(normed, cosine, sine).astype(jnp.bfloat16)
    window = pl.ds(pl.multiple_of(index * step, tile), span)
    probs = head_probs(query, keys[window, :], bias_ref[...], group, scale)
    mixed = dot(probs.astype(jnp.bfloat16), v_ref[window, :])
    o_ref[...] = join_heads(mixed.astype(jnp.bfloat16), group)


def attend_back_kernel(
    group,
    step,
    lead,
    q_ref,
    k_ref,
    v_ref,
    bias_ref,
    cos_ref,
    sin_ref,
    nq_ref,
    nk_ref,
    do_ref,
    dq_ref,
    prev_ref,
    own_ref,
    gq_ref,
    gk_ref,
    keys,
    dk,
    dv,
):
    tile, span = bias_ref.shape
    scale = HD ** (-0.5)
    index = pl.program_id(1)

    @pl.when((pl.program_id(0) == 0) & (index == 0))
    def _():
        gq_ref[...] = jnp.zeros_like(gq_ref)
        gk_ref[...] = jnp.zeros_like(gk_ref)

    @pl.when(index == 0)
    def _():
        normed = normalize_rows(k_ref[...])[0] * nk_ref[...]
        keys[...] = turn(normed, cos_ref[...], sin_ref[...]).astype(jnp.bfloat16)
        dk[...] = jnp.zeros_like(dk)
        dv[...] = jnp.zeros_like(dv)

    here = pl.ds(pl.multiple_of(lead + index * tile, tile), tile)
    cosine, sine = (cos_ref[here, :], sin_ref[here, :])
    cosine, sine = (jnp.concatenate([cosine] * group, 0), jnp.concatenate([sine] * group, 0))
    normed, factor = normalize_rows(split_heads(q_ref[...], group))
    query = turn(normed * nq_ref[...], cosine, sine).astype(jnp.bfloat16)
    window = pl.ds(pl.multiple_of(index * step, tile), span)
    probs = head_probs(query, keys[window, :], bias_ref[...], group, scale)
    grad_out = split_heads(do_ref[...], group)
    dv[window, :] += contract_first(probs.astype(jnp.bfloat16), grad_out)
    grad_probs = contract_last(grad_out, v_ref[window, :])
    centre = jnp.sum(probs * grad_probs, axis=-1, keepdims=True)
    grad_scores = (probs * (grad_probs - centre)).astype(jnp.bfloat16)
    dk[window, :] += contract_first(grad_scores, query) * scale
    grad_query = turn_back(dot(grad_scores, keys[window, :]) * scale, cosine, sine)
    gq_ref[...] += jnp.sum(grad_query * normed, axis=0, keepdims=True)
    grad_raw = norm_back(grad_query, normed, factor, nq_ref[...])
    dq_ref[...] = join_heads(grad_raw.astype(jnp.bfloat16), group)

    @pl.when(index == pl.num_programs(1) - 1)
    def _():
        normed_key, key_factor = normalize_rows(k_ref[...])
        grad_key = turn_back(dk[...], cos_ref[...], sin_ref[...])
        gk_ref[...] += jnp.sum(grad_key * normed_key, axis=0, keepdims=True)
        grad_key = norm_back(grad_key, normed_key, key_factor, nk_ref[...])
        if lead:
            prev_ref[0] = grad_key[:lead].astype(jnp.bfloat16)
            prev_ref[1] = dv[:lead, :].astype(jnp.bfloat16)
        own_ref[0] = grad_key[lead:]
        own_ref[1] = dv[lead:, :]


def attention_specs(own, rows, group, tile, span):
    whole = lambda g, t: (0, 0)
    return [
        pl.BlockSpec((tile, group * HD), lambda g, t: (t, g)),
        pl.BlockSpec((rows, HD), lambda g, t: (0, g)),
        pl.BlockSpec((rows, HD), lambda g, t: (0, g)),
        pl.BlockSpec((tile, span), lambda g, t: (t, 0)),
        pl.BlockSpec((rows, HD), whole),
        pl.BlockSpec((rows, HD), whole),
        pl.BlockSpec((1, HD), whole),
        pl.BlockSpec((1, HD), whole),
    ]


def attend(queries, keys, values, bias, cosine, sine, norm_query, norm_key, tile, step):
    own, rows = (queries.shape[0], keys.shape[0])
    heads = keys.shape[1] // HD
    group = queries.shape[1] // keys.shape[1]
    span = bias.shape[1]
    return pl.pallas_call(
        functools.partial(attend_kernel, group, step, rows - own),
        grid=(heads, own // tile),
        out_shape=jax.ShapeDtypeStruct(queries.shape, jnp.bfloat16),
        in_specs=attention_specs(own, rows, group, tile, span),
        out_specs=pl.BlockSpec((tile, group * HD), lambda g, t: (t, g)),
        scratch_shapes=[pltpu.VMEM((rows, HD), jnp.bfloat16)],
        compiler_params=pltpu.CompilerParams(vmem_limit_bytes=VMEM),
        cost_estimate=pl.CostEstimate(
            flops=16 * own * span * queries.shape[1],
            bytes_accessed=4 * queries.size + 6 * keys.size,
            transcendentals=own * span * heads * group,
        ),
        name="attend",
    )(queries, keys, values, bias, cosine, sine, norm_query, norm_key)


def attend_back(
    queries, keys, values, bias, cosine, sine, norm_query, norm_key, grad, tile, step
):
    own, rows = (queries.shape[0], keys.shape[0])
    heads = keys.shape[1] // HD
    group = queries.shape[1] // keys.shape[1]
    span = bias.shape[1]
    lead = rows - own
    whole = lambda g, t: (0, 0)
    return pl.pallas_call(
        functools.partial(attend_back_kernel, group, step, lead),
        grid=(heads, own // tile),
        out_shape=(
            jax.ShapeDtypeStruct(queries.shape, jnp.bfloat16),
            jax.ShapeDtypeStruct((2, lead, heads * HD), jnp.bfloat16),
            jax.ShapeDtypeStruct((2, own, heads * HD), jnp.float32),
            jax.ShapeDtypeStruct((1, HD), jnp.float32),
            jax.ShapeDtypeStruct((1, HD), jnp.float32),
        ),
        in_specs=attention_specs(own, rows, group, tile, span)
        + [pl.BlockSpec((tile, group * HD), lambda g, t: (t, g))],
        out_specs=(
            pl.BlockSpec((tile, group * HD), lambda g, t: (t, g)),
            pl.BlockSpec((2, lead, HD), lambda g, t: (0, 0, g)),
            pl.BlockSpec((2, own, HD), lambda g, t: (0, 0, g)),
            pl.BlockSpec((1, HD), whole),
            pl.BlockSpec((1, HD), whole),
        ),
        scratch_shapes=[
            pltpu.VMEM((rows, HD), jnp.bfloat16),
            pltpu.VMEM((rows, HD), jnp.float32),
            pltpu.VMEM((rows, HD), jnp.float32),
        ],
        compiler_params=pltpu.CompilerParams(vmem_limit_bytes=VMEM),
        cost_estimate=pl.CostEstimate(
            flops=40 * own * span * queries.shape[1],
            bytes_accessed=8 * queries.size + 16 * keys.size,
            transcendentals=own * span * heads * group,
        ),
        name="attend_back",
    )(queries, keys, values, bias, cosine, sine, norm_query, norm_key, grad)


def window_tables(length_row, pad_row, first, own, lead, tile, span):
    places = first - lead + jnp.arange(lead + own, dtype=jnp.int32)
    ends = jnp.cumsum(length_row)
    passed = places[:, None] >= ends[None, :]
    docs = jnp.sum(passed.astype(jnp.int32), axis=1)
    starts = jnp.sum(jnp.where(passed, length_row[None, :], 0), axis=1)
    freqs = THETA ** (-(jnp.arange(HD // 2).astype(jnp.float32) * 2.0 / HD))
    angles = (places - starts).astype(jnp.float32)[:, None] * freqs[None, :]
    cosine, sine = (jnp.cos(angles), jnp.sin(angles))
    padded = jnp.concatenate((jnp.zeros((lead,), pad_row.dtype), pad_row))
    live = lax.dynamic_slice_in_dim(padded, first, lead + own, 0)
    step = tile if lead + own > span else 0
    masks = []
    for index in range(own // tile):
        at = lead + index * tile
        query, key = (places[at : at + tile, None], places[None, index * step : index * step + span])
        same = docs[at : at + tile, None] == docs[None, index * step : index * step + span]
        seen = (live[None, index * step : index * step + span] == 1) | (key == query)
        masks.append((key >= 0) & (key <= query) & (query - key < WINDOW) & same & seen)
    bias = jnp.where(jnp.concatenate(masks, axis=0), 0.0, NEG).astype(jnp.float32)
    cosine = jnp.concatenate((cosine, cosine), axis=1)
    sine = jnp.concatenate((-sine, sine), axis=1)
    return (bias, cosine, sine, step, live[lead:].astype(jnp.float32))


def hidden_rows(weight_t):
    mine = lax.all_to_all(weight_t, "fsdp", 0, 1, tiled=True)
    return lax.all_gather(mine, "tp", axis=0, tiled=True)


def hidden_rows_grad(grad):
    mine = lax.psum_scatter(grad.astype(jnp.bfloat16), "tp", scatter_dimension=0, tiled=True)
    return lax.all_to_all(mine, "fsdp", 1, 0, tiled=True).astype(jnp.float32)


def scatter_grad(grad):
    rows = lax.psum_scatter(
        grad.astype(jnp.bfloat16), "fsdp", scatter_dimension=0, tiled=True
    )
    return lax.psum_scatter(rows, "tp", scatter_dimension=1, tiled=True).astype(jnp.float32)


def shards(
    states,
    lengths,
    padding,
    teacher,
    norm_attn,
    w_query,
    w_key,
    w_value,
    norm_query,
    norm_key,
    w_out,
    norm_mlp,
    w_gate,
    w_up,
    w_down,
):
    own = states.shape[0]
    n_tp, n_fsdp = (lax.axis_size("tp"), lax.axis_size("fsdp"))
    first = lax.axis_index("tp") * own
    back = min(n_tp - 1, -(-WINDOW // own))
    lead = back * own
    tile = min(256, own)
    span = WINDOW + tile if lead >= WINDOW else lead + own
    wq, wk = (w_query.shape[1], w_key.shape[1])
    count = lax.psum(jnp.sum(padding).astype(jnp.float32), "fsdp")
    bias, cosine, sine, step, live = window_tables(
        lengths[0], padding[0], first, own, lead, tile, span
    )
    joined = jnp.concatenate((w_query, w_key, w_value, w_out.T), axis=1)
    wo = w_out.shape[0]
    before, weights_attn = enter(n_fsdp, n_tp, back, states, joined)
    rows_gate = hidden_rows(w_gate.T)
    rows_up = hidden_rows(w_up.T)
    rows_down = hidden_rows(w_down)

    normed_in, query_raw, key_raw, value = project(
        before, states, norm_attn, weights_attn, wq, wk
    )
    gains = (norm_query.reshape(1, HD), norm_key.reshape(1, HD))
    attended = attend(query_raw, key_raw, value, bias, cosine, sine, *gains, tile, step)
    inputs = states.astype(jnp.float32)
    hidden_one = project_out(attended, weights_attn, states, wo)
    normed_two, factor_two = normalize_rows(hidden_one)
    whole_two, gate, up, product = gate_up(
        n_fsdp, (normed_two * norm_mlp).astype(jnp.bfloat16), rows_gate, rows_up
    )
    outputs = hidden_one + sum_products(n_fsdp, 2, (product,), (rows_down,))
    errors = (outputs - teacher.astype(jnp.float32)) * live[:, None]
    squares = jnp.sum(errors * errors)
    grad_out = errors * (2.0 / (count * D))

    grad_whole, grad_gate, grad_up = grad_hidden_units(
        n_fsdp, grad_out.astype(jnp.bfloat16), rows_down, gate, up
    )
    grad_mid = sum_products(n_fsdp, 4, (grad_gate, grad_up), (rows_gate, rows_up))
    grad_w_down = hidden_rows_grad(contract_first(product, grad_whole))
    grad_w_gate = hidden_rows_grad(contract_first(grad_gate, whole_two)).T
    grad_w_up = hidden_rows_grad(contract_first(grad_up, whole_two)).T
    grad_norm_mlp = jnp.sum(grad_mid * normed_two, axis=0)
    grad_hidden = grad_out + norm_back(grad_mid, normed_two, factor_two, norm_mlp)

    grad_low_out = grad_hidden.astype(jnp.bfloat16)
    grad_w_out = scatter_grad(contract_first(grad_low_out, attended)).T
    grad_attended = back_out(grad_low_out, weights_attn, wo)
    grad_query, grad_before, grad_own, grad_norm_query, grad_norm_key = attend_back(
        query_raw, key_raw, value, bias, cosine, sine, *gains, grad_attended, tile, step
    )
    for j in range(1, back + 1):
        block = grad_before[:, lead - j * own : lead - (j - 1) * own]
        block = lax.ppermute(block, "tp", [(i + j, i) for i in range(n_tp - j)])
        grad_own = grad_own + block.astype(jnp.float32)
    grad_key, grad_value = (grad_own[0].astype(jnp.bfloat16), grad_own[1].astype(jnp.bfloat16))
    grad_joined = jnp.concatenate(
        [
            part.reshape(own, n_tp, -1)
            for part in (grad_query, grad_key, grad_value)
        ],
        axis=2,
    )
    grad_low = back_in(grad_query, grad_key, grad_value, weights_attn)
    grad_weights = scatter_grad(
        contract_first(normed_in, grad_joined.reshape(own, n_tp * (wq + 2 * wk)))
    )
    normed_one, factor_one = normalize_rows(inputs)
    grad_norm_attn = jnp.sum(grad_low * normed_one, axis=0)
    grad_input = grad_hidden + norm_back(grad_low, normed_one, factor_one, norm_attn)
    squares, grad_norm_attn, grad_norm_query, grad_norm_key, grad_norm_mlp = lax.psum(
        (squares, grad_norm_attn, grad_norm_query[0], grad_norm_key[0], grad_norm_mlp),
        ("fsdp", "tp"),
    )
    return (
        outputs,
        squares / (count * D),
        grad_input,
        grad_norm_attn,
        grad_weights[:, :wq],
        grad_weights[:, wq : wq + wk],
        grad_weights[:, wq + wk :],
        grad_norm_query,
        grad_norm_key,
        grad_w_out,
        grad_norm_mlp,
        grad_w_gate,
        grad_w_up,
        grad_w_down,
    )


def solution(mesh):
    tokens = P(("fsdp", "tp"), None)
    rows, columns, sequences = (P("fsdp", "tp"), P("tp", "fsdp"), P("fsdp", None))
    in_specs = (
        tokens,
        sequences,
        sequences,
        tokens,
        P(),
        rows,
        rows,
        rows,
        P(),
        P(),
        columns,
        P(),
        rows,
        rows,
        columns,
    )
    out_specs = (
        tokens,
        P(),
        tokens,
        P(),
        rows,
        rows,
        rows,
        P(),
        P(),
        columns,
        P(),
        rows,
        rows,
        columns,
    )
    return jax.shard_map(shards, mesh=mesh, in_specs=in_specs, out_specs=out_specs, check_vma=False)
```

time: 2610 us -> 1420 us (0.54)
  waiting for transfers between devices: 1760 us -> 368 us
  Pallas kernels: 0 us -> 758 us
  matrix products: 470 us -> 79.2 us
  other arithmetic: 175 us -> 56.5 us
  local copies, waits for them, and re-layouts: 77.9 us -> 34.6 us
    reduce_scatter x8 -> x7, waiting for transfers between devices: 1110 us -> 261 us  [the longest x3 111 us: hidden_rows_grad(): lax.psum_scatter(grad.astype(jnp.bfloat16), 'tp', scatter_dimension=0, ti...]
    pallas_call x0 -> x11, Pallas kernels: none -> 758 us  [the longest x1 194 us: enter(): pl.pallas_call(functools.partial(enter_kernel, size, lanes, back), out_sh...]
    all_gather x8 -> x3, waiting for transfers between devices: 649 us -> 1.94 us  [hidden_rows(): return lax.all_gather(mine, 'tp', axis=0, tiled=True)]
    dot_general x36 -> x0, matrix products: 393 us -> none  [the longest x4 90.5 us: contract_last(): lax.dot_general(left, right, (((1,), (1,)), ((), ())), preferred_element_...]
    ppermute x0 -> x2, waiting for transfers between devices: none -> 103 us  [shards(): block = lax.ppermute(block, 'tp', [(i + j, i) for i in range(n_tp - j)])]
    convert_element_type x10 -> x6, other arithmetic: 77.9 us -> 17.1 us  [the longest x1 6.54 us: shards(): grad_out.astype(jnp.bfloat16)]
    reduce_sum x12 -> x2, other arithmetic: 29.6 us -> 0.75 us  [the longest x1 0.65 us: shards(): count = lax.psum(jnp.sum(padding).astype(jnp.float32), 'fsdp')]
    dot_general x4 -> x5, matrix products: 76.5 us -> 79.2 us  [contract_first(): lax.dot_general(left, right, (((0,), (0,)), ((), ())), preferred_element_...]
  transfers between devices with their start and end apart: 16 -> 17, of which waited for: 12 -> 10; matrix products, arithmetic and copies ran while one was open for 22% -> 10% of each run, Pallas kernels for 0% -> 34%
where the time goes in v1:
time: 1420 us
  Pallas kernels  758 us (53%)
  waiting for transfers between devices  368 us (26%)
  matrix products  79.2 us (6%)
  blocking collectives  79.1 us (6%)
  other arithmetic  56.5 us (4%)
  local copies, waits for them, and re-layouts  34.6 us (2%)
  starting transfers between devices  23.2 us (2%)
  between operations  18.1 us (1%)
    pallas_call x1, Pallas kernels, enter(): pl.pallas_call(functools.partial(enter_kernel, size, lanes, back), out_sh...  194 us
    pallas_call x2, Pallas kernels, sum_products(): pl.pallas_call(functools.partial(sum_products_kernel, size, terms), out_s...  187 us
    reduce_scatter x3, waiting for transfers between devices, hidden_rows_grad(): lax.psum_scatter(grad.astype(jnp.bfloat16), 'tp', scatter_dimension=0, ti...  111 us
    ppermute x2, waiting for transfers between devices, shards(): block = lax.ppermute(block, 'tp', [(i + j, i) for i in range(n_tp - j)])  103 us
    reduce_scatter x2, waiting for transfers between devices, scatter_grad(): lax.psum_scatter(grad.astype(jnp.bfloat16), 'fsdp', scatter_dimension=0,...  99.2 us
    pallas_call x1, Pallas kernels, grad_hidden_units(): pl.pallas_call(functools.partial(grad_hidden_kernel, size), out_shape=(sh...  90.6 us
    pallas_call x1, Pallas kernels, gate_up(): pl.pallas_call(functools.partial(gate_up_kernel, size), out_shape=(shape(...  87.3 us
    pallas_call x1, Pallas kernels, attend_back(): pl.pallas_call(functools.partial(attend_back_kernel, group, step, lead),...  81.7 us
  transfers between devices with their start and end apart: 17, of which 10 were waited for; matrix products, arithmetic and copies ran while one was open for 10% of the time, Pallas kernels for 34%

profile of v1, /device:TPU:0, one launch (start us, length us, event | category | flops | bytes accessed | tf_op | source)
XLA Modules:
  0.0 1416.6 jit_solution(15005000970960471360)
XLA Ops:
  8.8 17.7 %all_to_all.96 = bf16[8,192,256]{2,1,0:T(8,128)(2,1)S(1)} all-to-all(bf16[8,192,256]{2,1,0:T(8,128)(2,1)S(1)} %bitcast.106), channel_id=1, replica_groups=mesh['fsdp'=8,'tp'=4] {'fsdp'}, dimensions={0} | all-to-all | bytes 1572864 | tf_op jit(solution)/shard_map/all_to_all | solution.py:1009
  33.5 194.0 %enter.1 = (bf16[2,512,2048]{2,1,0:T(8,128)(2,1)}, bf16[8,4,256,1536]{3,2,1,0:T(8,128)(2,1)}) custom-call(bf16[512,2048]{1,0:T(8,128)(2,1)} %x_ref.5, bf16[256,1536]{1,0:T(8,128)(2,1)} %pad_maximum_fusion.1.w_ref), custom_call_target="tpu_custom_call" | custom-call | bytes 419430400 | tf_op jit(solution)/shard_map/enter/pallas_call | solution.py:593
  234.8 32.2 %project_in.1 = (bf16[512,2048]{1,0:T(8,128)(2,1)}, f32[512,2048]{1,0:T(8,128)}, f32[1536,1024]{1,0:T(8,128)}, bf16[1536,1024]{1,0:T(8,128)(2,1)}) custom-call(bf16[2,512,2048]{2,1,0:T(8,128)(2,1)} %get-tuple-element.32.before_ref, bf16[512,2048]{1,0:T(8,128)(2,1)} %x_ref.5, f32[1,2048]{1,0:T(1,128)} %bitcast.116, ...), custom_call_target="tpu_custom_call" | custom-call | flops 17179869184 | bytes 23068672 | tf_op jit(solution)/shard_map/project_in/pallas_call | solution.py:661
  277.0 49.8 %attend.1.a_ref = bf16[512,2048]{1,0:T(8,128)(2,1)} custom-call(f32[512,2048]{1,0:T(8,128)} %get-tuple-element.34.q_ref, f32[1536,1024]{1,0:T(8,128)} %get-tuple-element.35.k_ref, bf16[1536,1024]{1,0:T(8,128)(2,1)} %get-tuple-element.36.v_ref, f32[512,1280]{1,0:T(8,128)} %add_select_fusion.bias_ref, f32[1536,128]{1,0:T(8,128)} %get-tuple-element.145.cos_ref, ...), custom_call_target="tpu_custom_call" | custom-call | flops 21474836480 | bytes 13631488 | tf_op jit(solution)/shard_map/attend/pallas_call | solution.py:923
  326.9 15.7 %psum.43 = f32[]{:T(128)} all-reduce(f32[]{:T(128)S(6)} %convert_element_type.106), channel_id=1, replica_groups=mesh['fsdp'=8,'tp'=4] {'fsdp'}, use_global_device_ids=true, to_apply=%region_7.8 | all-reduce | flops 1 | bytes 8 | tf_op jit(solution)/shard_map/psum | solution.py:1050
  343.3 11.3 project_out.1
  361.8 87.3 %gate_up.1 = (bf16[8,2,256,2048]{3,2,1,0:T(8,128)(2,1)}, f32[8,2,256,768]{3,2,1,0:T(8,128)}, f32[8,2,256,768]{3,2,1,0:T(8,128)}, bf16[8,2,256,768]{3,2,1,0:T(8,128)(2,1)}) custom-call(bf16[2,256,2048]{2,1,0:T(8,128)(2,1)} %bitcast.107, bf16[768,2048]{1,0:T(8,128)(2,1)} %all-gather.4.cloned.1.call-done.wg_ref.refs_2_, ...), custom_call_target="tpu_custom_call" | custom-call | flops 25769803776 | bytes 209715200 | tf_op jit(solution)/shard_map/gate_up/pallas_call | solution.py:338
  449.1 89.0 %sum_products.2 = f32[2,256,2048]{2,1,0:T(8,128)} custom-call(bf16[8,2,256,768]{3,2,1,0:T(8,128)(2,1)} %get-tuple-element.37.refs_0_, bf16[768,2048]{1,0:T(8,128)(2,1)} %all-gather.8.cloned.1.call-done.refs_1_.wd_ref), custom_call_target="tpu_custom_call" | custom-call | flops 12884901888 | bytes 209715200 | tf_op jit(solution)/shard_map/sum_products/pallas_call | solution.py:505
  544.7 90.6 %grad_hidden_units.1 = (bf16[8,2,256,2048]{3,2,1,0:T(8,128)(2,1)}, bf16[8,2,256,768]{3,2,1,0:T(8,128)(2,1)}, bf16[8,2,256,768]{3,2,1,0:T(8,128)(2,1)}) custom-call(bf16[2,256,2048]{2,1,0:T(8,128)(2,1)} %bitcast.108, bf16[768,2048]{1,0:T(8,128)(2,1)} %all-gather.8.cloned.1.call-done.refs_1_.wd_ref, f32[8,2,256,768]{3,2,1,0:T(8,128)} %get-tuple-element.38.gate_in, ...), custom_call_target="tpu_custom_call" | custom-call | flops 12884901888 | bytes 209715200 | tf_op jit(solution)/shard_map/grad_hidden_units/pallas_call | solution.py:452
  635.3 97.6 %sum_products.3 = f32[2,256,2048]{2,1,0:T(8,128)} custom-call(bf16[8,2,256,768]{3,2,1,0:T(8,128)(2,1)} %get-tuple-element.40.refs_0_, bf16[8,2,256,768]{3,2,1,0:T(8,128)(2,1)} %get-tuple-element.41.refs_1_, bf16[768,2048]{1,0:T(8,128)(2,1)} %all-gather.4.cloned.1.call-done.wg_ref.refs_2_, bf16[768,2048]{1,0:T(8,128)(2,1)} %all-gather.6.cloned.1.call-done.wu_ref.refs_3_), custom_call_target="tpu_custom_call" | custom-call | flops 25769803776 | bytes 209715200 | tf_op jit(solution)/shard_map/sum_products/pallas_call | solution.py:505
  750.8 8.8 back_out.1.do_ref
  759.6 81.7 %attend_back.1 = (bf16[512,2048]{1,0:T(8,128)(2,1)}, bf16[2,1024,1024]{2,1,0:T(8,128)(2,1)}, f32[2,512,1024]{2,1,0:T(8,128)}, f32[1,128]{1,0:T(1,128)}, f32[1,128]{1,0:T(1,128)}) custom-call(f32[512,2048]{1,0:T(8,128)} %get-tuple-element.34.q_ref, f32[1536,1024]{1,0:T(8,128)} %get-tuple-element.35.k_ref, bf16[1536,1024]{1,0:T(8,128)(2,1)} %get-tuple-element.36.v_ref, ...), custom_call_target="tpu_custom_call" | custom-call | flops 53687091200 | bytes 33554432 | tf_op jit(solution)/shard_map/attend_back/pallas_call | solution.py:949
  852.2 57.7 %collective-permute-done.1 = bf16[2,512,1024]{2,1,0:T(8,128)(2,1)} collective-permute-done((bf16[2,512,1024]{2,1,0:T(8,128)(2,1)}, bf16[2,512,1024]{2,1,0:T(8,128)(2,1)}, u32[]{:S(2)}, u32[]{:S(2)}) %collective-permute-start.1) | collective-permute-done | bytes 2097184 | tf_op jit(solution)/shard_map/ppermute | solution.py:1095
  909.9 44.9 %collective-permute-done = bf16[2,512,1024]{2,1,0:T(8,128)(2,1)} collective-permute-done((bf16[2,512,1024]{2,1,0:T(8,128)(2,1)}, bf16[2,512,1024]{2,1,0:T(8,128)(2,1)}, u32[]{:S(2)}, u32[]{:S(2)}) %collective-permute-start) | collective-permute-done | bytes 2097184 | tf_op jit(solution)/shard_map/ppermute | solution.py:1095
  968.2 12.4 convolution_convert_fusion
  980.7 20.0 %bitcast_convert_fusion.2 = bf16[768,2048]{1,0:T(8,128)(2,1)} fusion(bf16[8,2,256,768]{3,2,1,0:T(8,128)(2,1)} %get-tuple-element.40.refs_0_, bf16[8,2,256,2048]{3,2,1,0:T(8,128)(2,1)} %get-tuple-element.48), kind=kOutput, calls=%fused_computation.4 | convolution fusion | flops 12886474752 | bytes 26214400 | tf_op jit(solution)/shard_map/dot_general | solution.py:37
  1000.7 19.9 %bitcast_convert_fusion.1 = bf16[768,2048]{1,0:T(8,128)(2,1)} fusion(bf16[8,2,256,768]{3,2,1,0:T(8,128)(2,1)} %get-tuple-element.41.refs_1_, bf16[8,2,256,2048]{3,2,1,0:T(8,128)(2,1)} %get-tuple-element.48), kind=kOutput, calls=%fused_computation.3 | convolution fusion | flops 12886474752 | bytes 26214400 | tf_op jit(solution)/shard_map/dot_general | solution.py:37
  1020.8 20.1 %bitcast_convert_fusion = bf16[768,2048]{1,0:T(8,128)(2,1)} fusion(bf16[8,2,256,768]{3,2,1,0:T(8,128)(2,1)} %get-tuple-element.37.refs_0_, bf16[8,2,256,2048]{3,2,1,0:T(8,128)(2,1)} %get-tuple-element.49), kind=kOutput, calls=%fused_computation.2 | convolution fusion | flops 12886474752 | bytes 26214400 | tf_op jit(solution)/shard_map/dot_general | solution.py:37
  1041.7 99.2 %reduce-scatter.8.cloned.1.call-done = bf16[256,4096]{1,0:T(8,128)(2,1)} async-done(((bf16[2048,4096]{1,0:T(8,128)(2,1)}), bf16[256,4096]{1,0:T(8,128)(2,1)}) %reduce-scatter.8.cloned.1.call-update) | async-done | bytes 2097168 | tf_op jit(solution)/shard_map/reduce_scatter | solution.py:1019
  1141.4 62.6 %reduce-scatter.16.cloned.1.call-done = bf16[192,2048]{1,0:T(8,128)(2,1)} async-done(((bf16[768,2048]{1,0:T(8,128)(2,1)}), bf16[192,2048]{1,0:T(8,128)(2,1)}) %reduce-scatter.16.cloned.1.call-update) | async-done | bytes 786448 | tf_op jit(solution)/shard_map/reduce_scatter | solution.py:1014
  1209.8 15.9 %back_in.1 = f32[512,2048]{1,0:T(8,128)} custom-call(bf16[512,2048]{1,0:T(8,128)(2,1)} %get-tuple-element.42.q_ref, bf16[512,1024]{1,0:T(8,128)(2,1)} %bitcast.96, bf16[512,1024]{1,0:T(8,128)(2,1)} %bitcast.95, bf16[8,4,256,1536]{3,2,1,0:T(8,128)(2,1)} %get-tuple-element.33.w_ref), custom_call_target="tpu_custom_call" | custom-call | flops 8589934592 | bytes 25165824 | tf_op jit(solution)/shard_map/back_in/pallas_call | solution.py:768
  1225.7 41.1 %reduce-scatter.18.cloned.1.call-done = bf16[192,2048]{1,0:T(8,128)(2,1)} async-done(((bf16[768,2048]{1,0:T(8,128)(2,1)}), bf16[192,2048]{1,0:T(8,128)(2,1)}) %reduce-scatter.18.cloned.1.call-update) | async-done | bytes 786448 | tf_op jit(solution)/shard_map/reduce_scatter | solution.py:1014
  1276.8 45.7 %all-reduce.1 = (f32[]{:T(128)}, f32[2048]{0:T(1024)}, f32[128]{0:T(128)}, f32[128]{0:T(128)}, f32[2048]{0:T(1024)}) all-reduce(f32[]{:T(128)} %get-tuple-element.121, f32[2048]{0:T(1024)S(1)} %get-tuple-element.108, f32[128]{0:T(128)S(1)} %bitcast.119, f32[128]{0:T(128)S(1)} %bitcast.120, ...), channel_id=1, replica_groups=mesh['fsdp'=8,'tp'=4] {'fsdp','tp'}, use_global_device_ids=true, to_apply=%region_5.6 | all-reduce | flops 4353 | bytes 34824 | tf_op jit(solution)/shard_map/psum | solution.py:1112
  1362.1 42.7 %reduce-scatter.10.cloned.1.call-done = bf16[256,1024]{1,0:T(8,128)(2,1)} async-done(((bf16[256,4096]{1,0:T(8,128)(2,1)}), bf16[256,1024]{1,0:T(8,128)(2,1)}) %reduce-scatter.10.cloned.1.call-update) | async-done | bytes 524304 | tf_op jit(solution)/shard_map/reduce_scatter | solution.py:1022
  (143 shorter events, 140.4 us)
Async XLA Ops:
  7.2 25.0 %copy-start.12 = (bf16[512,256]{1,0:T(8,128)(2,1)S(1)}, bf16[512,256]{1,0:T(8,128)(2,1)}, u32[]{:S(2)}) copy-start(bf16[512,256]{1,0:T(8,128)(2,1)} %param.25) | copy-start | bytes 786436
  7.2 352.7 %all-gather.4.cloned.1.call-start = ((), (), s32[]{:S(2)}) async-start(), calls=%async_computation.13 | async-start | bytes 3932160 | tf_op jit(solution)/shard_map/all_gather | solution.py:1010
  8.7 23.8 %copy-start.13 = (bf16[256,512]{1,0:T(8,128)(2,1)S(1)}, bf16[256,512]{1,0:T(8,128)(2,1)}, u32[]{:S(2)}) copy-start(bf16[256,512]{1,0:T(8,128)(2,1)} %param.20) | copy-start | bytes 786436
  27.4 200.0 %copy-start.16 = (s32[1,2048]{1,0:T(1,128)S(1)}, s32[1,2048]{1,0:T(1,128)}, u32[]{:S(2)}) copy-start(s32[1,2048]{1,0:T(1,128)} %param.17) | copy-start | bytes 24580
  28.6 199.1 %all-to-all-start.1 = ((bf16[8,192,256]{2,1,0:T(8,128)(2,1)}), bf16[8,192,256]{2,1,0:T(8,128)(2,1)S(1)}, u32[]{:S(2)}, u32[]{:S(2)}) async-start(bf16[8,192,256]{2,1,0:T(8,128)(2,1)} %bitcast.13), calls=%async_computation.1 | async-start | bytes 1572864 | tf_op jit(solution)/shard_map/all_to_all | solution.py:1009
  227.7 48.0 %all-to-all-start.2 = ((bf16[8,192,256]{2,1,0:T(8,128)(2,1)}), bf16[8,192,256]{2,1,0:T(8,128)(2,1)S(1)}, u32[]{:S(2)}, u32[]{:S(2)}) async-start(bf16[8,192,256]{2,1,0:T(8,128)(2,1)} %bitcast.15), calls=%async_computation.2 | async-start | bytes 1572864 | tf_op jit(solution)/shard_map/all_to_all | solution.py:1009
  231.7 130.1 %all-gather.6.cloned.1.call-start = ((), (), s32[]{:S(2)}) async-start(), calls=%async_computation.14 | async-start | bytes 3932160 | tf_op jit(solution)/shard_map/all_gather | solution.py:1010
  232.7 216.4 %all-gather.8.cloned.1.call-start = ((), (), s32[]{:S(2)}) async-start(), calls=%async_computation.15 | async-start | bytes 3932160 | tf_op jit(solution)/shard_map/all_gather | solution.py:1010
  276.7 764.3 %reduce-scatter.12.cloned.1.call-start = ((), (), s32[]{:S(2)}) async-start(), calls=%async_computation.18 | async-start | bytes 9437184 | tf_op jit(solution)/shard_map/reduce_scatter | solution.py:1019
  449.1 89.0 %copy-start.1 = (f32[512,2048]{1,0:T(8,128)S(1)}, f32[512,2048]{1,0:T(8,128)}, u32[]{:S(2)}) copy-start(f32[512,2048]{1,0:T(8,128)} %project_out.1) | copy-start | bytes 12582916
  449.1 89.0 %copy-start.9 = (bf16[512,2048]{1,0:T(8,128)(2,1)S(1)}, bf16[512,2048]{1,0:T(8,128)(2,1)}, u32[]{:S(2)}) copy-start(bf16[512,2048]{1,0:T(8,128)(2,1)} %param.18) | copy-start | bytes 6291460
  750.8 390.2 %reduce-scatter.8.cloned.1.call-start = ((), (), s32[]{:S(2)}) async-start(), calls=%async_computation.16 | async-start | bytes 18874368 | tf_op jit(solution)/shard_map/reduce_scatter | solution.py:1019
  846.4 63.5 %collective-permute-start.1 = (bf16[2,512,1024]{2,1,0:T(8,128)(2,1)}, bf16[2,512,1024]{2,1,0:T(8,128)(2,1)}, u32[]{:S(2)}, u32[]{:S(2)}) collective-permute-start(bf16[2,512,1024]{2,1,0:T(8,128)(2,1)} %get-tuple-element.123), channel_id=1, source_target_pairs={{2,0},{3,1},{6,4},{7,5},{10,8},{11,9},{14,12},{15,13},{18,16},{19,... | collective-permute-start | bytes 6291464 | tf_op jit(solution)/shard_map/ppermute | solution.py:1095
  847.7 107.1 %collective-permute-start = (bf16[2,512,1024]{2,1,0:T(8,128)(2,1)}, bf16[2,512,1024]{2,1,0:T(8,128)(2,1)}, u32[]{:S(2)}, u32[]{:S(2)}) collective-permute-start(bf16[2,512,1024]{2,1,0:T(8,128)(2,1)} %get-tuple-element.122), channel_id=1, source_target_pairs={{1,0},{2,1},{3,2},{5,4},{6,5},{7,6},{9,8},{10,9},{11,10},{13,12},{... | collective-permute-start | bytes 6291464 | tf_op jit(solution)/shard_map/ppermute | solution.py:1095
  980.6 223.4 %reduce-scatter.16.cloned.1.call-start = ((), (), s32[]{:S(2)}) async-start(), calls=%async_computation.20 | async-start | bytes 3932160 | tf_op jit(solution)/shard_map/reduce_scatter | solution.py:1014
  1000.7 266.1 %reduce-scatter.18.cloned.1.call-start = ((), (), s32[]{:S(2)}) async-start(), calls=%async_computation.21 | async-start | bytes 3932160 | tf_op jit(solution)/shard_map/reduce_scatter | solution.py:1014
  1020.7 309.8 %reduce-scatter.20.cloned.1.call-start = ((), (), s32[]{:S(2)}) async-start(), calls=%async_computation.22 | async-start | bytes 3932160 | tf_op jit(solution)/shard_map/reduce_scatter | solution.py:1014
  1040.9 100.1 %copy-start.2 = (bf16[512,2048]{1,0:T(8,128)(2,1)S(1)}, bf16[512,2048]{1,0:T(8,128)(2,1)}, u32[]{:S(2)}) copy-start(bf16[512,2048]{1,0:T(8,128)(2,1)} %x_ref.5) | copy-start | bytes 6291460
  1040.9 319.2 %reduce-scatter.14.cloned.1.call-start = ((), (), s32[]{:S(2)}) async-start(), calls=%async_computation.19 | async-start | bytes 1310720 | tf_op jit(solution)/shard_map/reduce_scatter | solution.py:1022
  1041.6 363.1 %reduce-scatter.10.cloned.1.call-start = ((), (), s32[]{:S(2)}) async-start(), calls=%async_computation.17 | async-start | bytes 2621440 | tf_op jit(solution)/shard_map/reduce_scatter | solution.py:1022
  1206.1 62.8 %all-to-all-start.3 = ((bf16[192,8,256]{2,0,1:T(8,128)(2,1)}), bf16[192,8,256]{2,0,1:T(8,128)(2,1)S(1)}, u32[]{:S(2)}, u32[]{:S(2)}) async-start(bf16[192,8,256]{2,0,1:T(8,128)(2,1)} %bitcast.93), calls=%async_computation.8 | async-start | bytes 1572864 | tf_op jit(solution)/shard_map/all_to_all | solution.py:1015
  1209.8 63.5 %copy-start.18 = (f32[2048]{0:T(1024)S(1)}, f32[2048]{0:T(1024)}, u32[]{:S(2)}) copy-start(f32[2048]{0:T(1024)} %param.19) | copy-start | bytes 24580
  1268.9 63.7 %all-to-all-start.4 = ((bf16[192,8,256]{2,0,1:T(8,128)(2,1)}), bf16[192,8,256]{2,0,1:T(8,128)(2,1)}, u32[]{:S(2)}, u32[]{:S(2)}) async-start(bf16[192,8,256]{2,0,1:T(8,128)(2,1)} %bitcast.92), calls=%async_computation.10 | async-start | bytes 1572864 | tf_op jit(solution)/shard_map/all_to_all | solution.py:1015
  1332.6 17.1 %all-to-all-start.5 = ((bf16[192,8,256]{2,0,1:T(8,128)(2,1)}), bf16[192,8,256]{2,0,1:T(8,128)(2,1)}, u32[]{:S(2)}, u32[]{:S(2)}) async-start(bf16[192,8,256]{2,0,1:T(8,128)(2,1)} %bitcast.91), calls=%async_computation.12 | async-start | bytes 1572864 | tf_op jit(solution)/shard_map/all_to_all | solution.py:1015
  (17 other events, 176.7 us)
Sparse Core Ops, SparseCore 0:
  27.5 110.8 all-gather.3
  234.1 127.6 all-gather.5
  363.3 62.1 all-gather.7
  750.9 130.9 reduce-scatter.11
  980.7 160.1 reduce-scatter.7
  1143.8 60.2 reduce-scatter.15
  1206.4 60.2 reduce-scatter.17
  1269.2 61.2 reduce-scatter.19
  1332.9 27.1 reduce-scatter.13
  1362.2 42.5 reduce-scatter.9

commit v2 on v1

--- a/solution.py
+++ b/solution.py
@@ -167,7 +167,7 @@
     ]
 
 
-def scatter_rows_in(size, me, made, held, sent, came, sems, partial, final):
+def scatter_rows_in(size, me, made, held, sent, came, sems, partial, final, between=None):
     chip_send, chip_recv, core_send, core_recv = sems
     steps = len(chip_bits(size))
     order = [bits[::-1] for bits in orders(size)]
@@ -247,6 +247,8 @@
         if q + 1 < len(patterns):
             for_sibling(q + 1)
         for_chips(q)
+        if between:
+            between(q + 1, len(patterns))
     for q in range(len(patterns)):
         for part in range(PARTS):
             core_copy(part, q).wait_send()
@@ -519,17 +521,29 @@
     return out.reshape(PARTS * rows, width)
 
 
-def enter_kernel(size, lanes, back, x_ref, w_ref, before, whole, load, z_send, z_recv, x_send, x_recv, *sems):
+def enter_kernel(
+    size, lanes, back, x_ref, w_ref, m_ref, c_ref,
+    before, whole, mine, count, counts, loads, z_send, z_recv, x_send, x_recv, m_send, m_recv, c_send, c_recv, *sems
+):
     me, z = (lax.axis_index("fsdp"), lax.axis_index("tp"))
-    own = pltpu.make_async_copy(w_ref, whole.at[me, z], load)
-    own.start()
+    part_of = lambda device: pl.ds(
+        pl.multiple_of(device * m_ref.shape[-1], m_ref.shape[-1]), m_ref.shape[-1]
+    )
+    local = [
+        pltpu.make_async_copy(w_ref, whole.at[me, z], loads.at[0]),
+        pltpu.make_async_copy(m_ref.at[me], mine.at[:, :, part_of(me)], loads.at[1]),
+    ]
+    for copy in local:
+        copy.start()
+    counts[me] = c_ref[...]
     barrier = pltpu.get_barrier_semaphore()
-    peers = [{"fsdp": flip(me, bit)} for bit in [1] + chip_bits(size)]
+    peers = [{"fsdp": flip(me, other)} for other in range(1, size)]
     peers += [{"tp": lax.rem(z + hop, lanes)} for hop in range(1, lanes)]
     for peer in peers:
         pl.semaphore_signal(barrier, inc=1, device_id=peer, device_id_type=MESH)
     pl.semaphore_wait(barrier, len(peers))
-    own.wait()
+    for copy in local:
+        copy.wait()
 
     def lane(part):
         return lax.rem(z + lanes - part, lanes)
@@ -546,70 +560,305 @@
 
     def token_copy(hop):
         return pltpu.make_async_remote_copy(
-            src_ref=x_ref,
+            src_ref=x_ref if hop == 1 else before.at[hop - 2],
             dst_ref=before.at[hop - 1],
             send_sem=x_send.at[hop - 1],
             recv_sem=x_recv.at[hop - 1],
-            device_id={"tp": lax.rem(z + hop, lanes)},
+            device_id={"tp": lax.rem(z + 1, lanes)},
             device_id_type=MESH,
         )
 
+    def unit_copy(other):
+        peer = flip(me, other)
+        return pltpu.make_async_remote_copy(
+            src_ref=m_ref.at[peer],
+            dst_ref=mine.at[:, :, part_of(me)],
+            send_sem=m_send.at[other - 1],
+            recv_sem=m_recv.at[other - 1],
+            device_id={"fsdp": peer},
+            device_id_type=MESH,
+        )
+
+    def count_copy(other):
+        return pltpu.make_async_remote_copy(
+            src_ref=c_ref,
+            dst_ref=counts.at[me],
+            send_sem=c_send.at[other - 1],
+            recv_sem=c_recv.at[other - 1],
+            device_id={"fsdp": flip(me, other)},
+            device_id_type=MESH,
+        )
+
+    def send_tokens(hop):
+        @pl.when((z >= hop - 1) & (z + 1 < lanes))
+        def _():
+            token_copy(hop).start()
+
+    def take_tokens(hop):
+        @pl.when(z >= hop)
+        def _():
+            token_copy(hop).wait_recv()
+
     gather = Gather(size, me, whole, sems, lanes, lane)
+    gather.forward(0, 0)
     for hop in range(1, lanes):
         lane_copy(hop).start()
-    gather.forward(0, 0)
-    for hop in range(1, back + 1):
-
-        @pl.when(z + hop < lanes)
-        def _():
-            token_copy(hop).start()
-
+    send_tokens(1)
+    for other in range(1, size):
+        count_copy(other).start()
     events = [(part, pattern) for part in range(lanes) for pattern in gather.patterns]
     events.sort(key=lambda event: (2 * event[0] + top(event[1]) + 1, event))
-    for part, pattern in events[1:]:
-        if pattern:
-            gather.arrive(part, pattern)
-        else:
-            lane_copy(part).wait_recv()
-        gather.forward(part, pattern)
+    for part, pattern in events:
+        if (part, pattern) != (0, 0):
+            if pattern:
+                gather.arrive(part, pattern)
+            else:
+                lane_copy(part).wait_recv()
+            gather.forward(part, pattern)
+        if (part, pattern) == (lanes - 1, 0):
+            for hop in range(1, back):
+                take_tokens(hop)
+                send_tokens(hop + 1)
+    for other in range(1, size):
+        unit_copy(other).start()
+    for other in range(1, size):
+        count_copy(other).wait_recv()
+    count[...] = sum(counts[other] for other in range(size))
     for part, pattern in events:
         gather.core_copy(part, pattern).wait_recv()
+    for other in range(1, size):
+        unit_copy(other).wait_recv()
+    take_tokens(back)
     gather.finish()
     for hop in range(1, lanes):
         lane_copy(hop).wait_send()
+    for other in range(1, size):
+        unit_copy(other).wait_send()
+        count_copy(other).wait_send()
     for hop in range(1, back + 1):
 
-        @pl.when(z + hop < lanes)
+        @pl.when((z >= hop - 1) & (z + 1 < lanes))
         def _():
             token_copy(hop).wait_send()
 
-        @pl.when(z >= hop)
-        def _():
-            token_copy(hop).wait_recv()
-
-
-def enter(size, lanes, back, values, weights):
+
+def enter(size, lanes, back, values, weights, units, count):
     any_space = pl.BlockSpec(memory_space=pl.ANY)
+    vmem = pl.BlockSpec(memory_space=pltpu.VMEM)
+    _, kinds, rows, columns = units.shape
+    others = pltpu.SemaphoreType.DMA((size - 1,))
+    lane = pltpu.SemaphoreType.DMA((lanes - 1,))
+    hop = pltpu.SemaphoreType.DMA((back,))
     return pl.pallas_call(
         functools.partial(enter_kernel, size, lanes, back),
         out_shape=(
             jax.ShapeDtypeStruct((back, *values.shape), values.dtype),
             jax.ShapeDtypeStruct((size, lanes, *weights.shape), weights.dtype),
-        ),
-        in_specs=[any_space, any_space],
-        out_specs=(any_space, any_space),
+            jax.ShapeDtypeStruct((kinds, rows, size * columns), units.dtype),
+            jax.ShapeDtypeStruct(count.shape, count.dtype),
+        ),
+        in_specs=[any_space, any_space, any_space, vmem],
+        out_specs=(any_space, any_space, any_space, vmem),
         scratch_shapes=[
-            pltpu.SemaphoreType.DMA,
-            pltpu.SemaphoreType.DMA((lanes - 1,)),
-            pltpu.SemaphoreType.DMA((lanes - 1,)),
-            pltpu.SemaphoreType.DMA((back,)),
-            pltpu.SemaphoreType.DMA((back,)),
+            pltpu.VMEM((size, *count.shape), count.dtype),
+            pltpu.SemaphoreType.DMA((2,)),
+            lane,
+            lane,
+            hop,
+            hop,
+            others,
+            others,
+            others,
+            others,
             *gather_semaphores(size, lanes),
         ],
         compiler_params=pltpu.CompilerParams(collective_id=5, has_side_effects=True),
         cost_estimate=pl.CostEstimate(flops=0, bytes_accessed=400 * 1024 * 1024, transcendentals=0),
         name="enter",
-    )(values, weights)
+    )(values, weights, units, count)
+
+
+def flow_kernel(size, lanes, terms, hops, *refs):
+    lefts, rights = (refs[:terms], refs[terms : 2 * terms])
+    at = 2 * terms + (1 if hops else 0)
+    parts_in = refs[2 * terms] if hops else None
+    out = refs[at]
+    arrived = refs[at + 1] if hops else None
+    at += 2 if hops else 1
+    left, right, loads, made, held, sent, came, *rest = refs[at:]
+    sems = rest[:4]
+    me, z = (lax.axis_index("fsdp"), lax.axis_index("tp"))
+    copies = [
+        pltpu.make_async_copy(source, target.at[i], loads.at[j, i])
+        for j, (sources, target) in enumerate(((lefts, left), (rights, right)))
+        for i, source in enumerate(sources)
+        if j or i < left.shape[0]
+    ]
+    for copy in copies:
+        copy.start()
+    barrier = pltpu.get_barrier_semaphore()
+    peers = [{"fsdp": flip(me, bit)} for bit in [1] + chip_bits(size)]
+    if hops:
+        peers += [{"tp": lax.rem(z + 1, lanes)}, {"tp": lax.rem(z + lanes - 1, lanes)}]
+    for peer in peers:
+        pl.semaphore_signal(barrier, inc=1, device_id=peer, device_id_type=MESH)
+    pl.semaphore_wait(barrier, len(peers))
+    rows = left.shape[2] // size
+
+    if hops:
+        mixed, got, mix_sem, hop_send, hop_recv = rest[4:]
+
+        def hop_copy(number):
+            return pltpu.make_async_remote_copy(
+                src_ref=mixed.at[number],
+                dst_ref=got.at[number],
+                send_sem=hop_send.at[number],
+                recv_sem=hop_recv.at[number],
+                device_id={"tp": lax.rem(z + lanes - 1, lanes)},
+                device_id_type=MESH,
+            )
+
+        def hop(number):
+            load = pltpu.make_async_copy(
+                parts_in.at[hops - 1 - number], mixed.at[number], mix_sem.at[number]
+            )
+            load.start()
+            load.wait()
+            if number:
+
+                @pl.when(z + 1 < lanes)
+                def _():
+                    hop_copy(number - 1).wait_recv()
+
+                    @pl.loop(0, 2)
+                    def _(kind):
+                        total = mixed[number, kind].astype(jnp.float32)
+                        total = total + got[number - 1, kind].astype(jnp.float32)
+                        mixed[number, kind] = total.astype(jnp.bfloat16)
+
+            @pl.when(z > 0)
+            def _():
+                hop_copy(number).start()
+
+        hop(0)
+    for copy in copies:
+        copy.wait()
+
+    def partial(part, slot, columns):
+        block = left[part if left.shape[0] > 1 else 0, :, pl.ds(pl.multiple_of(slot * rows, rows), rows)]
+        return contract_first(block, right[part, :, columns])
+
+    def between(q, count):
+        if hops:
+            for number in range(1, hops):
+                if q == number * count // hops:
+                    hop(number)
+
+    scatter_rows_in(size, me, made, held, sent, came, sems, partial, out, between)
+    if hops:
+
+        @pl.when(z + 1 < lanes)
+        def _():
+            hop_copy(hops - 1).wait_recv()
+            arrived[...] = got[hops - 1]
+
+        @pl.when(z + 1 == lanes)
+        def _():
+            arrived[...] = jnp.zeros_like(arrived)
+
+        @pl.when(z > 0)
+        def _():
+            for number in range(hops):
+                hop_copy(number).wait_send()
+
+
+def flow(size, lanes, number, lefts, rights, parts_in=None):
+    tokens, depth = lefts[0].shape
+    width = rights[0].shape[1]
+    any_space = pl.BlockSpec(memory_space=pl.ANY)
+    vmem = pl.BlockSpec(memory_space=pltpu.VMEM)
+    rows = depth // size
+    hops = parts_in.shape[0] if parts_in is not None else 0
+    distinct = 1 if lefts[0] is lefts[1] else PARTS
+    out_shape = [jax.ShapeDtypeStruct((PARTS, rows, width), jnp.float32)]
+    scratch = [
+        pltpu.VMEM((distinct, tokens, depth), jnp.bfloat16),
+        pltpu.VMEM((PARTS, tokens, width), jnp.bfloat16),
+        pltpu.SemaphoreType.DMA((2, PARTS)),
+        *scatter_scratch(size, rows, width),
+    ]
+    operands = [*lefts, *rights]
+    if hops:
+        out_shape.append(jax.ShapeDtypeStruct(parts_in.shape[1:], jnp.bfloat16))
+        scratch += [
+            pltpu.VMEM(parts_in.shape, jnp.bfloat16),
+            pltpu.VMEM(parts_in.shape, jnp.bfloat16),
+            pltpu.SemaphoreType.DMA((hops,)),
+            pltpu.SemaphoreType.DMA((hops,)),
+            pltpu.SemaphoreType.DMA((hops,)),
+        ]
+        operands.append(parts_in)
+    return pl.pallas_call(
+        functools.partial(flow_kernel, size, lanes, PARTS, hops),
+        out_shape=tuple(out_shape),
+        in_specs=[any_space] * len(operands),
+        out_specs=(vmem,) * len(out_shape),
+        scratch_shapes=scratch,
+        compiler_params=pltpu.CompilerParams(
+            collective_id=number, has_side_effects=True, vmem_limit_bytes=VMEM
+        ),
+        cost_estimate=pl.CostEstimate(
+            flops=4 * tokens * depth * width, bytes_accessed=200 * 1024 * 1024, transcendentals=0
+        ),
+        name="flow",
+    )(*operands)
+
+
+def sum_small_kernel(size, lanes, x_ref, o_ref, came, send, recv):
+    me, z = (lax.axis_index("fsdp"), lax.axis_index("tp"))
+    peers = []
+    for name, index, count in (("fsdp", me, size), ("tp", z, lanes)):
+        bit = 1
+        while bit < count:
+            peers.append({name: flip(index, bit)})
+            bit *= 2
+    barrier = pltpu.get_barrier_semaphore()
+    for peer in peers:
+        pl.semaphore_signal(barrier, inc=1, device_id=peer, device_id_type=MESH)
+    pl.semaphore_wait(barrier, len(peers))
+    sent = came.shape[0] // 2
+    came[sent] = x_ref[...]
+    for step, peer in enumerate(peers):
+        copy = pltpu.make_async_remote_copy(
+            src_ref=came.at[sent + step],
+            dst_ref=came.at[step],
+            send_sem=send.at[step],
+            recv_sem=recv.at[step],
+            device_id=peer,
+            device_id_type=MESH,
+        )
+        copy.start()
+        copy.wait()
+        came[sent + step + 1] = came[sent + step] + came[step]
+    o_ref[...] = came[sent + len(peers)]
+
+
+def sum_small(size, lanes, values):
+    steps = (size * lanes).bit_length() - 1
+    vmem = pl.BlockSpec(memory_space=pltpu.VMEM)
+    return pl.pallas_call(
+        functools.partial(sum_small_kernel, size, lanes),
+        out_shape=jax.ShapeDtypeStruct(values.shape, values.dtype),
+        in_specs=[vmem],
+        out_specs=vmem,
+        scratch_shapes=[
+            pltpu.VMEM((2 * (steps + 1), *values.shape), values.dtype),
+            pltpu.SemaphoreType.DMA((steps,)),
+            pltpu.SemaphoreType.DMA((steps,)),
+        ],
+        compiler_params=pltpu.CompilerParams(collective_id=8, has_side_effects=True),
+        name="sum_small",
+    )(values)
 
 
 def project_kernel(
@@ -894,9 +1143,11 @@
         grad_key = turn_back(dk[...], cos_ref[...], sin_ref[...])
         gk_ref[...] += jnp.sum(grad_key * normed_key, axis=0, keepdims=True)
         grad_key = norm_back(grad_key, normed_key, key_factor, nk_ref[...])
-        if lead:
-            prev_ref[0] = grad_key[:lead].astype(jnp.bfloat16)
-            prev_ref[1] = dv[:lead, :].astype(jnp.bfloat16)
+        back, _, own, _ = prev_ref.shape
+        for hop in range(back):
+            rows = slice(lead - (hop + 1) * own, lead - hop * own)
+            prev_ref[hop, 0] = grad_key[rows].astype(jnp.bfloat16)
+            prev_ref[hop, 1] = dv[rows, :].astype(jnp.bfloat16)
         own_ref[0] = grad_key[lead:]
         own_ref[1] = dv[lead:, :]
 
@@ -951,7 +1202,7 @@
         grid=(heads, own // tile),
         out_shape=(
             jax.ShapeDtypeStruct(queries.shape, jnp.bfloat16),
-            jax.ShapeDtypeStruct((2, lead, heads * HD), jnp.bfloat16),
+            jax.ShapeDtypeStruct((lead // own, 2, own, heads * HD), jnp.bfloat16),
             jax.ShapeDtypeStruct((2, own, heads * HD), jnp.float32),
             jax.ShapeDtypeStruct((1, HD), jnp.float32),
             jax.ShapeDtypeStruct((1, HD), jnp.float32),
@@ -960,7 +1211,7 @@
         + [pl.BlockSpec((tile, group * HD), lambda g, t: (t, g))],
         out_specs=(
             pl.BlockSpec((tile, group * HD), lambda g, t: (t, g)),
-            pl.BlockSpec((2, lead, HD), lambda g, t: (0, 0, g)),
+            pl.BlockSpec((lead // own, 2, own, HD), lambda g, t: (0, 0, 0, g)),
             pl.BlockSpec((2, own, HD), lambda g, t: (0, 0, g)),
             pl.BlockSpec((1, HD), whole),
             pl.BlockSpec((1, HD), whole),
@@ -1005,21 +1256,15 @@
     return (bias, cosine, sine, step, live[lead:].astype(jnp.float32))
 
 
-def hidden_rows(weight_t):
-    mine = lax.all_to_all(weight_t, "fsdp", 0, 1, tiled=True)
-    return lax.all_gather(mine, "tp", axis=0, tiled=True)
-
-
 def hidden_rows_grad(grad):
     mine = lax.psum_scatter(grad.astype(jnp.bfloat16), "tp", scatter_dimension=0, tiled=True)
     return lax.all_to_all(mine, "fsdp", 1, 0, tiled=True).astype(jnp.float32)
 
 
-def scatter_grad(grad):
-    rows = lax.psum_scatter(
-        grad.astype(jnp.bfloat16), "fsdp", scatter_dimension=0, tiled=True
-    )
-    return lax.psum_scatter(rows, "tp", scatter_dimension=1, tiled=True).astype(jnp.float32)
+def over_lanes(grad):
+    return lax.psum_scatter(
+        grad.astype(jnp.bfloat16), "tp", scatter_dimension=2, tiled=True
+    ).astype(jnp.float32)
 
 
 def shards(
@@ -1047,17 +1292,22 @@
     tile = min(256, own)
     span = WINDOW + tile if lead >= WINDOW else lead + own
     wq, wk = (w_query.shape[1], w_key.shape[1])
-    count = lax.psum(jnp.sum(padding).astype(jnp.float32), "fsdp")
     bias, cosine, sine, step, live = window_tables(
         lengths[0], padding[0], first, own, lead, tile, span
     )
     joined = jnp.concatenate((w_query, w_key, w_value, w_out.T), axis=1)
     wo = w_out.shape[0]
-    before, weights_attn = enter(n_fsdp, n_tp, back, states, joined)
-    rows_gate = hidden_rows(w_gate.T)
-    rows_up = hidden_rows(w_up.T)
-    rows_down = hidden_rows(w_down)
-
+    units = [
+        part.reshape(n_fsdp, -1, part.shape[1]) for part in (w_gate.T, w_up.T, w_down)
+    ]
+    live_here = jnp.full((8, 128), jnp.sum(padding).astype(jnp.float32))
+    before, weights_attn, mine, counts = enter(
+        n_fsdp, n_tp, back, states, joined, jnp.stack(units, axis=1), live_here
+    )
+    count = counts[0, 0]
+    rows_gate, rows_up, rows_down = [
+        lax.all_gather(mine[i], "tp", axis=0, tiled=True) for i in range(3)
+    ]
     normed_in, query_raw, key_raw, value = project(
         before, states, norm_attn, weights_attn, wq, wk
     )
@@ -1077,56 +1327,56 @@
     grad_whole, grad_gate, grad_up = grad_hidden_units(
         n_fsdp, grad_out.astype(jnp.bfloat16), rows_down, gate, up
     )
+    by_unit = (
+        contract_first(product, grad_whole).astype(jnp.bfloat16),
+        contract_first(grad_gate, whole_two).astype(jnp.bfloat16),
+        contract_first(grad_up, whole_two).astype(jnp.bfloat16),
+    )
+    by_unit, (grad_gate, grad_up) = lax.optimization_barrier((by_unit, (grad_gate, grad_up)))
     grad_mid = sum_products(n_fsdp, 4, (grad_gate, grad_up), (rows_gate, rows_up))
-    grad_w_down = hidden_rows_grad(contract_first(product, grad_whole))
-    grad_w_gate = hidden_rows_grad(contract_first(grad_gate, whole_two)).T
-    grad_w_up = hidden_rows_grad(contract_first(grad_up, whole_two)).T
+    grad_w_down, grad_w_gate, grad_w_up = [hidden_rows_grad(part) for part in by_unit]
     grad_norm_mlp = jnp.sum(grad_mid * normed_two, axis=0)
     grad_hidden = grad_out + norm_back(grad_mid, normed_two, factor_two, norm_mlp)
 
     grad_low_out = grad_hidden.astype(jnp.bfloat16)
-    grad_w_out = scatter_grad(contract_first(grad_low_out, attended)).T
     grad_attended = back_out(grad_low_out, weights_attn, wo)
     grad_query, grad_before, grad_own, grad_norm_query, grad_norm_key = attend_back(
         query_raw, key_raw, value, bias, cosine, sine, *gains, grad_attended, tile, step
     )
-    for j in range(1, back + 1):
-        block = grad_before[:, lead - j * own : lead - (j - 1) * own]
-        block = lax.ppermute(block, "tp", [(i + j, i) for i in range(n_tp - j)])
-        grad_own = grad_own + block.astype(jnp.float32)
-    grad_key, grad_value = (grad_own[0].astype(jnp.bfloat16), grad_own[1].astype(jnp.bfloat16))
-    grad_joined = jnp.concatenate(
-        [
-            part.reshape(own, n_tp, -1)
-            for part in (grad_query, grad_key, grad_value)
-        ],
-        axis=2,
+    sums_early, arrived = flow(
+        n_fsdp, n_tp, 6, (normed_in, grad_low_out), (grad_query, attended), grad_before
     )
+    grad_own = (grad_own + arrived.astype(jnp.float32)).astype(jnp.bfloat16)
+    grad_key, grad_value = (grad_own[0], grad_own[1])
+    (sums_late,) = flow(n_fsdp, n_tp, 7, (normed_in, normed_in), (grad_key, grad_value))
+    grad_early, grad_late = (over_lanes(sums_early), over_lanes(sums_late))
     grad_low = back_in(grad_query, grad_key, grad_value, weights_attn)
-    grad_weights = scatter_grad(
-        contract_first(normed_in, grad_joined.reshape(own, n_tp * (wq + 2 * wk)))
-    )
     normed_one, factor_one = normalize_rows(inputs)
     grad_norm_attn = jnp.sum(grad_low * normed_one, axis=0)
     grad_input = grad_hidden + norm_back(grad_low, normed_one, factor_one, norm_attn)
-    squares, grad_norm_attn, grad_norm_query, grad_norm_key, grad_norm_mlp = lax.psum(
-        (squares, grad_norm_attn, grad_norm_query[0], grad_norm_key[0], grad_norm_mlp),
-        ("fsdp", "tp"),
-    )
+    small = [grad_norm_attn, grad_norm_mlp, grad_norm_query[0], grad_norm_key[0]]
+    small.append(jnp.full((HD,), squares))
+    joined_small = jnp.concatenate(small).reshape(-1, HD)
+    filled = joined_small.shape[0]
+    joined_small = jnp.pad(joined_small, ((0, -filled % 8), (0, 0)))
+    summed = sum_small(n_fsdp, n_tp, joined_small)[:filled].reshape(-1)
+    grad_norm_attn, grad_norm_mlp = (summed[:D], summed[D : 2 * D])
+    grad_norm_query, grad_norm_key = (summed[2 * D : 2 * D + HD], summed[2 * D + HD : 2 * D + 2 * HD])
+    squares = summed[2 * D + 2 * HD]
     return (
         outputs,
         squares / (count * D),
         grad_input,
         grad_norm_attn,
-        grad_weights[:, :wq],
-        grad_weights[:, wq : wq + wk],
-        grad_weights[:, wq + wk :],
+        grad_early[0],
+        grad_late[0],
+        grad_late[1],
         grad_norm_query,
         grad_norm_key,
-        grad_w_out,
+        grad_early[1].T,
         grad_norm_mlp,
-        grad_w_gate,
-        grad_w_up,
+        grad_w_gate.T,
+        grad_w_up.T,
         grad_w_down,
     )
 

time: 1420 us -> 1140 us (0.80)
  waiting for transfers between devices: 368 us -> 28.1 us
  Pallas kernels: 758 us -> 925 us
  blocking collectives: 79.1 us -> 0 us
  matrix products: 79.2 us -> 60.1 us
    pallas_call x0 -> x3, Pallas kernels: none -> 164 us  [the longest x2 144 us: flow(): pl.pallas_call(functools.partial(flow_kernel, size, lanes, PARTS, hops),...]
    reduce_scatter x4 -> x2, waiting for transfers between devices: 150 us -> 0.01 us  [over_lanes(): lax.psum_scatter(grad.astype(jnp.bfloat16), 'tp', scatter_dimension=2, ti...]
    reduce_scatter x3, waiting for transfers between devices: 111 us -> 0.02 us  [hidden_rows_grad(): lax.psum_scatter(grad.astype(jnp.bfloat16), 'tp', scatter_dimension=0, ti...]
    ppermute x2 -> x0, waiting for transfers between devices: 103 us -> none  [shards(): block = lax.ppermute(block, 'tp', [(i + j, i) for i in range(n_tp - j)])]
    psum x2 -> x0, blocking collectives: 61.4 us -> none  [the longest x1 45.7 us: shards(): lax.psum((squares, grad_norm_attn, grad_norm_query[0], grad_norm_key[0],...]
    dot_general x5 -> x3, matrix products: 79.2 us -> 60.1 us  [contract_first(): lax.dot_general(left, right, (((0,), (0,)), ((), ())), preferred_element_...]
    all_gather x3, waiting for transfers between devices: 1.94 us -> 20.4 us  [shards(): lax.all_gather(mine[i], 'tp', axis=0, tiled=True)]
    all_to_all x1 -> x0, blocking collectives: 17.7 us -> none  [hidden_rows(): mine = lax.all_to_all(weight_t, 'fsdp', 0, 1, tiled=True)]
  transfers between devices with their start and end apart: 17 -> 11, of which waited for: 10 -> 3; matrix products, arithmetic and copies ran while one was open for 10% -> 6% of each run, Pallas kernels for 34% -> 49%
where the time goes in v2:
time: 1140 us; the launch traced here: 1130 us
  Pallas kernels  925 us (81%)
  matrix products  60.1 us (5%)
  other arithmetic  56.3 us (5%)
  local copies, waits for them, and re-layouts  30.2 us (3%)
  waiting for transfers between devices  28.1 us (2%)
  between operations  18 us (2%)
  starting transfers between devices  12.3 us (1%)
    pallas_call x1, Pallas kernels, enter(): pl.pallas_call(functools.partial(enter_kernel, size, lanes, back), out_sh...  199 us
    pallas_call x2, Pallas kernels, sum_products(): pl.pallas_call(functools.partial(sum_products_kernel, size, terms), out_s...  187 us
    pallas_call x2, Pallas kernels, flow(): pl.pallas_call(functools.partial(flow_kernel, size, lanes, PARTS, hops),...  144 us
    pallas_call x1, Pallas kernels, gate_up(): pl.pallas_call(functools.partial(gate_up_kernel, size), out_shape=(shape(...  87.3 us
    pallas_call x1, Pallas kernels, grad_hidden_units(): pl.pallas_call(functools.partial(grad_hidden_kernel, size), out_shape=(sh...  85.5 us
    pallas_call x1, Pallas kernels, attend_back(): pl.pallas_call(functools.partial(attend_back_kernel, group, step, lead),...  82.3 us
    dot_general x3, matrix products, contract_first(): lax.dot_general(left, right, (((0,), (0,)), ((), ())), preferred_element_...  60.1 us
    pallas_call x1, Pallas kernels, attend(): pl.pallas_call(functools.partial(attend_kernel, group, step, rows - own),...  49.9 us
  transfers between devices with their start and end apart: 11, of which 3 were waited for; matrix products, arithmetic and copies ran while one was open for 6% of the time, Pallas kernels for 49%

profile of v2, /device:TPU:0, one launch (start us, length us, event | category | flops | bytes accessed | tf_op | source)
XLA Modules:
  0.0 1129.8 jit_solution(11662974059478958394)
XLA Ops:
  16.5 199.2 %enter.1 = (bf16[2,512,2048]{2,1,0:T(8,128)(2,1)}, bf16[8,4,256,1536]{3,2,1,0:T(8,128)(2,1)}, bf16[3,192,2048]{2,1,0:T(8,128)(2,1)}, f32[8,128]{1,0:T(8,128)}) custom-call(bf16[512,2048]{1,0:T(8,128)(2,1)} %x_ref.5, bf16[256,1536]{1,0:T(8,128)(2,1)} %pad_maximum_fusion.1.w_ref, bf16[8,3,192,256]{3,2,1,0:T(8,128)(2,1)} %pad_maximum_fusion.m_ref, ...), custom_call_target="tpu_custom_call" | custom-call | bytes 419430400 | tf_op jit(solution)/shard_map/enter/pallas_call | solution.py:652
  228.6 33.2 %project_in.1 = (bf16[512,2048]{1,0:T(8,128)(2,1)}, f32[512,2048]{1,0:T(8,128)}, f32[1536,1024]{1,0:T(8,128)}, bf16[1536,1024]{1,0:T(8,128)(2,1)}) custom-call(bf16[2,512,2048]{2,1,0:T(8,128)(2,1)} %get-tuple-element.41.before_ref, bf16[512,2048]{1,0:T(8,128)(2,1)} %x_ref.5, f32[1,2048]{1,0:T(1,128)} %bitcast.126, ...), custom_call_target="tpu_custom_call" | custom-call | flops 17179869184 | bytes 23068672 | tf_op jit(solution)/shard_map/project_in/pallas_call | solution.py:910
  261.8 49.9 %attend.1.a_ref.refs_3_ = bf16[512,2048]{1,0:T(8,128)(2,1)} custom-call(f32[512,2048]{1,0:T(8,128)} %get-tuple-element.43.q_ref, f32[1536,1024]{1,0:T(8,128)} %get-tuple-element.44.k_ref, bf16[1536,1024]{1,0:T(8,128)(2,1)} %get-tuple-element.45.v_ref, f32[512,1280]{1,0:T(8,128)} %add_select_fusion.bias_ref, f32[1536,128]{1,0:T(8,128)} %get-tuple-element.164.cos_ref, ...), custom_call_target="tpu_custom_call" | custom-call | flops 21474836480 | bytes 13631488 | tf_op jit(solution)/shard_map/attend/pallas_call | solution.py:1174
  313.7 11.4 %project_out.1 = f32[512,2048]{1,0:T(8,128)} custom-call(bf16[512,2048]{1,0:T(8,128)(2,1)} %attend.1.a_ref.refs_3_, bf16[8,4,256,1536]{3,2,1,0:T(8,128)(2,1)} %get-tuple-element.42.w_ref, bf16[512,2048]{1,0:T(8,128)(2,1)} %x_ref.5), custom_call_target="tpu_custom_call" | custom-call | flops 4294967296 | bytes 25165824 | tf_op jit(solution)/shard_map/project_out/pallas_call | solution.py:954
  330.3 20.3 %all-gather.9.cloned.1.call-done = bf16[1,768,2048]{2,1,0:T(8,128)(2,1)} async-done(((bf16[1,192,2048]{2,1,0:T(8,128)(2,1)}), bf16[1,768,2048]{2,1,0:T(8,128)(2,1)}) %all-gather.9.cloned.1.call-update) | async-done | bytes 3145744 | tf_op jit(solution)/shard_map/all_gather | solution.py:1309
  350.7 87.3 %gate_up.1 = (bf16[8,2,256,2048]{3,2,1,0:T(8,128)(2,1)}, f32[8,2,256,768]{3,2,1,0:T(8,128)}, f32[8,2,256,768]{3,2,1,0:T(8,128)}, bf16[8,2,256,768]{3,2,1,0:T(8,128)(2,1)}) custom-call(bf16[2,256,2048]{2,1,0:T(8,128)(2,1)} %bitcast.113, bf16[768,2048]{1,0:T(8,128)(2,1)} %bitcast.130, bf16[768,2048]{1,0:T(8,128)(2,1)} %bitcast.132), custom_call_target="tpu_custom_call" | custom-call | flops 25769803776 | bytes 209715200 | tf_op jit(solution)/shard_map/gate_up/pallas_call | solution.py:340
  438.0 89.0 %sum_products.2 = f32[2,256,2048]{2,1,0:T(8,128)} custom-call(bf16[8,2,256,768]{3,2,1,0:T(8,128)(2,1)} %get-tuple-element.47.refs_0_, bf16[768,2048]{1,0:T(8,128)(2,1)} %bitcast.134), custom_call_target="tpu_custom_call" | custom-call | flops 12884901888 | bytes 209715200 | tf_op jit(solution)/shard_map/sum_products/pallas_call | solution.py:507
  527.1 4.4 multiply_reduce_fusion
  534.1 85.5 %grad_hidden_units.1 = (bf16[8,2,256,2048]{3,2,1,0:T(8,128)(2,1)}, bf16[8,2,256,768]{3,2,1,0:T(8,128)(2,1)}, bf16[8,2,256,768]{3,2,1,0:T(8,128)(2,1)}) custom-call(bf16[2,256,2048]{2,1,0:T(8,128)(2,1)} %bitcast.114, bf16[768,2048]{1,0:T(8,128)(2,1)} %bitcast.135, f32[8,2,256,768]{3,2,1,0:T(8,128)} %get-tuple-element.49.gate_in, ...), custom_call_target="tpu_custom_call" | custom-call | flops 12884901888 | bytes 209715200 | tf_op jit(solution)/shard_map/grad_hidden_units/pallas_call | solution.py:454
  619.6 20.1 %bitcast_convert_fusion = bf16[768,2048]{1,0:T(8,128)(2,1)} fusion(bf16[8,2,256,768]{3,2,1,0:T(8,128)(2,1)} %get-tuple-element.54, bf16[8,2,256,2048]{3,2,1,0:T(8,128)(2,1)} %get-tuple-element.53), kind=kOutput, calls=%fused_computation | convolution fusion | flops 12886474752 | bytes 26214400 | tf_op jit(solution)/shard_map/dot_general | solution.py:37
  639.8 20.0 %bitcast_convert_fusion.1 = bf16[768,2048]{1,0:T(8,128)(2,1)} fusion(bf16[8,2,256,768]{3,2,1,0:T(8,128)(2,1)} %get-tuple-element.52, bf16[8,2,256,2048]{3,2,1,0:T(8,128)(2,1)} %get-tuple-element.53), kind=kOutput, calls=%fused_computation.1 | convolution fusion | flops 12886474752 | bytes 26214400 | tf_op jit(solution)/shard_map/dot_general | solution.py:37
  659.8 20.0 %bitcast_convert_fusion.2 = bf16[768,2048]{1,0:T(8,128)(2,1)} fusion(bf16[8,2,256,768]{3,2,1,0:T(8,128)(2,1)} %get-tuple-element.47.refs_0_, bf16[8,2,256,2048]{3,2,1,0:T(8,128)(2,1)} %get-tuple-element.51), kind=kOutput, calls=%fused_computation.2 | convolution fusion | flops 12886474752 | bytes 26214400 | tf_op jit(solution)/shard_map/dot_general | solution.py:37
  680.5 98.0 %sum_products.3 = f32[2,256,2048]{2,1,0:T(8,128)} custom-call(bf16[8,2,256,768]{3,2,1,0:T(8,128)(2,1)} %get-tuple-element.52, bf16[8,2,256,768]{3,2,1,0:T(8,128)(2,1)} %get-tuple-element.54, bf16[768,2048]{1,0:T(8,128)(2,1)} %bitcast.131, bf16[768,2048]{1,0:T(8,128)(2,1)} %bitcast.133), custom_call_target="tpu_custom_call" | custom-call | flops 25769803776 | bytes 209715200 | tf_op jit(solution)/shard_map/sum_products/pallas_call | solution.py:507
  783.3 4.1 fusion.22
  787.5 8.9 back_out.1.do_ref
  796.4 82.3 %attend_back.1 = (bf16[512,2048]{1,0:T(8,128)(2,1)}, bf16[2,2,512,1024]{3,2,1,0:T(8,128)(2,1)}, f32[2,512,1024]{2,1,0:T(8,128)}, f32[1,128]{1,0:T(1,128)}, f32[1,128]{1,0:T(1,128)}) custom-call(f32[512,2048]{1,0:T(8,128)} %get-tuple-element.43.q_ref, f32[1536,1024]{1,0:T(8,128)} %get-tuple-element.44.k_ref, bf16[1536,1024]{1,0:T(8,128)(2,1)} %get-tuple-element.45.v_ref, ...), custom_call_target="tpu_custom_call" | custom-call | flops 53687091200 | bytes 33554432 | tf_op jit(solution)/shard_map/attend_back/pallas_call | solution.py:1200
  878.6 98.8 %flow.2 = (f32[2,256,2048]{2,1,0:T(8,128)}, bf16[2,512,1024]{2,1,0:T(8,128)(2,1)}) custom-call(bf16[512,2048]{1,0:T(8,128)(2,1)} %get-tuple-element.59.refs_0_.refs_1_, bf16[512,2048]{1,0:T(8,128)(2,1)} %get-tuple-element.132.g_ref.refs_1_, bf16[512,2048]{1,0:T(8,128)(2,1)} %get-tuple-element.57.refs_2_.q_ref, bf16[512,2048]{1,0:T(8,128)(2,1)} %attend.1.a_ref.refs_3_, ...), custom_call_target="tpu_custom_call" | custom-call | flops 8589934592 | bytes 209715200 | tf_op jit(solution)/shard_map/flow/pallas_call | solution.py:801
  981.3 45.7 %flow.3 = f32[2,256,1024]{2,1,0:T(8,128)} custom-call(bf16[512,2048]{1,0:T(8,128)(2,1)} %get-tuple-element.59.refs_0_.refs_1_, bf16[512,2048]{1,0:T(8,128)(2,1)} %get-tuple-element.59.refs_0_.refs_1_, bf16[512,1024]{1,0:T(8,128)(2,1)} %get-tuple-element.138.k_ref.refs_2_, bf16[512,1024]{1,0:T(8,128)(2,1)} %get-tuple-element.137.v_ref.refs_3_), custom_call_target="tpu_custom_call" | custom-call | flops 4294967296 | bytes 209715200 | tf_op jit(solution)/shard_map/flow/pallas_call | solution.py:801
  1034.3 16.0 %back_in.1 = f32[512,2048]{1,0:T(8,128)} custom-call(bf16[512,2048]{1,0:T(8,128)(2,1)} %get-tuple-element.57.refs_2_.q_ref, bf16[512,1024]{1,0:T(8,128)(2,1)} %get-tuple-element.138.k_ref.refs_2_, bf16[512,1024]{1,0:T(8,128)(2,1)} %get-tuple-element.137.v_ref.refs_3_, bf16[8,4,256,1536]{3,2,1,0:T(8,128)(2,1)} %get-tuple-element.42.w_ref), custom_call_target="tpu_custom_call" | custom-call | flops 8589934592 | bytes 25165824 | tf_op jit(solution)/shard_map/back_in/pallas_call | solution.py:1017
  1060.7 19.6 %sum_small.1 = f32[40,128]{1,0:T(8,128)} custom-call(f32[40,128]{1,0:T(8,128)} %pad.5.x_ref), custom_call_target="tpu_custom_call" | custom-call | tf_op jit(solution)/shard_map/sum_small/pallas_call | solution.py:849
  1085.5 4.2 all-to-all-start.1
  1089.8 6.7 fusion.7
  1098.5 3.9 all-to-all-done.1
  1102.4 4.2 all-to-all-start.2
  (126 shorter events, 79.1 us)
Async XLA Ops:
  7.2 6.1 copy-start.9
  7.2 323.1 %all-gather.7.cloned.1.call-start = ((), (), s32[]{:S(2)}) async-start(), calls=%async_computation.13 | async-start | bytes 3932160 | tf_op jit(solution)/shard_map/all_gather | solution.py:1309
  7.2 7.7 copy-start.10
  7.2 7.7 copy-start.11
  7.3 7.7 copy-start.12
  215.7 4.7 copy-start.16
  215.7 5.1 copy-start.14
  218.9 131.8 %all-gather.9.cloned.1.call-start = ((), (), s32[]{:S(2)}) async-start(), calls=%async_computation.14 | async-start | bytes 3932160 | tf_op jit(solution)/shard_map/all_gather | solution.py:1309
  219.6 218.4 %all-gather.11.cloned.1.call-start = ((), (), s32[]{:S(2)}) async-start(), calls=%async_computation.15 | async-start | bytes 3932160 | tf_op jit(solution)/shard_map/all_gather | solution.py:1309
  220.4 833.4 %reduce-scatter.10.cloned.1.call-start = ((), (), s32[]{:S(2)}) async-start(), calls=%async_computation.10 | async-start | bytes 3932160 | tf_op jit(solution)/shard_map/reduce_scatter | solution.py:1260
  313.7 14.1 %copy-start.13 = (f32[2048]{0:T(1024)S(1)}, f32[2048]{0:T(1024)}, u32[]{:S(2)}) copy-start(f32[2048]{0:T(1024)} %param.26) | copy-start | bytes 24580
  438.0 89.0 %copy-start.1 = (f32[512,2048]{1,0:T(8,128)S(1)}, f32[512,2048]{1,0:T(8,128)}, u32[]{:S(2)}) copy-start(f32[512,2048]{1,0:T(8,128)} %project_out.1) | copy-start | bytes 12582916
  438.0 89.0 %copy-start.6 = (bf16[512,2048]{1,0:T(8,128)(2,1)S(1)}, bf16[512,2048]{1,0:T(8,128)(2,1)}, u32[]{:S(2)}) copy-start(bf16[512,2048]{1,0:T(8,128)(2,1)} %param.18) | copy-start | bytes 6291460
  679.8 403.7 %reduce-scatter.12.cloned.1.call-start = ((), (), s32[]{:S(2)}) async-start(), calls=%async_computation.11 | async-start | bytes 3932160 | tf_op jit(solution)/shard_map/reduce_scatter | solution.py:1260
  680.4 416.0 %reduce-scatter.14.cloned.1.call-start = ((), (), s32[]{:S(2)}) async-start(), calls=%async_computation.12 | async-start | bytes 3932160 | tf_op jit(solution)/shard_map/reduce_scatter | solution.py:1260
  680.5 98.1 %copy-start.2 = (f32[512,2048]{1,0:T(8,128)S(1)}, f32[512,2048]{1,0:T(8,128)}, u32[]{:S(2)}) copy-start(f32[512,2048]{1,0:T(8,128)} %project_out.1) | copy-start | bytes 12582916
  778.5 4.8 copy-start.7
  796.3 311.5 %reduce-scatter.8.cloned.1.call-start = ((), (), s32[]{:S(2)}) async-start(), calls=%async_computation.9 | async-start | bytes 1310720 | tf_op jit(solution)/shard_map/reduce_scatter | solution.py:1265
  878.6 98.8 %copy-start.8 = (f32[2,512,1024]{2,1,0:T(8,128)S(1)}, f32[2,512,1024]{2,1,0:T(8,128)}, u32[]{:S(2)}) copy-start(f32[2,512,1024]{2,1,0:T(8,128)} %get-tuple-element.58) | copy-start | bytes 12582916
  1029.9 79.8 %reduce-scatter.6.cloned.1.call-start = ((), (), s32[]{:S(2)}) async-start(), calls=%async_computation.8 | async-start | bytes 2621440 | tf_op jit(solution)/shard_map/reduce_scatter | solution.py:1265
  1034.3 16.0 %copy-start.15 = (f32[2048]{0:T(1024)S(1)}, f32[2048]{0:T(1024)}, u32[]{:S(2)}) copy-start(f32[2048]{0:T(1024)} %param.19) | copy-start | bytes 24580
  1055.8 29.7 %all-to-all-start = ((bf16[192,8,256]{2,0,1:T(8,128)(2,1)}), bf16[192,8,256]{2,0,1:T(8,128)(2,1)S(1)}, u32[]{:S(2)}, u32[]{:S(2)}) async-start(bf16[192,8,256]{2,0,1:T(8,128)(2,1)} %bitcast.108), calls=%async_computation.3 | async-start | bytes 1572864 | tf_op jit(solution)/shard_map/all_to_all | solution.py:1261
  1085.5 16.8 %all-to-all-start.1 = ((bf16[192,8,256]{2,0,1:T(8,128)(2,1)}), bf16[192,8,256]{2,0,1:T(8,128)(2,1)}, u32[]{:S(2)}, u32[]{:S(2)}) async-start(bf16[192,8,256]{2,0,1:T(8,128)(2,1)} %bitcast.107), calls=%async_computation.5 | async-start | bytes 1572864 | tf_op jit(solution)/shard_map/all_to_all | solution.py:1261
  1102.4 16.8 %all-to-all-start.2 = ((bf16[192,8,256]{2,0,1:T(8,128)(2,1)}), bf16[192,8,256]{2,0,1:T(8,128)(2,1)}, u32[]{:S(2)}, u32[]{:S(2)}) async-start(bf16[192,8,256]{2,0,1:T(8,128)(2,1)} %bitcast.106), calls=%async_computation.7 | async-start | bytes 1572864 | tf_op jit(solution)/shard_map/all_to_all | solution.py:1261
  (6 other events, 19.4 us)
Sparse Core Ops, SparseCore 0:
  219.0 67.8 all-gather.6
  288.5 62.1 all-gather.8
  352.8 62.1 all-gather.10
  679.9 58.1 reduce-scatter.9
  740.3 60.2 reduce-scatter.11
  802.8 60.2 reduce-scatter.13
  1030.0 24.3 reduce-scatter.7
  1056.9 43.3 reduce-scatter.5

commit v3 on v2

--- a/solution.py
+++ b/solution.py
@@ -167,7 +167,7 @@
     ]
 
 
-def scatter_rows_in(size, me, made, held, sent, came, sems, partial, final, between=None):
+def scatter_steps(size, me, made, held, sent, came, sems, partial, final):
     chip_send, chip_recv, core_send, core_recv = sems
     steps = len(chip_bits(size))
     order = [bits[::-1] for bits in orders(size)]
@@ -242,18 +242,19 @@
             for part in range(PARTS):
                 chip_copy(part, q).start()
 
-    for_sibling(0)
+    def finish():
+        for q in range(len(patterns)):
+            for part in range(PARTS):
+                core_copy(part, q).wait_send()
+                if patterns[q]:
+                    chip_copy(part, q).wait_send()
+
+    calls = [functools.partial(for_sibling, 0)]
     for q in range(len(patterns)):
         if q + 1 < len(patterns):
-            for_sibling(q + 1)
-        for_chips(q)
-        if between:
-            between(q + 1, len(patterns))
-    for q in range(len(patterns)):
-        for part in range(PARTS):
-            core_copy(part, q).wait_send()
-            if patterns[q]:
-                chip_copy(part, q).wait_send()
+            calls.append(functools.partial(for_sibling, q + 1))
+        calls.append(functools.partial(for_chips, q))
+    return (calls, finish)
 
 
 def scatter_scratch(size, rows, width):
@@ -495,7 +496,10 @@
             dot(left[slot, part], right[:, columns]) for left, right in zip(lefts, rights)
         )
 
-    scatter_rows_in(size, me, made, held, sent, came, sems, partial, out)
+    calls, finish = scatter_steps(size, me, made, held, sent, came, sems, partial, out)
+    for call in calls:
+        call()
+    finish()
 
 
 def sum_products(size, number, lefts, rights):
@@ -678,140 +682,192 @@
     )(values, weights, units, count)
 
 
-def flow_kernel(size, lanes, terms, hops, *refs):
-    lefts, rights = (refs[:terms], refs[terms : 2 * terms])
-    at = 2 * terms + (1 if hops else 0)
-    parts_in = refs[2 * terms] if hops else None
-    out = refs[at]
-    arrived = refs[at + 1] if hops else None
-    at += 2 if hops else 1
-    left, right, loads, made, held, sent, came, *rest = refs[at:]
-    sems = rest[:4]
-    me, z = (lax.axis_index("fsdp"), lax.axis_index("tp"))
-    copies = [
-        pltpu.make_async_copy(source, target.at[i], loads.at[j, i])
-        for j, (sources, target) in enumerate(((lefts, left), (rights, right)))
-        for i, source in enumerate(sources)
-        if j or i < left.shape[0]
+def sum_query_kernel(
+    size, left_ref, right_ref, *refs
+):
+    units, (out, back), (left, right, loads, u_send, u_recv, u_own) = (refs[:3], refs[3:5], refs[5:11])
+    made, held, sent, came, *sems = refs[11:]
+    me = lax.axis_index("fsdp")
+    width, span = (out.shape[-1], back.shape[-1])
+    rows = left.shape[1] // size
+    copies = [pltpu.make_async_copy(left_ref, left, loads.at[PARTS])]
+    copies += [
+        pltpu.make_async_copy(
+            right_ref.at[:, pl.ds(part * width, width)], right.at[part], loads.at[part]
+        )
+        for part in range(PARTS)
+    ]
+    part_of = lambda device: pl.ds(pl.multiple_of(device * span, span), span)
+    copies += [
+        pltpu.make_async_copy(unit.at[:, part_of(me)], back.at[me, kind], u_own.at[kind])
+        for kind, unit in enumerate(units)
     ]
     for copy in copies:
         copy.start()
     barrier = pltpu.get_barrier_semaphore()
-    peers = [{"fsdp": flip(me, bit)} for bit in [1] + chip_bits(size)]
-    if hops:
-        peers += [{"tp": lax.rem(z + 1, lanes)}, {"tp": lax.rem(z + lanes - 1, lanes)}]
-    for peer in peers:
-        pl.semaphore_signal(barrier, inc=1, device_id=peer, device_id_type=MESH)
-    pl.semaphore_wait(barrier, len(peers))
-    rows = left.shape[2] // size
-
-    if hops:
-        mixed, got, mix_sem, hop_send, hop_recv = rest[4:]
-
-        def hop_copy(number):
-            return pltpu.make_async_remote_copy(
-                src_ref=mixed.at[number],
-                dst_ref=got.at[number],
-                send_sem=hop_send.at[number],
-                recv_sem=hop_recv.at[number],
-                device_id={"tp": lax.rem(z + lanes - 1, lanes)},
-                device_id_type=MESH,
-            )
-
-        def hop(number):
-            load = pltpu.make_async_copy(
-                parts_in.at[hops - 1 - number], mixed.at[number], mix_sem.at[number]
-            )
-            load.start()
-            load.wait()
-            if number:
-
-                @pl.when(z + 1 < lanes)
-                def _():
-                    hop_copy(number - 1).wait_recv()
-
-                    @pl.loop(0, 2)
-                    def _(kind):
-                        total = mixed[number, kind].astype(jnp.float32)
-                        total = total + got[number - 1, kind].astype(jnp.float32)
-                        mixed[number, kind] = total.astype(jnp.bfloat16)
-
-            @pl.when(z > 0)
-            def _():
-                hop_copy(number).start()
-
-        hop(0)
+    for other in range(1, size):
+        pl.semaphore_signal(
+            barrier, inc=1, device_id={"fsdp": flip(me, other)}, device_id_type=MESH
+        )
+    pl.semaphore_wait(barrier, size - 1)
     for copy in copies:
         copy.wait()
 
+    def unit_copy(other, kind):
+        peer = flip(me, other)
+        return pltpu.make_async_remote_copy(
+            src_ref=units[kind].at[:, part_of(peer)],
+            dst_ref=back.at[me, kind],
+            send_sem=u_send.at[other - 1, kind],
+            recv_sem=u_recv.at[other - 1, kind],
+            device_id={"fsdp": peer},
+            device_id_type=MESH,
+        )
+
     def partial(part, slot, columns):
-        block = left[part if left.shape[0] > 1 else 0, :, pl.ds(pl.multiple_of(slot * rows, rows), rows)]
+        block = left[:, pl.ds(pl.multiple_of(slot * rows, rows), rows)]
         return contract_first(block, right[part, :, columns])
 
-    def between(q, count):
-        if hops:
-            for number in range(1, hops):
-                if q == number * count // hops:
-                    hop(number)
-
-    scatter_rows_in(size, me, made, held, sent, came, sems, partial, out, between)
-    if hops:
-
-        @pl.when(z + 1 < lanes)
-        def _():
-            hop_copy(hops - 1).wait_recv()
-            arrived[...] = got[hops - 1]
-
-        @pl.when(z + 1 == lanes)
-        def _():
-            arrived[...] = jnp.zeros_like(arrived)
-
-        @pl.when(z > 0)
-        def _():
-            for number in range(hops):
-                hop_copy(number).wait_send()
-
-
-def flow(size, lanes, number, lefts, rights, parts_in=None):
-    tokens, depth = lefts[0].shape
-    width = rights[0].shape[1]
+    calls, finish = scatter_steps(size, me, made, held, sent, came, sems, partial, out)
+    for number, call in enumerate(calls):
+        call()
+        if number == len(calls) // 2:
+            for other in range(1, size):
+                for kind in range(3):
+                    unit_copy(other, kind).start()
+    for other in range(1, size):
+        for kind in range(3):
+            unit_copy(other, kind).wait()
+    finish()
+
+
+def sum_query(size, left, right, units):
+    tokens, depth = left.shape
+    width = right.shape[1] // PARTS
+    rows = depth // size
     any_space = pl.BlockSpec(memory_space=pl.ANY)
     vmem = pl.BlockSpec(memory_space=pltpu.VMEM)
+    return pl.pallas_call(
+        functools.partial(sum_query_kernel, size),
+        out_shape=(
+            jax.ShapeDtypeStruct((PARTS, rows, width), jnp.float32),
+            jax.ShapeDtypeStruct((size, 3, units[0].shape[0], rows), jnp.bfloat16),
+        ),
+        in_specs=[any_space] * 5,
+        out_specs=(vmem, any_space),
+        scratch_shapes=[
+            pltpu.VMEM((tokens, depth), jnp.bfloat16),
+            pltpu.VMEM((PARTS, tokens, width), jnp.bfloat16),
+            pltpu.SemaphoreType.DMA((PARTS + 1,)),
+            pltpu.SemaphoreType.DMA((size - 1, 3)),
+            pltpu.SemaphoreType.DMA((size - 1, 3)),
+            pltpu.SemaphoreType.DMA((3,)),
+            *scatter_scratch(size, rows, width),
+        ],
+        compiler_params=pltpu.CompilerParams(
+            collective_id=6, has_side_effects=True, vmem_limit_bytes=VMEM
+        ),
+        cost_estimate=pl.CostEstimate(
+            flops=4 * tokens * depth * width, bytes_accessed=100 * 1024 * 1024, transcendentals=0
+        ),
+        name="sum_query",
+    )(left, right, *units)
+
+
+def sum_key_kernel(size, left_ref, q_ref, kv_ref, w_ref, out, low, left, right, loads, tiles, fetch, *refs):
+    made, held, sent, came, *sems = refs
+    me = lax.axis_index("fsdp")
+    rows = left.shape[1] // size
+    parts, span = (w_ref.shape[1], tiles.shape[-1])
+    copies = [pltpu.make_async_copy(left_ref, left, loads.at[PARTS])]
+    copies += [
+        pltpu.make_async_copy(kv_ref.at[part], right.at[part], loads.at[part])
+        for part in range(PARTS)
+    ]
+    for copy in copies:
+        copy.start()
+
+    def tile_copy(f):
+        return pltpu.make_async_copy(
+            w_ref.at[f, :, :, pl.ds(0, span)], tiles.at[f % 2], fetch.at[f % 2]
+        )
+
+    tile_copy(0).start()
+    greet(me, size)
+    for copy in copies:
+        copy.wait()
+
+    def partial(part, slot, columns):
+        block = left[:, pl.ds(pl.multiple_of(slot * rows, rows), rows)]
+        return contract_first(block, right[part, :, columns])
+
+    def low_columns(f):
+        if f + 1 < size:
+            tile_copy(f + 1).start()
+        tile_copy(f).wait()
+        half = low.shape[0] // 2
+
+        @pl.loop(0, 2)
+        def _(index):
+            span_rows = pl.ds(pl.multiple_of(index * half, half), half)
+            total = jnp.zeros((half, rows), jnp.float32)
+            for z in range(parts):
+                start = 0
+                for source in (q_ref, right.at[0], right.at[1]):
+                    width = source.shape[1] // parts
+                    total += contract_last(
+                        source[span_rows, z * width : (z + 1) * width],
+                        tiles[f % 2, z, :, start : start + width],
+                    )
+                    start += width
+            low[span_rows, f * rows : (f + 1) * rows] = total
+
+    calls, finish = scatter_steps(size, me, made, held, sent, came, sems, partial, out)
+    done = 0
+    for number, call in enumerate(calls):
+        call()
+        goal = size * max(0, number - 1) // max(1, len(calls) - 3)
+        while done < min(size, goal):
+            low_columns(done)
+            done += 1
+    while done < size:
+        low_columns(done)
+        done += 1
+    finish()
+
+
+def sum_key(size, left, grad_query, grad_pair, weights):
+    tokens, depth = left.shape
+    width = grad_pair.shape[2]
     rows = depth // size
-    hops = parts_in.shape[0] if parts_in is not None else 0
-    distinct = 1 if lefts[0] is lefts[1] else PARTS
-    out_shape = [jax.ShapeDtypeStruct((PARTS, rows, width), jnp.float32)]
-    scratch = [
-        pltpu.VMEM((distinct, tokens, depth), jnp.bfloat16),
-        pltpu.VMEM((PARTS, tokens, width), jnp.bfloat16),
-        pltpu.SemaphoreType.DMA((2, PARTS)),
-        *scatter_scratch(size, rows, width),
-    ]
-    operands = [*lefts, *rights]
-    if hops:
-        out_shape.append(jax.ShapeDtypeStruct(parts_in.shape[1:], jnp.bfloat16))
-        scratch += [
-            pltpu.VMEM(parts_in.shape, jnp.bfloat16),
-            pltpu.VMEM(parts_in.shape, jnp.bfloat16),
-            pltpu.SemaphoreType.DMA((hops,)),
-            pltpu.SemaphoreType.DMA((hops,)),
-            pltpu.SemaphoreType.DMA((hops,)),
-        ]
-        operands.append(parts_in)
+    parts = weights.shape[1]
+    span = (grad_query.shape[1] + PARTS * width) // parts
+    any_space = pl.BlockSpec(memory_space=pl.ANY)
+    vmem = pl.BlockSpec(memory_space=pltpu.VMEM)
     return pl.pallas_call(
-        functools.partial(flow_kernel, size, lanes, PARTS, hops),
-        out_shape=tuple(out_shape),
-        in_specs=[any_space] * len(operands),
-        out_specs=(vmem,) * len(out_shape),
-        scratch_shapes=scratch,
+        functools.partial(sum_key_kernel, size),
+        out_shape=(
+            jax.ShapeDtypeStruct((PARTS, rows, width), jnp.float32),
+            jax.ShapeDtypeStruct((tokens, depth), jnp.float32),
+        ),
+        in_specs=[any_space, vmem, any_space, any_space],
+        out_specs=(vmem, vmem),
+        scratch_shapes=[
+            pltpu.VMEM((tokens, depth), jnp.bfloat16),
+            pltpu.VMEM((PARTS, tokens, width), jnp.bfloat16),
+            pltpu.SemaphoreType.DMA((PARTS + 1,)),
+            pltpu.VMEM((2, parts, rows, span), jnp.bfloat16),
+            pltpu.SemaphoreType.DMA((2,)),
+            *scatter_scratch(size, rows, width),
+        ],
         compiler_params=pltpu.CompilerParams(
-            collective_id=number, has_side_effects=True, vmem_limit_bytes=VMEM
+            collective_id=7, has_side_effects=True, vmem_limit_bytes=VMEM
         ),
         cost_estimate=pl.CostEstimate(
-            flops=4 * tokens * depth * width, bytes_accessed=200 * 1024 * 1024, transcendentals=0
-        ),
-        name="flow",
-    )(*operands)
+            flops=8 * tokens * depth * width, bytes_accessed=100 * 1024 * 1024, transcendentals=0
+        ),
+        name="sum_key",
+    )(left, grad_query, grad_pair, weights)
 
 
 def sum_small_kernel(size, lanes, x_ref, o_ref, came, send, recv):
@@ -995,44 +1051,6 @@
     )(grad, weights)
 
 
-def back_in_kernel(q_ref, k_ref, v_ref, w_ref, o_ref):
-    parts = w_ref.shape[1]
-    total = jnp.zeros(o_ref.shape, jnp.float32)
-    for z in range(parts):
-        start = 0
-        for ref in (q_ref, k_ref, v_ref):
-            width = ref.shape[1] // parts
-            total += contract_last(
-                ref[:, z * width : (z + 1) * width], w_ref[0, z, :, start : start + width]
-            )
-            start += width
-    o_ref[...] = total
-
-
-def back_in(grad_query, grad_key, grad_value, weights):
-    size, parts, rows, _ = weights.shape
-    own = grad_query.shape[0]
-    columns = (grad_query.shape[1] + 2 * grad_key.shape[1]) // parts
-    whole = lambda f: (0, 0)
-    return pl.pallas_call(
-        back_in_kernel,
-        grid=(size,),
-        out_shape=jax.ShapeDtypeStruct((own, D), jnp.float32),
-        in_specs=[
-            pl.BlockSpec(grad_query.shape, whole),
-            pl.BlockSpec(grad_key.shape, whole),
-            pl.BlockSpec(grad_value.shape, whole),
-            pl.BlockSpec((1, parts, rows, columns), lambda f: (f, 0, 0, 0)),
-        ],
-        out_specs=pl.BlockSpec((own, rows), lambda f: (0, f)),
-        compiler_params=pltpu.CompilerParams(vmem_limit_bytes=VMEM),
-        cost_estimate=pl.CostEstimate(
-            flops=2 * own * D * parts * columns, bytes_accessed=24 * 1024 * 1024, transcendentals=0
-        ),
-        name="back_in",
-    )(grad_query, grad_key, grad_value, weights)
-
-
 def turn(values, cosine, sine):
     return values * cosine + pltpu.roll(values, HD // 2, 1) * sine
 
@@ -1085,6 +1103,8 @@
     group,
     step,
     lead,
+    size,
+    lanes,
     q_ref,
     k_ref,
     v_ref,
@@ -1094,23 +1114,94 @@
     nq_ref,
     nk_ref,
     do_ref,
+    left_ref,
+    right_ref,
     dq_ref,
-    prev_ref,
-    own_ref,
+    pair_ref,
     gq_ref,
     gk_ref,
+    out_ref,
     keys,
     dk,
     dv,
+    mixed,
+    got,
+    own_sum,
+    left,
+    right,
+    loads,
+    hop_send,
+    hop_recv,
+    *refs,
 ):
+    made, held, sent, came, *sems = refs
     tile, span = bias_ref.shape
     scale = HD ** (-0.5)
-    index = pl.program_id(1)
-
-    @pl.when((pl.program_id(0) == 0) & (index == 0))
+    head, index = (pl.program_id(0), pl.program_id(1))
+    heads, tiles = (mixed.shape[0], (k_ref.shape[0] - lead) // tile)
+    back, own = (mixed.shape[1], mixed.shape[3])
+    me, z = (lax.axis_index("fsdp"), lax.axis_index("tp"))
+    width = out_ref.shape[-1]
+    rows = left.shape[1] // size
+
+    def hop_copy(at, number):
+        return pltpu.make_async_remote_copy(
+            src_ref=mixed.at[at, number],
+            dst_ref=got.at[at, number],
+            send_sem=hop_send.at[at, number],
+            recv_sem=hop_recv.at[at, number],
+            device_id={"tp": lax.rem(z + lanes - 1, lanes)},
+            device_id_type=MESH,
+        )
+
+    def relay(at, number):
+        @pl.when(z + 1 < lanes)
+        def _():
+            hop_copy(at, number - 1).wait_recv()
+            total = mixed[at, number].astype(jnp.float32)
+            total = total + got[at, number - 1].astype(jnp.float32)
+            mixed[at, number] = total.astype(jnp.bfloat16)
+
+        @pl.when(z > 0)
+        def _():
+            hop_copy(at, number).start()
+
+    loads_of = lambda: [pltpu.make_async_copy(left_ref, left, loads.at[PARTS])] + [
+        pltpu.make_async_copy(
+            right_ref.at[:, pl.ds(part * width, width)], right.at[part], loads.at[part]
+        )
+        for part in range(PARTS)
+    ]
+
+    @pl.when((head == 0) & (index == 0))
     def _():
+        for copy in loads_of():
+            copy.start()
+        barrier = pltpu.get_barrier_semaphore()
+        peers = [{"fsdp": flip(me, bit)} for bit in [1] + chip_bits(size)]
+        peers += [{"tp": lax.rem(z + 1, lanes)}, {"tp": lax.rem(z + lanes - 1, lanes)}]
+        for peer in peers:
+            pl.semaphore_signal(barrier, inc=1, device_id=peer, device_id_type=MESH)
+        pl.semaphore_wait(barrier, len(peers))
+        for copy in loads_of():
+            copy.wait()
         gq_ref[...] = jnp.zeros_like(gq_ref)
         gk_ref[...] = jnp.zeros_like(gk_ref)
+
+    def partial(part, slot, columns):
+        block = left[:, pl.ds(pl.multiple_of(slot * rows, rows), rows)]
+        return contract_first(block, right[part, :, columns])
+
+    calls, finish = scatter_steps(size, me, made, held, sent, came, sems, partial, out_ref)
+    at_step = {}
+    for number, call in enumerate(calls):
+        at_step.setdefault(number * heads * tiles // len(calls), []).append(call)
+    for number, some in at_step.items():
+
+        @pl.when(head * tiles + index == number)
+        def _():
+            for call in some:
+                call()
 
     @pl.when(index == 0)
     def _():
@@ -1137,19 +1228,53 @@
     grad_raw = norm_back(grad_query, normed, factor, nq_ref[...])
     dq_ref[...] = join_heads(grad_raw.astype(jnp.bfloat16), group)
 
-    @pl.when(index == pl.num_programs(1) - 1)
+    @pl.when(index == tiles - 1)
     def _():
         normed_key, key_factor = normalize_rows(k_ref[...])
         grad_key = turn_back(dk[...], cos_ref[...], sin_ref[...])
         gk_ref[...] += jnp.sum(grad_key * normed_key, axis=0, keepdims=True)
         grad_key = norm_back(grad_key, normed_key, key_factor, nk_ref[...])
-        back, _, own, _ = prev_ref.shape
-        for hop in range(back):
-            rows = slice(lead - (hop + 1) * own, lead - hop * own)
-            prev_ref[hop, 0] = grad_key[rows].astype(jnp.bfloat16)
-            prev_ref[hop, 1] = dv[rows, :].astype(jnp.bfloat16)
-        own_ref[0] = grad_key[lead:]
-        own_ref[1] = dv[lead:, :]
+        for number in range(back):
+            block = slice(number * own, (number + 1) * own)
+            mixed[head, number, 0] = grad_key[block].astype(jnp.bfloat16)
+            mixed[head, number, 1] = dv[block, :].astype(jnp.bfloat16)
+        own_sum[head, 0] = grad_key[lead:]
+        own_sum[head, 1] = dv[lead:, :]
+
+        @pl.when(z > 0)
+        def _():
+            hop_copy(head, 0).start()
+
+        for number in range(1, back):
+
+            @pl.when(head >= number)
+            def _():
+                relay(head - number, number)
+
+    @pl.when((head == heads - 1) & (index == tiles - 1))
+    def _():
+        for number in range(1, back):
+            for at in range(heads - number, heads):
+                relay(at, number)
+        for at in range(heads):
+            columns = slice(at * HD, (at + 1) * HD)
+
+            @pl.when(z + 1 < lanes)
+            def _():
+                hop_copy(at, back - 1).wait_recv()
+                total = own_sum[at] + got[at, back - 1].astype(jnp.float32)
+                pair_ref[:, :, columns] = total.astype(jnp.bfloat16)
+
+            @pl.when(z + 1 == lanes)
+            def _():
+                pair_ref[:, :, columns] = own_sum[at].astype(jnp.bfloat16)
+
+            @pl.when(z > 0)
+            def _():
+                for number in range(back):
+                    hop_copy(at, number).wait_send()
+
+        finish()
 
 
 def attention_specs(own, rows, group, tile, span):
@@ -1189,46 +1314,75 @@
 
 
 def attend_back(
-    queries, keys, values, bias, cosine, sine, norm_query, norm_key, grad, tile, step
+    queries,
+    keys,
+    values,
+    bias,
+    cosine,
+    sine,
+    norm_query,
+    norm_key,
+    grad,
+    tile,
+    step,
+    left,
+    right,
+    size,
+    lanes,
 ):
     own, rows = (queries.shape[0], keys.shape[0])
     heads = keys.shape[1] // HD
     group = queries.shape[1] // keys.shape[1]
     span = bias.shape[1]
     lead = rows - own
+    back = lead // own
+    tokens, depth = left.shape
+    width = right.shape[1] // PARTS
     whole = lambda g, t: (0, 0)
+    any_space = pl.BlockSpec(memory_space=pl.ANY)
     return pl.pallas_call(
-        functools.partial(attend_back_kernel, group, step, lead),
+        functools.partial(attend_back_kernel, group, step, lead, size, lanes),
         grid=(heads, own // tile),
         out_shape=(
             jax.ShapeDtypeStruct(queries.shape, jnp.bfloat16),
-            jax.ShapeDtypeStruct((lead // own, 2, own, heads * HD), jnp.bfloat16),
-            jax.ShapeDtypeStruct((2, own, heads * HD), jnp.float32),
+            jax.ShapeDtypeStruct((2, own, heads * HD), jnp.bfloat16),
             jax.ShapeDtypeStruct((1, HD), jnp.float32),
             jax.ShapeDtypeStruct((1, HD), jnp.float32),
+            jax.ShapeDtypeStruct((PARTS, depth // size, width), jnp.float32),
         ),
         in_specs=attention_specs(own, rows, group, tile, span)
-        + [pl.BlockSpec((tile, group * HD), lambda g, t: (t, g))],
+        + [pl.BlockSpec((tile, group * HD), lambda g, t: (t, g)), any_space, any_space],
         out_specs=(
             pl.BlockSpec((tile, group * HD), lambda g, t: (t, g)),
-            pl.BlockSpec((lead // own, 2, own, HD), lambda g, t: (0, 0, 0, g)),
-            pl.BlockSpec((2, own, HD), lambda g, t: (0, 0, g)),
+            pl.BlockSpec((2, own, heads * HD), lambda g, t: (0, 0, 0)),
             pl.BlockSpec((1, HD), whole),
             pl.BlockSpec((1, HD), whole),
+            pl.BlockSpec((PARTS, depth // size, width), lambda g, t: (0, 0, 0)),
         ),
         scratch_shapes=[
             pltpu.VMEM((rows, HD), jnp.bfloat16),
             pltpu.VMEM((rows, HD), jnp.float32),
             pltpu.VMEM((rows, HD), jnp.float32),
+            pltpu.VMEM((heads, back, 2, own, HD), jnp.bfloat16),
+            pltpu.VMEM((heads, back, 2, own, HD), jnp.bfloat16),
+            pltpu.VMEM((heads, 2, own, HD), jnp.float32),
+            pltpu.VMEM((tokens, depth), jnp.bfloat16),
+            pltpu.VMEM((PARTS, tokens, width), jnp.bfloat16),
+            pltpu.SemaphoreType.DMA((PARTS + 1,)),
+            pltpu.SemaphoreType.DMA((heads, back)),
+            pltpu.SemaphoreType.DMA((heads, back)),
+            *scatter_scratch(size, depth // size, width),
         ],
-        compiler_params=pltpu.CompilerParams(vmem_limit_bytes=VMEM),
+        compiler_params=pltpu.CompilerParams(
+            collective_id=9, has_side_effects=True, vmem_limit_bytes=60 * 1024 * 1024
+        ),
         cost_estimate=pl.CostEstimate(
             flops=40 * own * span * queries.shape[1],
             bytes_accessed=8 * queries.size + 16 * keys.size,
             transcendentals=own * span * heads * group,
         ),
         name="attend_back",
-    )(queries, keys, values, bias, cosine, sine, norm_query, norm_key, grad)
+    )(queries, keys, values, bias, cosine, sine, norm_query, norm_key, grad, left, right)
 
 
 def window_tables(length_row, pad_row, first, own, lead, tile, span):
@@ -1256,15 +1410,14 @@
     return (bias, cosine, sine, step, live[lead:].astype(jnp.float32))
 
 
-def hidden_rows_grad(grad):
-    mine = lax.psum_scatter(grad.astype(jnp.bfloat16), "tp", scatter_dimension=0, tiled=True)
-    return lax.all_to_all(mine, "fsdp", 1, 0, tiled=True).astype(jnp.float32)
-
-
 def over_lanes(grad):
     return lax.psum_scatter(
         grad.astype(jnp.bfloat16), "tp", scatter_dimension=2, tiled=True
     ).astype(jnp.float32)
+
+
+def join_parts(halves):
+    return jnp.concatenate([halves[part] for part in range(PARTS)], axis=1)
 
 
 def shards(
@@ -1334,23 +1487,38 @@
     )
     by_unit, (grad_gate, grad_up) = lax.optimization_barrier((by_unit, (grad_gate, grad_up)))
     grad_mid = sum_products(n_fsdp, 4, (grad_gate, grad_up), (rows_gate, rows_up))
-    grad_w_down, grad_w_gate, grad_w_up = [hidden_rows_grad(part) for part in by_unit]
+    by_unit = [lax.psum_scatter(part, "tp", scatter_dimension=0, tiled=True) for part in by_unit]
     grad_norm_mlp = jnp.sum(grad_mid * normed_two, axis=0)
     grad_hidden = grad_out + norm_back(grad_mid, normed_two, factor_two, norm_mlp)
 
     grad_low_out = grad_hidden.astype(jnp.bfloat16)
     grad_attended = back_out(grad_low_out, weights_attn, wo)
-    grad_query, grad_before, grad_own, grad_norm_query, grad_norm_key = attend_back(
-        query_raw, key_raw, value, bias, cosine, sine, *gains, grad_attended, tile, step
+    grad_query, grad_pair, grad_norm_query, grad_norm_key, sums_out = attend_back(
+        query_raw,
+        key_raw,
+        value,
+        bias,
+        cosine,
+        sine,
+        *gains,
+        grad_attended,
+        tile,
+        step,
+        grad_low_out,
+        attended,
+        n_fsdp,
+        n_tp,
     )
-    sums_early, arrived = flow(
-        n_fsdp, n_tp, 6, (normed_in, grad_low_out), (grad_query, attended), grad_before
-    )
-    grad_own = (grad_own + arrived.astype(jnp.float32)).astype(jnp.bfloat16)
-    grad_key, grad_value = (grad_own[0], grad_own[1])
-    (sums_late,) = flow(n_fsdp, n_tp, 7, (normed_in, normed_in), (grad_key, grad_value))
-    grad_early, grad_late = (over_lanes(sums_early), over_lanes(sums_late))
-    grad_low = back_in(grad_query, grad_key, grad_value, weights_attn)
+    sums_query, units_back = sum_query(n_fsdp, normed_in, grad_query, by_unit)
+    sums_pair, grad_low = sum_key(n_fsdp, normed_in, grad_query, grad_pair, weights_attn)
+    grad_w_out, grad_w_query = [
+        over_lanes(join_parts(sums)[None])[0] for sums in (sums_out, sums_query)
+    ]
+    grad_w_pair = over_lanes(sums_pair)
+    grad_w_down, grad_w_gate, grad_w_up = [
+        units_back[:, kind].reshape(-1, units_back.shape[3]).astype(jnp.float32)
+        for kind in range(3)
+    ]
     normed_one, factor_one = normalize_rows(inputs)
     grad_norm_attn = jnp.sum(grad_low * normed_one, axis=0)
     grad_input = grad_hidden + norm_back(grad_low, normed_one, factor_one, norm_attn)
@@ -1368,12 +1536,12 @@
         squares / (count * D),
         grad_input,
         grad_norm_attn,
-        grad_early[0],
-        grad_late[0],
-        grad_late[1],
+        grad_w_query,
+        grad_w_pair[0],
+        grad_w_pair[1],
         grad_norm_query,
         grad_norm_key,
-        grad_early[1].T,
+        grad_w_out.T,
         grad_norm_mlp,
         grad_w_gate.T,
         grad_w_up.T,

time: 1140 us -> 1310 us (1.15)
  waiting for transfers between devices: 28.1 us -> 217 us
    reduce_scatter x3, waiting for transfers between devices: 0.02 us -> 174 us  [shards(): lax.psum_scatter(part, 'tp', scatter_dimension=0, tiled=True)]
    reduce_scatter x2 -> x3, waiting for transfers between devices: 0.01 us -> 19.4 us  [over_lanes(): lax.psum_scatter(grad.astype(jnp.bfloat16), 'tp', scatter_dimension=2, ti...]
    pallas_call x4 -> x3, Pallas kernels: 243 us -> 243 us  [the longest x1 116 us: attend_back(): pl.pallas_call(functools.partial(attend_back_kernel, group, step, lead, s...]
  transfers between devices with their start and end apart: 11 -> 9, of which waited for: 3 -> 5; matrix products, arithmetic and copies ran while one was open for 6% -> 3% of each run, Pallas kernels for 49% -> 19%
where the time goes in v3:
time: 1310 us; the launch traced here: 1300 us
  Pallas kernels  924 us (71%)
  waiting for transfers between devices  217 us (17%)
  matrix products  60.5 us (5%)
  other arithmetic  54.9 us (4%)
  local copies, waits for them, and re-layouts  23.5 us (2%)
  between operations  18 us (1%)
    pallas_call x1, Pallas kernels, enter(): pl.pallas_call(functools.partial(enter_kernel, size, lanes, back), out_sh...  199 us
    pallas_call x2, Pallas kernels, sum_products(): pl.pallas_call(functools.partial(sum_products_kernel, size, terms), out_s...  187 us
    reduce_scatter x3, waiting for transfers between devices, shards(): lax.psum_scatter(part, 'tp', scatter_dimension=0, tiled=True)  174 us
    pallas_call x1, Pallas kernels, attend_back(): pl.pallas_call(functools.partial(attend_back_kernel, group, step, lead, s...  116 us
    pallas_call x1, Pallas kernels, gate_up(): pl.pallas_call(functools.partial(gate_up_kernel, size), out_shape=(shape(...  87.3 us
    pallas_call x1, Pallas kernels, grad_hidden_units(): pl.pallas_call(functools.partial(grad_hidden_kernel, size), out_shape=(sh...  85.6 us
    pallas_call x1, Pallas kernels, sum_query(): pl.pallas_call(functools.partial(sum_query_kernel, size), out_shape=(jax....  80.2 us
    dot_general x3, matrix products, contract_first(): lax.dot_general(left, right, (((0,), (0,)), ((), ())), preferred_element_...  60.5 us
  transfers between devices with their start and end apart: 9, of which 5 were waited for; matrix products, arithmetic and copies ran while one was open for 3% of the time, Pallas kernels for 19%

profile of v3, /device:TPU:0, one launch (start us, length us, event | category | flops | bytes accessed | tf_op | source)
XLA Modules:
  0.0 1298.6 jit_solution(1157986077335590288)
XLA Ops:
  16.5 199.2 %enter.1 = (bf16[2,512,2048]{2,1,0:T(8,128)(2,1)}, bf16[8,4,256,1536]{3,2,1,0:T(8,128)(2,1)}, bf16[3,192,2048]{2,1,0:T(8,128)(2,1)}, f32[8,128]{1,0:T(8,128)}) custom-call(bf16[512,2048]{1,0:T(8,128)(2,1)} %x_ref.5, bf16[256,1536]{1,0:T(8,128)(2,1)} %pad_maximum_fusion.3.w_ref, bf16[8,3,192,256]{3,2,1,0:T(8,128)(2,1)} %pad_maximum_fusion.m_ref, ...), custom_call_target="tpu_custom_call" | custom-call | bytes 419430400 | tf_op jit(solution)/shard_map/enter/pallas_call | solution.py:656
  227.0 32.8 %project_in.1 = (bf16[512,2048]{1,0:T(8,128)(2,1)}, f32[512,2048]{1,0:T(8,128)}, f32[1536,1024]{1,0:T(8,128)}, bf16[1536,1024]{1,0:T(8,128)(2,1)}) custom-call(bf16[2,512,2048]{2,1,0:T(8,128)(2,1)} %get-tuple-element.43.before_ref, bf16[512,2048]{1,0:T(8,128)(2,1)} %x_ref.5, f32[1,2048]{1,0:T(1,128)} %bitcast.106, ...), custom_call_target="tpu_custom_call" | custom-call | flops 17179869184 | bytes 23068672 | tf_op jit(solution)/shard_map/project_in/pallas_call | solution.py:966
  261.4 49.8 %attend.1.a_ref.right_ref = bf16[512,2048]{1,0:T(8,128)(2,1)} custom-call(f32[512,2048]{1,0:T(8,128)} %get-tuple-element.45.q_ref, f32[1536,1024]{1,0:T(8,128)} %get-tuple-element.46.k_ref, bf16[1536,1024]{1,0:T(8,128)(2,1)} %get-tuple-element.47.v_ref, f32[512,1280]{1,0:T(8,128)} %add_select_fusion.bias_ref, f32[1536,128]{1,0:T(8,128)} %get-tuple-element.143.cos_ref, ...), custom_call_target="tpu_custom_call" | custom-call | flops 21474836480 | bytes 13631488 | tf_op jit(solution)/shard_map/attend/pallas_call | solution.py:1299
  313.2 11.4 project_out.1
  329.9 20.8 %all-gather.9.cloned.1.call-done = bf16[1,768,2048]{2,1,0:T(8,128)(2,1)} async-done(((bf16[1,192,2048]{2,1,0:T(8,128)(2,1)}), bf16[1,768,2048]{2,1,0:T(8,128)(2,1)}) %all-gather.9.cloned.1.call-update) | async-done | bytes 3145744 | tf_op jit(solution)/shard_map/all_gather | solution.py:1462
  350.7 87.3 %gate_up.1 = (bf16[8,2,256,2048]{3,2,1,0:T(8,128)(2,1)}, f32[8,2,256,768]{3,2,1,0:T(8,128)}, f32[8,2,256,768]{3,2,1,0:T(8,128)}, bf16[8,2,256,768]{3,2,1,0:T(8,128)(2,1)}) custom-call(bf16[2,256,2048]{2,1,0:T(8,128)(2,1)} %bitcast.95, bf16[768,2048]{1,0:T(8,128)(2,1)} %bitcast.110, bf16[768,2048]{1,0:T(8,128)(2,1)} %bitcast.112), custom_call_target="tpu_custom_call" | custom-call | flops 25769803776 | bytes 209715200 | tf_op jit(solution)/shard_map/gate_up/pallas_call | solution.py:341
  438.0 89.2 %sum_products.2 = f32[2,256,2048]{2,1,0:T(8,128)} custom-call(bf16[8,2,256,768]{3,2,1,0:T(8,128)(2,1)} %get-tuple-element.49.refs_0_, bf16[768,2048]{1,0:T(8,128)(2,1)} %bitcast.114), custom_call_target="tpu_custom_call" | custom-call | flops 12884901888 | bytes 209715200 | tf_op jit(solution)/shard_map/sum_products/pallas_call | solution.py:511
  527.3 4.4 multiply_reduce_fusion
  534.3 85.6 %grad_hidden_units.1 = (bf16[8,2,256,2048]{3,2,1,0:T(8,128)(2,1)}, bf16[8,2,256,768]{3,2,1,0:T(8,128)(2,1)}, bf16[8,2,256,768]{3,2,1,0:T(8,128)(2,1)}) custom-call(bf16[2,256,2048]{2,1,0:T(8,128)(2,1)} %bitcast.96, bf16[768,2048]{1,0:T(8,128)(2,1)} %bitcast.115, f32[8,2,256,768]{3,2,1,0:T(8,128)} %get-tuple-element.52.gate_in, ...), custom_call_target="tpu_custom_call" | custom-call | flops 12884901888 | bytes 209715200 | tf_op jit(solution)/shard_map/grad_hidden_units/pallas_call | solution.py:455
  619.9 20.3 %bitcast_convert_fusion.2 = bf16[768,2048]{1,0:T(8,128)(2,1)} fusion(bf16[8,2,256,768]{3,2,1,0:T(8,128)(2,1)} %get-tuple-element.49.refs_0_, bf16[8,2,256,2048]{3,2,1,0:T(8,128)(2,1)} %get-tuple-element.54), kind=kOutput, calls=%fused_computation.2 | convolution fusion | flops 12886474752 | bytes 26214400 | tf_op jit(solution)/shard_map/dot_general | solution.py:37
  640.2 20.0 %bitcast_convert_fusion.1 = bf16[768,2048]{1,0:T(8,128)(2,1)} fusion(bf16[8,2,256,768]{3,2,1,0:T(8,128)(2,1)} %get-tuple-element.55, bf16[8,2,256,2048]{3,2,1,0:T(8,128)(2,1)} %get-tuple-element.56), kind=kOutput, calls=%fused_computation.1 | convolution fusion | flops 12886474752 | bytes 26214400 | tf_op jit(solution)/shard_map/dot_general | solution.py:37
  660.2 20.2 %bitcast_convert_fusion = bf16[768,2048]{1,0:T(8,128)(2,1)} fusion(bf16[8,2,256,768]{3,2,1,0:T(8,128)(2,1)} %get-tuple-element.57, bf16[8,2,256,2048]{3,2,1,0:T(8,128)(2,1)} %get-tuple-element.56), kind=kOutput, calls=%fused_computation | convolution fusion | flops 12886474752 | bytes 26214400 | tf_op jit(solution)/shard_map/dot_general | solution.py:37
  680.4 97.5 %sum_products.3 = f32[2,256,2048]{2,1,0:T(8,128)} custom-call(bf16[8,2,256,768]{3,2,1,0:T(8,128)(2,1)} %get-tuple-element.55, bf16[8,2,256,768]{3,2,1,0:T(8,128)(2,1)} %get-tuple-element.57, bf16[768,2048]{1,0:T(8,128)(2,1)} %bitcast.111, bf16[768,2048]{1,0:T(8,128)(2,1)} %bitcast.113), custom_call_target="tpu_custom_call" | custom-call | flops 25769803776 | bytes 209715200 | tf_op jit(solution)/shard_map/sum_products/pallas_call | solution.py:511
  782.6 4.1 fusion.22
  786.7 8.8 back_out.1.do_ref
  795.6 115.7 %attend_back.1 = (bf16[512,2048]{1,0:T(8,128)(2,1)}, bf16[2,512,1024]{2,1,0:T(8,128)(2,1)}, f32[1,128]{1,0:T(1,128)}, f32[1,128]{1,0:T(1,128)}, f32[2,256,1024]{2,1,0:T(8,128)}) custom-call(f32[512,2048]{1,0:T(8,128)} %get-tuple-element.45.q_ref, f32[1536,1024]{1,0:T(8,128)} %get-tuple-element.46.k_ref, bf16[1536,1024]{1,0:T(8,128)(2,1)} %get-tuple-element.47.v_ref, ...), custom_call_target="tpu_custom_call" | custom-call | flops 53687091200 | bytes 33554432 | tf_op jit(solution)/shard_map/attend_back/pallas_call | solution.py:1343
  914.2 47.6 %sum_key.1 = (f32[2,256,1024]{2,1,0:T(8,128)}, f32[512,2048]{1,0:T(8,128)}) custom-call(bf16[512,2048]{1,0:T(8,128)(2,1)} %get-tuple-element.50.left_ref, bf16[512,2048]{1,0:T(8,128)(2,1)} %get-tuple-element.60.q_ref.right_ref, bf16[2,512,1024]{2,1,0:T(8,128)(2,1)} %get-tuple-element.61.kv_ref, bf16[8,4,256,1536]{3,2,1,0:T(8,128)(2,1)} %get-tuple-element.44.w_ref), custom_call_target="tpu_custom_call" | custom-call | flops 8589934592 | bytes 104857600 | tf_op jit(solution)/shard_map/sum_key/pallas_call | solution.py:847
  971.8 18.8 %sum_small.1 = f32[40,128]{1,0:T(8,128)} custom-call(f32[40,128]{1,0:T(8,128)} %pad.5.x_ref), custom_call_target="tpu_custom_call" | custom-call | tf_op jit(solution)/shard_map/sum_small/pallas_call | solution.py:905
  995.2 6.6 fusion.7
  1004.7 48.7 %reduce-scatter.7.cloned.1.call-done.refs_0_ = bf16[192,2048]{1,0:T(8,128)(2,1)} async-done(((bf16[768,2048]{1,0:T(8,128)(2,1)}), bf16[192,2048]{1,0:T(8,128)(2,1)}) %reduce-scatter.7.cloned.1.call-update) | async-done | bytes 786448 | tf_op jit(solution)/shard_map/reduce_scatter | solution.py:1490
  1053.4 62.6 %reduce-scatter.9.cloned.1.call-done.refs_1_ = bf16[192,2048]{1,0:T(8,128)(2,1)} async-done(((bf16[768,2048]{1,0:T(8,128)(2,1)}), bf16[192,2048]{1,0:T(8,128)(2,1)}) %reduce-scatter.9.cloned.1.call-update) | async-done | bytes 786448 | tf_op jit(solution)/shard_map/reduce_scatter | solution.py:1490
  1116.0 62.6 %reduce-scatter.11.cloned.1.call-done.refs_2_ = bf16[192,2048]{1,0:T(8,128)(2,1)} async-done(((bf16[768,2048]{1,0:T(8,128)(2,1)}), bf16[192,2048]{1,0:T(8,128)(2,1)}) %reduce-scatter.11.cloned.1.call-update) | async-done | bytes 786448 | tf_op jit(solution)/shard_map/reduce_scatter | solution.py:1490
  1178.7 80.2 %sum_query.1 = (f32[2,256,1024]{2,1,0:T(8,128)}, bf16[8,3,192,256]{3,2,1,0:T(8,128)(2,1)}) custom-call(bf16[512,2048]{1,0:T(8,128)(2,1)} %get-tuple-element.50.left_ref, bf16[512,2048]{1,0:T(8,128)(2,1)} %get-tuple-element.60.q_ref.right_ref, bf16[192,2048]{1,0:T(8,128)(2,1)} %reduce-scatter.7.cloned.1.call-done.refs_0_, ...), custom_call_target="tpu_custom_call" | custom-call | flops 4294967296 | bytes 104857600 | tf_op jit(solution)/shard_map/sum_query/pallas_call | solution.py:750
  1269.2 19.3 %reduce-scatter.13.cloned.1.call-done = bf16[1,256,512]{2,1,0:T(8,128)(2,1)} async-done(((bf16[1,256,2048]{2,1,0:T(8,128)(2,1)}), bf16[1,256,512]{2,1,0:T(8,128)(2,1)}) %reduce-scatter.13.cloned.1.call-update) | async-done | bytes 262160 | tf_op jit(solution)/shard_map/reduce_scatter | solution.py:1414
  (121 shorter events, 67.0 us)
Async XLA Ops:
  7.2 6.1 copy-start.8
  7.2 7.8 copy-start.10
  7.2 7.7 copy-start.11
  7.2 7.7 copy-start.9
  7.2 322.7 %all-gather.7.cloned.1.call-start = ((), (), s32[]{:S(2)}) async-start(), calls=%async_computation.12 | async-start | bytes 3932160 | tf_op jit(solution)/shard_map/all_gather | solution.py:1462
  215.7 4.7 copy-start.15
  215.7 5.1 copy-start.13
  218.9 131.8 %all-gather.9.cloned.1.call-start = ((), (), s32[]{:S(2)}) async-start(), calls=%async_computation.13 | async-start | bytes 3932160 | tf_op jit(solution)/shard_map/all_gather | solution.py:1462
  219.6 218.4 %all-gather.11.cloned.1.call-start = ((), (), s32[]{:S(2)}) async-start(), calls=%async_computation.14 | async-start | bytes 3932160 | tf_op jit(solution)/shard_map/all_gather | solution.py:1462
  220.3 781.4 %reduce-scatter.17.cloned.1.call-start = ((), (), s32[]{:S(2)}) async-start(), calls=%async_computation.11 | async-start | bytes 1310720 | tf_op jit(solution)/shard_map/reduce_scatter | solution.py:1414
  313.2 14.1 %copy-start.12 = (f32[2048]{0:T(1024)S(1)}, f32[2048]{0:T(1024)}, u32[]{:S(2)}) copy-start(f32[2048]{0:T(1024)} %param.26) | copy-start | bytes 24580
  324.6 3.5 copy-start
  438.0 89.2 %copy-start.1 = (f32[512,2048]{1,0:T(8,128)S(1)}, f32[512,2048]{1,0:T(8,128)}, u32[]{:S(2)}) copy-start(f32[512,2048]{1,0:T(8,128)} %project_out.1) | copy-start | bytes 12582916
  438.0 89.2 %copy-start.6 = (bf16[512,2048]{1,0:T(8,128)(2,1)S(1)}, bf16[512,2048]{1,0:T(8,128)(2,1)}, u32[]{:S(2)}) copy-start(bf16[512,2048]{1,0:T(8,128)(2,1)} %param.18) | copy-start | bytes 6291460
  680.4 97.5 %copy-start.2 = (f32[512,2048]{1,0:T(8,128)S(1)}, f32[512,2048]{1,0:T(8,128)}, u32[]{:S(2)}) copy-start(f32[512,2048]{1,0:T(8,128)} %project_out.1) | copy-start | bytes 12582916
  777.9 3.5 copy-start.5
  777.9 4.7 copy-start.7
  914.2 89.6 %reduce-scatter.15.cloned.1.call-start = ((), (), s32[]{:S(2)}) async-start(), calls=%async_computation.10 | async-start | bytes 1310720 | tf_op jit(solution)/shard_map/reduce_scatter | solution.py:1414
  964.5 88.9 %reduce-scatter.7.cloned.1.call-start = ((), (), s32[]{:S(2)}) async-start(), calls=%async_computation.6 | async-start | bytes 3932160 | tf_op jit(solution)/shard_map/reduce_scatter | solution.py:1490
  965.1 150.9 %reduce-scatter.9.cloned.1.call-start = ((), (), s32[]{:S(2)}) async-start(), calls=%async_computation.7 | async-start | bytes 3932160 | tf_op jit(solution)/shard_map/reduce_scatter | solution.py:1490
  965.9 212.8 %reduce-scatter.11.cloned.1.call-start = ((), (), s32[]{:S(2)}) async-start(), calls=%async_computation.8 | async-start | bytes 3932160 | tf_op jit(solution)/shard_map/reduce_scatter | solution.py:1490
  966.6 3.9 copy-start.17
  966.6 3.9 copy-start.16
  966.7 321.9 %reduce-scatter.13.cloned.1.call-start = ((), (), s32[]{:S(2)}) async-start(), calls=%async_computation.9 | async-start | bytes 1310720 | tf_op jit(solution)/shard_map/reduce_scatter | solution.py:1414
  (3 other events, 6.9 us)
Sparse Core Ops, SparseCore 0:
  219.0 67.8 all-gather.6
  288.5 62.1 all-gather.8
  352.8 62.1 all-gather.10
  914.3 26.5 reduce-scatter.16
  964.7 27.6 reduce-scatter.14
  994.5 58.8 reduce-scatter.6
  1055.7 60.2 reduce-scatter.8
  1118.3 60.2 reduce-scatter.10
  1261.9 26.6 reduce-scatter.12

commit v4 on v3

--- a/solution.py
+++ b/solution.py
@@ -93,23 +93,27 @@
 
 
 class Gather:
-    def __init__(self, size, me, whole, sems, parts=PARTS, lane=lambda part: part):
-        self.size, self.me, self.whole, self.parts, self.lane = (size, me, whole, parts, lane)
+    def __init__(self, size, me, whole, sems, parts=PARTS, lane=lambda part: part, parity=lambda part: part, own=None):
+        self.size, self.me, self.whole, self.parts = (size, me, whole, parts)
+        self.lane, self.parity, self.own = (lane, parity, own)
         self.chip_send, self.chip_recv, self.core_send, self.core_recv = sems
         self.steps = len(chip_bits(size))
         self.patterns = sorted(range(1 << self.steps), key=lambda m: (top(m), m))
 
     def order(self, part):
-        return orders(self.size)[part % 2]
+        return orders(self.size)[self.parity(part) % 2]
 
     def slot(self, part, pattern, sibling):
         return flip(self.me, mask_of(pattern, self.order(part)) + sibling)
+
+    def source(self, part, pattern, block):
+        return self.own if self.own is not None and part == 0 and pattern == 0 else block
 
     def chip_copy(self, part, step, pattern):
         block = self.whole.at[self.slot(part, pattern, 0), self.lane(part)]
         number = (1 << step) - 1 + pattern
         return pltpu.make_async_remote_copy(
-            src_ref=block,
+            src_ref=self.source(part, pattern, block),
             dst_ref=block,
             send_sem=self.chip_send.at[part, number],
             recv_sem=self.chip_recv.at[part, number],
@@ -120,7 +124,7 @@
     def core_copy(self, part, pattern):
         block = self.whole.at[self.slot(part, pattern, 0), self.lane(part)]
         return pltpu.make_async_remote_copy(
-            src_ref=block,
+            src_ref=self.source(part, pattern, block),
             dst_ref=block,
             send_sem=self.core_send.at[part, pattern],
             recv_sem=self.core_recv.at[part, pattern],
@@ -167,12 +171,22 @@
     ]
 
 
-def scatter_steps(size, me, made, held, sent, came, sems, partial, final):
+def first_step(pattern, steps):
+    return (pattern & -pattern).bit_length() - 1 if pattern else steps
+
+
+def scatter_order(steps):
+    return sorted(range(1 << steps), key=lambda m: (first_step(m, steps), -bin(m).count("1"), m))
+
+
+def scatter_steps(
+    size, me, made, held, sent, came, sems, partial, final, ready=lambda part, slot, q, sibling: None
+):
     chip_send, chip_recv, core_send, core_recv = sems
     steps = len(chip_bits(size))
     order = [bits[::-1] for bits in orders(size)]
-    first = lambda m: (m & -m).bit_length() - 1 if m else steps
-    patterns = sorted(range(1 << steps), key=lambda m: (first(m), -bin(m).count("1"), m))
+    first = lambda m: first_step(m, steps)
+    patterns = scatter_order(steps)
     place = {m: q for q, m in enumerate(patterns)}
     width = final.shape[-1]
     chunk = min(512, width)
@@ -202,17 +216,14 @@
 
     def for_sibling(q):
         pair = slots(patterns[q], 1)
-
-        @pl.loop(0, PARTS)
-        def _(part):
+        for part in range(PARTS):
+            ready(part, pair[part], q, 1)
+
             @pl.loop(0, width // chunk)
             def _(index):
                 columns = pl.ds(pl.multiple_of(index * chunk, chunk), chunk)
-                made[part, q, :, columns] = partial(part, pick(part, pair), columns).astype(
-                    jnp.bfloat16
-                )
-
-        for part in range(PARTS):
+                made[part, q, :, columns] = partial(part, pair[part], columns).astype(jnp.bfloat16)
+
             core_copy(part, q).start()
 
     def for_chips(q):
@@ -220,27 +231,39 @@
         pair = slots(pattern, 0)
         arrivals = [place[pattern | 1 << step] for step in range(first(pattern))]
         for part in range(PARTS):
-            core_copy(part, q).wait_recv()
-            for arrival in arrivals:
-                chip_copy(part, arrival).wait_recv()
-
-        @pl.loop(0, PARTS)
-        def _(part):
+            ready(part, pair[part], q, 0)
+            if pattern:
+                core_copy(part, q).wait_recv()
+                for arrival in arrivals:
+                    chip_copy(part, arrival).wait_recv()
+
             @pl.loop(0, width // chunk)
             def _(index):
                 columns = pl.ds(pl.multiple_of(index * chunk, chunk), chunk)
-                total = partial(part, pick(part, pair), columns)
-                total = total + held[part, q, :, columns].astype(jnp.float32)
-                for arrival in arrivals:
-                    total = total + came[part, arrival, :, columns].astype(jnp.float32)
+                total = partial(part, pair[part], columns)
                 if pattern:
+                    total = total + held[part, q, :, columns].astype(jnp.float32)
+                    for arrival in arrivals:
+                        total = total + came[part, arrival, :, columns].astype(jnp.float32)
                     sent[part, q, :, columns] = total.astype(jnp.bfloat16)
                 else:
                     final[part, :, columns] = total
 
-        if pattern:
+            if pattern:
+                chip_copy(part, q).start()
+        if not pattern:
             for part in range(PARTS):
-                chip_copy(part, q).start()
+                core_copy(part, q).wait_recv()
+                for arrival in arrivals:
+                    chip_copy(part, arrival).wait_recv()
+
+                @pl.loop(0, width // chunk)
+                def _(index):
+                    columns = pl.ds(pl.multiple_of(index * chunk, chunk), chunk)
+                    total = final[part, :, columns] + held[part, q, :, columns].astype(jnp.float32)
+                    for arrival in arrivals:
+                        total = total + came[part, arrival, :, columns].astype(jnp.float32)
+                    final[part, :, columns] = total
 
     def finish():
         for q in range(len(patterns)):
@@ -249,11 +272,9 @@
                 if patterns[q]:
                     chip_copy(part, q).wait_send()
 
-    calls = [functools.partial(for_sibling, 0)]
+    calls = []
     for q in range(len(patterns)):
-        if q + 1 < len(patterns):
-            calls.append(functools.partial(for_sibling, q + 1))
-        calls.append(functools.partial(for_chips, q))
+        calls += [functools.partial(for_sibling, q), functools.partial(for_chips, q)]
     return (calls, finish)
 
 
@@ -273,15 +294,38 @@
 
 
 def gate_up_kernel(
-    size, x_ref, wg_ref, wu_ref, x_out, gate_out, up_out, prod_out, whole, gate, up, prod, load, keep, store, *sems
+    size,
+    x_ref,
+    wg_in,
+    wu_in,
+    x_out,
+    gate_out,
+    up_out,
+    prod_out,
+    whole,
+    wg_ref,
+    wu_ref,
+    gate,
+    up,
+    prod,
+    load,
+    keep,
+    store,
+    *sems,
 ):
     me = lax.axis_index("fsdp")
     hidden = wg_ref.shape[0]
     chunk = 256 if hidden % 256 == 0 else 128
-    own = pltpu.make_async_copy(x_ref, whole.at[me], load)
-    own.start()
-    own.wait()
+    loads = [
+        pltpu.make_async_copy(source, target, load.at[i])
+        for i, (source, target) in enumerate(
+            ((x_ref, whole.at[me]), (wg_in, wg_ref), (wu_in, wu_ref))
+        )
+    ]
+    for copy in loads:
+        copy.start()
     greet(me, size)
+    loads[0].wait()
     state = {"count": 0, "last": None}
 
     def stores(part, at):
@@ -296,6 +340,9 @@
             pltpu.make_async_copy(
                 whole.at[pair[part], part], x_out.at[pair[part], part], keep.at[part, count]
             ).start()
+        if last is None:
+            for copy in loads[1:]:
+                copy.wait()
 
         @pl.loop(0, PARTS)
         def _(part):
@@ -336,7 +383,6 @@
     own, width = values.shape
     rows, hidden = (own // PARTS, rows_gate.shape[0])
     any_space = pl.BlockSpec(memory_space=pl.ANY)
-    vmem = pl.BlockSpec(memory_space=pltpu.VMEM)
     shape = lambda columns, kind: jax.ShapeDtypeStruct((size, PARTS, rows, columns), kind)
     outs = pl.pallas_call(
         functools.partial(gate_up_kernel, size),
@@ -346,14 +392,16 @@
             shape(hidden, jnp.float32),
             shape(hidden, jnp.bfloat16),
         ),
-        in_specs=[any_space, vmem, vmem],
+        in_specs=[any_space] * 3,
         out_specs=(any_space,) * 4,
         scratch_shapes=[
             pltpu.VMEM((size, PARTS, rows, width), jnp.bfloat16),
+            pltpu.VMEM((hidden, width), jnp.bfloat16),
+            pltpu.VMEM((hidden, width), jnp.bfloat16),
             pltpu.VMEM((PARTS, rows, hidden), jnp.float32),
             pltpu.VMEM((PARTS, rows, hidden), jnp.float32),
             pltpu.VMEM((PARTS, rows, hidden), jnp.bfloat16),
-            pltpu.SemaphoreType.DMA,
+            pltpu.SemaphoreType.DMA((3,)),
             pltpu.SemaphoreType.DMA((PARTS, size)),
             pltpu.SemaphoreType.DMA((PARTS, 3)),
             *gather_semaphores(size),
@@ -370,16 +418,44 @@
 
 
 def grad_hidden_kernel(
-    size, x_ref, wd_ref, gate_in, up_in, x_out, dgate_out, dup_out, whole, gate, up, dprod, dgate, dup, load, keep, fetch, store, *sems
+    size,
+    x_ref,
+    wd_in,
+    gate_in,
+    up_in,
+    prod_in,
+    two_in,
+    dgate_out,
+    dup_out,
+    dwd_out,
+    dwg_out,
+    dwu_out,
+    whole,
+    wd_ref,
+    gate,
+    up,
+    prod,
+    two,
+    dprod,
+    dgate,
+    dup,
+    sums,
+    load,
+    fetch,
+    store,
+    flush,
+    *sems,
 ):
     me = lax.axis_index("fsdp")
-    hidden = wd_ref.shape[0]
+    hidden, width = wd_ref.shape
+    rows = dprod.shape[0]
     chunk = 256 if hidden % 256 == 0 else 128
-    own = pltpu.make_async_copy(x_ref, whole.at[me], load)
-    own.start()
-    own.wait()
-    greet(me, size)
-    state = {"count": 0, "last": None, "all": []}
+    loads = [
+        pltpu.make_async_copy(x_ref, whole.at[me], load.at[0]),
+        pltpu.make_async_copy(wd_in, wd_ref, load.at[1]),
+    ]
+    for copy in loads:
+        copy.start()
 
     def stores(part, at):
         return [
@@ -388,26 +464,47 @@
         ]
 
     def fetches(part, at):
+        pairs = ((gate_in, gate), (up_in, up), (prod_in, prod), (two_in, two))
         return [
-            pltpu.make_async_copy(source.at[at, part], buffer, fetch.at[i])
-            for i, (source, buffer) in enumerate(((gate_in, gate), (up_in, up)))
+            pltpu.make_async_copy(source.at[at, part], buffer.at[part], fetch.at[part, i])
+            for i, (source, buffer) in enumerate(pairs)
         ]
 
+    gather = Gather(size, me, whole, sems)
+    order = []
+    for pattern in gather.patterns:
+        for sibling in (0, 1):
+            order.append([gather.slot(part, pattern, sibling) for part in range(PARTS)])
+    for copy in fetches(0, order[0][0]):
+        copy.start()
+    sums[...] = jnp.zeros_like(sums)
+    greet(me, size)
+    loads[0].wait()
+    state = {"count": 0}
+
     def work(pair):
-        count, last = (state["count"], state["last"])
-        for part in range(PARTS):
-            pltpu.make_async_copy(
-                whole.at[pair[part], part], x_out.at[pair[part], part], keep.at[part, count]
-            ).start()
+        count = state["count"]
+        last = order[count - 1] if count else None
+        following = order[count + 1] if count + 1 < len(order) else None
+        state["count"] = count + 1
+        if count == 0:
+            loads[1].wait()
 
         @pl.loop(0, PARTS)
         def _(part):
             at = pick(part, pair)
-            for copy in fetches(part, at):
-                copy.start()
-            if last is not None:
-                for copy in stores(part, pick(part, last)):
-                    copy.wait()
+
+            @pl.when(part == 0)
+            def _():
+                for copy in fetches(1, pair[1]):
+                    copy.start()
+
+            if following is not None:
+
+                @pl.when(part == 1)
+                def _():
+                    for copy in fetches(0, following[0]):
+                        copy.start()
 
             @pl.loop(0, hidden // chunk)
             def _(index):
@@ -416,87 +513,140 @@
 
             for copy in fetches(part, at):
                 copy.wait()
+            if last is not None:
+                for copy in stores(part, pick(part, last)):
+                    copy.wait()
 
             @pl.loop(0, hidden // chunk)
             def _(index):
                 units = pl.ds(pl.multiple_of(index * chunk, chunk), chunk)
-                gates, grads = (gate[:, units], dprod[:, units])
+                gates, grads = (gate[part, :, units], dprod[:, units])
                 sigmoid = jax.nn.sigmoid(gates)
                 dgate[part, :, units] = (
-                    grads * up[:, units] * sigmoid * (1.0 + gates * (1.0 - sigmoid))
+                    grads * up[part, :, units] * sigmoid * (1.0 + gates * (1.0 - sigmoid))
                 ).astype(jnp.bfloat16)
                 dup[part, :, units] = (grads * (gates * sigmoid)).astype(jnp.bfloat16)
 
             for copy in stores(part, at):
                 copy.start()
 
-        state["count"], state["last"] = (count + 1, pair)
-        state["all"].append(pair)
-
-    gather = Gather(size, me, whole, sems)
+            @pl.loop(0, hidden // chunk)
+            def _(index):
+                units = pl.ds(pl.multiple_of(index * chunk, chunk), chunk)
+                sums[0, units, :] += contract_first(prod[part, :, units], whole[at, part])
+                sums[1, units, :] += contract_first(dgate[part, :, units], two[part])
+                sums[2, units, :] += contract_first(dup[part, :, units], two[part])
+
     gather.pairs(work)
     gather.finish()
     for part in range(PARTS):
-        for copy in stores(part, state["last"][part]):
+        for copy in stores(part, order[-1][part]):
             copy.wait()
-        for count, pair in enumerate(state["all"]):
-            pltpu.make_async_copy(
-                whole.at[pair[part], part], x_out.at[pair[part], part], keep.at[part, count]
-            ).wait()
-
-
-def grad_hidden_units(size, values, rows_down, gate, up):
+    outs = (dwd_out, dwg_out, dwu_out)
+    pieces = hidden // rows
+    copies = []
+    for piece in range(3 * pieces):
+        kind, first = (piece // pieces, piece % pieces * rows)
+        block = whole.at[piece // PARTS, piece % PARTS]
+        block[...] = sums[kind, first : first + rows, :].astype(jnp.bfloat16)
+        copy = pltpu.make_async_copy(
+            block, outs[kind].at[pl.ds(first, rows)], flush.at[piece]
+        )
+        copy.start()
+        copies.append(copy)
+    for copy in copies:
+        copy.wait()
+
+
+def grad_hidden_units(size, values, rows_down, gate, up, product, whole_two):
     own, width = values.shape
     rows, hidden = (own // PARTS, rows_down.shape[0])
     any_space = pl.BlockSpec(memory_space=pl.ANY)
-    vmem = pl.BlockSpec(memory_space=pltpu.VMEM)
     shape = lambda columns, kind: jax.ShapeDtypeStruct((size, PARTS, rows, columns), kind)
-    blocks = lambda array: array.reshape(size, PARTS, rows, hidden)
-    outs = pl.pallas_call(
+    blocks = lambda array: array.reshape(size, PARTS, rows, -1)
+    weight = jax.ShapeDtypeStruct((hidden, width), jnp.bfloat16)
+    dgate, dup, *grads = pl.pallas_call(
         functools.partial(grad_hidden_kernel, size),
-        out_shape=(
-            shape(width, jnp.bfloat16),
-            shape(hidden, jnp.bfloat16),
-            shape(hidden, jnp.bfloat16),
-        ),
-        in_specs=[any_space, vmem, any_space, any_space],
-        out_specs=(any_space,) * 3,
+        out_shape=(shape(hidden, jnp.bfloat16), shape(hidden, jnp.bfloat16), weight, weight, weight),
+        in_specs=[any_space] * 6,
+        out_specs=(any_space,) * 5,
         scratch_shapes=[
             pltpu.VMEM((size, PARTS, rows, width), jnp.bfloat16),
-            pltpu.VMEM((rows, hidden), jnp.float32),
-            pltpu.VMEM((rows, hidden), jnp.float32),
+            pltpu.VMEM((hidden, width), jnp.bfloat16),
+            pltpu.VMEM((PARTS, rows, hidden), jnp.float32),
+            pltpu.VMEM((PARTS, rows, hidden), jnp.float32),
+            pltpu.VMEM((PARTS, rows, hidden), jnp.bfloat16),
+            pltpu.VMEM((PARTS, rows, width), jnp.bfloat16),
             pltpu.VMEM((rows, hidden), jnp.float32),
             pltpu.VMEM((PARTS, rows, hidden), jnp.bfloat16),
             pltpu.VMEM((PARTS, rows, hidden), jnp.bfloat16),
-            pltpu.SemaphoreType.DMA,
-            pltpu.SemaphoreType.DMA((PARTS, size)),
+            pltpu.VMEM((3, hidden, width), jnp.float32),
             pltpu.SemaphoreType.DMA((2,)),
+            pltpu.SemaphoreType.DMA((PARTS, 4)),
             pltpu.SemaphoreType.DMA((PARTS, 2)),
+            pltpu.SemaphoreType.DMA((3 * (hidden // rows),)),
             *gather_semaphores(size),
         ],
         compiler_params=pltpu.CompilerParams(
             collective_id=3, has_side_effects=True, vmem_limit_bytes=VMEM
         ),
         cost_estimate=pl.CostEstimate(
-            flops=2 * size * own * width * hidden, bytes_accessed=200 * 1024 * 1024, transcendentals=0
+            flops=8 * size * own * width * hidden, bytes_accessed=200 * 1024 * 1024, transcendentals=0
         ),
         name="grad_hidden_units",
-    )(values.reshape(PARTS, rows, width), rows_down, blocks(gate), blocks(up))
-    return tuple(out.reshape(size * own, -1) for out in outs)
+    )(values.reshape(PARTS, rows, width), rows_down, *map(blocks, (gate, up, product, whole_two)))
+    return (dgate.reshape(size * own, hidden), dup.reshape(size * own, hidden), grads)
 
 
 def sum_products_kernel(size, terms, *refs):
-    lefts, rights, out = (refs[:terms], refs[terms : 2 * terms], refs[2 * terms])
-    made, held, sent, came, *sems = refs[2 * terms + 1 :]
+    left_in, right_in, out = (refs[:terms], refs[terms : 2 * terms], refs[2 * terms])
+    at = 2 * terms + 1
+    lefts, rights, (w_load, x_load) = (
+        refs[at : at + terms],
+        refs[at + terms : at + 2 * terms],
+        refs[at + 2 * terms : at + 2 * terms + 2],
+    )
+    made, held, sent, came, *sems = refs[at + 2 * terms + 2 :]
     me = lax.axis_index("fsdp")
-    greet(me, size)
 
     def partial(part, slot, columns):
         return sum(
             dot(left[slot, part], right[:, columns]) for left, right in zip(lefts, rights)
         )
 
-    calls, finish = scatter_steps(size, me, made, held, sent, came, sems, partial, out)
+    def tiles(part, slot, q, sibling):
+        return [
+            pltpu.make_async_copy(
+                source.at[slot, part], left.at[slot, part], x_load.at[2 * q + sibling, part, i]
+            )
+            for i, (source, left) in enumerate(zip(left_in, lefts))
+        ]
+
+    seen = []
+
+    def ready(part, slot, q, sibling):
+        if not seen:
+            for copy in weights:
+                copy.wait()
+        seen.append(slot)
+        for copy in tiles(part, slot, q, sibling):
+            copy.wait()
+
+    weights = [
+        pltpu.make_async_copy(source, right, w_load.at[i])
+        for i, (source, right) in enumerate(zip(right_in, rights))
+    ]
+    for copy in weights:
+        copy.start()
+    order = [bits[::-1] for bits in orders(size)]
+    for q, pattern in enumerate(scatter_order(len(order[0]))):
+        for sibling in (1, 0):
+            for part in range(PARTS):
+                slot = flip(me, mask_of(pattern, order[part]) + sibling)
+                for copy in tiles(part, slot, q, sibling):
+                    copy.start()
+    greet(me, size)
+    calls, finish = scatter_steps(size, me, made, held, sent, came, sems, partial, out, ready)
     for call in calls:
         call()
     finish()
@@ -511,9 +661,15 @@
     out = pl.pallas_call(
         functools.partial(sum_products_kernel, size, terms),
         out_shape=jax.ShapeDtypeStruct((PARTS, rows, width), jnp.float32),
-        in_specs=[vmem] * (2 * terms),
+        in_specs=[pl.BlockSpec(memory_space=pl.ANY)] * (2 * terms),
         out_specs=vmem,
-        scratch_shapes=scatter_scratch(size, rows, width),
+        scratch_shapes=[
+            *[pltpu.VMEM((size, PARTS, rows, hidden), jnp.bfloat16)] * terms,
+            *[pltpu.VMEM((hidden, width), jnp.bfloat16)] * terms,
+            pltpu.SemaphoreType.DMA((terms,)),
+            pltpu.SemaphoreType.DMA((size, PARTS, terms)),
+            *scatter_scratch(size, rows, width),
+        ],
         compiler_params=pltpu.CompilerParams(
             collective_id=number, has_side_effects=True, vmem_limit_bytes=VMEM
         ),
@@ -526,41 +682,76 @@
 
 
 def enter_kernel(
-    size, lanes, back, x_ref, w_ref, m_ref, c_ref,
-    before, whole, mine, count, counts, loads, z_send, z_recv, x_send, x_recv, m_send, m_recv, c_send, c_recv, *sems
+    size,
+    lanes,
+    back,
+    x_ref,
+    w_ref,
+    m_ref,
+    c_ref,
+    before,
+    whole,
+    mine_gate,
+    mine_up,
+    mine_down,
+    count,
+    counts,
+    loads,
+    z_send,
+    z_recv,
+    x_send,
+    x_recv,
+    m_send,
+    m_recv,
+    c_send,
+    c_recv,
+    *sems,
 ):
     me, z = (lax.axis_index("fsdp"), lax.axis_index("tp"))
-    part_of = lambda device: pl.ds(
-        pl.multiple_of(device * m_ref.shape[-1], m_ref.shape[-1]), m_ref.shape[-1]
-    )
-    local = [
-        pltpu.make_async_copy(w_ref, whole.at[me, z], loads.at[0]),
-        pltpu.make_async_copy(m_ref.at[me], mine.at[:, :, part_of(me)], loads.at[1]),
+    mine = (mine_gate, mine_up, mine_down)
+    span = m_ref.shape[-1]
+    part_of = lambda device: pl.ds(pl.multiple_of(device * span, span), span)
+    local = [pltpu.make_async_copy(w_ref, whole.at[me, z], loads.at[0])]
+    local += [
+        pltpu.make_async_copy(m_ref.at[me, kind], mine[kind].at[:, part_of(me)], loads.at[kind + 1])
+        for kind in range(3)
     ]
     for copy in local:
         copy.start()
     counts[me] = c_ref[...]
+    up, down = (lax.rem(z + 1, lanes), lax.rem(z + lanes - 1, lanes))
     barrier = pltpu.get_barrier_semaphore()
-    peers = [{"fsdp": flip(me, other)} for other in range(1, size)]
-    peers += [{"tp": lax.rem(z + hop, lanes)} for hop in range(1, lanes)]
+    peers = [{"fsdp": flip(me, other)} for other in range(1, size)] + [{"tp": up}, {"tp": down}]
     for peer in peers:
         pl.semaphore_signal(barrier, inc=1, device_id=peer, device_id_type=MESH)
     pl.semaphore_wait(barrier, len(peers))
-    for copy in local:
-        copy.wait()
+
+    def far(part):
+        return (part + 1) // 2
 
     def lane(part):
-        return lax.rem(z + lanes - part, lanes)
-
-    def lane_copy(hop):
+        if part == 0:
+            return z
+        return z - far(part) if part % 2 else z + far(part)
+
+    def exists(part):
+        return z >= far(part) if part % 2 else z + far(part) < lanes
+
+    def lane_copy(part):
+        block = whole.at[me, lane(part - 2) if part > 2 else z]
         return pltpu.make_async_remote_copy(
-            src_ref=w_ref,
-            dst_ref=whole.at[me, z],
-            send_sem=z_send.at[hop - 1],
-            recv_sem=z_recv.at[hop - 1],
-            device_id={"tp": lax.rem(z + hop, lanes)},
+            src_ref=block if part > 2 else w_ref,
+            dst_ref=block,
+            send_sem=z_send.at[part - 1],
+            recv_sem=z_recv.at[part - 1],
+            device_id={"tp": up if part % 2 else down},
             device_id_type=MESH,
         )
+
+    def lane_sends(part):
+        if part % 2:
+            return (z >= far(part) - 1) & (z + 1 < lanes)
+        return (z + far(part) - 1 < lanes) & (z > 0)
 
     def token_copy(hop):
         return pltpu.make_async_remote_copy(
@@ -568,17 +759,17 @@
             dst_ref=before.at[hop - 1],
             send_sem=x_send.at[hop - 1],
             recv_sem=x_recv.at[hop - 1],
-            device_id={"tp": lax.rem(z + 1, lanes)},
+            device_id={"tp": up},
             device_id_type=MESH,
         )
 
-    def unit_copy(other):
+    def unit_copy(other, kind):
         peer = flip(me, other)
         return pltpu.make_async_remote_copy(
-            src_ref=m_ref.at[peer],
-            dst_ref=mine.at[:, :, part_of(me)],
-            send_sem=m_send.at[other - 1],
-            recv_sem=m_recv.at[other - 1],
+            src_ref=m_ref.at[peer, kind],
+            dst_ref=mine[kind].at[:, part_of(me)],
+            send_sem=m_send.at[other - 1, kind],
+            recv_sem=m_recv.at[other - 1, kind],
             device_id={"fsdp": peer},
             device_id_type=MESH,
         )
@@ -593,57 +784,62 @@
             device_id_type=MESH,
         )
 
-    def send_tokens(hop):
-        @pl.when((z >= hop - 1) & (z + 1 < lanes))
-        def _():
-            token_copy(hop).start()
-
-    def take_tokens(hop):
-        @pl.when(z >= hop)
-        def _():
-            token_copy(hop).wait_recv()
-
-    gather = Gather(size, me, whole, sems, lanes, lane)
+    def when(condition, run):
+        pl.when(condition)(run)
+
+    gather = Gather(size, me, whole, sems, 2 * lanes - 1, lane, far, w_ref)
+    for part in (1, 2):
+        when(lane_sends(part), lambda: lane_copy(part).start())
     gather.forward(0, 0)
-    for hop in range(1, lanes):
-        lane_copy(hop).start()
-    send_tokens(1)
+    when(z + 1 < lanes, lambda: token_copy(1).start())
     for other in range(1, size):
         count_copy(other).start()
-    events = [(part, pattern) for part in range(lanes) for pattern in gather.patterns]
-    events.sort(key=lambda event: (2 * event[0] + top(event[1]) + 1, event))
-    for part, pattern in events:
-        if (part, pattern) != (0, 0):
-            if pattern:
-                gather.arrive(part, pattern)
-            else:
-                lane_copy(part).wait_recv()
-            gather.forward(part, pattern)
-        if (part, pattern) == (lanes - 1, 0):
+        for kind in range(3):
+            unit_copy(other, kind).start()
+    events = [(part, pattern) for part in range(2 * lanes - 1) for pattern in gather.patterns]
+    wave = lambda pattern: 3.5 * top(pattern) + 2.5 if pattern else 0
+    events.sort(key=lambda event: (2 * far(event[0]) + wave(event[1]), event))
+
+    def run_event(part, pattern):
+        if pattern:
+            gather.arrive(part, pattern)
+        elif part:
+            lane_copy(part).wait_recv()
+            if part + 2 < 2 * lanes - 1:
+                when(lane_sends(part + 2), lambda: lane_copy(part + 2).start())
+        gather.forward(part, pattern)
+
+    for part, pattern in events[1:]:
+        if part == 0:
+            run_event(part, pattern)
+        else:
+            when(exists(part), lambda: run_event(part, pattern))
+        if (part, pattern) == (2 * lanes - 2, 0):
             for hop in range(1, back):
-                take_tokens(hop)
-                send_tokens(hop + 1)
+                when(z >= hop, lambda: token_copy(hop).wait_recv())
+                when((z >= hop) & (z + 1 < lanes), lambda: token_copy(hop + 1).start())
     for other in range(1, size):
-        unit_copy(other).start()
+        count_copy(other).wait()
+    count[...] = sum(counts[other] for other in range(size))
+
+    def close(part):
+        for pattern in gather.patterns:
+            gather.core_copy(part, pattern).wait()
+            for step in range(top(pattern) + 1, gather.steps):
+                gather.chip_copy(part, step, pattern).wait_send()
+
+    close(0)
+    for part in range(1, 2 * lanes - 1):
+        when(exists(part), lambda: close(part))
+        when(lane_sends(part), lambda: lane_copy(part).wait_send())
     for other in range(1, size):
-        count_copy(other).wait_recv()
-    count[...] = sum(counts[other] for other in range(size))
-    for part, pattern in events:
-        gather.core_copy(part, pattern).wait_recv()
-    for other in range(1, size):
-        unit_copy(other).wait_recv()
-    take_tokens(back)
-    gather.finish()
-    for hop in range(1, lanes):
-        lane_copy(hop).wait_send()
-    for other in range(1, size):
-        unit_copy(other).wait_send()
-        count_copy(other).wait_send()
+        for kind in range(3):
+            unit_copy(other, kind).wait()
     for hop in range(1, back + 1):
-
-        @pl.when((z >= hop - 1) & (z + 1 < lanes))
-        def _():
-            token_copy(hop).wait_send()
+        when((z >= hop - 1) & (z + 1 < lanes), lambda: token_copy(hop).wait_send())
+    when(z >= back, lambda: token_copy(back).wait_recv())
+    for copy in local:
+        copy.wait()
 
 
 def enter(size, lanes, back, values, weights, units, count):
@@ -651,30 +847,34 @@
     vmem = pl.BlockSpec(memory_space=pltpu.VMEM)
     _, kinds, rows, columns = units.shape
     others = pltpu.SemaphoreType.DMA((size - 1,))
-    lane = pltpu.SemaphoreType.DMA((lanes - 1,))
+    other_kinds = pltpu.SemaphoreType.DMA((size - 1, kinds))
+    line = pltpu.SemaphoreType.DMA((2 * lanes - 2,))
     hop = pltpu.SemaphoreType.DMA((back,))
+    mine = jax.ShapeDtypeStruct((rows, size * columns), units.dtype)
     return pl.pallas_call(
         functools.partial(enter_kernel, size, lanes, back),
         out_shape=(
             jax.ShapeDtypeStruct((back, *values.shape), values.dtype),
             jax.ShapeDtypeStruct((size, lanes, *weights.shape), weights.dtype),
-            jax.ShapeDtypeStruct((kinds, rows, size * columns), units.dtype),
+            mine,
+            mine,
+            mine,
             jax.ShapeDtypeStruct(count.shape, count.dtype),
         ),
         in_specs=[any_space, any_space, any_space, vmem],
-        out_specs=(any_space, any_space, any_space, vmem),
+        out_specs=(any_space,) * 5 + (vmem,),
         scratch_shapes=[
             pltpu.VMEM((size, *count.shape), count.dtype),
-            pltpu.SemaphoreType.DMA((2,)),
-            lane,
-            lane,
+            pltpu.SemaphoreType.DMA((kinds + 1,)),
+            line,
+            line,
             hop,
             hop,
+            other_kinds,
+            other_kinds,
             others,
             others,
-            others,
-            others,
-            *gather_semaphores(size, lanes),
+            *gather_semaphores(size, 2 * lanes - 1),
         ],
         compiler_params=pltpu.CompilerParams(collective_id=5, has_side_effects=True),
         cost_estimate=pl.CostEstimate(flops=0, bytes_accessed=400 * 1024 * 1024, transcendentals=0),
@@ -698,11 +898,11 @@
         for part in range(PARTS)
     ]
     part_of = lambda device: pl.ds(pl.multiple_of(device * span, span), span)
-    copies += [
+    stay = [
         pltpu.make_async_copy(unit.at[:, part_of(me)], back.at[me, kind], u_own.at[kind])
         for kind, unit in enumerate(units)
     ]
-    for copy in copies:
+    for copy in copies + stay:
         copy.start()
     barrier = pltpu.get_barrier_semaphore()
     for other in range(1, size):
@@ -739,6 +939,8 @@
         for kind in range(3):
             unit_copy(other, kind).wait()
     finish()
+    for copy in stay:
+        copy.wait()
 
 
 def sum_query(size, left, right, units):
@@ -1454,12 +1656,12 @@
         part.reshape(n_fsdp, -1, part.shape[1]) for part in (w_gate.T, w_up.T, w_down)
     ]
     live_here = jnp.full((8, 128), jnp.sum(padding).astype(jnp.float32))
-    before, weights_attn, mine, counts = enter(
+    before, weights_attn, *mine, counts = enter(
         n_fsdp, n_tp, back, states, joined, jnp.stack(units, axis=1), live_here
     )
     count = counts[0, 0]
     rows_gate, rows_up, rows_down = [
-        lax.all_gather(mine[i], "tp", axis=0, tiled=True) for i in range(3)
+        lax.all_gather(part, "tp", axis=0, tiled=True) for part in mine
     ]
     normed_in, query_raw, key_raw, value = project(
         before, states, norm_attn, weights_attn, wq, wk
@@ -1477,15 +1679,9 @@
     squares = jnp.sum(errors * errors)
     grad_out = errors * (2.0 / (count * D))
 
-    grad_whole, grad_gate, grad_up = grad_hidden_units(
-        n_fsdp, grad_out.astype(jnp.bfloat16), rows_down, gate, up
+    grad_gate, grad_up, by_unit = grad_hidden_units(
+        n_fsdp, grad_out.astype(jnp.bfloat16), rows_down, gate, up, product, whole_two
     )
-    by_unit = (
-        contract_first(product, grad_whole).astype(jnp.bfloat16),
-        contract_first(grad_gate, whole_two).astype(jnp.bfloat16),
-        contract_first(grad_up, whole_two).astype(jnp.bfloat16),
-    )
-    by_unit, (grad_gate, grad_up) = lax.optimization_barrier((by_unit, (grad_gate, grad_up)))
     grad_mid = sum_products(n_fsdp, 4, (grad_gate, grad_up), (rows_gate, rows_up))
     by_unit = [lax.psum_scatter(part, "tp", scatter_dimension=0, tiled=True) for part in by_unit]
     grad_norm_mlp = jnp.sum(grad_mid * normed_two, axis=0)
@@ -1509,11 +1705,16 @@
         n_fsdp,
         n_tp,
     )
+    by_unit, sums_out = lax.optimization_barrier((by_unit, sums_out))
     sums_query, units_back = sum_query(n_fsdp, normed_in, grad_query, by_unit)
+    sums_query, grad_pair = lax.optimization_barrier((sums_query, grad_pair))
     sums_pair, grad_low = sum_key(n_fsdp, normed_in, grad_query, grad_pair, weights_attn)
     grad_w_out, grad_w_query = [
         over_lanes(join_parts(sums)[None])[0] for sums in (sums_out, sums_query)
     ]
+    sums_pair, grad_w_query, grad_w_out = lax.optimization_barrier(
+        (sums_pair, grad_w_query, grad_w_out)
+    )
     grad_w_pair = over_lanes(sums_pair)
     grad_w_down, grad_w_gate, grad_w_up = [
         units_back[:, kind].reshape(-1, units_back.shape[3]).astype(jnp.float32)

time: 1310 us -> 1060 us (0.81)
  waiting for transfers between devices: 217 us -> 45.9 us
  matrix products: 60.5 us -> 0 us
  Pallas kernels: 924 us -> 905 us
    reduce_scatter x3, waiting for transfers between devices: 174 us -> 0.06 us  [shards(): lax.psum_scatter(part, 'tp', scatter_dimension=0, tiled=True)]
    dot_general x3 -> x0, matrix products: 60.5 us -> none  [contract_first(): lax.dot_general(left, right, (((0,), (0,)), ((), ())), preferred_element_...]
    pallas_call x1, Pallas kernels: 199 us -> 142 us  [enter(): pl.pallas_call(functools.partial(enter_kernel, size, lanes, back), out_sh...]
    pallas_call x1, Pallas kernels: 116 us -> 160 us  [attend_back(): pl.pallas_call(functools.partial(attend_back_kernel, group, step, lead, s...]
    pallas_call x1, Pallas kernels: 85.6 us -> 112 us  [grad_hidden_units(): pl.pallas_call(functools.partial(grad_hidden_kernel, size), out_shape=(sh...]
    pallas_call x2, Pallas kernels: 187 us -> 171 us  [sum_products(): pl.pallas_call(functools.partial(sum_products_kernel, size, terms), out_s...]
    all_gather x3, waiting for transfers between devices: 20.8 us -> 34 us  [shards(): lax.all_gather(part, 'tp', axis=0, tiled=True)]
  transfers between devices with their start and end apart: 9 -> 9, of which waited for: 5 -> 3; matrix products, arithmetic and copies ran while one was open for 3% -> 5% of each run, Pallas kernels for 19% -> 48%
where the time goes in v4:
time: 1060 us; the launch traced here: 1050 us
  Pallas kernels  905 us (85%)
  other arithmetic  61.7 us (6%)
  waiting for transfers between devices  45.9 us (4%)
  local copies, waits for them, and re-layouts  20.6 us (2%)
  between operations  17.7 us (2%)
    pallas_call x2, Pallas kernels, sum_products(): pl.pallas_call(functools.partial(sum_products_kernel, size, terms), out_s...  171 us
    pallas_call x1, Pallas kernels, attend_back(): pl.pallas_call(functools.partial(attend_back_kernel, group, step, lead, s...  160 us
    pallas_call x1, Pallas kernels, enter(): pl.pallas_call(functools.partial(enter_kernel, size, lanes, back), out_sh...  142 us
    pallas_call x1, Pallas kernels, grad_hidden_units(): pl.pallas_call(functools.partial(grad_hidden_kernel, size), out_shape=(sh...  112 us
    pallas_call x1, Pallas kernels, gate_up(): pl.pallas_call(functools.partial(gate_up_kernel, size), out_shape=(shape(...  83.5 us
    pallas_call x1, Pallas kernels, sum_query(): pl.pallas_call(functools.partial(sum_query_kernel, size), out_shape=(jax....  69.8 us
    pallas_call x1, Pallas kernels, attend(): pl.pallas_call(functools.partial(attend_kernel, group, step, rows - own),...  49.8 us
    pallas_call x1, Pallas kernels, sum_key(): pl.pallas_call(functools.partial(sum_key_kernel, size), out_shape=(jax.Sh...  46.6 us
  transfers between devices with their start and end apart: 9, of which 3 were waited for; matrix products, arithmetic and copies ran while one was open for 5% of the time, Pallas kernels for 48%

profile of v4, /device:TPU:0, one launch (start us, length us, event | category | flops | bytes accessed | tf_op | source)
XLA Modules:
  0.0 1051.7 jit_solution(3693840264313036019)
XLA Ops:
  16.5 141.5 %enter.1 = (bf16[2,512,2048]{2,1,0:T(8,128)(2,1)}, bf16[8,4,256,1536]{3,2,1,0:T(8,128)(2,1)}, bf16[192,2048]{1,0:T(8,128)(2,1)}, bf16[192,2048]{1,0:T(8,128)(2,1...) custom-call(bf16[512,2048]{1,0:T(8,128)(2,1)} %x_ref.5, bf16[256,1536]{1,0:T(8,128)(2,1)} %pad_maximum_fusion.3.w_ref, ...), custom_call_target="tpu_custom_call" | custom-call | bytes 419430400 | tf_op jit(solution)/shard_map/enter/pallas_call | solution.py:854
  163.3 2.8 fusion.16
  166.1 32.4 %project_in.1 = (bf16[512,2048]{1,0:T(8,128)(2,1)}, f32[512,2048]{1,0:T(8,128)}, f32[1536,1024]{1,0:T(8,128)}, bf16[1536,1024]{1,0:T(8,128)(2,1)}) custom-call(bf16[2,512,2048]{2,1,0:T(8,128)(2,1)} %get-tuple-element.51.before_ref, bf16[512,2048]{1,0:T(8,128)(2,1)} %x_ref.5, f32[1,2048]{1,0:T(1,128)} %bitcast.81, ...), custom_call_target="tpu_custom_call" | custom-call | flops 17179869184 | bytes 23068672 | tf_op jit(solution)/shard_map/project_in/pallas_call | solution.py:1168
  200.1 49.8 %attend.1.a_ref.right_ref = bf16[512,2048]{1,0:T(8,128)(2,1)} custom-call(f32[512,2048]{1,0:T(8,128)} %get-tuple-element.53.q_ref, f32[1536,1024]{1,0:T(8,128)} %get-tuple-element.54.k_ref, bf16[1536,1024]{1,0:T(8,128)(2,1)} %get-tuple-element.55.v_ref, f32[512,1280]{1,0:T(8,128)} %add_select_fusion.bias_ref, f32[1536,128]{1,0:T(8,128)} %get-tuple-element.156.cos_ref, ...), custom_call_target="tpu_custom_call" | custom-call | flops 21474836480 | bytes 13631488 | tf_op jit(solution)/shard_map/attend/pallas_call | solution.py:1501
  251.9 11.4 %project_out.1 = f32[512,2048]{1,0:T(8,128)} custom-call(bf16[512,2048]{1,0:T(8,128)(2,1)} %attend.1.a_ref.right_ref, bf16[8,4,256,1536]{3,2,1,0:T(8,128)(2,1)} %get-tuple-element.52.w_ref, bf16[512,2048]{1,0:T(8,128)(2,1)} %x_ref.5), custom_call_target="tpu_custom_call" | custom-call | flops 4294967296 | bytes 25165824 | tf_op jit(solution)/shard_map/project_out/pallas_call | solution.py:1212
  268.5 34.0 %all-gather.6.cloned.1.call-done.wu_in.refs_3_ = bf16[768,2048]{1,0:T(8,128)(2,1)} async-done(((bf16[192,2048]{1,0:T(8,128)(2,1)}), bf16[768,2048]{1,0:T(8,128)(2,1)}) %all-gather.6.cloned.1.call-update) | async-done | bytes 3145744 | tf_op jit(solution)/shard_map/all_gather | solution.py:1664
  302.5 83.5 %gate_up.1 = (bf16[8,2,256,2048]{3,2,1,0:T(8,128)(2,1)}, f32[8,2,256,768]{3,2,1,0:T(8,128)}, f32[8,2,256,768]{3,2,1,0:T(8,128)}, bf16[8,2,256,768]{3,2,1,0:T(8,128)(2,1)}) custom-call(bf16[2,256,2048]{2,1,0:T(8,128)(2,1)} %bitcast.69, bf16[768,2048]{1,0:T(8,128)(2,1)} %all-gather.4.cloned.1.call-done.wg_in.refs_2_, ...), custom_call_target="tpu_custom_call" | custom-call | flops 25769803776 | bytes 209715200 | tf_op jit(solution)/shard_map/gate_up/pallas_call | solution.py:387
  386.1 81.3 %sum_products.2 = f32[2,256,2048]{2,1,0:T(8,128)} custom-call(bf16[8,2,256,768]{3,2,1,0:T(8,128)(2,1)} %get-tuple-element.58.refs_0_.prod_in, bf16[768,2048]{1,0:T(8,128)(2,1)} %all-gather.8.cloned.1.call-done.refs_1_.wd_in), custom_call_target="tpu_custom_call" | custom-call | flops 12884901888 | bytes 209715200 | tf_op jit(solution)/shard_map/sum_products/pallas_call | solution.py:661
  467.4 4.4 multiply_reduce_fusion
  474.4 112.5 %grad_hidden_units.1 = (bf16[8,2,256,768]{3,2,1,0:T(8,128)(2,1)}, bf16[8,2,256,768]{3,2,1,0:T(8,128)(2,1)}, bf16[768,2048]{1,0:T(8,128)(2,1)}, bf16[768,2048]{1,0:T(8,128)(2,1)}, bf16[768,2048]{1,0:T(8,128)(2,1)}) custom-call(bf16[2,256,2048]{2,1,0:T(8,128)(2,1)} %bitcast.70, bf16[768,2048]{1,0:T(8,128)(2,1)} %all-gather.8.cloned.1.call-done.refs_1_.wd_in, ...), custom_call_target="tpu_custom_call" | custom-call | flops 51539607552 | bytes 209715200 | tf_op jit(solution)/shard_map/grad_hidden_units/pallas_call | solution.py:568
  589.0 89.5 %sum_products.3 = f32[2,256,2048]{2,1,0:T(8,128)} custom-call(bf16[8,2,256,768]{3,2,1,0:T(8,128)(2,1)} %get-tuple-element.65.refs_0_, bf16[8,2,256,768]{3,2,1,0:T(8,128)(2,1)} %get-tuple-element.66.refs_1_, bf16[768,2048]{1,0:T(8,128)(2,1)} %all-gather.4.cloned.1.call-done.wg_in.refs_2_, bf16[768,2048]{1,0:T(8,128)(2,1)} %all-gather.6.cloned.1.call-done.wu_in.refs_3_), custom_call_target="tpu_custom_call" | custom-call | flops 25769803776 | bytes 209715200 | tf_op jit(solution)/shard_map/sum_products/pallas_call | solution.py:661
  678.5 3.2 fusion.9
  681.8 8.8 fusion.22
  690.6 8.8 back_out.1.do_ref
  699.4 159.5 %attend_back.1 = (bf16[512,2048]{1,0:T(8,128)(2,1)}, bf16[2,512,1024]{2,1,0:T(8,128)(2,1)}, f32[1,128]{1,0:T(1,128)}, f32[1,128]{1,0:T(1,128)}, f32[2,256,1024]{2,1,0:T(8,128)}) custom-call(f32[512,2048]{1,0:T(8,128)} %get-tuple-element.53.q_ref, f32[1536,1024]{1,0:T(8,128)} %get-tuple-element.54.k_ref, bf16[1536,1024]{1,0:T(8,128)(2,1)} %get-tuple-element.55.v_ref, ...), custom_call_target="tpu_custom_call" | custom-call | flops 53687091200 | bytes 33554432 | tf_op jit(solution)/shard_map/attend_back/pallas_call | solution.py:1545
  859.0 69.8 %sum_query.1 = (f32[2,256,1024]{2,1,0:T(8,128)}, bf16[8,3,192,256]{3,2,1,0:T(8,128)(2,1)}) custom-call(bf16[512,2048]{1,0:T(8,128)(2,1)} %get-tuple-element.60.left_ref, bf16[512,2048]{1,0:T(8,128)(2,1)} %get-tuple-element.67.right_ref.q_ref, bf16[192,2048]{1,0:T(8,128)(2,1)} %reduce-scatter.7.cloned.1.call-done.refs_0_, ...), custom_call_target="tpu_custom_call" | custom-call | flops 4294967296 | bytes 104857600 | tf_op jit(solution)/shard_map/sum_query/pallas_call | solution.py:952
  933.6 46.6 %sum_key.1 = (f32[2,256,1024]{2,1,0:T(8,128)}, f32[512,2048]{1,0:T(8,128)}) custom-call(bf16[512,2048]{1,0:T(8,128)(2,1)} %get-tuple-element.60.left_ref, bf16[512,2048]{1,0:T(8,128)(2,1)} %get-tuple-element.67.right_ref.q_ref, bf16[2,512,1024]{2,1,0:T(8,128)(2,1)} %get-tuple-element.77.kv_ref, bf16[8,4,256,1536]{3,2,1,0:T(8,128)(2,1)} %get-tuple-element.52.w_ref), custom_call_target="tpu_custom_call" | custom-call | flops 8589934592 | bytes 104857600 | tf_op jit(solution)/shard_map/sum_key/pallas_call | solution.py:1049
  980.3 3.3 fusion.4
  986.3 18.5 %sum_small.1 = f32[40,128]{1,0:T(8,128)} custom-call(f32[40,128]{1,0:T(8,128)} %pad.5.x_ref), custom_call_target="tpu_custom_call" | custom-call | tf_op jit(solution)/shard_map/sum_small/pallas_call | solution.py:1107
  1013.2 2.7 convert_element_type.90
  1017.2 3.0 copy.38
  1020.2 3.1 copy.39
  1025.7 6.7 fusion.7
  1033.4 8.6 reduce-scatter.17.cloned.1.call-done
  (115 shorter events, 48.2 us)
Async XLA Ops:
  7.2 6.1 copy-start.6
  7.2 7.8 copy-start.9
  7.2 7.7 copy-start.10
  7.2 7.7 copy-start.7
  7.2 261.3 %all-gather.4.cloned.1.call-start = ((), (), s32[]{:S(2)}) async-start(), calls=%async_computation.6 | async-start | bytes 3932160 | tf_op jit(solution)/shard_map/all_gather | solution.py:1664
  15.9 143.7 %copy-start.14 = (s32[1,4]{1,0:T(1,128)S(1)}, s32[1,4]{1,0:T(1,128)}, u32[]{:S(2)}) copy-start(s32[1,4]{1,0:T(1,128)} %param.16) | copy-start | bytes 52
  15.9 144.1 %copy-start.12 = (s32[1,2048]{1,0:T(1,128)S(1)}, s32[1,2048]{1,0:T(1,128)}, u32[]{:S(2)}) copy-start(s32[1,2048]{1,0:T(1,128)} %param.17) | copy-start | bytes 24580
  158.0 144.4 %all-gather.6.cloned.1.call-start = ((), (), s32[]{:S(2)}) async-start(), calls=%async_computation.7 | async-start | bytes 3932160 | tf_op jit(solution)/shard_map/all_gather | solution.py:1664
  158.8 227.3 %all-gather.8.cloned.1.call-start = ((), (), s32[]{:S(2)}) async-start(), calls=%async_computation.8 | async-start | bytes 3932160 | tf_op jit(solution)/shard_map/all_gather | solution.py:1664
  159.5 699.4 %reduce-scatter.7.cloned.1.call-start = ((), (), s32[]{:S(2)}) async-start(), calls=%async_computation.9 | async-start | bytes 3932160 | tf_op jit(solution)/shard_map/reduce_scatter | solution.py:1686
  251.9 14.1 %copy-start.11 = (f32[2048]{0:T(1024)S(1)}, f32[2048]{0:T(1024)}, u32[]{:S(2)}) copy-start(f32[2048]{0:T(1024)} %param.26) | copy-start | bytes 24580
  263.3 3.5 copy-start
  386.1 81.3 %copy-start.1 = (f32[512,2048]{1,0:T(8,128)S(1)}, f32[512,2048]{1,0:T(8,128)}, u32[]{:S(2)}) copy-start(f32[512,2048]{1,0:T(8,128)} %project_out.1) | copy-start | bytes 12582916
  386.1 81.3 %copy-start.5 = (bf16[512,2048]{1,0:T(8,128)(2,1)S(1)}, bf16[512,2048]{1,0:T(8,128)(2,1)}, u32[]{:S(2)}) copy-start(bf16[512,2048]{1,0:T(8,128)(2,1)} %param.18) | copy-start | bytes 6291460
  471.8 2.6 copy-start.4
  586.9 1.6 copy-start.3
  586.9 272.1 %reduce-scatter.9.cloned.1.call-start = ((), (), s32[]{:S(2)}) async-start(), calls=%async_computation.10 | async-start | bytes 3932160 | tf_op jit(solution)/shard_map/reduce_scatter | solution.py:1686
  587.5 271.5 %reduce-scatter.11.cloned.1.call-start = ((), (), s32[]{:S(2)}) async-start(), calls=%async_computation.11 | async-start | bytes 3932160 | tf_op jit(solution)/shard_map/reduce_scatter | solution.py:1686
  589.0 89.5 %copy-start.2 = (f32[512,2048]{1,0:T(8,128)S(1)}, f32[512,2048]{1,0:T(8,128)}, u32[]{:S(2)}) copy-start(f32[512,2048]{1,0:T(8,128)} %project_out.1) | copy-start | bytes 12582916
  681.8 327.4 %reduce-scatter.13.cloned.1.call-start = ((), (), s32[]{:S(2)}) async-start(), calls=%async_computation.12 | async-start | bytes 1310720 | tf_op jit(solution)/shard_map/reduce_scatter | solution.py:1616
  931.8 80.4 %reduce-scatter.15.cloned.1.call-start = ((), (), s32[]{:S(2)}) async-start(), calls=%async_computation.13 | async-start | bytes 1310720 | tf_op jit(solution)/shard_map/reduce_scatter | solution.py:1616
  933.6 46.7 %copy-start.13 = (f32[2048]{0:T(1024)S(1)}, f32[2048]{0:T(1024)}, u32[]{:S(2)}) copy-start(f32[2048]{0:T(1024)} %param.19) | copy-start | bytes 24580
  984.8 57.2 %reduce-scatter.17.cloned.1.call-start = ((), (), s32[]{:S(2)}) async-start(), calls=%async_computation.14 | async-start | bytes 1310720 | tf_op jit(solution)/shard_map/reduce_scatter | solution.py:1616
  1007.9 8.1 copy-start.8
  (2 other events, 2.9 us)
Sparse Core Ops, SparseCore 0:
  158.2 80.5 all-gather.3
  240.3 62.1 all-gather.5
  304.1 62.1 all-gather.7
  587.1 58.3 reduce-scatter.6
  647.6 60.2 reduce-scatter.8
  710.1 105.6 reduce-scatter.10
  931.9 26.4 reduce-scatter.12
  984.9 27.2 reduce-scatter.14
  1016.1 25.7 reduce-scatter.16

commit v5 on v4

--- a/solution.py
+++ b/solution.py
@@ -90,6 +90,16 @@
 
 def pick(part, pair):
     return pair[0] + part * (pair[1] - pair[0])
+
+
+def unit_loads(source, kind, target, sems):
+    lanes, _, rows, _ = source.shape
+    return [
+        pltpu.make_async_copy(
+            source.at[lane, kind], target.at[pl.ds(lane * rows, rows)], sems.at[lane]
+        )
+        for lane in range(lanes)
+    ]
 
 
 class Gather:
@@ -296,8 +306,7 @@
 def gate_up_kernel(
     size,
     x_ref,
-    wg_in,
-    wu_in,
+    w_in,
     x_out,
     gate_out,
     up_out,
@@ -316,12 +325,10 @@
     me = lax.axis_index("fsdp")
     hidden = wg_ref.shape[0]
     chunk = 256 if hidden % 256 == 0 else 128
-    loads = [
-        pltpu.make_async_copy(source, target, load.at[i])
-        for i, (source, target) in enumerate(
-            ((x_ref, whole.at[me]), (wg_in, wg_ref), (wu_in, wu_ref))
-        )
-    ]
+    lanes = w_in.shape[0]
+    loads = [pltpu.make_async_copy(x_ref, whole.at[me], load.at[0])]
+    loads += unit_loads(w_in, 0, wg_ref, load.at[pl.ds(1, lanes)])
+    loads += unit_loads(w_in, 1, wu_ref, load.at[pl.ds(1 + lanes, lanes)])
     for copy in loads:
         copy.start()
     greet(me, size)
@@ -379,9 +386,10 @@
             ).wait()
 
 
-def gate_up(size, values, rows_gate, rows_up):
+def gate_up(size, values, units):
     own, width = values.shape
-    rows, hidden = (own // PARTS, rows_gate.shape[0])
+    lanes, _, each, _ = units.shape
+    rows, hidden = (own // PARTS, lanes * each)
     any_space = pl.BlockSpec(memory_space=pl.ANY)
     shape = lambda columns, kind: jax.ShapeDtypeStruct((size, PARTS, rows, columns), kind)
     outs = pl.pallas_call(
@@ -392,7 +400,7 @@
             shape(hidden, jnp.float32),
             shape(hidden, jnp.bfloat16),
         ),
-        in_specs=[any_space] * 3,
+        in_specs=[any_space] * 2,
         out_specs=(any_space,) * 4,
         scratch_shapes=[
             pltpu.VMEM((size, PARTS, rows, width), jnp.bfloat16),
@@ -401,7 +409,7 @@
             pltpu.VMEM((PARTS, rows, hidden), jnp.float32),
             pltpu.VMEM((PARTS, rows, hidden), jnp.float32),
             pltpu.VMEM((PARTS, rows, hidden), jnp.bfloat16),
-            pltpu.SemaphoreType.DMA((3,)),
+            pltpu.SemaphoreType.DMA((1 + 2 * lanes,)),
             pltpu.SemaphoreType.DMA((PARTS, size)),
             pltpu.SemaphoreType.DMA((PARTS, 3)),
             *gather_semaphores(size),
@@ -413,7 +421,7 @@
             flops=4 * size * own * width * hidden, bytes_accessed=200 * 1024 * 1024, transcendentals=0
         ),
         name="gate_up",
-    )(values.reshape(PARTS, rows, width), rows_gate, rows_up)
+    )(values.reshape(PARTS, rows, width), units)
     return tuple(out.reshape(size * own, -1) for out in outs)
 
 
@@ -427,16 +435,14 @@
     two_in,
     dgate_out,
     dup_out,
-    dwd_out,
-    dwg_out,
-    dwu_out,
+    early_out,
+    late_out,
     whole,
     wd_ref,
     gate,
     up,
     prod,
     two,
-    dprod,
     dgate,
     dup,
     sums,
@@ -448,12 +454,10 @@
 ):
     me = lax.axis_index("fsdp")
     hidden, width = wd_ref.shape
-    rows = dprod.shape[0]
+    lanes, _, each, _ = wd_in.shape
     chunk = 256 if hidden % 256 == 0 else 128
-    loads = [
-        pltpu.make_async_copy(x_ref, whole.at[me], load.at[0]),
-        pltpu.make_async_copy(wd_in, wd_ref, load.at[1]),
-    ]
+    loads = [pltpu.make_async_copy(x_ref, whole.at[me], load.at[0])]
+    loads += unit_loads(wd_in, 0, wd_ref, load.at[pl.ds(1, lanes)])
     for copy in loads:
         copy.start()
 
@@ -463,144 +467,152 @@
             for i, (buffer, out) in enumerate(((dgate, dgate_out), (dup, dup_out)))
         ]
 
-    def fetches(part, at):
-        pairs = ((gate_in, gate), (up_in, up), (prod_in, prod), (two_in, two))
-        return [
-            pltpu.make_async_copy(source.at[at, part], buffer.at[part], fetch.at[part, i])
-            for i, (source, buffer) in enumerate(pairs)
-        ]
+    def fetches(count, kinds):
+        copies = []
+        for part in range(PARTS):
+            at = order[count][part]
+            pairs = (
+                (gate_in, gate.at[part]),
+                (up_in, up.at[part]),
+                (prod_in, prod.at[count % 2, part]),
+                (two_in, two.at[count % 2, part]),
+            )
+            copies += [
+                pltpu.make_async_copy(pairs[i][0].at[at, part], pairs[i][1], fetch.at[count % 2, part, i])
+                for i in kinds
+            ]
+        return copies
 
     gather = Gather(size, me, whole, sems)
     order = []
     for pattern in gather.patterns:
         for sibling in (0, 1):
             order.append([gather.slot(part, pattern, sibling) for part in range(PARTS)])
-    for copy in fetches(0, order[0][0]):
+    for copy in fetches(0, (0, 1, 2, 3)):
         copy.start()
-    sums[...] = jnp.zeros_like(sums)
     greet(me, size)
     loads[0].wait()
     state = {"count": 0}
 
     def work(pair):
         count = state["count"]
-        last = order[count - 1] if count else None
-        following = order[count + 1] if count + 1 < len(order) else None
         state["count"] = count + 1
+        more = count + 1 < len(order)
         if count == 0:
-            loads[1].wait()
+            for copy in loads[1:]:
+                copy.wait()
+        if more:
+            for copy in fetches(count + 1, (2, 3)):
+                copy.start()
+        for copy in fetches(count, (0, 1)):
+            copy.wait()
+        if count:
+            for part in range(PARTS):
+                for copy in stores(part, order[count - 1][part]):
+                    copy.wait()
 
         @pl.loop(0, PARTS)
         def _(part):
             at = pick(part, pair)
 
-            @pl.when(part == 0)
-            def _():
-                for copy in fetches(1, pair[1]):
-                    copy.start()
-
-            if following is not None:
-
-                @pl.when(part == 1)
-                def _():
-                    for copy in fetches(0, following[0]):
-                        copy.start()
-
             @pl.loop(0, hidden // chunk)
             def _(index):
                 units = pl.ds(pl.multiple_of(index * chunk, chunk), chunk)
-                dprod[:, units] = contract_last(whole[at, part], wd_ref[units, :])
-
-            for copy in fetches(part, at):
-                copy.wait()
-            if last is not None:
-                for copy in stores(part, pick(part, last)):
-                    copy.wait()
-
-            @pl.loop(0, hidden // chunk)
-            def _(index):
-                units = pl.ds(pl.multiple_of(index * chunk, chunk), chunk)
-                gates, grads = (gate[part, :, units], dprod[:, units])
+                grads = contract_last(whole[at, part], wd_ref[units, :])
+                gates = gate[part, :, units]
                 sigmoid = jax.nn.sigmoid(gates)
                 dgate[part, :, units] = (
                     grads * up[part, :, units] * sigmoid * (1.0 + gates * (1.0 - sigmoid))
                 ).astype(jnp.bfloat16)
                 dup[part, :, units] = (grads * (gates * sigmoid)).astype(jnp.bfloat16)
 
-            for copy in stores(part, at):
+        for part in range(PARTS):
+            for copy in stores(part, pair[part]):
                 copy.start()
-
-            @pl.loop(0, hidden // chunk)
-            def _(index):
-                units = pl.ds(pl.multiple_of(index * chunk, chunk), chunk)
-                sums[0, units, :] += contract_first(prod[part, :, units], whole[at, part])
-                sums[1, units, :] += contract_first(dgate[part, :, units], two[part])
-                sums[2, units, :] += contract_first(dup[part, :, units], two[part])
+        if more:
+            for copy in fetches(count + 1, (0, 1)):
+                copy.start()
+        for copy in fetches(count, (2, 3)):
+            copy.wait()
+
+        @pl.loop(0, hidden // chunk)
+        def _(index):
+            units = pl.ds(pl.multiple_of(index * chunk, chunk), chunk)
+            here = count % 2
+            for kind, (lefts, rights) in enumerate(
+                (
+                    ((prod.at[here, 0], prod.at[here, 1]), (whole.at[pair[0], 0], whole.at[pair[1], 1])),
+                    ((dgate.at[0], dgate.at[1]), (two.at[here, 0], two.at[here, 1])),
+                    ((dup.at[0], dup.at[1]), (two.at[here, 0], two.at[here, 1])),
+                )
+            ):
+                total = contract_first(lefts[0][:, units], rights[0][...])
+                total += contract_first(lefts[1][:, units], rights[1][...])
+                if count:
+                    total += sums[kind, units, :]
+                sums[kind, units, :] = total
 
     gather.pairs(work)
     gather.finish()
     for part in range(PARTS):
         for copy in stores(part, order[-1][part]):
             copy.wait()
-    outs = (dwd_out, dwg_out, dwu_out)
-    pieces = hidden // rows
     copies = []
-    for piece in range(3 * pieces):
-        kind, first = (piece // pieces, piece % pieces * rows)
-        block = whole.at[piece // PARTS, piece % PARTS]
-        block[...] = sums[kind, first : first + rows, :].astype(jnp.bfloat16)
-        copy = pltpu.make_async_copy(
-            block, outs[kind].at[pl.ds(first, rows)], flush.at[piece]
-        )
+    for piece in range(3 * lanes):
+        kind, lane = (piece // lanes, piece % lanes)
+        block = whole.at[piece // PARTS, piece % PARTS, pl.ds(0, each)]
+        block[...] = sums[kind, lane * each : (lane + 1) * each, :].astype(jnp.bfloat16)
+        out = early_out.at[lane, kind] if kind < 2 else late_out.at[lane, 0]
+        copy = pltpu.make_async_copy(block, out, flush.at[piece])
         copy.start()
         copies.append(copy)
     for copy in copies:
         copy.wait()
 
 
-def grad_hidden_units(size, values, rows_down, gate, up, product, whole_two):
+def grad_hidden_units(size, values, units, gate, up, product, whole_two):
     own, width = values.shape
-    rows, hidden = (own // PARTS, rows_down.shape[0])
+    lanes, _, each, _ = units.shape
+    rows, hidden = (own // PARTS, lanes * each)
     any_space = pl.BlockSpec(memory_space=pl.ANY)
     shape = lambda columns, kind: jax.ShapeDtypeStruct((size, PARTS, rows, columns), kind)
     blocks = lambda array: array.reshape(size, PARTS, rows, -1)
-    weight = jax.ShapeDtypeStruct((hidden, width), jnp.bfloat16)
-    dgate, dup, *grads = pl.pallas_call(
+    weight = lambda kinds: jax.ShapeDtypeStruct((lanes, kinds, each, width), jnp.bfloat16)
+    dgate, dup, early, late = pl.pallas_call(
         functools.partial(grad_hidden_kernel, size),
-        out_shape=(shape(hidden, jnp.bfloat16), shape(hidden, jnp.bfloat16), weight, weight, weight),
+        out_shape=(shape(hidden, jnp.bfloat16), shape(hidden, jnp.bfloat16), weight(2), weight(1)),
         in_specs=[any_space] * 6,
-        out_specs=(any_space,) * 5,
+        out_specs=(any_space,) * 4,
         scratch_shapes=[
             pltpu.VMEM((size, PARTS, rows, width), jnp.bfloat16),
             pltpu.VMEM((hidden, width), jnp.bfloat16),
             pltpu.VMEM((PARTS, rows, hidden), jnp.float32),
             pltpu.VMEM((PARTS, rows, hidden), jnp.float32),
-            pltpu.VMEM((PARTS, rows, hidden), jnp.bfloat16),
-            pltpu.VMEM((PARTS, rows, width), jnp.bfloat16),
-            pltpu.VMEM((rows, hidden), jnp.float32),
+            pltpu.VMEM((2, PARTS, rows, hidden), jnp.bfloat16),
+            pltpu.VMEM((2, PARTS, rows, width), jnp.bfloat16),
             pltpu.VMEM((PARTS, rows, hidden), jnp.bfloat16),
             pltpu.VMEM((PARTS, rows, hidden), jnp.bfloat16),
             pltpu.VMEM((3, hidden, width), jnp.float32),
-            pltpu.SemaphoreType.DMA((2,)),
-            pltpu.SemaphoreType.DMA((PARTS, 4)),
+            pltpu.SemaphoreType.DMA((1 + lanes,)),
+            pltpu.SemaphoreType.DMA((2, PARTS, 4)),
             pltpu.SemaphoreType.DMA((PARTS, 2)),
-            pltpu.SemaphoreType.DMA((3 * (hidden // rows),)),
+            pltpu.SemaphoreType.DMA((3 * lanes,)),
             *gather_semaphores(size),
         ],
         compiler_params=pltpu.CompilerParams(
-            collective_id=3, has_side_effects=True, vmem_limit_bytes=VMEM
+            collective_id=3, has_side_effects=True, vmem_limit_bytes=60 * 1024 * 1024
         ),
         cost_estimate=pl.CostEstimate(
             flops=8 * size * own * width * hidden, bytes_accessed=200 * 1024 * 1024, transcendentals=0
         ),
         name="grad_hidden_units",
-    )(values.reshape(PARTS, rows, width), rows_down, *map(blocks, (gate, up, product, whole_two)))
-    return (dgate.reshape(size * own, hidden), dup.reshape(size * own, hidden), grads)
+    )(values.reshape(PARTS, rows, width), units, *map(blocks, (gate, up, product, whole_two)))
+    return (dgate.reshape(size * own, hidden), dup.reshape(size * own, hidden), early, late)
 
 
 def sum_products_kernel(size, terms, *refs):
-    left_in, right_in, out = (refs[:terms], refs[terms : 2 * terms], refs[2 * terms])
-    at = 2 * terms + 1
+    left_in, right_in, out = (refs[:terms], refs[terms], refs[terms + 1])
+    at = terms + 2
     lefts, rights, (w_load, x_load) = (
         refs[at : at + terms],
         refs[at + terms : at + 2 * terms],
@@ -632,10 +644,9 @@
         for copy in tiles(part, slot, q, sibling):
             copy.wait()
 
-    weights = [
-        pltpu.make_async_copy(source, right, w_load.at[i])
-        for i, (source, right) in enumerate(zip(right_in, rights))
-    ]
+    weights = []
+    for kind, right in enumerate(rights):
+        weights += unit_loads(right_in, kind, right, w_load.at[kind])
     for copy in weights:
         copy.start()
     order = [bits[::-1] for bits in orders(size)]
@@ -652,21 +663,21 @@
     finish()
 
 
-def sum_products(size, number, lefts, rights):
+def sum_products(size, number, lefts, units):
     total, hidden = lefts[0].shape
-    width = rights[0].shape[1]
+    lanes, _, _, width = units.shape
     rows = total // size // PARTS
     vmem = pl.BlockSpec(memory_space=pltpu.VMEM)
     terms = len(lefts)
     out = pl.pallas_call(
         functools.partial(sum_products_kernel, size, terms),
         out_shape=jax.ShapeDtypeStruct((PARTS, rows, width), jnp.float32),
-        in_specs=[pl.BlockSpec(memory_space=pl.ANY)] * (2 * terms),
+        in_specs=[pl.BlockSpec(memory_space=pl.ANY)] * (terms + 1),
         out_specs=vmem,
         scratch_shapes=[
             *[pltpu.VMEM((size, PARTS, rows, hidden), jnp.bfloat16)] * terms,
             *[pltpu.VMEM((hidden, width), jnp.bfloat16)] * terms,
-            pltpu.SemaphoreType.DMA((terms,)),
+            pltpu.SemaphoreType.DMA((terms, lanes)),
             pltpu.SemaphoreType.DMA((size, PARTS, terms)),
             *scatter_scratch(size, rows, width),
         ],
@@ -677,7 +688,7 @@
             flops=2 * total * hidden * width * terms, bytes_accessed=200 * 1024 * 1024, transcendentals=0
         ),
         name="sum_products",
-    )(*[left.reshape(size, PARTS, rows, hidden) for left in lefts], *rights)
+    )(*[left.reshape(size, PARTS, rows, hidden) for left in lefts], units)
     return out.reshape(PARTS * rows, width)
 
 
@@ -691,8 +702,7 @@
     c_ref,
     before,
     whole,
-    mine_gate,
-    mine_up,
+    mine_pair,
     mine_down,
     count,
     counts,
@@ -708,7 +718,7 @@
     *sems,
 ):
     me, z = (lax.axis_index("fsdp"), lax.axis_index("tp"))
-    mine = (mine_gate, mine_up, mine_down)
+    mine = (mine_pair.at[0], mine_pair.at[1], mine_down.at[0])
     span = m_ref.shape[-1]
     part_of = lambda device: pl.ds(pl.multiple_of(device * span, span), span)
     local = [pltpu.make_async_copy(w_ref, whole.at[me, z], loads.at[0])]
@@ -850,19 +860,18 @@
     other_kinds = pltpu.SemaphoreType.DMA((size - 1, kinds))
     line = pltpu.SemaphoreType.DMA((2 * lanes - 2,))
     hop = pltpu.SemaphoreType.DMA((back,))
-    mine = jax.ShapeDtypeStruct((rows, size * columns), units.dtype)
+    mine = lambda number: jax.ShapeDtypeStruct((number, rows, size * columns), units.dtype)
     return pl.pallas_call(
         functools.partial(enter_kernel, size, lanes, back),
         out_shape=(
             jax.ShapeDtypeStruct((back, *values.shape), values.dtype),
             jax.ShapeDtypeStruct((size, lanes, *weights.shape), weights.dtype),
-            mine,
-            mine,
-            mine,
+            mine(2),
+            mine(1),
             jax.ShapeDtypeStruct(count.shape, count.dtype),
         ),
         in_specs=[any_space, any_space, any_space, vmem],
-        out_specs=(any_space,) * 5 + (vmem,),
+        out_specs=(any_space,) * 4 + (vmem,),
         scratch_shapes=[
             pltpu.VMEM((size, *count.shape), count.dtype),
             pltpu.SemaphoreType.DMA((kinds + 1,)),
@@ -882,13 +891,119 @@
     )(values, weights, units, count)
 
 
+class Units:
+    def __init__(self, size, me, units, back, sems):
+        self.size, self.me, self.units, self.back = (size, me, units, back)
+        self.send, self.recv, self.own = sems
+        self.kinds, self.span = (units.shape[0], back.shape[-1])
+
+    def part_of(self, device):
+        return pl.ds(pl.multiple_of(device * self.span, self.span), self.span)
+
+    def stay(self):
+        return [
+            pltpu.make_async_copy(
+                self.units.at[kind, :, self.part_of(self.me)],
+                self.back.at[self.me, kind],
+                self.own.at[kind],
+            )
+            for kind in range(self.kinds)
+        ]
+
+    def moves(self):
+        copies = []
+        for other in range(1, self.size):
+            peer = flip(self.me, other)
+            copies += [
+                pltpu.make_async_remote_copy(
+                    src_ref=self.units.at[kind, :, self.part_of(peer)],
+                    dst_ref=self.back.at[self.me, kind],
+                    send_sem=self.send.at[other - 1, kind],
+                    recv_sem=self.recv.at[other - 1, kind],
+                    device_id={"fsdp": peer},
+                    device_id_type=MESH,
+                )
+                for kind in range(self.kinds)
+            ]
+        return copies
+
+    def start(self):
+        for copy in self.stay() + self.moves():
+            copy.start()
+
+    def finish(self):
+        for copy in self.moves() + self.stay():
+            copy.wait()
+
+
+def units_scratch(size, kinds):
+    return [
+        pltpu.SemaphoreType.DMA((size - 1, kinds)),
+        pltpu.SemaphoreType.DMA((size - 1, kinds)),
+        pltpu.SemaphoreType.DMA((kinds,)),
+    ]
+
+
+class Lanes:
+    def __init__(self, lanes, z, values, out, low, came, send, recv):
+        self.lanes, self.z, self.values, self.out = (lanes, z, values, out)
+        self.low, self.came, self.send, self.recv = (low, came, send, recv)
+
+    def block(self, lane):
+        each = self.lanes // PARTS
+        width = self.out.shape[1]
+        start = pl.multiple_of(lax.rem(lane, each) * width, width)
+        return self.values[lax.div(lane, each), :, pl.ds(start, width)]
+
+    def copy(self, hop):
+        return pltpu.make_async_remote_copy(
+            src_ref=self.low.at[hop - 1],
+            dst_ref=self.came.at[hop - 1],
+            send_sem=self.send.at[hop - 1],
+            recv_sem=self.recv.at[hop - 1],
+            device_id={"tp": lax.rem(self.z + hop, self.lanes)},
+            device_id_type=MESH,
+        )
+
+    def start(self):
+        for hop in range(1, self.lanes):
+            self.low[hop - 1] = self.block(lax.rem(self.z + hop, self.lanes)).astype(jnp.bfloat16)
+            self.copy(hop).start()
+
+    def finish(self):
+        for hop in range(1, self.lanes):
+            self.copy(hop).wait()
+        total = self.block(self.z)
+        for hop in range(1, self.lanes):
+            total = total + self.came[hop - 1].astype(jnp.float32)
+        self.out[...] = total
+
+
+def lanes_scratch(lanes, rows, width):
+    return [
+        pltpu.VMEM((lanes - 1, rows, width), jnp.bfloat16),
+        pltpu.VMEM((lanes - 1, rows, width), jnp.bfloat16),
+        pltpu.SemaphoreType.DMA((lanes - 1,)),
+        pltpu.SemaphoreType.DMA((lanes - 1,)),
+    ]
+
+
+def greet_all(me, z, size, lanes):
+    barrier = pltpu.get_barrier_semaphore()
+    peers = [{"fsdp": flip(me, other)} for other in range(1, size)]
+    peers += [{"tp": lax.rem(z + hop, lanes)} for hop in range(1, lanes)]
+    for peer in peers:
+        pl.semaphore_signal(barrier, inc=1, device_id=peer, device_id_type=MESH)
+    pl.semaphore_wait(barrier, len(peers))
+
+
 def sum_query_kernel(
-    size, left_ref, right_ref, *refs
+    size, lanes, left_ref, right_ref, units_ref, sums_ref, out, back, lane_out, left, right, loads, *refs
 ):
-    units, (out, back), (left, right, loads, u_send, u_recv, u_own) = (refs[:3], refs[3:5], refs[5:11])
-    made, held, sent, came, *sems = refs[11:]
-    me = lax.axis_index("fsdp")
-    width, span = (out.shape[-1], back.shape[-1])
+    units_sems, lane_refs = (refs[:3], refs[3:7])
+    made, held, sent, came, *sems = refs[7:]
+    me, z = (lax.axis_index("fsdp"), lax.axis_index("tp"))
+    width = out.shape[-1]
     rows = left.shape[1] // size
     copies = [pltpu.make_async_copy(left_ref, left, loads.at[PARTS])]
     copies += [
@@ -897,73 +1012,52 @@
         )
         for part in range(PARTS)
     ]
-    part_of = lambda device: pl.ds(pl.multiple_of(device * span, span), span)
-    stay = [
-        pltpu.make_async_copy(unit.at[:, part_of(me)], back.at[me, kind], u_own.at[kind])
-        for kind, unit in enumerate(units)
-    ]
-    for copy in copies + stay:
+    for copy in copies:
         copy.start()
-    barrier = pltpu.get_barrier_semaphore()
-    for other in range(1, size):
-        pl.semaphore_signal(
-            barrier, inc=1, device_id={"fsdp": flip(me, other)}, device_id_type=MESH
-        )
-    pl.semaphore_wait(barrier, size - 1)
+    greet_all(me, z, size, lanes)
     for copy in copies:
         copy.wait()
-
-    def unit_copy(other, kind):
-        peer = flip(me, other)
-        return pltpu.make_async_remote_copy(
-            src_ref=units[kind].at[:, part_of(peer)],
-            dst_ref=back.at[me, kind],
-            send_sem=u_send.at[other - 1, kind],
-            recv_sem=u_recv.at[other - 1, kind],
-            device_id={"fsdp": peer},
-            device_id_type=MESH,
-        )
 
     def partial(part, slot, columns):
         block = left[:, pl.ds(pl.multiple_of(slot * rows, rows), rows)]
         return contract_first(block, right[part, :, columns])
 
+    units = Units(size, me, units_ref, back, units_sems)
+    across = Lanes(lanes, z, sums_ref, lane_out, *lane_refs)
     calls, finish = scatter_steps(size, me, made, held, sent, came, sems, partial, out)
     for number, call in enumerate(calls):
         call()
+        if number == 1:
+            across.start()
         if number == len(calls) // 2:
-            for other in range(1, size):
-                for kind in range(3):
-                    unit_copy(other, kind).start()
-    for other in range(1, size):
-        for kind in range(3):
-            unit_copy(other, kind).wait()
+            units.start()
+    across.finish()
+    units.finish()
     finish()
-    for copy in stay:
-        copy.wait()
-
-
-def sum_query(size, left, right, units):
+
+
+def sum_query(size, lanes, left, right, units, sums):
     tokens, depth = left.shape
     width = right.shape[1] // PARTS
     rows = depth // size
+    lane_width = sums.shape[2] * PARTS // lanes
     any_space = pl.BlockSpec(memory_space=pl.ANY)
     vmem = pl.BlockSpec(memory_space=pltpu.VMEM)
     return pl.pallas_call(
-        functools.partial(sum_query_kernel, size),
+        functools.partial(sum_query_kernel, size, lanes),
         out_shape=(
             jax.ShapeDtypeStruct((PARTS, rows, width), jnp.float32),
-            jax.ShapeDtypeStruct((size, 3, units[0].shape[0], rows), jnp.bfloat16),
-        ),
-        in_specs=[any_space] * 5,
-        out_specs=(vmem, any_space),
+            jax.ShapeDtypeStruct((size, *units.shape[:2], rows), jnp.bfloat16),
+            jax.ShapeDtypeStruct((rows, lane_width), jnp.float32),
+        ),
+        in_specs=[any_space] * 3 + [vmem],
+        out_specs=(vmem, any_space, vmem),
         scratch_shapes=[
             pltpu.VMEM((tokens, depth), jnp.bfloat16),
             pltpu.VMEM((PARTS, tokens, width), jnp.bfloat16),
             pltpu.SemaphoreType.DMA((PARTS + 1,)),
-            pltpu.SemaphoreType.DMA((size - 1, 3)),
-            pltpu.SemaphoreType.DMA((size - 1, 3)),
-            pltpu.SemaphoreType.DMA((3,)),
+            *units_scratch(size, units.shape[0]),
+            *lanes_scratch(lanes, rows, lane_width),
             *scatter_scratch(size, rows, width),
         ],
         compiler_params=pltpu.CompilerParams(
@@ -973,12 +1067,32 @@
             flops=4 * tokens * depth * width, bytes_accessed=100 * 1024 * 1024, transcendentals=0
         ),
         name="sum_query",
-    )(left, right, *units)
-
-
-def sum_key_kernel(size, left_ref, q_ref, kv_ref, w_ref, out, low, left, right, loads, tiles, fetch, *refs):
-    made, held, sent, came, *sems = refs
-    me = lax.axis_index("fsdp")
+    )(left, right, units, sums)
+
+
+def sum_key_kernel(
+    size,
+    lanes,
+    left_ref,
+    q_ref,
+    kv_ref,
+    w_ref,
+    units_ref,
+    sums_ref,
+    out,
+    low,
+    back,
+    lane_out,
+    left,
+    right,
+    loads,
+    tiles,
+    fetch,
+    *refs,
+):
+    units_sems, lane_refs = (refs[:3], refs[3:7])
+    made, held, sent, came, *sems = refs[7:]
+    me, z = (lax.axis_index("fsdp"), lax.axis_index("tp"))
     rows = left.shape[1] // size
     parts, span = (w_ref.shape[1], tiles.shape[-1])
     copies = [pltpu.make_async_copy(left_ref, left, loads.at[PARTS])]
@@ -995,7 +1109,7 @@
         )
 
     tile_copy(0).start()
-    greet(me, size)
+    greet_all(me, z, size, lanes)
     for copy in copies:
         copy.wait()
 
@@ -1024,10 +1138,16 @@
                     start += width
             low[span_rows, f * rows : (f + 1) * rows] = total
 
+    units = Units(size, me, units_ref, back, units_sems)
+    across = Lanes(lanes, z, sums_ref, lane_out, *lane_refs)
     calls, finish = scatter_steps(size, me, made, held, sent, came, sems, partial, out)
     done = 0
     for number, call in enumerate(calls):
         call()
+        if number == 1:
+            across.start()
+        if number == len(calls) // 2:
+            units.start()
         goal = size * max(0, number - 1) // max(1, len(calls) - 3)
         while done < min(size, goal):
             low_columns(done)
@@ -1035,31 +1155,38 @@
     while done < size:
         low_columns(done)
         done += 1
+    across.finish()
+    units.finish()
     finish()
 
 
-def sum_key(size, left, grad_query, grad_pair, weights):
+def sum_key(size, lanes, left, grad_query, grad_pair, weights, units, sums):
     tokens, depth = left.shape
     width = grad_pair.shape[2]
     rows = depth // size
     parts = weights.shape[1]
     span = (grad_query.shape[1] + PARTS * width) // parts
+    lane_width = sums.shape[2] * PARTS // lanes
     any_space = pl.BlockSpec(memory_space=pl.ANY)
     vmem = pl.BlockSpec(memory_space=pltpu.VMEM)
     return pl.pallas_call(
-        functools.partial(sum_key_kernel, size),
+        functools.partial(sum_key_kernel, size, lanes),
         out_shape=(
             jax.ShapeDtypeStruct((PARTS, rows, width), jnp.float32),
             jax.ShapeDtypeStruct((tokens, depth), jnp.float32),
-        ),
-        in_specs=[any_space, vmem, any_space, any_space],
-        out_specs=(vmem, vmem),
+            jax.ShapeDtypeStruct((size, *units.shape[:2], rows), jnp.bfloat16),
+            jax.ShapeDtypeStruct((rows, lane_width), jnp.float32),
+        ),
+        in_specs=[any_space, vmem, any_space, any_space, any_space, vmem],
+        out_specs=(vmem, vmem, any_space, vmem),
         scratch_shapes=[
             pltpu.VMEM((tokens, depth), jnp.bfloat16),
             pltpu.VMEM((PARTS, tokens, width), jnp.bfloat16),
             pltpu.SemaphoreType.DMA((PARTS + 1,)),
             pltpu.VMEM((2, parts, rows, span), jnp.bfloat16),
             pltpu.SemaphoreType.DMA((2,)),
+            *units_scratch(size, units.shape[0]),
+            *lanes_scratch(lanes, rows, lane_width),
             *scatter_scratch(size, rows, width),
         ],
         compiler_params=pltpu.CompilerParams(
@@ -1069,7 +1196,7 @@
             flops=8 * tokens * depth * width, bytes_accessed=100 * 1024 * 1024, transcendentals=0
         ),
         name="sum_key",
-    )(left, grad_query, grad_pair, weights)
+    )(left, grad_query, grad_pair, weights, units, sums)
 
 
 def sum_small_kernel(size, lanes, x_ref, o_ref, came, send, recv):
@@ -1618,10 +1745,6 @@
     ).astype(jnp.float32)
 
 
-def join_parts(halves):
-    return jnp.concatenate([halves[part] for part in range(PARTS)], axis=1)
-
-
 def shards(
     states,
     lengths,
@@ -1656,13 +1779,12 @@
         part.reshape(n_fsdp, -1, part.shape[1]) for part in (w_gate.T, w_up.T, w_down)
     ]
     live_here = jnp.full((8, 128), jnp.sum(padding).astype(jnp.float32))
-    before, weights_attn, *mine, counts = enter(
+    before, weights_attn, mine_pair, mine_down, counts = enter(
         n_fsdp, n_tp, back, states, joined, jnp.stack(units, axis=1), live_here
     )
     count = counts[0, 0]
-    rows_gate, rows_up, rows_down = [
-        lax.all_gather(part, "tp", axis=0, tiled=True) for part in mine
-    ]
+    units_pair = lax.all_gather(mine_pair, "tp", axis=0)
+    units_down = lax.all_gather(mine_down, "tp", axis=0)
     normed_in, query_raw, key_raw, value = project(
         before, states, norm_attn, weights_attn, wq, wk
     )
@@ -1672,18 +1794,18 @@
     hidden_one = project_out(attended, weights_attn, states, wo)
     normed_two, factor_two = normalize_rows(hidden_one)
     whole_two, gate, up, product = gate_up(
-        n_fsdp, (normed_two * norm_mlp).astype(jnp.bfloat16), rows_gate, rows_up
+        n_fsdp, (normed_two * norm_mlp).astype(jnp.bfloat16), units_pair
     )
-    outputs = hidden_one + sum_products(n_fsdp, 2, (product,), (rows_down,))
+    outputs = hidden_one + sum_products(n_fsdp, 2, (product,), units_down)
     errors = (outputs - teacher.astype(jnp.float32)) * live[:, None]
     squares = jnp.sum(errors * errors)
     grad_out = errors * (2.0 / (count * D))
 
-    grad_gate, grad_up, by_unit = grad_hidden_units(
-        n_fsdp, grad_out.astype(jnp.bfloat16), rows_down, gate, up, product, whole_two
+    grad_gate, grad_up, units_early, units_late = grad_hidden_units(
+        n_fsdp, grad_out.astype(jnp.bfloat16), units_down, gate, up, product, whole_two
     )
-    grad_mid = sum_products(n_fsdp, 4, (grad_gate, grad_up), (rows_gate, rows_up))
-    by_unit = [lax.psum_scatter(part, "tp", scatter_dimension=0, tiled=True) for part in by_unit]
+    units_early = lax.psum_scatter(units_early, "tp", scatter_dimension=0)
+    grad_mid = sum_products(n_fsdp, 4, (grad_gate, grad_up), units_pair)
     grad_norm_mlp = jnp.sum(grad_mid * normed_two, axis=0)
     grad_hidden = grad_out + norm_back(grad_mid, normed_two, factor_two, norm_mlp)
 
@@ -1705,20 +1827,18 @@
         n_fsdp,
         n_tp,
     )
-    by_unit, sums_out = lax.optimization_barrier((by_unit, sums_out))
-    sums_query, units_back = sum_query(n_fsdp, normed_in, grad_query, by_unit)
-    sums_query, grad_pair = lax.optimization_barrier((sums_query, grad_pair))
-    sums_pair, grad_low = sum_key(n_fsdp, normed_in, grad_query, grad_pair, weights_attn)
-    grad_w_out, grad_w_query = [
-        over_lanes(join_parts(sums)[None])[0] for sums in (sums_out, sums_query)
-    ]
-    sums_pair, grad_w_query, grad_w_out = lax.optimization_barrier(
-        (sums_pair, grad_w_query, grad_w_out)
+    units_late, grad_query = lax.optimization_barrier((units_late, grad_query))
+    units_late = lax.psum_scatter(units_late, "tp", scatter_dimension=0)
+    sums_query, back_early, grad_w_out = sum_query(
+        n_fsdp, n_tp, normed_in, grad_query, units_early, sums_out
+    )
+    sums_pair, grad_low, back_late, grad_w_query = sum_key(
+        n_fsdp, n_tp, normed_in, grad_query, grad_pair, weights_attn, units_late, sums_query
     )
     grad_w_pair = over_lanes(sums_pair)
     grad_w_down, grad_w_gate, grad_w_up = [
-        units_back[:, kind].reshape(-1, units_back.shape[3]).astype(jnp.float32)
-        for kind in range(3)
+        part.reshape(-1, part.shape[2]).astype(jnp.float32)
+        for part in (back_early[:, 0], back_early[:, 1], back_late[:, 0])
     ]
     normed_one, factor_one = normalize_rows(inputs)
     grad_norm_attn = jnp.sum(grad_low * normed_one, axis=0)

time: 1060 us -> 998 us (0.942)
  Pallas kernels: 905 us -> 862 us
  other arithmetic: 61.7 us -> 50.1 us
    pallas_call x1, Pallas kernels: 160 us -> 116 us  [attend_back(): pl.pallas_call(functools.partial(attend_back_kernel, group, step, lead, s...]
    reduce_scatter x3 -> x2, waiting for transfers between devices: 0.06 us -> 11.6 us  [the longest x1 11.6 us: shards(): units_late = lax.psum_scatter(units_late, 'tp', scatter_dimension=0)]
    all_gather x3 -> x2, waiting for transfers between devices: 34 us -> 22.7 us  [the longest x1 22.7 us: shards(): units_pair = lax.all_gather(mine_pair, 'tp', axis=0)]
  transfers between devices with their start and end apart: 9 -> 5, of which waited for: 3 -> 3; matrix products, arithmetic and copies ran while one was open for 5% -> 4% of each run, Pallas kernels for 48% -> 46%
where the time goes in v5:
time: 998 us; the launch traced here: 991 us
  Pallas kernels  862 us (86%)
  other arithmetic  50.1 us (5%)
  waiting for transfers between devices  37.8 us (4%)
  local copies, waits for them, and re-layouts  22.9 us (2%)
  between operations  17.9 us (2%)
    pallas_call x2, Pallas kernels, sum_products(): pl.pallas_call(functools.partial(sum_products_kernel, size, terms), out_s...  172 us
    pallas_call x1, Pallas kernels, enter(): pl.pallas_call(functools.partial(enter_kernel, size, lanes, back), out_sh...  142 us
    pallas_call x1, Pallas kernels, attend_back(): pl.pallas_call(functools.partial(attend_back_kernel, group, step, lead, s...  116 us
    pallas_call x1, Pallas kernels, grad_hidden_units(): pl.pallas_call(functools.partial(grad_hidden_kernel, size), out_shape=(sh...  105 us
    pallas_call x1, Pallas kernels, gate_up(): pl.pallas_call(functools.partial(gate_up_kernel, size), out_shape=(shape(...  84.1 us
    pallas_call x1, Pallas kernels, sum_query(): pl.pallas_call(functools.partial(sum_query_kernel, size, lanes), out_shap...  63.1 us
    pallas_call x1, Pallas kernels, sum_key(): pl.pallas_call(functools.partial(sum_key_kernel, size, lanes), out_shape=...  60.4 us
    pallas_call x1, Pallas kernels, attend(): pl.pallas_call(functools.partial(attend_kernel, group, step, rows - own),...  49.9 us
  transfers between devices with their start and end apart: 5, of which 3 were waited for; matrix products, arithmetic and copies ran while one was open for 4% of the time, Pallas kernels for 46%

profile of v5, /device:TPU:0, one launch (start us, length us, event | category | flops | bytes accessed | tf_op | source)
XLA Modules:
  0.0 991.3 jit_solution(7863392132094346764)
XLA Ops:
  16.5 141.5 %enter.1 = (bf16[2,512,2048]{2,1,0:T(8,128)(2,1)}, bf16[8,4,256,1536]{3,2,1,0:T(8,128)(2,1)}, bf16[2,192,2048]{2,1,0:T(8,128)(2,1)}, bf16[1,192,2048]{2,1,0:T(8,128)(2,1)}, f32[8,128]{1,0:T(8,128)}) custom-call(bf16[512,2048]{1,0:T(8,128)(2,1)} %x_ref.5, bf16[256,1536]{1,0:T(8,128)(2,1)} %pad_maximum_fusion.1.w_ref, ...), custom_call_target="tpu_custom_call" | custom-call | bytes 419430400 | tf_op jit(solution)/shard_map/enter/pallas_call | solution.py:864
  162.5 2.8 fusion.16
  165.4 32.4 %project_in.1 = (bf16[512,2048]{1,0:T(8,128)(2,1)}, f32[512,2048]{1,0:T(8,128)}, f32[1536,1024]{1,0:T(8,128)}, bf16[1536,1024]{1,0:T(8,128)(2,1)}) custom-call(bf16[2,512,2048]{2,1,0:T(8,128)(2,1)} %get-tuple-element.45.before_ref, bf16[512,2048]{1,0:T(8,128)(2,1)} %x_ref.5, f32[1,2048]{1,0:T(1,128)} %bitcast.80, ...), custom_call_target="tpu_custom_call" | custom-call | flops 17179869184 | bytes 23068672 | tf_op jit(solution)/shard_map/project_in/pallas_call | solution.py:1295
  199.4 49.9 %attend.1.a_ref.right_ref = bf16[512,2048]{1,0:T(8,128)(2,1)} custom-call(f32[512,2048]{1,0:T(8,128)} %get-tuple-element.47.q_ref, f32[1536,1024]{1,0:T(8,128)} %get-tuple-element.48.k_ref, bf16[1536,1024]{1,0:T(8,128)(2,1)} %get-tuple-element.49.v_ref, f32[512,1280]{1,0:T(8,128)} %add_select_fusion.bias_ref, f32[1536,128]{1,0:T(8,128)} %get-tuple-element.153.cos_ref, ...), custom_call_target="tpu_custom_call" | custom-call | flops 21474836480 | bytes 13631488 | tf_op jit(solution)/shard_map/attend/pallas_call | solution.py:1628
  251.3 11.4 %project_out.1 = f32[512,2048]{1,0:T(8,128)} custom-call(bf16[512,2048]{1,0:T(8,128)(2,1)} %attend.1.a_ref.right_ref, bf16[8,4,256,1536]{3,2,1,0:T(8,128)(2,1)} %get-tuple-element.46.w_ref, bf16[512,2048]{1,0:T(8,128)(2,1)} %x_ref.5), custom_call_target="tpu_custom_call" | custom-call | flops 4294967296 | bytes 25165824 | tf_op jit(solution)/shard_map/project_out/pallas_call | solution.py:1339
  267.8 22.7 %all-gather.5.cloned.1.call-done = bf16[8,192,2048]{2,1,0:T(8,128)(2,1)} async-done(((bf16[2,192,2048]{2,1,0:T(8,128)(2,1)}), bf16[8,192,2048]{2,1,0:T(8,128)(2,1)}) %all-gather.5.cloned.1.call-update) | async-done | bytes 6291472 | tf_op jit(solution)/shard_map/all_gather | solution.py:1786
  290.6 84.1 %gate_up.1 = (bf16[8,2,256,2048]{3,2,1,0:T(8,128)(2,1)}, f32[8,2,256,768]{3,2,1,0:T(8,128)}, f32[8,2,256,768]{3,2,1,0:T(8,128)}, bf16[8,2,256,768]{3,2,1,0:T(8,128)(2,1)}) custom-call(bf16[2,256,2048]{2,1,0:T(8,128)(2,1)} %bitcast.68, bf16[4,2,192,2048]{3,2,1,0:T(8,128)(2,1)} %bitcast.84), custom_call_target="tpu_custom_call" | custom-call | flops 25769803776 | bytes 209715200 | tf_op jit(solution)/shard_map/gate_up/pallas_call | solution.py:395
  374.8 82.8 %sum_products.2 = f32[2,256,2048]{2,1,0:T(8,128)} custom-call(bf16[8,2,256,768]{3,2,1,0:T(8,128)(2,1)} %get-tuple-element.51.refs_0_.prod_in, bf16[4,1,192,2048]{3,2,1,0:T(8,128)(2,1)} %bitcast.86), custom_call_target="tpu_custom_call" | custom-call | flops 12884901888 | bytes 209715200 | tf_op jit(solution)/shard_map/sum_products/pallas_call | solution.py:672
  457.6 4.4 multiply_reduce_fusion
  464.6 105.5 %grad_hidden_units.1 = (bf16[8,2,256,768]{3,2,1,0:T(8,128)(2,1)}, bf16[8,2,256,768]{3,2,1,0:T(8,128)(2,1)}, bf16[4,2,192,2048]{3,2,1,0:T(8,128)(2,1)}, bf16[4,1,192,2048]{3,2,1,0:T(8,128)(2,1)}) custom-call(bf16[2,256,2048]{2,1,0:T(8,128)(2,1)} %bitcast.67, bf16[4,1,192,2048]{3,2,1,0:T(8,128)(2,1)} %bitcast.87, ...), custom_call_target="tpu_custom_call" | custom-call | flops 51539607552 | bytes 209715200 | tf_op jit(solution)/shard_map/grad_hidden_units/pallas_call | solution.py:581
  570.2 89.7 %sum_products.3 = f32[2,256,2048]{2,1,0:T(8,128)} custom-call(bf16[8,2,256,768]{3,2,1,0:T(8,128)(2,1)} %get-tuple-element.59.refs_0_, bf16[8,2,256,768]{3,2,1,0:T(8,128)(2,1)} %get-tuple-element.60.refs_1_, bf16[4,2,192,2048]{3,2,1,0:T(8,128)(2,1)} %bitcast.85), custom_call_target="tpu_custom_call" | custom-call | flops 25769803776 | bytes 209715200 | tf_op jit(solution)/shard_map/sum_products/pallas_call | solution.py:672
  659.9 3.5 fusion.9
  664.8 4.1 fusion.22
  668.9 8.9 back_out.1.do_ref
  677.8 115.5 %attend_back.1 = (bf16[512,2048]{1,0:T(8,128)(2,1)}, bf16[2,512,1024]{2,1,0:T(8,128)(2,1)}, f32[1,128]{1,0:T(1,128)}, f32[1,128]{1,0:T(1,128)}, f32[2,256,1024]{2,1,0:T(8,128)}) custom-call(f32[512,2048]{1,0:T(8,128)} %get-tuple-element.47.q_ref, f32[1536,1024]{1,0:T(8,128)} %get-tuple-element.48.k_ref, bf16[1536,1024]{1,0:T(8,128)(2,1)} %get-tuple-element.49.v_ref, ...), custom_call_target="tpu_custom_call" | custom-call | flops 53687091200 | bytes 33554432 | tf_op jit(solution)/shard_map/attend_back/pallas_call | solution.py:1672
  795.5 63.1 %sum_query.1 = (f32[2,256,1024]{2,1,0:T(8,128)}, bf16[8,2,192,256]{3,2,1,0:T(8,128)(2,1)}, f32[256,512]{1,0:T(8,128)}) custom-call(bf16[512,2048]{1,0:T(8,128)(2,1)} %get-tuple-element.53.left_ref, bf16[512,2048]{1,0:T(8,128)(2,1)} %get-tuple-element.62.right_ref.q_ref, bf16[2,192,2048]{2,1,0:T(8,128)(2,1)} %bitcast.88, ...), custom_call_target="tpu_custom_call" | custom-call | flops 4294967296 | bytes 104857600 | tf_op jit(solution)/shard_map/sum_query/pallas_call | solution.py:1046
  858.6 11.6 %reduce-scatter.4.cloned.1.call-done = bf16[1,1,192,2048]{3,2,1,0:T(8,128)(2,1)} async-done(((bf16[4,1,192,2048]{3,2,1,0:T(8,128)(2,1)}), bf16[1,1,192,2048]{3,2,1,0:T(8,128)(2,1)}) %reduce-scatter.4.cloned.1.call-update) | async-done | bytes 786448 | tf_op jit(solution)/shard_map/reduce_scatter | solution.py:1831
  870.1 60.4 %sum_key.1 = (f32[2,256,1024]{2,1,0:T(8,128)}, f32[512,2048]{1,0:T(8,128)}, bf16[8,1,192,256]{3,2,1,0:T(8,128)(2,1)}, f32[256,512]{1,0:T(8,128)}) custom-call(bf16[512,2048]{1,0:T(8,128)(2,1)} %get-tuple-element.53.left_ref, bf16[512,2048]{1,0:T(8,128)(2,1)} %get-tuple-element.62.right_ref.q_ref, bf16[2,512,1024]{2,1,0:T(8,128)(2,1)} %get-tuple-element.63.kv_ref, ...), custom_call_target="tpu_custom_call" | custom-call | flops 8589934592 | bytes 104857600 | tf_op jit(solution)/shard_map/sum_key/pallas_call | solution.py:1172
  930.6 3.3 fusion.4
  935.2 17.1 %sum_small.1 = f32[40,128]{1,0:T(8,128)} custom-call(f32[40,128]{1,0:T(8,128)} %pad.5.x_ref), custom_call_target="tpu_custom_call" | custom-call | tf_op jit(solution)/shard_map/sum_small/pallas_call | solution.py:1234
  962.6 3.0 copy.44
  965.6 3.0 copy.45
  971.1 6.7 fusion.7
  977.8 2.8 reduce-scatter.8.cloned.1.call-done
  (104 shorter events, 43.1 us)
Async XLA Ops:
  7.2 6.1 copy-start.8
  7.2 7.8 copy-start.13
  7.2 7.7 copy-start.14
  7.2 7.7 copy-start.11
  7.2 283.3 %all-gather.5.cloned.1.call-start = ((), (), s32[]{:S(2)}) async-start(), calls=%async_computation.6 | async-start | bytes 7864320 | tf_op jit(solution)/shard_map/all_gather | solution.py:1786
  15.9 143.0 %copy-start.18 = (s32[1,4]{1,0:T(1,128)S(1)}, s32[1,4]{1,0:T(1,128)}, u32[]{:S(2)}) copy-start(s32[1,4]{1,0:T(1,128)} %param.16) | copy-start | bytes 52
  15.9 143.3 %copy-start.16 = (s32[1,2048]{1,0:T(1,128)S(1)}, s32[1,2048]{1,0:T(1,128)}, u32[]{:S(2)}) copy-start(s32[1,2048]{1,0:T(1,128)} %param.17) | copy-start | bytes 24580
  158.0 216.7 %all-gather.7.cloned.1.call-start = ((), (), s32[]{:S(2)}) async-start(), calls=%async_computation.7 | async-start | bytes 3932160 | tf_op jit(solution)/shard_map/all_gather | solution.py:1787
  158.8 636.7 %reduce-scatter.6.cloned.1.call-start = ((), (), s32[]{:S(2)}) async-start(), calls=%async_computation.4 | async-start | bytes 7864320 | tf_op jit(solution)/shard_map/reduce_scatter | solution.py:1807
  251.3 14.1 %copy-start.15 = (f32[2048]{0:T(1024)S(1)}, f32[2048]{0:T(1024)}, u32[]{:S(2)}) copy-start(f32[2048]{0:T(1024)} %param.26) | copy-start | bytes 24580
  262.7 3.4 copy-start
  374.7 82.8 %copy-start.1 = (f32[512,2048]{1,0:T(8,128)S(1)}, f32[512,2048]{1,0:T(8,128)}, u32[]{:S(2)}) copy-start(f32[512,2048]{1,0:T(8,128)} %project_out.1) | copy-start | bytes 12582916
  374.8 82.8 %copy-start.6 = (bf16[512,2048]{1,0:T(8,128)(2,1)S(1)}, bf16[512,2048]{1,0:T(8,128)(2,1)}, u32[]{:S(2)}) copy-start(bf16[512,2048]{1,0:T(8,128)(2,1)} %param.18) | copy-start | bytes 6291460
  570.1 300.0 %reduce-scatter.4.cloned.1.call-start = ((), (), s32[]{:S(2)}) async-start(), calls=%async_computation.3 | async-start | bytes 3932160 | tf_op jit(solution)/shard_map/reduce_scatter | solution.py:1831
  570.2 89.7 %copy-start.2 = (f32[512,2048]{1,0:T(8,128)S(1)}, f32[512,2048]{1,0:T(8,128)}, u32[]{:S(2)}) copy-start(f32[512,2048]{1,0:T(8,128)} %project_out.1) | copy-start | bytes 12582916
  659.9 3.6 copy-start.5
  659.9 4.9 copy-start.7
  793.4 187.1 %reduce-scatter.8.cloned.1.call-start = ((), (), s32[]{:S(2)}) async-start(), calls=%async_computation.5 | async-start | bytes 1310720 | tf_op jit(solution)/shard_map/reduce_scatter | solution.py:1743
  870.1 60.4 %copy-start.17 = (f32[2048]{0:T(1024)S(1)}, f32[2048]{0:T(1024)}, u32[]{:S(2)}) copy-start(f32[2048]{0:T(1024)} %param.19) | copy-start | bytes 24580
  930.5 3.4 copy-start.20
  930.5 3.4 copy-start.19
  955.1 5.3 copy-start.12
  955.1 6.5 copy-start.10
  971.1 11.3 %copy-start.9 = (f32[256,512]{1,0:T(8,128)S(1)}, f32[256,512]{1,0:T(8,128)}, u32[]{:S(2)}) copy-start(f32[256,512]{1,0:T(8,128)} %get-tuple-element.173) | copy-start | bytes 1572868
  (2 other events, 4.2 us)
Sparse Core Ops, SparseCore 0:
  158.2 132.3 all-gather.4
  292.1 61.7 all-gather.6
  570.2 107.9 reduce-scatter.5
  793.5 76.5 reduce-scatter.3
  955.2 25.2 reduce-scatter.7

commit v6 on v5

--- a/solution.py
+++ b/solution.py
@@ -14,6 +14,7 @@
 EPS = 1e-06
 THETA = 1000000.0
 NEG = -1e30
+LOG2E = 1.4426950408889634
 VMEM = 56 * 1024 * 1024
 
 
@@ -199,7 +200,7 @@
     patterns = scatter_order(steps)
     place = {m: q for q, m in enumerate(patterns)}
     width = final.shape[-1]
-    chunk = min(512, width)
+    chunk = min(1024, width)
 
     def slots(pattern, sibling):
         return [flip(me, mask_of(pattern, order[part]) + sibling) for part in range(PARTS)]
@@ -306,11 +307,13 @@
 def gate_up_kernel(
     size,
     x_ref,
-    w_in,
+    wg_in,
+    mine_in,
     x_out,
     gate_out,
     up_out,
     prod_out,
+    wu_out,
     whole,
     wg_ref,
     wu_ref,
@@ -319,99 +322,221 @@
     prod,
     load,
     keep,
+    keep_gate,
+    keep_units,
     store,
+    z_send,
+    z_recv,
     *sems,
 ):
-    me = lax.axis_index("fsdp")
+    me, z = (lax.axis_index("fsdp"), lax.axis_index("tp"))
+    lanes, _, each, _ = wg_in.shape
     hidden = wg_ref.shape[0]
-    chunk = 256 if hidden % 256 == 0 else 128
-    lanes = w_in.shape[0]
-    loads = [pltpu.make_async_copy(x_ref, whole.at[me], load.at[0])]
-    loads += unit_loads(w_in, 0, wg_ref, load.at[pl.ds(1, lanes)])
-    loads += unit_loads(w_in, 1, wu_ref, load.at[pl.ds(1 + lanes, lanes)])
+    chunk = hidden
+    above, below = (lax.rem(z + 1, lanes), lax.rem(z + lanes - 1, lanes))
+    rows_of = lambda lane: wu_ref.at[pl.ds(pl.multiple_of(lane * each, each), each)]
+    loads = [
+        pltpu.make_async_copy(x_ref, whole.at[me], load.at[0]),
+        pltpu.make_async_copy(mine_in.at[0], rows_of(z), load.at[1]),
+    ]
+    loads += unit_loads(wg_in, 0, wg_ref, load.at[pl.ds(2, lanes)])
     for copy in loads:
         copy.start()
-    greet(me, size)
-    loads[0].wait()
-    state = {"count": 0, "last": None}
+    barrier = pltpu.get_barrier_semaphore()
+    peers = [{"fsdp": flip(me, bit)} for bit in [1] + chip_bits(size)] + [{"tp": above}, {"tp": below}]
+    for peer in peers:
+        pl.semaphore_signal(barrier, inc=1, device_id=peer, device_id_type=MESH)
+    pl.semaphore_wait(barrier, len(peers))
+    for copy in loads[:2]:
+        copy.wait()
+
+    def lane_copy(side, distance):
+        lane = z - (distance - 1) if side == 0 else z + (distance - 1)
+        return pltpu.make_async_remote_copy(
+            src_ref=rows_of(lane),
+            dst_ref=rows_of(lane),
+            send_sem=z_send.at[side, distance - 1],
+            recv_sem=z_recv.at[side, distance - 1],
+            device_id={"tp": above if side == 0 else below},
+            device_id_type=MESH,
+        )
+
+    def sends(side, distance):
+        if side == 0:
+            return (z >= distance - 1) & (z + 1 < lanes)
+        return (z + distance - 1 < lanes) & (z > 0)
+
+    def comes(side, distance):
+        return z >= distance if side == 0 else z + distance < lanes
+
+    def lane_send(distance):
+        for side in (0, 1):
+
+            @pl.when(sends(side, distance))
+            def _():
+                lane_copy(side, distance).start()
+
+    def lane_take(distance):
+        for side in (0, 1):
+
+            @pl.when(comes(side, distance))
+            def _():
+                lane_copy(side, distance).wait_recv()
+
+    def relay(distance):
+        lane_take(distance)
+        if distance + 1 < lanes:
+            lane_send(distance + 1)
+
+    gather = Gather(size, me, whole, sems)
+    groups = [(pattern, sibling) for pattern in gather.patterns for sibling in (0, 1)]
+
+    def pair_of(number):
+        pattern, sibling = groups[number]
+        return [gather.slot(part, pattern, sibling) for part in range(PARTS)]
+
+    def keeps(number):
+        pair = pair_of(number)
+        copies = []
+        for part in range(PARTS):
+            copies += [
+                pltpu.make_async_copy(
+                    whole.at[pair[part], part], x_out.at[pair[part], part], keep.at[part, number]
+                ),
+                pltpu.make_async_copy(
+                    gate.at[number, part], gate_out.at[pair[part], part], keep_gate.at[part, number]
+                ),
+            ]
+        return copies
 
     def stores(part, at):
         return [
             pltpu.make_async_copy(buffer.at[part], out.at[at, part], store.at[part, i])
-            for i, (buffer, out) in enumerate(((gate, gate_out), (up, up_out), (prod, prod_out)))
+            for i, (buffer, out) in enumerate(((up, up_out), (prod, prod_out)))
         ]
 
-    def work(pair):
-        count, last = (state["count"], state["last"])
-        for part in range(PARTS):
-            pltpu.make_async_copy(
-                whole.at[pair[part], part], x_out.at[pair[part], part], keep.at[part, count]
-            ).start()
-        if last is None:
-            for copy in loads[1:]:
-                copy.wait()
+    def gates(number):
+        pair = pair_of(number)
 
         @pl.loop(0, PARTS)
         def _(part):
             at = pick(part, pair)
-            if last is not None:
-                for copy in stores(part, pick(part, last)):
-                    copy.wait()
 
             @pl.loop(0, hidden // chunk)
             def _(index):
                 units = pl.ds(pl.multiple_of(index * chunk, chunk), chunk)
-                rows = whole[at, part]
-                gates = contract_last(rows, wg_ref[units, :])
-                ups = contract_last(rows, wu_ref[units, :])
-                gate[part, :, units] = gates
-                up[part, :, units] = ups
-                prod[part, :, units] = (gates * jax.nn.sigmoid(gates) * ups).astype(jnp.bfloat16)
+                gate[number, part, :, units] = contract_last(whole[at, part], wg_ref[units, :])
+
+        for copy in keeps(number):
+            copy.start()
+
+    def ups(number):
+        pair = pair_of(number)
+
+        @pl.loop(0, PARTS)
+        def _(part):
+            at = pick(part, pair)
+            if number:
+                for copy in stores(part, pick(part, pair_of(number - 1))):
+                    copy.wait()
+
+            @pl.loop(0, hidden // chunk)
+            def _(index):
+                units = pl.ds(pl.multiple_of(index * chunk, chunk), chunk)
+                value = contract_last(whole[at, part], wu_ref[units, :])
+                gates = gate[number, part, :, units]
+                up[part, :, units] = value
+                prod[part, :, units] = (gates * jax.nn.sigmoid(gates) * value).astype(jnp.bfloat16)
 
             for copy in stores(part, at):
                 copy.start()
 
-        state["count"], state["last"] = (count + 1, pair)
-        state.setdefault("all", []).append(pair)
-
-    gather = Gather(size, me, whole, sems)
-    gather.pairs(work)
+    def unit_stores():
+        return [
+            pltpu.make_async_copy(
+                wu_ref.at[pl.ds(lane * each, each)], wu_out.at[lane, 0], keep_units.at[lane]
+            )
+            for lane in range(lanes)
+        ]
+
+    last = len(gather.patterns) - 1
+    done = 0
+    lane_send(1)
+    for index, pattern in enumerate(gather.patterns):
+        if index:
+            passed = range(index, index + 1) if index < last else range(last, lanes)
+            for distance in passed:
+                if distance < lanes:
+                    relay(distance)
+        if index == last:
+            for copy in unit_stores():
+                copy.start()
+            while done < 2 * last:
+                ups(done)
+                done += 1
+        for part in range(PARTS):
+            gather.arrive(part, pattern)
+        for part in range(PARTS):
+            gather.forward(part, pattern)
+        if index == 0:
+            for copy in loads[2:]:
+                copy.wait()
+        gates(2 * index)
+        for part in range(PARTS):
+            gather.core_copy(part, pattern).wait_recv()
+        gates(2 * index + 1)
+    while done < len(groups):
+        ups(done)
+        done += 1
     gather.finish()
+    for distance in range(1, lanes):
+        for side in (0, 1):
+
+            @pl.when(sends(side, distance))
+            def _():
+                lane_copy(side, distance).wait_send()
+
     for part in range(PARTS):
-        for copy in stores(part, state["last"][part]):
+        for copy in stores(part, pair_of(len(groups) - 1)[part]):
             copy.wait()
-        for count, pair in enumerate(state["all"]):
-            pltpu.make_async_copy(
-                whole.at[pair[part], part], x_out.at[pair[part], part], keep.at[part, count]
-            ).wait()
-
-
-def gate_up(size, values, units):
+    for number in range(len(groups)):
+        for copy in keeps(number):
+            copy.wait()
+    for copy in unit_stores():
+        copy.wait()
+
+
+def gate_up(size, values, units_gate, mine_up):
     own, width = values.shape
-    lanes, _, each, _ = units.shape
+    lanes, _, each, _ = units_gate.shape
     rows, hidden = (own // PARTS, lanes * each)
     any_space = pl.BlockSpec(memory_space=pl.ANY)
     shape = lambda columns, kind: jax.ShapeDtypeStruct((size, PARTS, rows, columns), kind)
-    outs = pl.pallas_call(
+    *outs, units_up = pl.pallas_call(
         functools.partial(gate_up_kernel, size),
         out_shape=(
             shape(width, jnp.bfloat16),
             shape(hidden, jnp.float32),
             shape(hidden, jnp.float32),
             shape(hidden, jnp.bfloat16),
-        ),
-        in_specs=[any_space] * 2,
-        out_specs=(any_space,) * 4,
+            jax.ShapeDtypeStruct(units_gate.shape, jnp.bfloat16),
+        ),
+        in_specs=[any_space] * 3,
+        out_specs=(any_space,) * 5,
         scratch_shapes=[
             pltpu.VMEM((size, PARTS, rows, width), jnp.bfloat16),
             pltpu.VMEM((hidden, width), jnp.bfloat16),
             pltpu.VMEM((hidden, width), jnp.bfloat16),
-            pltpu.VMEM((PARTS, rows, hidden), jnp.float32),
+            pltpu.VMEM((size, PARTS, rows, hidden), jnp.float32),
             pltpu.VMEM((PARTS, rows, hidden), jnp.float32),
             pltpu.VMEM((PARTS, rows, hidden), jnp.bfloat16),
-            pltpu.SemaphoreType.DMA((1 + 2 * lanes,)),
+            pltpu.SemaphoreType.DMA((2 + lanes,)),
             pltpu.SemaphoreType.DMA((PARTS, size)),
-            pltpu.SemaphoreType.DMA((PARTS, 3)),
+            pltpu.SemaphoreType.DMA((PARTS, size)),
+            pltpu.SemaphoreType.DMA((lanes,)),
+            pltpu.SemaphoreType.DMA((PARTS, 2)),
+            pltpu.SemaphoreType.DMA((2, lanes - 1)),
+            pltpu.SemaphoreType.DMA((2, lanes - 1)),
             *gather_semaphores(size),
         ],
         compiler_params=pltpu.CompilerParams(
@@ -421,8 +546,8 @@
             flops=4 * size * own * width * hidden, bytes_accessed=200 * 1024 * 1024, transcendentals=0
         ),
         name="gate_up",
-    )(values.reshape(PARTS, rows, width), units)
-    return tuple(out.reshape(size * own, -1) for out in outs)
+    )(values.reshape(PARTS, rows, width), units_gate, mine_up)
+    return (*[out.reshape(size * own, -1) for out in outs], units_up)
 
 
 def grad_hidden_kernel(
@@ -515,16 +640,13 @@
         def _(part):
             at = pick(part, pair)
 
-            @pl.loop(0, hidden // chunk)
-            def _(index):
-                units = pl.ds(pl.multiple_of(index * chunk, chunk), chunk)
-                grads = contract_last(whole[at, part], wd_ref[units, :])
-                gates = gate[part, :, units]
-                sigmoid = jax.nn.sigmoid(gates)
-                dgate[part, :, units] = (
-                    grads * up[part, :, units] * sigmoid * (1.0 + gates * (1.0 - sigmoid))
-                ).astype(jnp.bfloat16)
-                dup[part, :, units] = (grads * (gates * sigmoid)).astype(jnp.bfloat16)
+            grads = contract_last(whole[at, part], wd_ref[...])
+            gates = gate[part]
+            sigmoid = jax.nn.sigmoid(gates)
+            dgate[part] = (
+                grads * up[part] * sigmoid * (1.0 + gates * (1.0 - sigmoid))
+            ).astype(jnp.bfloat16)
+            dup[part] = (grads * (gates * sigmoid)).astype(jnp.bfloat16)
 
         for part in range(PARTS):
             for copy in stores(part, pair[part]):
@@ -611,8 +733,8 @@
 
 
 def sum_products_kernel(size, terms, *refs):
-    left_in, right_in, out = (refs[:terms], refs[terms], refs[terms + 1])
-    at = terms + 2
+    left_in, right_in, out = (refs[:terms], refs[terms : 2 * terms], refs[2 * terms])
+    at = 2 * terms + 1
     lefts, rights, (w_load, x_load) = (
         refs[at : at + terms],
         refs[at + terms : at + 2 * terms],
@@ -645,8 +767,8 @@
             copy.wait()
 
     weights = []
-    for kind, right in enumerate(rights):
-        weights += unit_loads(right_in, kind, right, w_load.at[kind])
+    for i, (source, right) in enumerate(zip(right_in, rights)):
+        weights += unit_loads(source, 0, right, w_load.at[i])
     for copy in weights:
         copy.start()
     order = [bits[::-1] for bits in orders(size)]
@@ -665,14 +787,14 @@
 
 def sum_products(size, number, lefts, units):
     total, hidden = lefts[0].shape
-    lanes, _, _, width = units.shape
+    lanes, _, _, width = units[0].shape
     rows = total // size // PARTS
     vmem = pl.BlockSpec(memory_space=pltpu.VMEM)
     terms = len(lefts)
     out = pl.pallas_call(
         functools.partial(sum_products_kernel, size, terms),
         out_shape=jax.ShapeDtypeStruct((PARTS, rows, width), jnp.float32),
-        in_specs=[pl.BlockSpec(memory_space=pl.ANY)] * (terms + 1),
+        in_specs=[pl.BlockSpec(memory_space=pl.ANY)] * (2 * terms),
         out_specs=vmem,
         scratch_shapes=[
             *[pltpu.VMEM((size, PARTS, rows, hidden), jnp.bfloat16)] * terms,
@@ -688,7 +810,7 @@
             flops=2 * total * hidden * width * terms, bytes_accessed=200 * 1024 * 1024, transcendentals=0
         ),
         name="sum_products",
-    )(*[left.reshape(size, PARTS, rows, hidden) for left in lefts], units)
+    )(*[left.reshape(size, PARTS, rows, hidden) for left in lefts], *units)
     return out.reshape(PARTS * rows, width)
 
 
@@ -702,7 +824,8 @@
     c_ref,
     before,
     whole,
-    mine_pair,
+    mine_gate,
+    mine_up,
     mine_down,
     count,
     counts,
@@ -718,7 +841,7 @@
     *sems,
 ):
     me, z = (lax.axis_index("fsdp"), lax.axis_index("tp"))
-    mine = (mine_pair.at[0], mine_pair.at[1], mine_down.at[0])
+    mine = (mine_gate.at[0], mine_up.at[0], mine_down.at[0])
     span = m_ref.shape[-1]
     part_of = lambda device: pl.ds(pl.multiple_of(device * span, span), span)
     local = [pltpu.make_async_copy(w_ref, whole.at[me, z], loads.at[0])]
@@ -860,18 +983,17 @@
     other_kinds = pltpu.SemaphoreType.DMA((size - 1, kinds))
     line = pltpu.SemaphoreType.DMA((2 * lanes - 2,))
     hop = pltpu.SemaphoreType.DMA((back,))
-    mine = lambda number: jax.ShapeDtypeStruct((number, rows, size * columns), units.dtype)
+    mine = jax.ShapeDtypeStruct((1, rows, size * columns), units.dtype)
     return pl.pallas_call(
         functools.partial(enter_kernel, size, lanes, back),
         out_shape=(
             jax.ShapeDtypeStruct((back, *values.shape), values.dtype),
             jax.ShapeDtypeStruct((size, lanes, *weights.shape), weights.dtype),
-            mine(2),
-            mine(1),
+            *[mine] * kinds,
             jax.ShapeDtypeStruct(count.shape, count.dtype),
         ),
         in_specs=[any_space, any_space, any_space, vmem],
-        out_specs=(any_space,) * 4 + (vmem,),
+        out_specs=(any_space,) * 5 + (vmem,),
         scratch_shapes=[
             pltpu.VMEM((size, *count.shape), count.dtype),
             pltpu.SemaphoreType.DMA((kinds + 1,)),
@@ -979,10 +1101,16 @@
         self.out[...] = total
 
 
-def lanes_scratch(lanes, rows, width):
+class PartLanes(Lanes):
+    def block(self, lane):
+        width = self.out.shape[2]
+        return self.values[:, :, pl.ds(pl.multiple_of(lane * width, width), width)]
+
+
+def lanes_scratch(lanes, shape):
     return [
-        pltpu.VMEM((lanes - 1, rows, width), jnp.bfloat16),
-        pltpu.VMEM((lanes - 1, rows, width), jnp.bfloat16),
+        pltpu.VMEM((lanes - 1, *shape), jnp.bfloat16),
+        pltpu.VMEM((lanes - 1, *shape), jnp.bfloat16),
         pltpu.SemaphoreType.DMA((lanes - 1,)),
         pltpu.SemaphoreType.DMA((lanes - 1,)),
     ]
@@ -998,11 +1126,11 @@
 
 
 def sum_query_kernel(
-    size, lanes, left_ref, right_ref, units_ref, sums_ref, out, back, lane_out, left, right, loads, *refs
+    size, left_ref, right_ref, units_ref, out, back, left, right, loads, *refs
 ):
-    units_sems, lane_refs = (refs[:3], refs[3:7])
-    made, held, sent, came, *sems = refs[7:]
-    me, z = (lax.axis_index("fsdp"), lax.axis_index("tp"))
+    units_sems = refs[:3]
+    made, held, sent, came, *sems = refs[3:]
+    me = lax.axis_index("fsdp")
     width = out.shape[-1]
     rows = left.shape[1] // size
     copies = [pltpu.make_async_copy(left_ref, left, loads.at[PARTS])]
@@ -1014,7 +1142,12 @@
     ]
     for copy in copies:
         copy.start()
-    greet_all(me, z, size, lanes)
+    barrier = pltpu.get_barrier_semaphore()
+    for other in range(1, size):
+        pl.semaphore_signal(
+            barrier, inc=1, device_id={"fsdp": flip(me, other)}, device_id_type=MESH
+        )
+    pl.semaphore_wait(barrier, size - 1)
     for copy in copies:
         copy.wait()
 
@@ -1023,41 +1156,34 @@
         return contract_first(block, right[part, :, columns])
 
     units = Units(size, me, units_ref, back, units_sems)
-    across = Lanes(lanes, z, sums_ref, lane_out, *lane_refs)
     calls, finish = scatter_steps(size, me, made, held, sent, came, sems, partial, out)
     for number, call in enumerate(calls):
         call()
-        if number == 1:
-            across.start()
         if number == len(calls) // 2:
             units.start()
-    across.finish()
     units.finish()
     finish()
 
 
-def sum_query(size, lanes, left, right, units, sums):
+def sum_query(size, left, right, units):
     tokens, depth = left.shape
     width = right.shape[1] // PARTS
     rows = depth // size
-    lane_width = sums.shape[2] * PARTS // lanes
     any_space = pl.BlockSpec(memory_space=pl.ANY)
     vmem = pl.BlockSpec(memory_space=pltpu.VMEM)
     return pl.pallas_call(
-        functools.partial(sum_query_kernel, size, lanes),
+        functools.partial(sum_query_kernel, size),
         out_shape=(
             jax.ShapeDtypeStruct((PARTS, rows, width), jnp.float32),
             jax.ShapeDtypeStruct((size, *units.shape[:2], rows), jnp.bfloat16),
-            jax.ShapeDtypeStruct((rows, lane_width), jnp.float32),
-        ),
-        in_specs=[any_space] * 3 + [vmem],
-        out_specs=(vmem, any_space, vmem),
+        ),
+        in_specs=[any_space] * 3,
+        out_specs=(vmem, any_space),
         scratch_shapes=[
             pltpu.VMEM((tokens, depth), jnp.bfloat16),
             pltpu.VMEM((PARTS, tokens, width), jnp.bfloat16),
             pltpu.SemaphoreType.DMA((PARTS + 1,)),
             *units_scratch(size, units.shape[0]),
-            *lanes_scratch(lanes, rows, lane_width),
             *scatter_scratch(size, rows, width),
         ],
         compiler_params=pltpu.CompilerParams(
@@ -1067,7 +1193,7 @@
             flops=4 * tokens * depth * width, bytes_accessed=100 * 1024 * 1024, transcendentals=0
         ),
         name="sum_query",
-    )(left, right, units, sums)
+    )(left, right, units)
 
 
 def sum_key_kernel(
@@ -1078,11 +1204,13 @@
     kv_ref,
     w_ref,
     units_ref,
-    sums_ref,
+    out_sums,
+    query_sums,
     out,
     low,
     back,
     lane_out,
+    lane_query,
     left,
     right,
     loads,
@@ -1090,8 +1218,8 @@
     fetch,
     *refs,
 ):
-    units_sems, lane_refs = (refs[:3], refs[3:7])
-    made, held, sent, came, *sems = refs[7:]
+    units_sems, lane_refs = (refs[:3], refs[3:11])
+    made, held, sent, came, *sems = refs[11:]
     me, z = (lax.axis_index("fsdp"), lax.axis_index("tp"))
     rows = left.shape[1] // size
     parts, span = (w_ref.shape[1], tiles.shape[-1])
@@ -1139,13 +1267,16 @@
             low[span_rows, f * rows : (f + 1) * rows] = total
 
     units = Units(size, me, units_ref, back, units_sems)
-    across = Lanes(lanes, z, sums_ref, lane_out, *lane_refs)
+    across = (
+        Lanes(lanes, z, out_sums, lane_out, *lane_refs[:4]),
+        Lanes(lanes, z, query_sums, lane_query, *lane_refs[4:]),
+    )
     calls, finish = scatter_steps(size, me, made, held, sent, came, sems, partial, out)
     done = 0
     for number, call in enumerate(calls):
         call()
-        if number == 1:
-            across.start()
+        if number < 2:
+            across[number].start()
         if number == len(calls) // 2:
             units.start()
         goal = size * max(0, number - 1) // max(1, len(calls) - 3)
@@ -1155,18 +1286,19 @@
     while done < size:
         low_columns(done)
         done += 1
-    across.finish()
+    for one in across:
+        one.finish()
     units.finish()
     finish()
 
 
-def sum_key(size, lanes, left, grad_query, grad_pair, weights, units, sums):
+def sum_key(size, lanes, left, grad_query, grad_pair, weights, units, *sums):
     tokens, depth = left.shape
     width = grad_pair.shape[2]
     rows = depth // size
     parts = weights.shape[1]
     span = (grad_query.shape[1] + PARTS * width) // parts
-    lane_width = sums.shape[2] * PARTS // lanes
+    lane_width = sums[0].shape[2] * PARTS // lanes
     any_space = pl.BlockSpec(memory_space=pl.ANY)
     vmem = pl.BlockSpec(memory_space=pltpu.VMEM)
     return pl.pallas_call(
@@ -1175,10 +1307,10 @@
             jax.ShapeDtypeStruct((PARTS, rows, width), jnp.float32),
             jax.ShapeDtypeStruct((tokens, depth), jnp.float32),
             jax.ShapeDtypeStruct((size, *units.shape[:2], rows), jnp.bfloat16),
-            jax.ShapeDtypeStruct((rows, lane_width), jnp.float32),
-        ),
-        in_specs=[any_space, vmem, any_space, any_space, any_space, vmem],
-        out_specs=(vmem, vmem, any_space, vmem),
+            *[jax.ShapeDtypeStruct((rows, lane_width), jnp.float32)] * 2,
+        ),
+        in_specs=[any_space, vmem, any_space, any_space, any_space, vmem, vmem],
+        out_specs=(vmem, vmem, any_space, vmem, vmem),
         scratch_shapes=[
             pltpu.VMEM((tokens, depth), jnp.bfloat16),
             pltpu.VMEM((PARTS, tokens, width), jnp.bfloat16),
@@ -1186,7 +1318,8 @@
             pltpu.VMEM((2, parts, rows, span), jnp.bfloat16),
             pltpu.SemaphoreType.DMA((2,)),
             *units_scratch(size, units.shape[0]),
-            *lanes_scratch(lanes, rows, lane_width),
+            *lanes_scratch(lanes, (rows, lane_width)),
+            *lanes_scratch(lanes, (rows, lane_width)),
             *scatter_scratch(size, rows, width),
         ],
         compiler_params=pltpu.CompilerParams(
@@ -1196,10 +1329,10 @@
             flops=8 * tokens * depth * width, bytes_accessed=100 * 1024 * 1024, transcendentals=0
         ),
         name="sum_key",
-    )(left, grad_query, grad_pair, weights, units, sums)
-
-
-def sum_small_kernel(size, lanes, x_ref, o_ref, came, send, recv):
+    )(left, grad_query, grad_pair, weights, units, *sums)
+
+
+def last_kernel(size, lanes, x_ref, sums_ref, o_ref, lane_out, came, send, recv, *lane_refs):
     me, z = (lax.axis_index("fsdp"), lax.axis_index("tp"))
     peers = []
     for name, index, count in (("fsdp", me, size), ("tp", z, lanes)):
@@ -1208,9 +1341,13 @@
             peers.append({name: flip(index, bit)})
             bit *= 2
     barrier = pltpu.get_barrier_semaphore()
-    for peer in peers:
+    greeted = [{"fsdp": flip(me, bit)} for bit in [1] + chip_bits(size)]
+    greeted += [{"tp": lax.rem(z + hop, lanes)} for hop in range(1, lanes)]
+    for peer in greeted:
         pl.semaphore_signal(barrier, inc=1, device_id=peer, device_id_type=MESH)
-    pl.semaphore_wait(barrier, len(peers))
+    pl.semaphore_wait(barrier, len(greeted))
+    across = PartLanes(lanes, z, sums_ref, lane_out, *lane_refs)
+    across.start()
     sent = came.shape[0] // 2
     came[sent] = x_ref[...]
     for step, peer in enumerate(peers):
@@ -1226,24 +1363,33 @@
         copy.wait()
         came[sent + step + 1] = came[sent + step] + came[step]
     o_ref[...] = came[sent + len(peers)]
-
-
-def sum_small(size, lanes, values):
+    across.finish()
+
+
+def last_sums(size, lanes, values, sums):
     steps = (size * lanes).bit_length() - 1
     vmem = pl.BlockSpec(memory_space=pltpu.VMEM)
+    parts, rows, columns = sums.shape
+    shape = (parts, rows, columns // lanes)
     return pl.pallas_call(
-        functools.partial(sum_small_kernel, size, lanes),
-        out_shape=jax.ShapeDtypeStruct(values.shape, values.dtype),
-        in_specs=[vmem],
-        out_specs=vmem,
+        functools.partial(last_kernel, size, lanes),
+        out_shape=(
+            jax.ShapeDtypeStruct(values.shape, values.dtype),
+            jax.ShapeDtypeStruct(shape, jnp.float32),
+        ),
+        in_specs=[vmem, vmem],
+        out_specs=(vmem, vmem),
         scratch_shapes=[
             pltpu.VMEM((2 * (steps + 1), *values.shape), values.dtype),
             pltpu.SemaphoreType.DMA((steps,)),
             pltpu.SemaphoreType.DMA((steps,)),
+            *lanes_scratch(lanes, shape),
         ],
-        compiler_params=pltpu.CompilerParams(collective_id=8, has_side_effects=True),
-        name="sum_small",
-    )(values)
+        compiler_params=pltpu.CompilerParams(
+            collective_id=8, has_side_effects=True, vmem_limit_bytes=VMEM
+        ),
+        name="last_sums",
+    )(values, sums)
 
 
 def project_kernel(
@@ -1251,7 +1397,7 @@
 ):
     back, own, _ = before_ref.shape
     lead = back * own
-    tile = min(256, own)
+    tile = min(512, own)
     z = lax.axis_index("tp")
 
     @pl.when(pl.program_id(0) == 0)
@@ -1398,10 +1544,10 @@
 
 
 def head_probs(query, keys, bias, group, scale):
-    scores = contract_last(query, keys) * scale
+    scores = contract_last(query, keys) * (scale * LOG2E)
     rows, span = scores.shape
     scores = (scores.reshape(group, rows // group, span) + bias[None]).reshape(rows, span)
-    weights = jnp.exp(scores - jnp.max(scores, axis=-1, keepdims=True))
+    weights = jnp.exp2(scores)
     return weights * (1.0 / jnp.sum(weights, axis=-1, keepdims=True))
 
 
@@ -1739,12 +1885,6 @@
     return (bias, cosine, sine, step, live[lead:].astype(jnp.float32))
 
 
-def over_lanes(grad):
-    return lax.psum_scatter(
-        grad.astype(jnp.bfloat16), "tp", scatter_dimension=2, tiled=True
-    ).astype(jnp.float32)
-
-
 def shards(
     states,
     lengths,
@@ -1779,11 +1919,11 @@
         part.reshape(n_fsdp, -1, part.shape[1]) for part in (w_gate.T, w_up.T, w_down)
     ]
     live_here = jnp.full((8, 128), jnp.sum(padding).astype(jnp.float32))
-    before, weights_attn, mine_pair, mine_down, counts = enter(
+    before, weights_attn, mine_gate, mine_up, mine_down, counts = enter(
         n_fsdp, n_tp, back, states, joined, jnp.stack(units, axis=1), live_here
     )
     count = counts[0, 0]
-    units_pair = lax.all_gather(mine_pair, "tp", axis=0)
+    units_gate = lax.all_gather(mine_gate, "tp", axis=0)
     units_down = lax.all_gather(mine_down, "tp", axis=0)
     normed_in, query_raw, key_raw, value = project(
         before, states, norm_attn, weights_attn, wq, wk
@@ -1793,10 +1933,10 @@
     inputs = states.astype(jnp.float32)
     hidden_one = project_out(attended, weights_attn, states, wo)
     normed_two, factor_two = normalize_rows(hidden_one)
-    whole_two, gate, up, product = gate_up(
-        n_fsdp, (normed_two * norm_mlp).astype(jnp.bfloat16), units_pair
+    whole_two, gate, up, product, units_up = gate_up(
+        n_fsdp, (normed_two * norm_mlp).astype(jnp.bfloat16), units_gate, mine_up
     )
-    outputs = hidden_one + sum_products(n_fsdp, 2, (product,), units_down)
+    outputs = hidden_one + sum_products(n_fsdp, 2, (product,), (units_down,))
     errors = (outputs - teacher.astype(jnp.float32)) * live[:, None]
     squares = jnp.sum(errors * errors)
     grad_out = errors * (2.0 / (count * D))
@@ -1805,7 +1945,7 @@
         n_fsdp, grad_out.astype(jnp.bfloat16), units_down, gate, up, product, whole_two
     )
     units_early = lax.psum_scatter(units_early, "tp", scatter_dimension=0)
-    grad_mid = sum_products(n_fsdp, 4, (grad_gate, grad_up), units_pair)
+    grad_mid = sum_products(n_fsdp, 4, (grad_gate, grad_up), (units_gate, units_up))
     grad_norm_mlp = jnp.sum(grad_mid * normed_two, axis=0)
     grad_hidden = grad_out + norm_back(grad_mid, normed_two, factor_two, norm_mlp)
 
@@ -1829,13 +1969,18 @@
     )
     units_late, grad_query = lax.optimization_barrier((units_late, grad_query))
     units_late = lax.psum_scatter(units_late, "tp", scatter_dimension=0)
-    sums_query, back_early, grad_w_out = sum_query(
-        n_fsdp, n_tp, normed_in, grad_query, units_early, sums_out
+    sums_query, back_early = sum_query(n_fsdp, normed_in, grad_query, units_early)
+    sums_pair, grad_low, back_late, grad_w_out, grad_w_query = sum_key(
+        n_fsdp,
+        n_tp,
+        normed_in,
+        grad_query,
+        grad_pair,
+        weights_attn,
+        units_late,
+        sums_out,
+        sums_query,
     )
-    sums_pair, grad_low, back_late, grad_w_query = sum_key(
-        n_fsdp, n_tp, normed_in, grad_query, grad_pair, weights_attn, units_late, sums_query
-    )
-    grad_w_pair = over_lanes(sums_pair)
     grad_w_down, grad_w_gate, grad_w_up = [
         part.reshape(-1, part.shape[2]).astype(jnp.float32)
         for part in (back_early[:, 0], back_early[:, 1], back_late[:, 0])
@@ -1848,7 +1993,8 @@
     joined_small = jnp.concatenate(small).reshape(-1, HD)
     filled = joined_small.shape[0]
     joined_small = jnp.pad(joined_small, ((0, -filled % 8), (0, 0)))
-    summed = sum_small(n_fsdp, n_tp, joined_small)[:filled].reshape(-1)
+    summed, grad_w_pair = last_sums(n_fsdp, n_tp, joined_small, sums_pair)
+    summed = summed[:filled].reshape(-1)
     grad_norm_attn, grad_norm_mlp = (summed[:D], summed[D : 2 * D])
     grad_norm_query, grad_norm_key = (summed[2 * D : 2 * D + HD], summed[2 * D + HD : 2 * D + 2 * HD])
     squares = summed[2 * D + 2 * HD]

time: 998 us -> 984 us (0.986)
  waiting for transfers between devices: 37.8 us -> 0.81 us
  Pallas kernels: 862 us -> 886 us
    pallas_call x1, Pallas kernels: 84.1 us -> 119 us  [gate_up(): pl.pallas_call(functools.partial(gate_up_kernel, size), out_shape=(shape(...]
    all_gather x1, waiting for transfers between devices: 22.7 us -> 0.01 us  [shards(): units_gate = lax.all_gather(mine_gate, 'tp', axis=0)]
    reduce_scatter x1, waiting for transfers between devices: 11.6 us -> 0.02 us  [shards(): units_late = lax.psum_scatter(units_late, 'tp', scatter_dimension=0)]
  transfers between devices with their start and end apart: 5 -> 4, of which waited for: 3 -> 0; matrix products, arithmetic and copies ran while one was open for 4% -> 2% of each run, Pallas kernels for 46% -> 48%
where the time goes in v6:
time: 984 us; the launch traced here: 977 us
  Pallas kernels  886 us (90%)
  other arithmetic  46.5 us (5%)
  local copies, waits for them, and re-layouts  26.2 us (3%)
  between operations  17.6 us (2%)
    pallas_call x2, Pallas kernels, sum_products(): pl.pallas_call(functools.partial(sum_products_kernel, size, terms), out_s...  174 us
    pallas_call x1, Pallas kernels, enter(): pl.pallas_call(functools.partial(enter_kernel, size, lanes, back), out_sh...  142 us
    pallas_call x1, Pallas kernels, gate_up(): pl.pallas_call(functools.partial(gate_up_kernel, size), out_shape=(shape(...  119 us
    pallas_call x1, Pallas kernels, attend_back(): pl.pallas_call(functools.partial(attend_back_kernel, group, step, lead, s...  113 us
    pallas_call x1, Pallas kernels, grad_hidden_units(): pl.pallas_call(functools.partial(grad_hidden_kernel, size), out_shape=(sh...  98.8 us
    pallas_call x1, Pallas kernels, sum_query(): pl.pallas_call(functools.partial(sum_query_kernel, size), out_shape=(jax....  59.5 us
    pallas_call x1, Pallas kernels, sum_key(): pl.pallas_call(functools.partial(sum_key_kernel, size, lanes), out_shape=...  58.3 us
    pallas_call x1, Pallas kernels, attend(): pl.pallas_call(functools.partial(attend_kernel, group, step, rows - own),...  43.7 us
  transfers between devices with their start and end apart: 4, of which 0 were waited for; matrix products, arithmetic and copies ran while one was open for 2% of the time, Pallas kernels for 48%

profile of v6, /device:TPU:0, one launch (start us, length us, event | category | flops | bytes accessed | tf_op | source)
XLA Modules:
  0.0 977.2 jit_solution(15978779540507788910)
XLA Ops:
  16.5 141.5 %enter.1 = (bf16[2,512,2048]{2,1,0:T(8,128)(2,1)}, bf16[8,4,256,1536]{3,2,1,0:T(8,128)(2,1)}, bf16[1,192,2048]{2,1,0:T(8,128)(2,1)}, bf16[1,192,2048]{2,1,0:T(8,...) custom-call(bf16[512,2048]{1,0:T(8,128)(2,1)} %x_ref.5, bf16[256,1536]{1,0:T(8,128)(2,1)} %pad_maximum_fusion.1.w_ref, ...), custom_call_target="tpu_custom_call" | custom-call | bytes 419430400 | tf_op jit(solution)/shard_map/enter/pallas_call | solution.py:987
  162.6 2.8 fusion.16
  165.4 28.4 %project_in.1 = (bf16[512,2048]{1,0:T(8,128)(2,1)}, f32[512,2048]{1,0:T(8,128)}, f32[1536,1024]{1,0:T(8,128)}, bf16[1536,1024]{1,0:T(8,128)(2,1)}) custom-call(bf16[2,512,2048]{2,1,0:T(8,128)(2,1)} %get-tuple-element.49.before_ref, bf16[512,2048]{1,0:T(8,128)(2,1)} %x_ref.5, f32[1,2048]{1,0:T(1,128)} %bitcast.80, ...), custom_call_target="tpu_custom_call" | custom-call | flops 17179869184 | bytes 23068672 | tf_op jit(solution)/shard_map/project_in/pallas_call | solution.py:1441
  195.4 43.7 %attend.1.a_ref.right_ref = bf16[512,2048]{1,0:T(8,128)(2,1)} custom-call(f32[512,2048]{1,0:T(8,128)} %get-tuple-element.51.q_ref, f32[1536,1024]{1,0:T(8,128)} %get-tuple-element.52.k_ref, bf16[1536,1024]{1,0:T(8,128)(2,1)} %get-tuple-element.53.v_ref, f32[512,1280]{1,0:T(8,128)} %add_select_fusion.bias_ref, f32[1536,128]{1,0:T(8,128)} %get-tuple-element.161.cos_ref, ...), custom_call_target="tpu_custom_call" | custom-call | flops 21474836480 | bytes 13631488 | tf_op jit(solution)/shard_map/attend/pallas_call | solution.py:1774
  241.1 11.6 %project_out.1 = f32[512,2048]{1,0:T(8,128)} custom-call(bf16[512,2048]{1,0:T(8,128)(2,1)} %attend.1.a_ref.right_ref, bf16[8,4,256,1536]{3,2,1,0:T(8,128)(2,1)} %get-tuple-element.50.w_ref, bf16[512,2048]{1,0:T(8,128)(2,1)} %x_ref.5), custom_call_target="tpu_custom_call" | custom-call | flops 4294967296 | bytes 25165824 | tf_op jit(solution)/shard_map/project_out/pallas_call | solution.py:1485
  252.7 2.7 multiply_reduce_fusion.2
  257.9 118.9 %gate_up.1 = (bf16[8,2,256,2048]{3,2,1,0:T(8,128)(2,1)}, f32[8,2,256,768]{3,2,1,0:T(8,128)}, f32[8,2,256,768]{3,2,1,0:T(8,128)}, bf16[8,2,256,768]{3,2,1,0:T(8,128)(2,1)}, bf16[4,1,192,2048]{3,2,1,0:T(8,128)(2,1)}) custom-call(bf16[2,256,2048]{2,1,0:T(8,128)(2,1)} %bitcast.67, bf16[4,1,192,2048]{3,2,1,0:T(8,128)(2,1)} %bitcast.84, ...), custom_call_target="tpu_custom_call" | custom-call | flops 25769803776 | bytes 209715200 | tf_op jit(solution)/shard_map/gate_up/pallas_call | solution.py:515
  376.8 83.7 %sum_products.2 = f32[2,256,2048]{2,1,0:T(8,128)} custom-call(bf16[8,2,256,768]{3,2,1,0:T(8,128)(2,1)} %get-tuple-element.56.refs_0_.prod_in, bf16[4,1,192,2048]{3,2,1,0:T(8,128)(2,1)} %bitcast.86), custom_call_target="tpu_custom_call" | custom-call | flops 12884901888 | bytes 209715200 | tf_op jit(solution)/shard_map/sum_products/pallas_call | solution.py:794
  460.5 4.4 multiply_reduce_fusion
  465.0 2.4 multiply_convert_fusion.1
  467.6 98.8 %grad_hidden_units.1 = (bf16[8,2,256,768]{3,2,1,0:T(8,128)(2,1)}, bf16[8,2,256,768]{3,2,1,0:T(8,128)(2,1)}, bf16[4,2,192,2048]{3,2,1,0:T(8,128)(2,1)}, bf16[4,1,192,2048]{3,2,1,0:T(8,128)(2,1)}) custom-call(bf16[2,256,2048]{2,1,0:T(8,128)(2,1)} %bitcast.68, bf16[4,1,192,2048]{3,2,1,0:T(8,128)(2,1)} %bitcast.87, ...), custom_call_target="tpu_custom_call" | custom-call | flops 51539607552 | bytes 209715200 | tf_op jit(solution)/shard_map/grad_hidden_units/pallas_call | solution.py:703
  566.5 89.9 %sum_products.3 = f32[2,256,2048]{2,1,0:T(8,128)} custom-call(bf16[8,2,256,768]{3,2,1,0:T(8,128)(2,1)} %get-tuple-element.64.refs_0_, bf16[8,2,256,768]{3,2,1,0:T(8,128)(2,1)} %get-tuple-element.65.refs_1_, bf16[4,1,192,2048]{3,2,1,0:T(8,128)(2,1)} %bitcast.85, bf16[4,1,192,2048]{3,2,1,0:T(8,128)(2,1)} %get-tuple-element.66.refs_3_), custom_call_target="tpu_custom_call" | custom-call | flops 25769803776 | bytes 209715200 | tf_op jit(solution)/shard_map/sum_products/pallas_call | solution.py:794
  656.5 3.3 fusion.9
  661.2 4.5 fusion.22
  665.7 8.8 back_out.1.do_ref
  674.6 112.6 %attend_back.1 = (bf16[512,2048]{1,0:T(8,128)(2,1)}, bf16[2,512,1024]{2,1,0:T(8,128)(2,1)}, f32[1,128]{1,0:T(1,128)}, f32[1,128]{1,0:T(1,128)}, f32[2,256,1024]{2,1,0:T(8,128)}) custom-call(f32[512,2048]{1,0:T(8,128)} %get-tuple-element.51.q_ref, f32[1536,1024]{1,0:T(8,128)} %get-tuple-element.52.k_ref, bf16[1536,1024]{1,0:T(8,128)(2,1)} %get-tuple-element.53.v_ref, ...), custom_call_target="tpu_custom_call" | custom-call | flops 53687091200 | bytes 33554432 | tf_op jit(solution)/shard_map/attend_back/pallas_call | solution.py:1818
  789.2 59.5 %sum_query.1 = (f32[2,256,1024]{2,1,0:T(8,128)}, bf16[8,2,192,256]{3,2,1,0:T(8,128)(2,1)}) custom-call(bf16[512,2048]{1,0:T(8,128)(2,1)} %get-tuple-element.58.left_ref, bf16[512,2048]{1,0:T(8,128)(2,1)} %get-tuple-element.68.right_ref.q_ref, bf16[2,192,2048]{2,1,0:T(8,128)(2,1)} %bitcast.88), custom_call_target="tpu_custom_call" | custom-call | flops 4294967296 | bytes 104857600 | tf_op jit(solution)/shard_map/sum_query/pallas_call | solution.py:1174
  848.8 58.3 %sum_key.1 = (f32[2,256,1024]{2,1,0:T(8,128)}, f32[512,2048]{1,0:T(8,128)}, bf16[8,1,192,256]{3,2,1,0:T(8,128)(2,1)}, f32[256,512]{1,0:T(8,128)}, f32[256,512]{1,0:T(8,128)}) custom-call(bf16[512,2048]{1,0:T(8,128)(2,1)} %get-tuple-element.58.left_ref, bf16[512,2048]{1,0:T(8,128)(2,1)} %get-tuple-element.68.right_ref.q_ref, ...), custom_call_target="tpu_custom_call" | custom-call | flops 8589934592 | bytes 104857600 | tf_op jit(solution)/shard_map/sum_key/pallas_call | solution.py:1304
  907.1 3.3 fusion.4
  911.8 30.2 %last_sums.1 = (f32[40,128]{1,0:T(8,128)}, f32[2,256,256]{2,1,0:T(8,128)}) custom-call(f32[40,128]{1,0:T(8,128)} %pad.5.x_ref, f32[2,256,1024]{2,1,0:T(8,128)} %get-tuple-element.77.sums_ref), custom_call_target="tpu_custom_call" | custom-call | tf_op jit(solution)/shard_map/last_sums/pallas_call | solution.py:1374
  952.1 3.0 copy.44
  955.2 2.4 bitcast_convert_fusion.1
  957.6 3.0 copy.45
  961.9 6.6 fusion.7
  (97 shorter events, 35.2 us)
Async XLA Ops:
  7.2 6.1 copy-start.8
  7.2 7.8 copy-start.12
  7.2 7.7 copy-start.13
  7.2 7.7 copy-start.11
  7.2 250.6 %all-gather.5.cloned.1.call-start = ((), (), s32[]{:S(2)}) async-start(), calls=%async_computation.4 | async-start | bytes 3932160 | tf_op jit(solution)/shard_map/all_gather | solution.py:1926
  15.0 143.9 %copy-start.17 = (s32[1,4]{1,0:T(1,128)S(1)}, s32[1,4]{1,0:T(1,128)}, u32[]{:S(2)}) copy-start(s32[1,4]{1,0:T(1,128)} %param.16) | copy-start | bytes 52
  15.0 144.3 %copy-start.15 = (s32[1,2048]{1,0:T(1,128)S(1)}, s32[1,2048]{1,0:T(1,128)}, u32[]{:S(2)}) copy-start(s32[1,2048]{1,0:T(1,128)} %param.17) | copy-start | bytes 24580
  158.1 218.7 %all-gather.7.cloned.1.call-start = ((), (), s32[]{:S(2)}) async-start(), calls=%async_computation.5 | async-start | bytes 3932160 | tf_op jit(solution)/shard_map/all_gather | solution.py:1927
  158.8 630.4 %reduce-scatter.5.cloned.1.call-start = ((), (), s32[]{:S(2)}) async-start(), calls=%async_computation.3 | async-start | bytes 7864320 | tf_op jit(solution)/shard_map/reduce_scatter | solution.py:1947
  241.1 14.3 %copy-start.14 = (f32[2048]{0:T(1024)S(1)}, f32[2048]{0:T(1024)}, u32[]{:S(2)}) copy-start(f32[2048]{0:T(1024)} %param.26) | copy-start | bytes 24580
  252.7 3.5 copy-start
  376.8 83.7 %copy-start.1 = (f32[512,2048]{1,0:T(8,128)S(1)}, f32[512,2048]{1,0:T(8,128)}, u32[]{:S(2)}) copy-start(f32[512,2048]{1,0:T(8,128)} %project_out.1) | copy-start | bytes 12582916
  376.8 83.7 %copy-start.6 = (bf16[512,2048]{1,0:T(8,128)(2,1)S(1)}, bf16[512,2048]{1,0:T(8,128)(2,1)}, u32[]{:S(2)}) copy-start(bf16[512,2048]{1,0:T(8,128)(2,1)} %param.18) | copy-start | bytes 6291460
  464.9 2.6 copy-start.4
  566.5 282.3 %reduce-scatter.3.cloned.1.call-start = ((), (), s32[]{:S(2)}) async-start(), calls=%async_computation.2 | async-start | bytes 3932160 | tf_op jit(solution)/shard_map/reduce_scatter | solution.py:1971
  566.5 89.9 %copy-start.2 = (f32[512,2048]{1,0:T(8,128)S(1)}, f32[512,2048]{1,0:T(8,128)}, u32[]{:S(2)}) copy-start(f32[512,2048]{1,0:T(8,128)} %project_out.1) | copy-start | bytes 12582916
  656.5 3.5 copy-start.5
  656.5 4.8 copy-start.7
  787.1 1.6 copy-start.3
  848.7 58.4 %copy-start.16 = (f32[2048]{0:T(1024)S(1)}, f32[2048]{0:T(1024)}, u32[]{:S(2)}) copy-start(f32[2048]{0:T(1024)} %param.19) | copy-start | bytes 24580
  907.1 3.4 copy-start.19
  907.1 3.4 copy-start.18
  907.1 41.2 %copy-start.10 = (f32[256,512]{1,0:T(8,128)S(1)}, f32[256,512]{1,0:T(8,128)}, u32[]{:S(2)}) copy-start(f32[256,512]{1,0:T(8,128)} %get-tuple-element.81) | copy-start | bytes 1572868
  961.9 6.6 copy-start.9
Sparse Core Ops, SparseCore 0:
  158.2 80.5 all-gather.4
  240.3 75.2 all-gather.6
  566.6 110.9 reduce-scatter.4
  787.3 59.8 reduce-scatter.2

commit v7 on v5

--- a/solution.py
+++ b/solution.py
@@ -14,6 +14,7 @@
 EPS = 1e-06
 THETA = 1000000.0
 NEG = -1e30
+LOG2E = 1.4426950408889634
 VMEM = 56 * 1024 * 1024
 
 
@@ -199,7 +200,7 @@
     patterns = scatter_order(steps)
     place = {m: q for q, m in enumerate(patterns)}
     width = final.shape[-1]
-    chunk = min(512, width)
+    chunk = min(1024, width)
 
     def slots(pattern, sibling):
         return [flip(me, mask_of(pattern, order[part]) + sibling) for part in range(PARTS)]
@@ -324,7 +325,6 @@
 ):
     me = lax.axis_index("fsdp")
     hidden = wg_ref.shape[0]
-    chunk = 256 if hidden % 256 == 0 else 128
     lanes = w_in.shape[0]
     loads = [pltpu.make_async_copy(x_ref, whole.at[me], load.at[0])]
     loads += unit_loads(w_in, 0, wg_ref, load.at[pl.ds(1, lanes)])
@@ -358,15 +358,12 @@
                 for copy in stores(part, pick(part, last)):
                     copy.wait()
 
-            @pl.loop(0, hidden // chunk)
-            def _(index):
-                units = pl.ds(pl.multiple_of(index * chunk, chunk), chunk)
-                rows = whole[at, part]
-                gates = contract_last(rows, wg_ref[units, :])
-                ups = contract_last(rows, wu_ref[units, :])
-                gate[part, :, units] = gates
-                up[part, :, units] = ups
-                prod[part, :, units] = (gates * jax.nn.sigmoid(gates) * ups).astype(jnp.bfloat16)
+            rows = whole[at, part]
+            gates = contract_last(rows, wg_ref[...])
+            ups = contract_last(rows, wu_ref[...])
+            gate[part] = gates
+            up[part] = ups
+            prod[part] = (gates * jax.nn.sigmoid(gates) * ups).astype(jnp.bfloat16)
 
             for copy in stores(part, at):
                 copy.start()
@@ -515,16 +512,13 @@
         def _(part):
             at = pick(part, pair)
 
-            @pl.loop(0, hidden // chunk)
-            def _(index):
-                units = pl.ds(pl.multiple_of(index * chunk, chunk), chunk)
-                grads = contract_last(whole[at, part], wd_ref[units, :])
-                gates = gate[part, :, units]
-                sigmoid = jax.nn.sigmoid(gates)
-                dgate[part, :, units] = (
-                    grads * up[part, :, units] * sigmoid * (1.0 + gates * (1.0 - sigmoid))
-                ).astype(jnp.bfloat16)
-                dup[part, :, units] = (grads * (gates * sigmoid)).astype(jnp.bfloat16)
+            grads = contract_last(whole[at, part], wd_ref[...])
+            gates = gate[part]
+            sigmoid = jax.nn.sigmoid(gates)
+            dgate[part] = (
+                grads * up[part] * sigmoid * (1.0 + gates * (1.0 - sigmoid))
+            ).astype(jnp.bfloat16)
+            dup[part] = (grads * (gates * sigmoid)).astype(jnp.bfloat16)
 
         for part in range(PARTS):
             for copy in stores(part, pair[part]):
@@ -610,9 +604,10 @@
     return (dgate.reshape(size * own, hidden), dup.reshape(size * own, hidden), early, late)
 
 
-def sum_products_kernel(size, terms, *refs):
-    left_in, right_in, out = (refs[:terms], refs[terms], refs[terms + 1])
-    at = terms + 2
+def sum_products_kernel(size, kinds, *refs):
+    terms = len(kinds)
+    left_in, right_in, out = (refs[:terms], refs[terms : 2 * terms], refs[2 * terms])
+    at = 2 * terms + 1
     lefts, rights, (w_load, x_load) = (
         refs[at : at + terms],
         refs[at + terms : at + 2 * terms],
@@ -645,8 +640,8 @@
             copy.wait()
 
     weights = []
-    for kind, right in enumerate(rights):
-        weights += unit_loads(right_in, kind, right, w_load.at[kind])
+    for i, (source, right) in enumerate(zip(right_in, rights)):
+        weights += unit_loads(source, kinds[i], right, w_load.at[i])
     for copy in weights:
         copy.start()
     order = [bits[::-1] for bits in orders(size)]
@@ -665,14 +660,14 @@
 
 def sum_products(size, number, lefts, units):
     total, hidden = lefts[0].shape
-    lanes, _, _, width = units.shape
+    lanes, _, _, width = units[0][0].shape
     rows = total // size // PARTS
     vmem = pl.BlockSpec(memory_space=pltpu.VMEM)
     terms = len(lefts)
     out = pl.pallas_call(
-        functools.partial(sum_products_kernel, size, terms),
+        functools.partial(sum_products_kernel, size, tuple(kind for _, kind in units)),
         out_shape=jax.ShapeDtypeStruct((PARTS, rows, width), jnp.float32),
-        in_specs=[pl.BlockSpec(memory_space=pl.ANY)] * (terms + 1),
+        in_specs=[pl.BlockSpec(memory_space=pl.ANY)] * (2 * terms),
         out_specs=vmem,
         scratch_shapes=[
             *[pltpu.VMEM((size, PARTS, rows, hidden), jnp.bfloat16)] * terms,
@@ -688,7 +683,7 @@
             flops=2 * total * hidden * width * terms, bytes_accessed=200 * 1024 * 1024, transcendentals=0
         ),
         name="sum_products",
-    )(*[left.reshape(size, PARTS, rows, hidden) for left in lefts], units)
+    )(*[left.reshape(size, PARTS, rows, hidden) for left in lefts], *[array for array, _ in units])
     return out.reshape(PARTS * rows, width)
 
 
@@ -866,7 +861,7 @@
         out_shape=(
             jax.ShapeDtypeStruct((back, *values.shape), values.dtype),
             jax.ShapeDtypeStruct((size, lanes, *weights.shape), weights.dtype),
-            mine(2),
+            mine(kinds - 1),
             mine(1),
             jax.ShapeDtypeStruct(count.shape, count.dtype),
         ),
@@ -979,10 +974,10 @@
         self.out[...] = total
 
 
-def lanes_scratch(lanes, rows, width):
+def lanes_scratch(lanes, shape):
     return [
-        pltpu.VMEM((lanes - 1, rows, width), jnp.bfloat16),
-        pltpu.VMEM((lanes - 1, rows, width), jnp.bfloat16),
+        pltpu.VMEM((lanes - 1, *shape), jnp.bfloat16),
+        pltpu.VMEM((lanes - 1, *shape), jnp.bfloat16),
         pltpu.SemaphoreType.DMA((lanes - 1,)),
         pltpu.SemaphoreType.DMA((lanes - 1,)),
     ]
@@ -998,11 +993,11 @@
 
 
 def sum_query_kernel(
-    size, lanes, left_ref, right_ref, units_ref, sums_ref, out, back, lane_out, left, right, loads, *refs
+    size, left_ref, right_ref, units_ref, out, back, left, right, loads, *refs
 ):
-    units_sems, lane_refs = (refs[:3], refs[3:7])
-    made, held, sent, came, *sems = refs[7:]
-    me, z = (lax.axis_index("fsdp"), lax.axis_index("tp"))
+    units_sems = refs[:3]
+    made, held, sent, came, *sems = refs[3:]
+    me = lax.axis_index("fsdp")
     width = out.shape[-1]
     rows = left.shape[1] // size
     copies = [pltpu.make_async_copy(left_ref, left, loads.at[PARTS])]
@@ -1014,7 +1009,12 @@
     ]
     for copy in copies:
         copy.start()
-    greet_all(me, z, size, lanes)
+    barrier = pltpu.get_barrier_semaphore()
+    for other in range(1, size):
+        pl.semaphore_signal(
+            barrier, inc=1, device_id={"fsdp": flip(me, other)}, device_id_type=MESH
+        )
+    pl.semaphore_wait(barrier, size - 1)
     for copy in copies:
         copy.wait()
 
@@ -1023,41 +1023,34 @@
         return contract_first(block, right[part, :, columns])
 
     units = Units(size, me, units_ref, back, units_sems)
-    across = Lanes(lanes, z, sums_ref, lane_out, *lane_refs)
     calls, finish = scatter_steps(size, me, made, held, sent, came, sems, partial, out)
     for number, call in enumerate(calls):
         call()
-        if number == 1:
-            across.start()
         if number == len(calls) // 2:
             units.start()
-    across.finish()
     units.finish()
     finish()
 
 
-def sum_query(size, lanes, left, right, units, sums):
+def sum_query(size, left, right, units):
     tokens, depth = left.shape
     width = right.shape[1] // PARTS
     rows = depth // size
-    lane_width = sums.shape[2] * PARTS // lanes
     any_space = pl.BlockSpec(memory_space=pl.ANY)
     vmem = pl.BlockSpec(memory_space=pltpu.VMEM)
     return pl.pallas_call(
-        functools.partial(sum_query_kernel, size, lanes),
+        functools.partial(sum_query_kernel, size),
         out_shape=(
             jax.ShapeDtypeStruct((PARTS, rows, width), jnp.float32),
             jax.ShapeDtypeStruct((size, *units.shape[:2], rows), jnp.bfloat16),
-            jax.ShapeDtypeStruct((rows, lane_width), jnp.float32),
-        ),
-        in_specs=[any_space] * 3 + [vmem],
-        out_specs=(vmem, any_space, vmem),
+        ),
+        in_specs=[any_space] * 3,
+        out_specs=(vmem, any_space),
         scratch_shapes=[
             pltpu.VMEM((tokens, depth), jnp.bfloat16),
             pltpu.VMEM((PARTS, tokens, width), jnp.bfloat16),
             pltpu.SemaphoreType.DMA((PARTS + 1,)),
             *units_scratch(size, units.shape[0]),
-            *lanes_scratch(lanes, rows, lane_width),
             *scatter_scratch(size, rows, width),
         ],
         compiler_params=pltpu.CompilerParams(
@@ -1067,7 +1060,7 @@
             flops=4 * tokens * depth * width, bytes_accessed=100 * 1024 * 1024, transcendentals=0
         ),
         name="sum_query",
-    )(left, right, units, sums)
+    )(left, right, units)
 
 
 def sum_key_kernel(
@@ -1078,20 +1071,23 @@
     kv_ref,
     w_ref,
     units_ref,
-    sums_ref,
-    out,
+    out_sums,
+    query_sums,
+    pair_out,
     low,
     back,
     lane_out,
+    lane_query,
     left,
     right,
     loads,
     tiles,
     fetch,
+    out,
     *refs,
 ):
-    units_sems, lane_refs = (refs[:3], refs[3:7])
-    made, held, sent, came, *sems = refs[7:]
+    units_sems, lane_refs = (refs[:3], refs[3:11])
+    made, held, sent, came, *sems = refs[11:]
     me, z = (lax.axis_index("fsdp"), lax.axis_index("tp"))
     rows = left.shape[1] // size
     parts, span = (w_ref.shape[1], tiles.shape[-1])
@@ -1139,13 +1135,16 @@
             low[span_rows, f * rows : (f + 1) * rows] = total
 
     units = Units(size, me, units_ref, back, units_sems)
-    across = Lanes(lanes, z, sums_ref, lane_out, *lane_refs)
+    across = (
+        Lanes(lanes, z, out_sums, lane_out, *lane_refs[:4]),
+        Lanes(lanes, z, query_sums, lane_query, *lane_refs[4:]),
+    )
     calls, finish = scatter_steps(size, me, made, held, sent, came, sems, partial, out)
     done = 0
     for number, call in enumerate(calls):
         call()
-        if number == 1:
-            across.start()
+        if number < 2:
+            across[number].start()
         if number == len(calls) // 2:
             units.start()
         goal = size * max(0, number - 1) // max(1, len(calls) - 3)
@@ -1155,38 +1154,42 @@
     while done < size:
         low_columns(done)
         done += 1
-    across.finish()
+    for one in across:
+        one.finish()
     units.finish()
     finish()
-
-
-def sum_key(size, lanes, left, grad_query, grad_pair, weights, units, sums):
+    pair_out[...] = out[...].astype(jnp.bfloat16)
+
+
+def sum_key(size, lanes, left, grad_query, grad_pair, weights, units, *sums):
     tokens, depth = left.shape
     width = grad_pair.shape[2]
     rows = depth // size
     parts = weights.shape[1]
     span = (grad_query.shape[1] + PARTS * width) // parts
-    lane_width = sums.shape[2] * PARTS // lanes
+    lane_width = sums[0].shape[2] * PARTS // lanes
     any_space = pl.BlockSpec(memory_space=pl.ANY)
     vmem = pl.BlockSpec(memory_space=pltpu.VMEM)
     return pl.pallas_call(
         functools.partial(sum_key_kernel, size, lanes),
         out_shape=(
-            jax.ShapeDtypeStruct((PARTS, rows, width), jnp.float32),
+            jax.ShapeDtypeStruct((PARTS, rows, width), jnp.bfloat16),
             jax.ShapeDtypeStruct((tokens, depth), jnp.float32),
             jax.ShapeDtypeStruct((size, *units.shape[:2], rows), jnp.bfloat16),
-            jax.ShapeDtypeStruct((rows, lane_width), jnp.float32),
-        ),
-        in_specs=[any_space, vmem, any_space, any_space, any_space, vmem],
-        out_specs=(vmem, vmem, any_space, vmem),
+            *[jax.ShapeDtypeStruct((rows, lane_width), jnp.float32)] * 2,
+        ),
+        in_specs=[any_space, vmem, any_space, any_space, any_space, vmem, vmem],
+        out_specs=(vmem, vmem, any_space, vmem, vmem),
         scratch_shapes=[
             pltpu.VMEM((tokens, depth), jnp.bfloat16),
             pltpu.VMEM((PARTS, tokens, width), jnp.bfloat16),
             pltpu.SemaphoreType.DMA((PARTS + 1,)),
             pltpu.VMEM((2, parts, rows, span), jnp.bfloat16),
             pltpu.SemaphoreType.DMA((2,)),
+            pltpu.VMEM((PARTS, rows, width), jnp.float32),
             *units_scratch(size, units.shape[0]),
-            *lanes_scratch(lanes, rows, lane_width),
+            *lanes_scratch(lanes, (rows, lane_width)),
+            *lanes_scratch(lanes, (rows, lane_width)),
             *scatter_scratch(size, rows, width),
         ],
         compiler_params=pltpu.CompilerParams(
@@ -1196,10 +1199,11 @@
             flops=8 * tokens * depth * width, bytes_accessed=100 * 1024 * 1024, transcendentals=0
         ),
         name="sum_key",
-    )(left, grad_query, grad_pair, weights, units, sums)
-
-
-def sum_small_kernel(size, lanes, x_ref, o_ref, came, send, recv):
+    )(left, grad_query, grad_pair, weights, units, *sums)
+
+
+def sum_small_kernel(size, lanes, sizes, x_ref, *refs):
+    outs, (came, send, recv) = (refs[: len(sizes)], refs[len(sizes) :])
     me, z = (lax.axis_index("fsdp"), lax.axis_index("tp"))
     peers = []
     for name, index, count in (("fsdp", me, size), ("tp", z, lanes)):
@@ -1225,17 +1229,20 @@
         copy.start()
         copy.wait()
         came[sent + step + 1] = came[sent + step] + came[step]
-    o_ref[...] = came[sent + len(peers)]
-
-
-def sum_small(size, lanes, values):
+    start = 0
+    for out, rows in zip(outs, sizes):
+        out[...] = came[sent + len(peers), start : start + rows]
+        start += rows
+
+
+def sum_small(size, lanes, values, sizes):
     steps = (size * lanes).bit_length() - 1
     vmem = pl.BlockSpec(memory_space=pltpu.VMEM)
     return pl.pallas_call(
-        functools.partial(sum_small_kernel, size, lanes),
-        out_shape=jax.ShapeDtypeStruct(values.shape, values.dtype),
+        functools.partial(sum_small_kernel, size, lanes, sizes),
+        out_shape=tuple(jax.ShapeDtypeStruct((rows, values.shape[1]), values.dtype) for rows in sizes),
         in_specs=[vmem],
-        out_specs=vmem,
+        out_specs=(vmem,) * len(sizes),
         scratch_shapes=[
             pltpu.VMEM((2 * (steps + 1), *values.shape), values.dtype),
             pltpu.SemaphoreType.DMA((steps,)),
@@ -1251,7 +1258,7 @@
 ):
     back, own, _ = before_ref.shape
     lead = back * own
-    tile = min(256, own)
+    tile = min(512, own)
     z = lax.axis_index("tp")
 
     @pl.when(pl.program_id(0) == 0)
@@ -1398,10 +1405,10 @@
 
 
 def head_probs(query, keys, bias, group, scale):
-    scores = contract_last(query, keys) * scale
+    scores = contract_last(query, keys) * (scale * LOG2E)
     rows, span = scores.shape
     scores = (scores.reshape(group, rows // group, span) + bias[None]).reshape(rows, span)
-    weights = jnp.exp(scores - jnp.max(scores, axis=-1, keepdims=True))
+    weights = jnp.exp2(scores)
     return weights * (1.0 / jnp.sum(weights, axis=-1, keepdims=True))
 
 
@@ -1737,12 +1744,6 @@
     cosine = jnp.concatenate((cosine, cosine), axis=1)
     sine = jnp.concatenate((-sine, sine), axis=1)
     return (bias, cosine, sine, step, live[lead:].astype(jnp.float32))
-
-
-def over_lanes(grad):
-    return lax.psum_scatter(
-        grad.astype(jnp.bfloat16), "tp", scatter_dimension=2, tiled=True
-    ).astype(jnp.float32)
 
 
 def shards(
@@ -1796,7 +1797,7 @@
     whole_two, gate, up, product = gate_up(
         n_fsdp, (normed_two * norm_mlp).astype(jnp.bfloat16), units_pair
     )
-    outputs = hidden_one + sum_products(n_fsdp, 2, (product,), units_down)
+    outputs = hidden_one + sum_products(n_fsdp, 2, (product,), ((units_down, 0),))
     errors = (outputs - teacher.astype(jnp.float32)) * live[:, None]
     squares = jnp.sum(errors * errors)
     grad_out = errors * (2.0 / (count * D))
@@ -1805,7 +1806,7 @@
         n_fsdp, grad_out.astype(jnp.bfloat16), units_down, gate, up, product, whole_two
     )
     units_early = lax.psum_scatter(units_early, "tp", scatter_dimension=0)
-    grad_mid = sum_products(n_fsdp, 4, (grad_gate, grad_up), units_pair)
+    grad_mid = sum_products(n_fsdp, 4, (grad_gate, grad_up), ((units_pair, 0), (units_pair, 1)))
     grad_norm_mlp = jnp.sum(grad_mid * normed_two, axis=0)
     grad_hidden = grad_out + norm_back(grad_mid, normed_two, factor_two, norm_mlp)
 
@@ -1829,13 +1830,18 @@
     )
     units_late, grad_query = lax.optimization_barrier((units_late, grad_query))
     units_late = lax.psum_scatter(units_late, "tp", scatter_dimension=0)
-    sums_query, back_early, grad_w_out = sum_query(
-        n_fsdp, n_tp, normed_in, grad_query, units_early, sums_out
+    sums_query, back_early = sum_query(n_fsdp, normed_in, grad_query, units_early)
+    sums_pair, grad_low, back_late, grad_w_out, grad_w_query = sum_key(
+        n_fsdp,
+        n_tp,
+        normed_in,
+        grad_query,
+        grad_pair,
+        weights_attn,
+        units_late,
+        sums_out,
+        sums_query,
     )
-    sums_pair, grad_low, back_late, grad_w_query = sum_key(
-        n_fsdp, n_tp, normed_in, grad_query, grad_pair, weights_attn, units_late, sums_query
-    )
-    grad_w_pair = over_lanes(sums_pair)
     grad_w_down, grad_w_gate, grad_w_up = [
         part.reshape(-1, part.shape[2]).astype(jnp.float32)
         for part in (back_early[:, 0], back_early[:, 1], back_late[:, 0])
@@ -1843,15 +1849,22 @@
     normed_one, factor_one = normalize_rows(inputs)
     grad_norm_attn = jnp.sum(grad_low * normed_one, axis=0)
     grad_input = grad_hidden + norm_back(grad_low, normed_one, factor_one, norm_attn)
-    small = [grad_norm_attn, grad_norm_mlp, grad_norm_query[0], grad_norm_key[0]]
-    small.append(jnp.full((HD,), squares))
-    joined_small = jnp.concatenate(small).reshape(-1, HD)
-    filled = joined_small.shape[0]
-    joined_small = jnp.pad(joined_small, ((0, -filled % 8), (0, 0)))
-    summed = sum_small(n_fsdp, n_tp, joined_small)[:filled].reshape(-1)
-    grad_norm_attn, grad_norm_mlp = (summed[:D], summed[D : 2 * D])
-    grad_norm_query, grad_norm_key = (summed[2 * D : 2 * D + HD], summed[2 * D + HD : 2 * D + 2 * HD])
-    squares = summed[2 * D + 2 * HD]
+    lines = D // HD
+    small = [
+        grad_norm_attn.reshape(lines, HD),
+        grad_norm_mlp.reshape(lines, HD),
+        grad_norm_query,
+        grad_norm_key,
+        jnp.full((6, HD), squares),
+    ]
+    small, grad_input, grad_w_down, grad_w_gate, grad_w_up = lax.optimization_barrier(
+        (jnp.concatenate(small, axis=0), grad_input, grad_w_down, grad_w_gate.T, grad_w_up.T)
+    )
+    grad_norm_attn, grad_norm_mlp, rest = sum_small(n_fsdp, n_tp, small, (lines, lines, 8))
+    grad_norm_attn, grad_norm_mlp = (grad_norm_attn.reshape(D), grad_norm_mlp.reshape(D))
+    grad_norm_query, grad_norm_key, squares = (rest[0], rest[1], rest[2, 0])
+    grad_w_pair = lax.psum_scatter(sums_pair, "tp", scatter_dimension=2, tiled=True)
+    grad_w_pair = grad_w_pair.astype(jnp.float32)
     return (
         outputs,
         squares / (count * D),
@@ -1864,8 +1877,8 @@
         grad_norm_key,
         grad_w_out.T,
         grad_norm_mlp,
-        grad_w_gate.T,
-        grad_w_up.T,
+        grad_w_gate,
+        grad_w_up,
         grad_w_down,
     )
 

time: 998 us -> 966 us (0.968)
  Pallas kernels: 862 us -> 833 us
    reduce_scatter x1, waiting for transfers between devices: 11.6 us -> 0.01 us  [shards(): units_late = lax.psum_scatter(units_late, 'tp', scatter_dimension=0)]
    all_gather x1, waiting for transfers between devices: 22.7 us -> 32.9 us  [shards(): units_pair = lax.all_gather(mine_pair, 'tp', axis=0)]
  transfers between devices with their start and end apart: 5 -> 5, of which waited for: 3 -> 1; matrix products, arithmetic and copies ran while one was open for 4% -> 5% of each run, Pallas kernels for 46% -> 47%
where the time goes in v7:
time: 966 us; the launch traced here: 959 us
  Pallas kernels  833 us (86%)
  other arithmetic  47.3 us (5%)
  waiting for transfers between devices  33.7 us (3%)
  local copies, waits for them, and re-layouts  27.2 us (3%)
  between operations  17.5 us (2%)
    pallas_call x2, Pallas kernels, sum_products(): pl.pallas_call(functools.partial(sum_products_kernel, size, tuple((kind f...  171 us
    pallas_call x1, Pallas kernels, enter(): pl.pallas_call(functools.partial(enter_kernel, size, lanes, back), out_sh...  142 us
    pallas_call x1, Pallas kernels, attend_back(): pl.pallas_call(functools.partial(attend_back_kernel, group, step, lead, s...  112 us
    pallas_call x1, Pallas kernels, grad_hidden_units(): pl.pallas_call(functools.partial(grad_hidden_kernel, size), out_shape=(sh...  100 us
    pallas_call x1, Pallas kernels, gate_up(): pl.pallas_call(functools.partial(gate_up_kernel, size), out_shape=(shape(...  82.2 us
    pallas_call x1, Pallas kernels, sum_query(): pl.pallas_call(functools.partial(sum_query_kernel, size), out_shape=(jax....  60.4 us
    pallas_call x1, Pallas kernels, sum_key(): pl.pallas_call(functools.partial(sum_key_kernel, size, lanes), out_shape=...  56.9 us
    pallas_call x1, Pallas kernels, attend(): pl.pallas_call(functools.partial(attend_kernel, group, step, rows - own),...  43.6 us
  transfers between devices with their start and end apart: 5, of which 1 were waited for; matrix products, arithmetic and copies ran while one was open for 5% of the time, Pallas kernels for 47%

profile of v7, /device:TPU:0, one launch (start us, length us, event | category | flops | bytes accessed | tf_op | source)
XLA Modules:
  0.0 958.9 jit_solution(14502286879137782664)
XLA Ops:
  16.5 141.5 %enter.1 = (bf16[2,512,2048]{2,1,0:T(8,128)(2,1)}, bf16[8,4,256,1536]{3,2,1,0:T(8,128)(2,1)}, bf16[2,192,2048]{2,1,0:T(8,128)(2,1)}, bf16[1,192,2048]{2,1,0:T(8,128)(2,1)}, f32[8,128]{1,0:T(8,128)}) custom-call(bf16[512,2048]{1,0:T(8,128)(2,1)} %x_ref.5, bf16[256,1536]{1,0:T(8,128)(2,1)} %pad_maximum_fusion.1.w_ref, ...), custom_call_target="tpu_custom_call" | custom-call | bytes 419430400 | tf_op jit(solution)/shard_map/enter/pallas_call | solution.py:859
  162.5 2.8 fusion.16
  165.4 28.4 %project_in.1 = (bf16[512,2048]{1,0:T(8,128)(2,1)}, f32[512,2048]{1,0:T(8,128)}, f32[1536,1024]{1,0:T(8,128)}, bf16[1536,1024]{1,0:T(8,128)(2,1)}) custom-call(bf16[2,512,2048]{2,1,0:T(8,128)(2,1)} %get-tuple-element.53.before_ref, bf16[512,2048]{1,0:T(8,128)(2,1)} %x_ref.5, f32[1,2048]{1,0:T(1,128)} %bitcast.72, ...), custom_call_target="tpu_custom_call" | custom-call | flops 17179869184 | bytes 23068672 | tf_op jit(solution)/shard_map/project_in/pallas_call | solution.py:1302
  195.4 43.6 %attend.1.a_ref.right_ref = bf16[512,2048]{1,0:T(8,128)(2,1)} custom-call(f32[512,2048]{1,0:T(8,128)} %get-tuple-element.55.q_ref, f32[1536,1024]{1,0:T(8,128)} %get-tuple-element.56.k_ref, bf16[1536,1024]{1,0:T(8,128)(2,1)} %get-tuple-element.57.v_ref, f32[512,1280]{1,0:T(8,128)} %add_select_fusion.bias_ref, f32[1536,128]{1,0:T(8,128)} %get-tuple-element.167.cos_ref, ...), custom_call_target="tpu_custom_call" | custom-call | flops 21474836480 | bytes 13631488 | tf_op jit(solution)/shard_map/attend/pallas_call | solution.py:1635
  241.0 11.5 %project_out.1 = f32[512,2048]{1,0:T(8,128)} custom-call(bf16[512,2048]{1,0:T(8,128)(2,1)} %attend.1.a_ref.right_ref, bf16[8,4,256,1536]{3,2,1,0:T(8,128)(2,1)} %get-tuple-element.54.w_ref, bf16[512,2048]{1,0:T(8,128)(2,1)} %x_ref.5), custom_call_target="tpu_custom_call" | custom-call | flops 4294967296 | bytes 25165824 | tf_op jit(solution)/shard_map/project_out/pallas_call | solution.py:1346
  252.5 2.7 multiply_reduce_fusion.2
  257.6 32.9 %all-gather.5.cloned.1.call-done = bf16[8,192,2048]{2,1,0:T(8,128)(2,1)} async-done(((bf16[2,192,2048]{2,1,0:T(8,128)(2,1)}), bf16[8,192,2048]{2,1,0:T(8,128)(2,1)}) %all-gather.5.cloned.1.call-update) | async-done | bytes 6291472 | tf_op jit(solution)/shard_map/all_gather | solution.py:1787
  290.6 82.2 %gate_up.1 = (bf16[8,2,256,2048]{3,2,1,0:T(8,128)(2,1)}, f32[8,2,256,768]{3,2,1,0:T(8,128)}, f32[8,2,256,768]{3,2,1,0:T(8,128)}, bf16[8,2,256,768]{3,2,1,0:T(8,128)(2,1)}) custom-call(bf16[2,256,2048]{2,1,0:T(8,128)(2,1)} %bitcast.61, bf16[4,2,192,2048]{3,2,1,0:T(8,128)(2,1)} %bitcast.80), custom_call_target="tpu_custom_call" | custom-call | flops 25769803776 | bytes 209715200 | tf_op jit(solution)/shard_map/gate_up/pallas_call | solution.py:392
  372.9 82.3 %sum_products.2 = f32[2,256,2048]{2,1,0:T(8,128)} custom-call(bf16[8,2,256,768]{3,2,1,0:T(8,128)(2,1)} %get-tuple-element.59.refs_0_.prod_in, bf16[4,1,192,2048]{3,2,1,0:T(8,128)(2,1)} %bitcast.83), custom_call_target="tpu_custom_call" | custom-call | flops 12884901888 | bytes 209715200 | tf_op jit(solution)/shard_map/sum_products/pallas_call | solution.py:667
  455.2 4.4 multiply_reduce_fusion
  462.3 100.4 %grad_hidden_units.1 = (bf16[8,2,256,768]{3,2,1,0:T(8,128)(2,1)}, bf16[8,2,256,768]{3,2,1,0:T(8,128)(2,1)}, bf16[4,2,192,2048]{3,2,1,0:T(8,128)(2,1)}, bf16[4,1,192,2048]{3,2,1,0:T(8,128)(2,1)}) custom-call(bf16[2,256,2048]{2,1,0:T(8,128)(2,1)} %bitcast.60, bf16[4,1,192,2048]{3,2,1,0:T(8,128)(2,1)} %bitcast.84, ...), custom_call_target="tpu_custom_call" | custom-call | flops 51539607552 | bytes 209715200 | tf_op jit(solution)/shard_map/grad_hidden_units/pallas_call | solution.py:575
  562.8 88.7 %sum_products.3 = f32[2,256,2048]{2,1,0:T(8,128)} custom-call(bf16[8,2,256,768]{3,2,1,0:T(8,128)(2,1)} %get-tuple-element.67.refs_0_, bf16[8,2,256,768]{3,2,1,0:T(8,128)(2,1)} %get-tuple-element.68.refs_1_, bf16[4,2,192,2048]{3,2,1,0:T(8,128)(2,1)} %bitcast.81, bf16[4,2,192,2048]{3,2,1,0:T(8,128)(2,1)} %bitcast.82), custom_call_target="tpu_custom_call" | custom-call | flops 25769803776 | bytes 209715200 | tf_op jit(solution)/shard_map/sum_products/pallas_call | solution.py:667
  651.5 3.3 fusion.9
  656.4 4.4 fusion.22
  660.7 8.9 back_out.1.do_ref
  669.6 112.3 %attend_back.1 = (bf16[512,2048]{1,0:T(8,128)(2,1)}, bf16[2,512,1024]{2,1,0:T(8,128)(2,1)}, f32[1,128]{1,0:T(1,128)}, f32[1,128]{1,0:T(1,128)}, f32[2,256,1024]{2,1,0:T(8,128)}) custom-call(f32[512,2048]{1,0:T(8,128)} %get-tuple-element.55.q_ref, f32[1536,1024]{1,0:T(8,128)} %get-tuple-element.56.k_ref, bf16[1536,1024]{1,0:T(8,128)(2,1)} %get-tuple-element.57.v_ref, ...), custom_call_target="tpu_custom_call" | custom-call | flops 53687091200 | bytes 33554432 | tf_op jit(solution)/shard_map/attend_back/pallas_call | solution.py:1679
  784.0 60.4 %sum_query.1 = (f32[2,256,1024]{2,1,0:T(8,128)}, bf16[8,2,192,256]{3,2,1,0:T(8,128)(2,1)}) custom-call(bf16[512,2048]{1,0:T(8,128)(2,1)} %get-tuple-element.61.left_ref, bf16[512,2048]{1,0:T(8,128)(2,1)} %get-tuple-element.70.right_ref.q_ref, bf16[2,192,2048]{2,1,0:T(8,128)(2,1)} %bitcast.85), custom_call_target="tpu_custom_call" | custom-call | flops 4294967296 | bytes 104857600 | tf_op jit(solution)/shard_map/sum_query/pallas_call | solution.py:1041
  847.2 3.0 copy.44
  850.2 56.9 %sum_key.1 = (bf16[2,256,1024]{2,1,0:T(8,128)(2,1)}, f32[512,2048]{1,0:T(8,128)}, bf16[8,1,192,256]{3,2,1,0:T(8,128)(2,1)}, f32[256,512]{1,0:T(8,128)}, f32[256,512]{1,0:T(8,128)}) custom-call(bf16[512,2048]{1,0:T(8,128)(2,1)} %get-tuple-element.61.left_ref, bf16[512,2048]{1,0:T(8,128)(2,1)} %get-tuple-element.70.right_ref.q_ref, ...), custom_call_target="tpu_custom_call" | custom-call | flops 8589934592 | bytes 104857600 | tf_op jit(solution)/shard_map/sum_key/pallas_call | solution.py:1173
  907.2 2.4 bitcast_convert_fusion
  909.6 3.0 copy.45
  912.6 3.3 fusion.4
  919.7 6.6 fusion.7
  926.3 15.4 %sum_small.1 = (f32[16,128]{1,0:T(8,128)}, f32[16,128]{1,0:T(8,128)}, f32[8,128]{1,0:T(8,128)}) custom-call(f32[40,128]{1,0:T(8,128)} %concatenate.23.x_ref), custom_call_target="tpu_custom_call" | custom-call | tf_op jit(solution)/shard_map/sum_small/pallas_call | solution.py:1241
  (97 shorter events, 40.0 us)
Async XLA Ops:
  7.2 6.1 copy-start.8
  7.2 7.8 copy-start.12
  7.2 7.7 copy-start.13
  7.2 7.7 copy-start.11
  7.2 283.4 %all-gather.5.cloned.1.call-start = ((), (), s32[]{:S(2)}) async-start(), calls=%async_computation.6 | async-start | bytes 7864320 | tf_op jit(solution)/shard_map/all_gather | solution.py:1787
  15.9 143.0 %copy-start.19 = (s32[1,4]{1,0:T(1,128)S(1)}, s32[1,4]{1,0:T(1,128)}, u32[]{:S(2)}) copy-start(s32[1,4]{1,0:T(1,128)} %param.16) | copy-start | bytes 52
  15.9 143.4 %copy-start.15 = (s32[1,2048]{1,0:T(1,128)S(1)}, s32[1,2048]{1,0:T(1,128)}, u32[]{:S(2)}) copy-start(s32[1,2048]{1,0:T(1,128)} %param.17) | copy-start | bytes 24580
  158.0 214.8 %all-gather.7.cloned.1.call-start = ((), (), s32[]{:S(2)}) async-start(), calls=%async_computation.7 | async-start | bytes 3932160 | tf_op jit(solution)/shard_map/all_gather | solution.py:1788
  158.8 625.2 %reduce-scatter.6.cloned.1.call-start = ((), (), s32[]{:S(2)}) async-start(), calls=%async_computation.4 | async-start | bytes 7864320 | tf_op jit(solution)/shard_map/reduce_scatter | solution.py:1808
  241.0 14.2 %copy-start.14 = (f32[2048]{0:T(1024)S(1)}, f32[2048]{0:T(1024)}, u32[]{:S(2)}) copy-start(f32[2048]{0:T(1024)} %param.26) | copy-start | bytes 24580
  252.5 3.5 copy-start
  372.8 82.4 %copy-start.1 = (f32[512,2048]{1,0:T(8,128)S(1)}, f32[512,2048]{1,0:T(8,128)}, u32[]{:S(2)}) copy-start(f32[512,2048]{1,0:T(8,128)} %project_out.1) | copy-start | bytes 12582916
  372.9 82.4 %copy-start.6 = (bf16[512,2048]{1,0:T(8,128)(2,1)S(1)}, bf16[512,2048]{1,0:T(8,128)(2,1)}, u32[]{:S(2)}) copy-start(bf16[512,2048]{1,0:T(8,128)(2,1)} %param.18) | copy-start | bytes 6291460
  459.6 2.6 copy-start.4
  562.7 287.5 %reduce-scatter.4.cloned.1.call-start = ((), (), s32[]{:S(2)}) async-start(), calls=%async_computation.3 | async-start | bytes 3932160 | tf_op jit(solution)/shard_map/reduce_scatter | solution.py:1832
  562.7 88.7 %copy-start.2 = (f32[512,2048]{1,0:T(8,128)S(1)}, f32[512,2048]{1,0:T(8,128)}, u32[]{:S(2)}) copy-start(f32[512,2048]{1,0:T(8,128)} %project_out.1) | copy-start | bytes 12582916
  651.5 3.6 copy-start.5
  651.5 4.9 copy-start.7
  781.9 163.9 %reduce-scatter.8.cloned.1.call-start = ((), (), s32[]{:S(2)}) async-start(), calls=%async_computation.5 | async-start | bytes 1310720 | tf_op jit(solution)/shard_map/reduce_scatter | solution.py:1866
  907.2 5.5 copy-start.16
  912.6 4.0 copy-start.17
  912.6 4.0 copy-start.18
  919.7 23.9 %copy-start.10 = (f32[256,512]{1,0:T(8,128)S(1)}, f32[256,512]{1,0:T(8,128)}, u32[]{:S(2)}) copy-start(f32[256,512]{1,0:T(8,128)} %get-tuple-element.87) | copy-start | bytes 1572868
  919.7 29.3 %copy-start.9 = (f32[256,512]{1,0:T(8,128)S(1)}, f32[256,512]{1,0:T(8,128)}, u32[]{:S(2)}) copy-start(f32[256,512]{1,0:T(8,128)} %get-tuple-element.187) | copy-start | bytes 1572868
  (1 other events, 1.6 us)
Sparse Core Ops, SparseCore 0:
  158.2 132.3 all-gather.4
  292.1 61.7 all-gather.6
  562.8 107.9 reduce-scatter.5
  782.1 59.2 reduce-scatter.3
  912.7 26.0 reduce-scatter.7

commit v8 on v7

--- a/solution.py
+++ b/solution.py
@@ -433,7 +433,6 @@
     dgate_out,
     dup_out,
     early_out,
-    late_out,
     whole,
     wd_ref,
     gate,
@@ -537,7 +536,6 @@
                 (
                     ((prod.at[here, 0], prod.at[here, 1]), (whole.at[pair[0], 0], whole.at[pair[1], 1])),
                     ((dgate.at[0], dgate.at[1]), (two.at[here, 0], two.at[here, 1])),
-                    ((dup.at[0], dup.at[1]), (two.at[here, 0], two.at[here, 1])),
                 )
             ):
                 total = contract_first(lefts[0][:, units], rights[0][...])
@@ -552,12 +550,11 @@
         for copy in stores(part, order[-1][part]):
             copy.wait()
     copies = []
-    for piece in range(3 * lanes):
+    for piece in range(2 * lanes):
         kind, lane = (piece // lanes, piece % lanes)
         block = whole.at[piece // PARTS, piece % PARTS, pl.ds(0, each)]
         block[...] = sums[kind, lane * each : (lane + 1) * each, :].astype(jnp.bfloat16)
-        out = early_out.at[lane, kind] if kind < 2 else late_out.at[lane, 0]
-        copy = pltpu.make_async_copy(block, out, flush.at[piece])
+        copy = pltpu.make_async_copy(block, early_out.at[lane, kind], flush.at[piece])
         copy.start()
         copies.append(copy)
     for copy in copies:
@@ -571,12 +568,12 @@
     any_space = pl.BlockSpec(memory_space=pl.ANY)
     shape = lambda columns, kind: jax.ShapeDtypeStruct((size, PARTS, rows, columns), kind)
     blocks = lambda array: array.reshape(size, PARTS, rows, -1)
-    weight = lambda kinds: jax.ShapeDtypeStruct((lanes, kinds, each, width), jnp.bfloat16)
-    dgate, dup, early, late = pl.pallas_call(
+    weights = jax.ShapeDtypeStruct((lanes, 2, each, width), jnp.bfloat16)
+    dgate, dup, early = pl.pallas_call(
         functools.partial(grad_hidden_kernel, size),
-        out_shape=(shape(hidden, jnp.bfloat16), shape(hidden, jnp.bfloat16), weight(2), weight(1)),
+        out_shape=(shape(hidden, jnp.bfloat16), shape(hidden, jnp.bfloat16), weights),
         in_specs=[any_space] * 6,
-        out_specs=(any_space,) * 4,
+        out_specs=(any_space,) * 3,
         scratch_shapes=[
             pltpu.VMEM((size, PARTS, rows, width), jnp.bfloat16),
             pltpu.VMEM((hidden, width), jnp.bfloat16),
@@ -586,22 +583,22 @@
             pltpu.VMEM((2, PARTS, rows, width), jnp.bfloat16),
             pltpu.VMEM((PARTS, rows, hidden), jnp.bfloat16),
             pltpu.VMEM((PARTS, rows, hidden), jnp.bfloat16),
-            pltpu.VMEM((3, hidden, width), jnp.float32),
+            pltpu.VMEM((2, hidden, width), jnp.float32),
             pltpu.SemaphoreType.DMA((1 + lanes,)),
             pltpu.SemaphoreType.DMA((2, PARTS, 4)),
             pltpu.SemaphoreType.DMA((PARTS, 2)),
-            pltpu.SemaphoreType.DMA((3 * lanes,)),
+            pltpu.SemaphoreType.DMA((2 * lanes,)),
             *gather_semaphores(size),
         ],
         compiler_params=pltpu.CompilerParams(
             collective_id=3, has_side_effects=True, vmem_limit_bytes=60 * 1024 * 1024
         ),
         cost_estimate=pl.CostEstimate(
-            flops=8 * size * own * width * hidden, bytes_accessed=200 * 1024 * 1024, transcendentals=0
+            flops=6 * size * own * width * hidden, bytes_accessed=200 * 1024 * 1024, transcendentals=0
         ),
         name="grad_hidden_units",
     )(values.reshape(PARTS, rows, width), units, *map(blocks, (gate, up, product, whole_two)))
-    return (dgate.reshape(size * own, hidden), dup.reshape(size * own, hidden), early, late)
+    return (dgate.reshape(size * own, hidden), dup.reshape(size * own, hidden), early)
 
 
 def sum_products_kernel(size, kinds, *refs):
@@ -685,6 +682,155 @@
         name="sum_products",
     )(*[left.reshape(size, PARTS, rows, hidden) for left in lefts], *[array for array, _ in units])
     return out.reshape(PARTS * rows, width)
+
+
+def sum_gradients_kernel(
+    size,
+    dgate_in,
+    dup_in,
+    two_in,
+    wg_in,
+    wu_in,
+    out,
+    units_out,
+    lefts,
+    two,
+    wg_ref,
+    wu_ref,
+    sums,
+    w_load,
+    fetch,
+    flush,
+    made,
+    held,
+    sent,
+    came,
+    *sems,
+):
+    me = lax.axis_index("fsdp")
+    lanes, _, each, _ = units_out.shape
+    hidden = wg_ref.shape[0]
+    chunk = 256 if hidden % 256 == 0 else 128
+    weights = unit_loads(wg_in, 0, wg_ref, w_load.at[0]) + unit_loads(wu_in, 1, wu_ref, w_load.at[1])
+    order = [bits[::-1] for bits in orders(size)]
+    patterns = scatter_order(len(order[0]))
+    state = {"block": 0, "first": True}
+    taken = []
+
+    def fetches(q, sibling, part, kinds=(0, 1, 2)):
+        slot = flip(me, mask_of(patterns[q], order[part]) + sibling)
+        block = 1 - sibling
+        pairs = (
+            (dgate_in, lefts.at[0, block, part]),
+            (dup_in, lefts.at[1, block, part]),
+            (two_in, two.at[block, part]),
+        )
+        return [
+            pltpu.make_async_copy(
+                pairs[i][0].at[slot, part], pairs[i][1], fetch.at[block, part, i]
+            )
+            for i in kinds
+        ]
+
+    def fetch_all(q):
+        for sibling in (1, 0):
+            for part in range(PARTS):
+                for copy in fetches(q, sibling, part):
+                    copy.start()
+
+    def ready(part, slot, q, sibling):
+        if state["first"]:
+            for copy in weights:
+                copy.wait()
+        state["first"], state["block"] = (False, 1 - sibling)
+        take(q, sibling, part)
+
+    def take(q, sibling, part):
+        if (q, sibling, part) not in taken:
+            taken.append((q, sibling, part))
+            for copy in fetches(q, sibling, part, (0, 1)):
+                copy.wait()
+
+    def partial(part, slot, columns):
+        block = state["block"]
+        return dot(lefts[0, block, part], wg_ref[:, columns]) + dot(
+            lefts[1, block, part], wu_ref[:, columns]
+        )
+
+    def add_units(q):
+        for sibling in (1, 0):
+            for part in range(PARTS):
+                take(q, sibling, part)
+                fetches(q, sibling, part, (2,))[0].wait()
+
+        @pl.loop(0, hidden // chunk)
+        def _(index):
+            units = pl.ds(pl.multiple_of(index * chunk, chunk), chunk)
+            total = sums[units, :] if q else 0.0
+            for block in (0, 1):
+                for part in range(PARTS):
+                    total += contract_first(lefts[1, block, part, :, units], two[block, part])
+            sums[units, :] = total
+
+    for copy in weights:
+        copy.start()
+    fetch_all(0)
+    greet(me, size)
+    calls, finish = scatter_steps(size, me, made, held, sent, came, sems, partial, out, ready)
+    copies = []
+    for number, call in enumerate(calls):
+        if number + 1 < len(calls):
+            call()
+            if number % 2:
+                add_units(number // 2)
+                fetch_all(number // 2 + 1)
+            continue
+        add_units(number // 2)
+        for lane in range(lanes):
+            block = two.at[lane % 2, lane // 2 % PARTS, pl.ds(lane // 4 * each, each)]
+            block[...] = sums[lane * each : (lane + 1) * each, :].astype(jnp.bfloat16)
+            copies.append(pltpu.make_async_copy(block, units_out.at[lane, 0], flush.at[lane]))
+            copies[-1].start()
+        call()
+    finish()
+    for copy in copies:
+        copy.wait()
+
+
+def sum_gradients(size, grad_gate, grad_up, whole_two, units):
+    lanes, _, each, width = units.shape
+    hidden = lanes * each
+    rows = grad_gate.shape[0] // size // PARTS
+    any_space = pl.BlockSpec(memory_space=pl.ANY)
+    blocks = lambda array: array.reshape(size, PARTS, rows, -1)
+    out, late = pl.pallas_call(
+        functools.partial(sum_gradients_kernel, size),
+        out_shape=(
+            jax.ShapeDtypeStruct((PARTS, rows, width), jnp.float32),
+            jax.ShapeDtypeStruct((lanes, 1, each, width), jnp.bfloat16),
+        ),
+        in_specs=[any_space] * 5,
+        out_specs=(pl.BlockSpec(memory_space=pltpu.VMEM), any_space),
+        scratch_shapes=[
+            pltpu.VMEM((2, 2, PARTS, rows, hidden), jnp.bfloat16),
+            pltpu.VMEM((2, PARTS, rows, width), jnp.bfloat16),
+            pltpu.VMEM((hidden, width), jnp.bfloat16),
+            pltpu.VMEM((hidden, width), jnp.bfloat16),
+            pltpu.VMEM((hidden, width), jnp.float32),
+            pltpu.SemaphoreType.DMA((2, lanes)),
+            pltpu.SemaphoreType.DMA((2, PARTS, 3)),
+            pltpu.SemaphoreType.DMA((lanes,)),
+            *scatter_scratch(size, rows, width),
+        ],
+        compiler_params=pltpu.CompilerParams(
+            collective_id=4, has_side_effects=True, vmem_limit_bytes=60 * 1024 * 1024
+        ),
+        cost_estimate=pl.CostEstimate(
+            flops=6 * grad_gate.size * width, bytes_accessed=200 * 1024 * 1024, transcendentals=0
+        ),
+        name="sum_gradients",
+    )(*map(blocks, (grad_gate, grad_up, whole_two)), units, units)
+    return (out.reshape(PARTS * rows, width), late)
 
 
 def enter_kernel(
@@ -1802,11 +1948,11 @@
     squares = jnp.sum(errors * errors)
     grad_out = errors * (2.0 / (count * D))
 
-    grad_gate, grad_up, units_early, units_late = grad_hidden_units(
+    grad_gate, grad_up, units_early = grad_hidden_units(
         n_fsdp, grad_out.astype(jnp.bfloat16), units_down, gate, up, product, whole_two
     )
     units_early = lax.psum_scatter(units_early, "tp", scatter_dimension=0)
-    grad_mid = sum_products(n_fsdp, 4, (grad_gate, grad_up), ((units_pair, 0), (units_pair, 1)))
+    grad_mid, units_late = sum_gradients(n_fsdp, grad_gate, grad_up, whole_two, units_pair)
     grad_norm_mlp = jnp.sum(grad_mid * normed_two, axis=0)
     grad_hidden = grad_out + norm_back(grad_mid, normed_two, factor_two, norm_mlp)
 

time: 966 us -> 955 us (0.989)
  Pallas kernels: 833 us -> 819 us
    pallas_call x2 -> x1, Pallas kernels: 171 us -> 82.3 us  [sum_products(): pl.pallas_call(functools.partial(sum_products_kernel, size, tuple((kind f...]
    pallas_call x0 -> x1, Pallas kernels: none -> 86.2 us  [sum_gradients(): pl.pallas_call(functools.partial(sum_gradients_kernel, size), out_shape=(...]
    pallas_call x1, Pallas kernels: 100 us -> 89.3 us  [grad_hidden_units(): pl.pallas_call(functools.partial(grad_hidden_kernel, size), out_shape=(sh...]
where the time goes in v8:
time: 955 us; the launch traced here: 948 us
  Pallas kernels  819 us (86%)
  other arithmetic  49.8 us (5%)
  waiting for transfers between devices  33.8 us (4%)
  local copies, waits for them, and re-layouts  27.1 us (3%)
  between operations  17.5 us (2%)
    pallas_call x1, Pallas kernels, enter(): pl.pallas_call(functools.partial(enter_kernel, size, lanes, back), out_sh...  142 us
    pallas_call x1, Pallas kernels, attend_back(): pl.pallas_call(functools.partial(attend_back_kernel, group, step, lead, s...  112 us
    pallas_call x1, Pallas kernels, grad_hidden_units(): pl.pallas_call(functools.partial(grad_hidden_kernel, size), out_shape=(sh...  89.3 us
    pallas_call x1, Pallas kernels, sum_gradients(): pl.pallas_call(functools.partial(sum_gradients_kernel, size), out_shape=(...  86.2 us
    pallas_call x1, Pallas kernels, sum_products(): pl.pallas_call(functools.partial(sum_products_kernel, size, tuple((kind f...  82.3 us
    pallas_call x1, Pallas kernels, gate_up(): pl.pallas_call(functools.partial(gate_up_kernel, size), out_shape=(shape(...  82.2 us
    pallas_call x1, Pallas kernels, sum_query(): pl.pallas_call(functools.partial(sum_query_kernel, size), out_shape=(jax....  60.6 us
    pallas_call x1, Pallas kernels, sum_key(): pl.pallas_call(functools.partial(sum_key_kernel, size, lanes), out_shape=...  57 us
  transfers between devices with their start and end apart: 5, of which 1 were waited for; matrix products, arithmetic and copies ran while one was open for 5% of the time, Pallas kernels for 47%

profile of v8, /device:TPU:0, one launch (start us, length us, event | category | flops | bytes accessed | tf_op | source)
XLA Modules:
  0.0 948.1 jit_solution(14487160302633227684)
XLA Ops:
  16.5 141.5 %enter.1 = (bf16[2,512,2048]{2,1,0:T(8,128)(2,1)}, bf16[8,4,256,1536]{3,2,1,0:T(8,128)(2,1)}, bf16[2,192,2048]{2,1,0:T(8,128)(2,1)}, bf16[1,192,2048]{2,1,0:T(8,128)(2,1)}, f32[8,128]{1,0:T(8,128)}) custom-call(bf16[512,2048]{1,0:T(8,128)(2,1)} %x_ref.5, bf16[256,1536]{1,0:T(8,128)(2,1)} %pad_maximum_fusion.1.w_ref, ...), custom_call_target="tpu_custom_call" | custom-call | bytes 419430400 | tf_op jit(solution)/shard_map/enter/pallas_call | solution.py:1005
  162.6 2.8 fusion.16
  165.4 28.4 %project_in.1 = (bf16[512,2048]{1,0:T(8,128)(2,1)}, f32[512,2048]{1,0:T(8,128)}, f32[1536,1024]{1,0:T(8,128)}, bf16[1536,1024]{1,0:T(8,128)(2,1)}) custom-call(bf16[2,512,2048]{2,1,0:T(8,128)(2,1)} %get-tuple-element.54.before_ref, bf16[512,2048]{1,0:T(8,128)(2,1)} %x_ref.5, f32[1,2048]{1,0:T(1,128)} %bitcast.72, ...), custom_call_target="tpu_custom_call" | custom-call | flops 17179869184 | bytes 23068672 | tf_op jit(solution)/shard_map/project_in/pallas_call | solution.py:1448
  195.4 43.6 %attend.1.a_ref.right_ref = bf16[512,2048]{1,0:T(8,128)(2,1)} custom-call(f32[512,2048]{1,0:T(8,128)} %get-tuple-element.56.q_ref, f32[1536,1024]{1,0:T(8,128)} %get-tuple-element.57.k_ref, bf16[1536,1024]{1,0:T(8,128)(2,1)} %get-tuple-element.58.v_ref, f32[512,1280]{1,0:T(8,128)} %add_select_fusion.bias_ref, f32[1536,128]{1,0:T(8,128)} %get-tuple-element.169.cos_ref, ...), custom_call_target="tpu_custom_call" | custom-call | flops 21474836480 | bytes 13631488 | tf_op jit(solution)/shard_map/attend/pallas_call | solution.py:1781
  241.0 11.5 %project_out.1 = f32[512,2048]{1,0:T(8,128)} custom-call(bf16[512,2048]{1,0:T(8,128)(2,1)} %attend.1.a_ref.right_ref, bf16[8,4,256,1536]{3,2,1,0:T(8,128)(2,1)} %get-tuple-element.55.w_ref, bf16[512,2048]{1,0:T(8,128)(2,1)} %x_ref.5), custom_call_target="tpu_custom_call" | custom-call | flops 4294967296 | bytes 25165824 | tf_op jit(solution)/shard_map/project_out/pallas_call | solution.py:1492
  252.4 2.7 multiply_reduce_fusion.2
  257.6 33.0 %all-gather.5.cloned.1.call-done = bf16[8,192,2048]{2,1,0:T(8,128)(2,1)} async-done(((bf16[2,192,2048]{2,1,0:T(8,128)(2,1)}), bf16[8,192,2048]{2,1,0:T(8,128)(2,1)}) %all-gather.5.cloned.1.call-update) | async-done | bytes 6291472 | tf_op jit(solution)/shard_map/all_gather | solution.py:1933
  290.6 82.2 %gate_up.1 = (bf16[8,2,256,2048]{3,2,1,0:T(8,128)(2,1)}, f32[8,2,256,768]{3,2,1,0:T(8,128)}, f32[8,2,256,768]{3,2,1,0:T(8,128)}, bf16[8,2,256,768]{3,2,1,0:T(8,128)(2,1)}) custom-call(bf16[2,256,2048]{2,1,0:T(8,128)(2,1)} %bitcast.60, bf16[4,2,192,2048]{3,2,1,0:T(8,128)(2,1)} %bitcast.80), custom_call_target="tpu_custom_call" | custom-call | flops 25769803776 | bytes 209715200 | tf_op jit(solution)/shard_map/gate_up/pallas_call | solution.py:392
  372.8 82.3 %sum_products.1 = f32[2,256,2048]{2,1,0:T(8,128)} custom-call(bf16[8,2,256,768]{3,2,1,0:T(8,128)(2,1)} %get-tuple-element.60.refs_0_.prod_in, bf16[4,1,192,2048]{3,2,1,0:T(8,128)(2,1)} %bitcast.83), custom_call_target="tpu_custom_call" | custom-call | flops 12884901888 | bytes 209715200 | tf_op jit(solution)/shard_map/sum_products/pallas_call | solution.py:664
  455.2 4.4 multiply_reduce_fusion
  462.3 89.3 %grad_hidden_units.1 = (bf16[8,2,256,768]{3,2,1,0:T(8,128)(2,1)}, bf16[8,2,256,768]{3,2,1,0:T(8,128)(2,1)}, bf16[4,2,192,2048]{3,2,1,0:T(8,128)(2,1)}) custom-call(bf16[2,256,2048]{2,1,0:T(8,128)(2,1)} %bitcast.61, bf16[4,1,192,2048]{3,2,1,0:T(8,128)(2,1)} %bitcast.84, f32[8,2,256,768]{3,2,1,0:T(8,128)} %get-tuple-element.64.gate_in, ...), custom_call_target="tpu_custom_call" | custom-call | flops 38654705664 | bytes 209715200 | tf_op jit(solution)/shard_map/grad_hidden_units/pallas_call | solution.py:572
  551.6 86.2 %sum_gradients.1 = (f32[2,256,2048]{2,1,0:T(8,128)}, bf16[4,1,192,2048]{3,2,1,0:T(8,128)(2,1)}) custom-call(bf16[8,2,256,768]{3,2,1,0:T(8,128)(2,1)} %get-tuple-element.67.dgate_in, bf16[8,2,256,768]{3,2,1,0:T(8,128)(2,1)} %get-tuple-element.68.dup_in, bf16[8,2,256,2048]{3,2,1,0:T(8,128)(2,1)} %get-tuple-element.66.two_in, ...), custom_call_target="tpu_custom_call" | custom-call | flops 38654705664 | bytes 209715200 | tf_op jit(solution)/shard_map/sum_gradients/pallas_call | solution.py:806
  637.8 4.6 fusion.9
  643.9 5.5 fusion.22
  649.3 8.8 back_out.1.do_ref
  658.2 112.4 %attend_back.1 = (bf16[512,2048]{1,0:T(8,128)(2,1)}, bf16[2,512,1024]{2,1,0:T(8,128)(2,1)}, f32[1,128]{1,0:T(1,128)}, f32[1,128]{1,0:T(1,128)}, f32[2,256,1024]{2,1,0:T(8,128)}) custom-call(f32[512,2048]{1,0:T(8,128)} %get-tuple-element.56.q_ref, f32[1536,1024]{1,0:T(8,128)} %get-tuple-element.57.k_ref, bf16[1536,1024]{1,0:T(8,128)(2,1)} %get-tuple-element.58.v_ref, ...), custom_call_target="tpu_custom_call" | custom-call | flops 53687091200 | bytes 33554432 | tf_op jit(solution)/shard_map/attend_back/pallas_call | solution.py:1825
  772.6 60.6 %sum_query.1 = (f32[2,256,1024]{2,1,0:T(8,128)}, bf16[8,2,192,256]{3,2,1,0:T(8,128)(2,1)}) custom-call(bf16[512,2048]{1,0:T(8,128)(2,1)} %get-tuple-element.62.left_ref, bf16[512,2048]{1,0:T(8,128)(2,1)} %get-tuple-element.72.right_ref.q_ref, bf16[2,192,2048]{2,1,0:T(8,128)(2,1)} %bitcast.85), custom_call_target="tpu_custom_call" | custom-call | flops 4294967296 | bytes 104857600 | tf_op jit(solution)/shard_map/sum_query/pallas_call | solution.py:1187
  836.1 3.0 copy.44
  839.1 57.0 %sum_key.1 = (bf16[2,256,1024]{2,1,0:T(8,128)(2,1)}, f32[512,2048]{1,0:T(8,128)}, bf16[8,1,192,256]{3,2,1,0:T(8,128)(2,1)}, f32[256,512]{1,0:T(8,128)}, f32[256,512]{1,0:T(8,128)}) custom-call(bf16[512,2048]{1,0:T(8,128)(2,1)} %get-tuple-element.62.left_ref, bf16[512,2048]{1,0:T(8,128)(2,1)} %get-tuple-element.72.right_ref.q_ref, ...), custom_call_target="tpu_custom_call" | custom-call | flops 8589934592 | bytes 104857600 | tf_op jit(solution)/shard_map/sum_key/pallas_call | solution.py:1319
  896.2 2.4 bitcast_convert_fusion
  898.6 3.0 copy.45
  901.6 3.3 fusion.4
  908.7 6.6 fusion.7
  915.3 15.6 %sum_small.1 = (f32[16,128]{1,0:T(8,128)}, f32[16,128]{1,0:T(8,128)}, f32[8,128]{1,0:T(8,128)}) custom-call(f32[40,128]{1,0:T(8,128)} %concatenate.23.x_ref), custom_call_target="tpu_custom_call" | custom-call | tf_op jit(solution)/shard_map/sum_small/pallas_call | solution.py:1387
  (95 shorter events, 39.9 us)
Async XLA Ops:
  7.2 6.1 copy-start.7
  7.2 7.8 copy-start.11
  7.2 7.7 copy-start.12
  7.2 7.7 copy-start.10
  7.2 283.4 %all-gather.5.cloned.1.call-start = ((), (), s32[]{:S(2)}) async-start(), calls=%async_computation.6 | async-start | bytes 7864320 | tf_op jit(solution)/shard_map/all_gather | solution.py:1933
  15.9 143.0 %copy-start.18 = (s32[1,4]{1,0:T(1,128)S(1)}, s32[1,4]{1,0:T(1,128)}, u32[]{:S(2)}) copy-start(s32[1,4]{1,0:T(1,128)} %param.16) | copy-start | bytes 52
  15.9 143.4 %copy-start.14 = (s32[1,2048]{1,0:T(1,128)S(1)}, s32[1,2048]{1,0:T(1,128)}, u32[]{:S(2)}) copy-start(s32[1,2048]{1,0:T(1,128)} %param.17) | copy-start | bytes 24580
  158.0 214.8 %all-gather.7.cloned.1.call-start = ((), (), s32[]{:S(2)}) async-start(), calls=%async_computation.7 | async-start | bytes 3932160 | tf_op jit(solution)/shard_map/all_gather | solution.py:1934
  158.8 613.8 %reduce-scatter.6.cloned.1.call-start = ((), (), s32[]{:S(2)}) async-start(), calls=%async_computation.4 | async-start | bytes 7864320 | tf_op jit(solution)/shard_map/reduce_scatter | solution.py:1954
  241.0 14.2 %copy-start.13 = (f32[2048]{0:T(1024)S(1)}, f32[2048]{0:T(1024)}, u32[]{:S(2)}) copy-start(f32[2048]{0:T(1024)} %param.26) | copy-start | bytes 24580
  252.4 3.5 copy-start
  372.8 82.4 %copy-start.1 = (f32[512,2048]{1,0:T(8,128)S(1)}, f32[512,2048]{1,0:T(8,128)}, u32[]{:S(2)}) copy-start(f32[512,2048]{1,0:T(8,128)} %project_out.1) | copy-start | bytes 12582916
  372.8 82.4 %copy-start.6 = (bf16[512,2048]{1,0:T(8,128)(2,1)S(1)}, bf16[512,2048]{1,0:T(8,128)(2,1)}, u32[]{:S(2)}) copy-start(bf16[512,2048]{1,0:T(8,128)(2,1)} %param.18) | copy-start | bytes 6291460
  459.6 2.6 copy-start.4
  551.5 287.5 %reduce-scatter.4.cloned.1.call-start = ((), (), s32[]{:S(2)}) async-start(), calls=%async_computation.3 | async-start | bytes 3932160 | tf_op jit(solution)/shard_map/reduce_scatter | solution.py:1978
  637.8 4.6 copy-start.2
  637.8 6.0 copy-start.5
  770.5 1.6 copy-start.3
  770.6 164.5 %reduce-scatter.8.cloned.1.call-start = ((), (), s32[]{:S(2)}) async-start(), calls=%async_computation.5 | async-start | bytes 1310720 | tf_op jit(solution)/shard_map/reduce_scatter | solution.py:2012
  896.1 5.5 copy-start.15
  901.6 4.0 copy-start.16
  901.6 4.0 copy-start.17
  908.7 24.1 %copy-start.9 = (f32[256,512]{1,0:T(8,128)S(1)}, f32[256,512]{1,0:T(8,128)}, u32[]{:S(2)}) copy-start(f32[256,512]{1,0:T(8,128)} %get-tuple-element.89) | copy-start | bytes 1572868
  908.7 29.5 %copy-start.8 = (f32[256,512]{1,0:T(8,128)S(1)}, f32[256,512]{1,0:T(8,128)}, u32[]{:S(2)}) copy-start(f32[256,512]{1,0:T(8,128)} %get-tuple-element.189) | copy-start | bytes 1572868
Sparse Core Ops, SparseCore 0:
  158.2 132.3 all-gather.4
  292.1 61.7 all-gather.6
  551.7 108.0 reduce-scatter.5
  770.7 59.8 reduce-scatter.3
  901.7 26.1 reduce-scatter.7
